TPU v7x, 32 devices: a whole 2x2x4 slice. The times are simulated.
32 devices in a mesh: row: 4 (over y, core), ma: 8 (over z, x).
Axes of the slice: x: 2, y: 2, z: 4, core: 2. Of those that a mesh axis runs over, the one named last changes fastest.
Arguments:
- coeffs: float32 [2, 2048, 2048], P(None, 'ma', 'row'), may hold values from -6 to 6
- legendre: bfloat16 [2048, 32, 2048], P('ma', None, 'row'), may hold values from -0.0029296875 to 0.0029296875
- alpha_table: float32 [64, 2048], P(None, 'row'), may hold values from -4 to 4
- beta_table: float32 [64, 2048], P(None, 'row'), may hold values from -4 to 4
- radial_weight: float32 [64], replicated, may hold values from 0.1 to 1
- radius_index: int32 [64], replicated, may hold values from 0 to 63
- orders: int32 [2048], replicated, may hold values from 0 to 2047, as said below
- cycle_offset: int32 [32], P('ma'), may hold values from 0 to 1
- cycle_weight: float32 [32], P('ma'), may hold values from 0.5 to 2
Outputs:
- gradient: float32 [2, 2048, 2048], P(None, 'ma', 'row')
Inputs may be any that keep to these rules, and one draw needn't show every extreme that they name: orders names every order 0 to 2047 once. The orders 0 to 2047 fall into blocks of 16 consecutive ones; the 256 slots of each index of ma hold exactly two orders of each block, one of its lower half and its mirror in the upper half.
All inputs are finite; a program needn't handle non-finite values.
Results may differ from a plain program's by a relative error of at most 0.0049.
Values may be sent and summed in bfloat16 or wider, within the bound.
No kernel may reach another device: no remote copies, remote signals or barrier semaphores. Data moves between devices by JAX's collectives and lax.ppermute only.
A program may use at most 384 MiB of HBM per device.

v0:
```python
import math

import jax
import jax.numpy as jnp
from jax import lax
from jax.sharding import PartitionSpec as P

NPIX = 4096


def synth_rows(row_count, coeff_rows, alpha_table, beta_table, radius_index, legendre):
    filters = jnp.stack([alpha_table[radius_index], beta_table[radius_index]], axis=1)
    local_orders = coeff_rows.shape[0]
    local_degrees = coeff_rows.shape[2]
    cycle_count = legendre.shape[1]
    filtered = (filters[None, :, :, None, :] * coeff_rows[:, None, None, :, :]).astype(jnp.bfloat16)
    filtered = filtered.reshape(local_orders, row_count * 4, local_degrees)
    harmonic = lax.dot_general(
        filtered, legendre, (((2,), (2,)), ((0,), (0,))), preferred_element_type=jnp.float32
    )
    harmonic = harmonic.reshape(local_orders, row_count, 2, 2, cycle_count)
    return jnp.transpose(harmonic, (1, 4, 2, 0, 3)).reshape(
        row_count, cycle_count, 2, 2 * local_orders
    )


def cycle_work(shard_piece, orders, cycle_offset, cycle_weight):
    row_count = shard_piece.shape[0]
    cycle_local = shard_piece.shape[1]
    peer_count = shard_piece.shape[3]
    order_count = orders.shape[0]
    row_total = row_count * cycle_local * 2
    rotation = (orders[None, :] * cycle_offset[:, None]).astype(jnp.float32) * (math.pi / NPIX)
    cos_turn = jnp.cos(rotation)[None, :, None, :]
    sin_turn = jnp.sin(rotation)[None, :, None, :]
    separated = shard_piece.reshape(row_count, cycle_local, 2, order_count, 2)
    real_part = separated[..., 0]
    imag_part = separated[..., 1]
    doubling = jnp.where(orders == 0, 1.0, 2.0).astype(jnp.float32)
    rotated_re = ((cos_turn * real_part - sin_turn * imag_part) * doubling).reshape(
        row_total, order_count
    )
    rotated_im = ((sin_turn * real_part + cos_turn * imag_part) * doubling).reshape(
        row_total, order_count
    )
    block_width = 512
    block_count = NPIX // block_width
    pixel_ids = jnp.arange(block_width, dtype=jnp.int32)

    def block_step(block_id, carry):
        cos_sum, sin_sum, totals = carry
        first_pixel = block_id * block_width + pixel_ids
        phase_index = orders[:, None] * first_pixel[None, :] % NPIX
        angles = phase_index.astype(jnp.float32) * (2.0 * math.pi / NPIX)
        cos_table = jnp.cos(angles)
        sin_table = jnp.sin(angles)
        pixels = jnp.dot(
            rotated_re,
            cos_table,
            precision=lax.Precision.HIGHEST,
            preferred_element_type=jnp.float32,
        )
        pixels = pixels - jnp.dot(
            rotated_im,
            sin_table,
            precision=lax.Precision.HIGHEST,
            preferred_element_type=jnp.float32,
        )
        pixels = pixels.reshape(row_count, cycle_local, 2, block_width)
        field_a = pixels[:, :, 0]
        field_b = pixels[:, :, 1]
        products = jnp.stack([field_b * field_b, field_a * field_b], axis=2).reshape(
            row_total, block_width
        )
        contract = (((1,), (1,)), ((), ()))
        cos_sum = cos_sum + lax.dot_general(
            products,
            cos_table,
            contract,
            precision=lax.Precision.HIGHEST,
            preferred_element_type=jnp.float32,
        )
        sin_sum = sin_sum - lax.dot_general(
            products,
            sin_table,
            contract,
            precision=lax.Precision.HIGHEST,
            preferred_element_type=jnp.float32,
        )
        totals = totals + jnp.sum(products, axis=1)
        return (cos_sum, sin_sum, totals)

    start_spec = jnp.zeros((row_total, order_count), jnp.float32)
    cos_sum, sin_sum, totals = lax.fori_loop(
        0, block_count, block_step, (start_spec, start_spec, jnp.zeros((row_total,), jnp.float32))
    )
    is_zero = (orders == 0).astype(jnp.float32)
    cos_sum = cos_sum - totals[:, None] * is_zero[None, :]
    cos_part = cos_sum.reshape(row_count, cycle_local, 2, order_count)
    sin_part = sin_sum.reshape(row_count, cycle_local, 2, order_count)
    cycle_scale = cycle_weight[None, :, None, None]
    analysed_re = (cos_turn * cos_part + sin_turn * sin_part) * cycle_scale
    analysed_im = (cos_turn * sin_part - sin_turn * cos_part) * cycle_scale
    analysed = jnp.stack([analysed_re, analysed_im], axis=-1)
    analysed = analysed.reshape(
        row_count, cycle_local, 2, peer_count, 2 * order_count // peer_count
    )
    return analysed.astype(jnp.bfloat16)


def adjoint_rows(shard_piece, legendre, alpha_table, beta_table, radial_weight, radius_index):
    local_orders = shard_piece.shape[0]
    row_count = shard_piece.shape[1]
    cycle_count = shard_piece.shape[3]
    local_degrees = legendre.shape[2]
    left_rows = shard_piece.reshape(local_orders, row_count * 4, cycle_count)
    adjoint_terms = lax.dot_general(
        left_rows, legendre, (((2,), (1,)), ((0,), (0,))), preferred_element_type=jnp.float32
    )
    adjoint_terms = adjoint_terms.reshape(local_orders, row_count, 2, 2, local_degrees)
    radial = radial_weight[radius_index][:, None]
    alpha_weighted = (radial * alpha_table[radius_index])[None, :, None, :]
    beta_weighted = (2.0 * radial * beta_table[radius_index])[None, :, None, :]
    return jnp.sum(
        adjoint_terms[:, :, 0] * alpha_weighted + adjoint_terms[:, :, 1] * beta_weighted, axis=1
    )


def body(
    coeffs,
    legendre,
    alpha_table,
    beta_table,
    radial_weight,
    radius_index,
    orders,
    cycle_offset,
    cycle_weight,
):
    row_id = lax.axis_index("row")
    ma_id = lax.axis_index("ma")
    local_orders = coeffs.shape[1]
    local_degrees = coeffs.shape[2]
    cycle_count = legendre.shape[1]
    radius_count = radius_index.shape[0]
    radii_here = radius_count // lax.axis_size("row")
    my_orders = lax.dynamic_slice_in_dim(orders, ma_id * local_orders, local_orders)
    degree = row_id * local_degrees + jnp.arange(local_degrees, dtype=jnp.int32)
    live_mask = (degree[None, :] >= my_orders[:, None]).astype(jnp.float32)
    coeff_rows = jnp.transpose(coeffs * live_mask[None], (1, 0, 2))
    summed = lax.psum(
        synth_rows(radius_count, coeff_rows, alpha_table, beta_table, radius_index, legendre), "row"
    )
    own_fields = lax.dynamic_slice_in_dim(summed, row_id * radii_here, radii_here, 0)
    own_fields = own_fields.reshape(radii_here, cycle_count, 2, 1, 2 * local_orders)
    shard_piece = lax.all_to_all(own_fields, "ma", split_axis=1, concat_axis=3, tiled=True)
    flat_piece = shard_piece.reshape(
        shard_piece.shape[0], shard_piece.shape[1], 2, shard_piece.shape[3] * shard_piece.shape[4]
    )
    analysed = cycle_work(flat_piece, orders, cycle_offset, cycle_weight)
    returned = lax.all_to_all(analysed, "ma", split_axis=3, concat_axis=1, tiled=True)
    returned = returned.reshape(radii_here, cycle_count, 2, local_orders, 2)
    returned = jnp.transpose(returned, (3, 0, 2, 4, 1)).reshape(
        local_orders, radii_here, 4, cycle_count
    )
    gradient = adjoint_rows(
        lax.all_gather(returned, "row", axis=1, tiled=True),
        legendre,
        alpha_table,
        beta_table,
        radial_weight,
        radius_index,
    )
    gradient = gradient * live_mask[:, None, :]
    return jnp.transpose(gradient, (1, 0, 2))


def solution(mesh):
    in_specs = (
        P(None, "ma", "row"),
        P("ma", None, "row"),
        P(None, "row"),
        P(None, "row"),
        P(),
        P(),
        P(),
        P("ma"),
        P("ma"),
    )
    out_specs = P(None, "ma", "row")
    return jax.shard_map(body, mesh=mesh, in_specs=in_specs, out_specs=out_specs, check_vma=False)
```

profile of v0, /device:TPU:0, one launch (start us, length us, event | category | flops | bytes accessed | tf_op | source)
XLA Modules:
  0.0 1810.7 jit_solution(5965398969004131030)
XLA Ops:
  10.5 41.1 %mul.384 = f32[256,64,2,2,512]{4,3,2,1,0:T(2,128)} broadcast(f32[256,2,512]{2,1,0:T(2,128)S(1)} %copy.101), dimensions={0,3,4} | broadcast | bytes 135266304 | tf_op jit(solution)/shard_map/mul | solution.py:16
  51.6 155.2 %mul.385 = f32[256,256,512]{2,1,0:T(8,128)} reshape(f32[256,64,2,2,512]{4,3,2,1,0:T(2,128)} %mul.384) | data formatting | bytes 268435456 | tf_op jit(solution)/shard_map/mul | solution.py:16
  209.0 48.7 %fusion.36 = f32[256,256,32]{1,2,0:T(8,128)} fusion(bf16[256,32,512]{2,1,0:T(8,128)(2,1)} %param.12, f32[256,256,512]{2,1,0:T(8,128)} %mul.385, f32[256,512]{1,0:T(8,128)S(1)} %mul.378), kind=kOutput, calls=%fused_computation.43 | convolution fusion | flops 2214592512 | bytes 151519232 | tf_op jit(solution)/shard_map/dot_general | solution.py:18
  284.8 291.2 %all-reduce.2.cloned.1.call-done = f32[64,32,2,512]{0,1,3,2:T(8,128)} async-done(((f32[64,32,2,512]{0,1,3,2:T(8,128)}), f32[64,32,2,512]{0,1,3,2:T(8,128)}) %all-reduce.2.cloned.1.call-update) | async-done | bytes 8388624 | tf_op jit(solution)/shard_map/psum | solution.py:151
  612.9 44.2 %all-to-all-done = f32[16,32,2,1,512]{4,3,2,0,1:T(1,128)} async-done(((f32[16,32,2,1,512]{4,3,2,0,1:T(1,128)}), f32[16,32,2,1,512]{4,3,2,0,1:T(1,128)}, u32[]{:S(2)}, u32[]{:S(2)}) %all-to-all-start) | async-done | bytes 2097184 | tf_op jit(solution)/shard_map/all_to_all | solution.py:156
  667.7 19.5 %fusion.46 = (f32[16,4,2,2048,1]{0,4,3,2,1:T(1,128)}, f32[16,4,2,2048,1]{0,4,3,2,1:T(1,128)}) fusion(f32[16,4,2,2048,2]{0,4,3,2,1:T(2,128)} %bitcast.72), kind=kLoop, calls=%fused_computation.75 | loop fusion | bytes 4194304 | tf_op jit(solution)/shard_map/slice | solution.py:37
  729.0 652.2 %while.20 = (s32[]{:T(128)}, f32[128,2048]{1,0:T(8,128)}, f32[128,2048]{1,0:T(8,128)}, f32[128]{0:T(128)S(1)}, s32[2048]{0:T(1024)S(1)}, /*index=5*/f32[128,2048...) while((s32[]{:T(128)}, f32[128,2048]{1,0:T(8,128)}, f32[128,2048]{1,0:T(8,128)}, ...), condition=%wide.region_3.4_spmd.clone, body=%wide.region_1.3_spmd.clone.sunk | while | flops 6502482944 | bytes 30717196 | solution.py:94
  787.2 19.5 %convolution_add_fusion.2 = f32[128,2048]{1,0:T(8,128)S(1)} fusion(f32[128,512]{1,0:T(8,128)S(1)} %reshape.326, s32[512]{0:T(512)S(1)} %iota_add_fusion.3, s32[2048]{0:T(1024)S(1)} %get-tuple-element.340, f32[128,2048]{1,0:T(8,128)S(1)} %copy-done.11, pred[]{:T(512)S(6)} %compare.4), kind=kOutput, calls=%fused_computation.13.clone.1 | convolution fusion | flops 1625817088 | bytes 2369537 | tf_op jit(solution)/shard_map/while/body/eval_jaxpr/dot_general | solution.py:76
  868.0 19.5 %convolution_add_fusion.2 = f32[128,2048]{1,0:T(8,128)S(1)} fusion(f32[128,512]{1,0:T(8,128)S(1)} %reshape.326, s32[512]{0:T(512)S(1)} %iota_add_fusion.3, s32[2048]{0:T(1024)S(1)} %get-tuple-element.340, f32[128,2048]{1,0:T(8,128)S(1)} %copy-done.11, pred[]{:T(512)S(6)} %compare.4), kind=kOutput, calls=%fused_computation.13.clone.1 | convolution fusion | flops 1625817088 | bytes 2369537 | tf_op jit(solution)/shard_map/while/body/eval_jaxpr/dot_general | solution.py:76
  891.0 19.4 %fusion.75 = f32[512,128]{0,1:T(8,128)S(1)} fusion(f32[128,2048]{1,0:T(8,128)} %get-tuple-element.341, s32[512]{0:T(512)S(1)} %iota_add_fusion.3, s32[2048]{0:T(1024)S(1)} %get-tuple-element.340), kind=kOutput, calls=%fused_computation.16.clone.1 | convolution fusion | flops 1625292800 | bytes 1320960 | tf_op jit(solution)/shard_map/while/body/eval_jaxpr/dot_general | solution.py:57
  929.6 19.4 %convolution_subtract_fusion.2 = f32[128,2048]{1,0:T(8,128)S(1)} fusion(f32[128,512]{1,0:T(8,128)S(1)} %reshape.326, s32[512]{0:T(512)S(1)} %iota_add_fusion.3, s32[2048]{0:T(1024)S(1)} %get-tuple-element.340, f32[128,2048]{1,0:T(8,128)S(1)} %copy-done.13, pred[]{:T(512)S(6)} %compare.4), kind=kOutput, calls=%fused_computation.12.clone.1 | convolution fusion | flops 1625817088 | bytes 2369537 | tf_op jit(solution)/shard_map/while/body/eval_jaxpr/dot_general | solution.py:83
  949.0 19.3 %convolution_add_fusion.2 = f32[128,2048]{1,0:T(8,128)S(1)} fusion(f32[128,512]{1,0:T(8,128)S(1)} %reshape.326, s32[512]{0:T(512)S(1)} %iota_add_fusion.3, s32[2048]{0:T(1024)S(1)} %get-tuple-element.340, f32[128,2048]{1,0:T(8,128)S(1)} %copy-done.11, pred[]{:T(512)S(6)} %compare.4), kind=kOutput, calls=%fused_computation.13.clone.1 | convolution fusion | flops 1625817088 | bytes 2369537 | tf_op jit(solution)/shard_map/while/body/eval_jaxpr/dot_general | solution.py:76
  1029.8 19.5 %convolution_add_fusion.2 = f32[128,2048]{1,0:T(8,128)S(1)} fusion(f32[128,512]{1,0:T(8,128)S(1)} %reshape.326, s32[512]{0:T(512)S(1)} %iota_add_fusion.3, s32[2048]{0:T(1024)S(1)} %get-tuple-element.340, f32[128,2048]{1,0:T(8,128)S(1)} %copy-done.11, pred[]{:T(512)S(6)} %compare.4), kind=kOutput, calls=%fused_computation.13.clone.1 | convolution fusion | flops 1625817088 | bytes 2369537 | tf_op jit(solution)/shard_map/while/body/eval_jaxpr/dot_general | solution.py:76
  1110.6 19.5 %convolution_add_fusion.2 = f32[128,2048]{1,0:T(8,128)S(1)} fusion(f32[128,512]{1,0:T(8,128)S(1)} %reshape.326, s32[512]{0:T(512)S(1)} %iota_add_fusion.3, s32[2048]{0:T(1024)S(1)} %get-tuple-element.340, f32[128,2048]{1,0:T(8,128)S(1)} %copy-done.11, pred[]{:T(512)S(6)} %compare.4), kind=kOutput, calls=%fused_computation.13.clone.1 | convolution fusion | flops 1625817088 | bytes 2369537 | tf_op jit(solution)/shard_map/while/body/eval_jaxpr/dot_general | solution.py:76
  1133.5 19.4 %fusion.75 = f32[512,128]{0,1:T(8,128)S(1)} fusion(f32[128,2048]{1,0:T(8,128)} %get-tuple-element.341, s32[512]{0:T(512)S(1)} %iota_add_fusion.3, s32[2048]{0:T(1024)S(1)} %get-tuple-element.340), kind=kOutput, calls=%fused_computation.16.clone.1 | convolution fusion | flops 1625292800 | bytes 1320960 | tf_op jit(solution)/shard_map/while/body/eval_jaxpr/dot_general | solution.py:57
  1172.1 19.4 %convolution_subtract_fusion.2 = f32[128,2048]{1,0:T(8,128)S(1)} fusion(f32[128,512]{1,0:T(8,128)S(1)} %reshape.326, s32[512]{0:T(512)S(1)} %iota_add_fusion.3, s32[2048]{0:T(1024)S(1)} %get-tuple-element.340, f32[128,2048]{1,0:T(8,128)S(1)} %copy-done.13, pred[]{:T(512)S(6)} %compare.4), kind=kOutput, calls=%fused_computation.12.clone.1 | convolution fusion | flops 1625817088 | bytes 2369537 | tf_op jit(solution)/shard_map/while/body/eval_jaxpr/dot_general | solution.py:83
  1191.6 19.3 %convolution_add_fusion.2 = f32[128,2048]{1,0:T(8,128)S(1)} fusion(f32[128,512]{1,0:T(8,128)S(1)} %reshape.326, s32[512]{0:T(512)S(1)} %iota_add_fusion.3, s32[2048]{0:T(1024)S(1)} %get-tuple-element.340, f32[128,2048]{1,0:T(8,128)S(1)} %copy-done.11, pred[]{:T(512)S(6)} %compare.4), kind=kOutput, calls=%fused_computation.13.clone.1 | convolution fusion | flops 1625817088 | bytes 2369537 | tf_op jit(solution)/shard_map/while/body/eval_jaxpr/dot_general | solution.py:76
  1272.3 19.5 %convolution_add_fusion.2 = f32[128,2048]{1,0:T(8,128)S(1)} fusion(f32[128,512]{1,0:T(8,128)S(1)} %reshape.326, s32[512]{0:T(512)S(1)} %iota_add_fusion.3, s32[2048]{0:T(1024)S(1)} %get-tuple-element.340, f32[128,2048]{1,0:T(8,128)S(1)} %copy-done.11, pred[]{:T(512)S(6)} %compare.4), kind=kOutput, calls=%fused_computation.13.clone.1 | convolution fusion | flops 1625817088 | bytes 2369537 | tf_op jit(solution)/shard_map/while/body/eval_jaxpr/dot_general | solution.py:76
  1353.1 19.5 %convolution_add_fusion.2 = f32[128,2048]{1,0:T(8,128)S(1)} fusion(f32[128,512]{1,0:T(8,128)S(1)} %reshape.326, s32[512]{0:T(512)S(1)} %iota_add_fusion.3, s32[2048]{0:T(1024)S(1)} %get-tuple-element.340, f32[128,2048]{1,0:T(8,128)S(1)} %copy-done.11, pred[]{:T(512)S(6)} %compare.4), kind=kOutput, calls=%fused_computation.13.clone.1 | convolution fusion | flops 1625817088 | bytes 2369537 | tf_op jit(solution)/shard_map/while/body/eval_jaxpr/dot_general | solution.py:76
  1428.5 29.6 %all_to_all.30 = bf16[8,2,32768]{2,1,0:T(2,128)(2,1)S(1)} all-to-all(bf16[8,2,32768]{2,1,0:T(2,128)(2,1)S(1)} %reshape.321), channel_id=1, replica_groups=mesh['row'=4,'ma'=8] {'ma'}, dimensions={0} | all-to-all | bytes 2097152 | tf_op jit(solution)/shard_map/all_to_all | solution.py:161
  1497.3 32.0 %all-gather.2.cloned.1.call-done = bf16[256,64,4,32]{0,3,2,1:T(8,128)(2,1)} async-done(((bf16[256,16,4,32]{0,3,2,1:T(8,128)(2,1)}), bf16[256,64,4,32]{0,3,2,1:T(8,128)(2,1)}) %all-gather.2.cloned.1.call-update) | async-done | bytes 4194320 | tf_op jit(solution)/shard_map/all_gather | solution.py:167
  1537.9 49.0 %fusion.47 = f32[256,256,512]{2,1,0:T(8,128)} fusion(bf16[256,256,32]{1,2,0:T(8,128)(2,1)} %copy.115, bf16[256,32,512]{2,1,0:T(8,128)(2,1)} %param.12), kind=kOutput, calls=%fused_computation.77 | convolution fusion | flops 2147483648 | bytes 146800640 | tf_op jit(solution)/shard_map/dot_general | solution.py:117
  1586.9 152.6 %reshape.291 = f32[256,64,2,2,512]{4,3,2,1,0:T(2,128)} reshape(f32[256,256,512]{2,1,0:T(8,128)} %fusion.47) | data formatting | bytes 268435456 | tf_op jit(solution)/shard_map/reshape | solution.py:120
  1739.5 62.2 %fusion.41 = f32[256,2,512]{2,1,0:T(2,128)S(1)} fusion(f32[256,64,2,2,512]{4,3,2,1,0:T(2,128)} %reshape.291, f32[64,512]{1,0:T(8,128)S(1)} %get-tuple-element.263, f32[64,512]{1,0:T(8,128)S(1)} %get-tuple-element.264), kind=kLoop, calls=%fused_computation.50 | loop fusion | flops 66846720 | bytes 135528448 | tf_op jit(solution)/shard_map/reduce_sum | solution.py:124
  (247 shorter events, 611.3 us)
Async XLA Ops:
  6.5 200.3 %copy-start = (f32[64,512]{1,0:T(8,128)S(1)}, f32[64,512]{1,0:T(8,128)}, u32[]{:S(2)}) copy-start(f32[64,512]{1,0:T(8,128)} %param.13) | copy-start | bytes 393220
  6.5 569.4 %all-reduce.2.cloned.1.call-start = ((), (), s32[]{:S(2)}) async-start(), calls=%async_computation.2 | async-start | bytes 33554432 | tf_op jit(solution)/shard_map/psum | solution.py:151
  51.6 155.2 %copy-start.21 = (s32[64]{0:T(128)S(1)}, s32[64]{0:T(128)}, u32[]{:S(2)}) copy-start(s32[64]{0:T(128)} %param.16) | copy-start | bytes 772
  51.6 155.9 %copy-start.3 = (f32[64,512]{1,0:T(8,128)S(1)}, f32[64,512]{1,0:T(8,128)}, u32[]{:S(2)}) copy-start(f32[64,512]{1,0:T(8,128)} %param.14) | copy-start | bytes 393220
  208.2 49.6 %copy-start.9 = (f32[64,512]{1,0:T(8,128)}, f32[64,512]{1,0:T(8,128)S(1)}, u32[]{:S(2)}) copy-start(f32[64,512]{1,0:T(8,128)S(1)} %gather_fusion.1) | copy-start | bytes 393220
  603.2 54.0 %all-to-all-start = ((f32[16,32,2,1,512]{4,3,2,0,1:T(1,128)}), f32[16,32,2,1,512]{4,3,2,0,1:T(1,128)}, u32[]{:S(2)}, u32[]{:S(2)}) async-start(f32[16,32,2,1,512]{4,3,2,0,1:T(1,128)} %copy.105), calls=%async_computation | async-start | bytes 4194304 | tf_op jit(solution)/shard_map/all_to_all | solution.py:156
  608.8 920.5 %all-gather.2.cloned.1.call-start = ((), (), s32[]{:S(2)}) async-start(), calls=%async_computation.3 | async-start | bytes 5242880 | tf_op jit(solution)/shard_map/all_gather | solution.py:167
  748.6 19.4 %copy-start.13 = (f32[128,2048]{1,0:T(8,128)S(1)}, f32[128,2048]{1,0:T(8,128)}, u32[]{:S(2)}) copy-start(f32[128,2048]{1,0:T(8,128)} %get-tuple-element.328) | copy-start | bytes 3145732 | tf_op jit(solution)/shard_map/while
  787.2 19.6 %copy-start.14 = (f32[128,2048]{1,0:T(8,128)}, f32[128,2048]{1,0:T(8,128)S(1)}, u32[]{:S(2)}) copy-start(f32[128,2048]{1,0:T(8,128)S(1)} %convolution_subtract_fusion.2) | copy-start | bytes 3145732 | tf_op jit(solution)/shard_map/while
  829.4 19.3 %copy-start.13 = (f32[128,2048]{1,0:T(8,128)S(1)}, f32[128,2048]{1,0:T(8,128)}, u32[]{:S(2)}) copy-start(f32[128,2048]{1,0:T(8,128)} %get-tuple-element.328) | copy-start | bytes 3145732 | tf_op jit(solution)/shard_map/while
  868.0 19.5 %copy-start.14 = (f32[128,2048]{1,0:T(8,128)}, f32[128,2048]{1,0:T(8,128)S(1)}, u32[]{:S(2)}) copy-start(f32[128,2048]{1,0:T(8,128)S(1)} %convolution_subtract_fusion.2) | copy-start | bytes 3145732 | tf_op jit(solution)/shard_map/while
  891.0 19.4 %copy-start.16 = (f32[128,2048]{1,0:T(8,128)S(1)}, f32[128,2048]{1,0:T(8,128)}, u32[]{:S(2)}) copy-start(f32[128,2048]{1,0:T(8,128)} %get-tuple-element.342) | copy-start | bytes 3145732 | tf_op jit(solution)/shard_map/while
  929.5 19.5 %copy-start.11 = (f32[128,2048]{1,0:T(8,128)S(1)}, f32[128,2048]{1,0:T(8,128)}, u32[]{:S(2)}) copy-start(f32[128,2048]{1,0:T(8,128)} %get-tuple-element.327) | copy-start | bytes 3145732 | tf_op jit(solution)/shard_map/while
  991.2 19.4 %copy-start.13 = (f32[128,2048]{1,0:T(8,128)S(1)}, f32[128,2048]{1,0:T(8,128)}, u32[]{:S(2)}) copy-start(f32[128,2048]{1,0:T(8,128)} %get-tuple-element.328) | copy-start | bytes 3145732 | tf_op jit(solution)/shard_map/while
  1029.8 19.6 %copy-start.14 = (f32[128,2048]{1,0:T(8,128)}, f32[128,2048]{1,0:T(8,128)S(1)}, u32[]{:S(2)}) copy-start(f32[128,2048]{1,0:T(8,128)S(1)} %convolution_subtract_fusion.2) | copy-start | bytes 3145732 | tf_op jit(solution)/shard_map/while
  1072.0 19.3 %copy-start.13 = (f32[128,2048]{1,0:T(8,128)S(1)}, f32[128,2048]{1,0:T(8,128)}, u32[]{:S(2)}) copy-start(f32[128,2048]{1,0:T(8,128)} %get-tuple-element.328) | copy-start | bytes 3145732 | tf_op jit(solution)/shard_map/while
  1110.6 19.5 %copy-start.14 = (f32[128,2048]{1,0:T(8,128)}, f32[128,2048]{1,0:T(8,128)S(1)}, u32[]{:S(2)}) copy-start(f32[128,2048]{1,0:T(8,128)S(1)} %convolution_subtract_fusion.2) | copy-start | bytes 3145732 | tf_op jit(solution)/shard_map/while
  1133.5 19.4 %copy-start.16 = (f32[128,2048]{1,0:T(8,128)S(1)}, f32[128,2048]{1,0:T(8,128)}, u32[]{:S(2)}) copy-start(f32[128,2048]{1,0:T(8,128)} %get-tuple-element.342) | copy-start | bytes 3145732 | tf_op jit(solution)/shard_map/while
  1172.1 19.5 %copy-start.11 = (f32[128,2048]{1,0:T(8,128)S(1)}, f32[128,2048]{1,0:T(8,128)}, u32[]{:S(2)}) copy-start(f32[128,2048]{1,0:T(8,128)} %get-tuple-element.327) | copy-start | bytes 3145732 | tf_op jit(solution)/shard_map/while
  1233.7 19.4 %copy-start.13 = (f32[128,2048]{1,0:T(8,128)S(1)}, f32[128,2048]{1,0:T(8,128)}, u32[]{:S(2)}) copy-start(f32[128,2048]{1,0:T(8,128)} %get-tuple-element.328) | copy-start | bytes 3145732 | tf_op jit(solution)/shard_map/while
  1272.3 19.6 %copy-start.14 = (f32[128,2048]{1,0:T(8,128)}, f32[128,2048]{1,0:T(8,128)S(1)}, u32[]{:S(2)}) copy-start(f32[128,2048]{1,0:T(8,128)S(1)} %convolution_subtract_fusion.2) | copy-start | bytes 3145732 | tf_op jit(solution)/shard_map/while
  1353.1 19.5 %copy-start.14 = (f32[128,2048]{1,0:T(8,128)}, f32[128,2048]{1,0:T(8,128)S(1)}, u32[]{:S(2)}) copy-start(f32[128,2048]{1,0:T(8,128)S(1)} %convolution_subtract_fusion.2) | copy-start | bytes 3145732 | tf_op jit(solution)/shard_map/while
  1739.5 62.2 %copy-start.5 = (f32[256,512]{1,0:T(8,128)S(1)}, f32[256,512]{1,0:T(8,128)}, u32[]{:S(2)}) copy-start(f32[256,512]{1,0:T(8,128)} %copy-done.4) | copy-start | bytes 1572868
  1739.5 63.9 %copy-start.1 = (f32[64,512]{1,0:T(8,128)S(1)}, f32[64,512]{1,0:T(8,128)}, u32[]{:S(2)}) copy-start(f32[64,512]{1,0:T(8,128)} %param.13) | copy-start | bytes 393220
  (36 other events, 414.3 us)
Sparse Core Ops, SparseCore 0:
  284.9 290.9 all-reduce.1
  1496.4 32.8 all-gather.1
where the time goes:
time: 1830 us; the launch traced here: 1810 us
  matrix products  709 us (39%)
  local copies, waits for them, and re-layouts  582 us (32%)
  waiting for transfers between devices  367 us (20%)
  other arithmetic  76.8 us (4%)
  blocking collectives  29.6 us (2%)
  loops' own time  26.5 us (1%)
    psum x1, waiting for transfers between devices, body(): lax.psum(synth_rows(radius_count, coeff_rows, alpha_table, beta_table, ra...  291 us
    mul x4, local copies, waits for them, and re-layouts, synth_rows(): filters[None, :, :, None, :] * coeff_rows[:, None, None, :, :]  197 us
    dot_general x8, matrix products, block_step(): lax.dot_general(products, cos_table, contract, precision=lax.Precision.HI...  156 us
    dot_general x8, matrix products, block_step(): lax.dot_general(products, sin_table, contract, precision=lax.Precision.HI...  154 us
    dot_general x8, matrix products, block_step(): jnp.dot(rotated_re, cos_table, precision=lax.Precision.HIGHEST, preferred...  154 us
    reshape x1, local copies, waits for them, and re-layouts, adjoint_rows(): adjoint_terms.reshape(local_orders, row_count, 2, 2, local_degrees)  153 us
    dot_general x8, matrix products, block_step(): jnp.dot(rotated_im, sin_table, precision=lax.Precision.HIGHEST, preferred...  147 us
    reduce_sum x1, other arithmetic, adjoint_rows(): jnp.sum(adjoint_terms[:, :, 0] * alpha_weighted + adjoint_terms[:, :, 1]...  62.2 us
  transfers between devices with their start and end apart: 3, of which 3 were waited for; matrix products, arithmetic and copies ran while one was open for 0% of the time, Pallas kernels for 0%

commit v1 on v0

v1 whole, which is shorter than its diff:
```python
import functools
import math

import jax
import jax.numpy as jnp
import numpy as np
from jax import lax
from jax.experimental import pallas as pl
from jax.experimental.pallas import tpu as pltpu
from jax.sharding import PartitionSpec as P

NPIX = 4096
SIDE = 64
PADDED = 136
CHUNKS = 2
MIB = 1 << 20
F32 = jnp.float32
BF16 = jnp.bfloat16


def split_table(table):
    high = table.astype(jnp.bfloat16)
    low = (table - high.astype(np.float64)).astype(jnp.bfloat16)
    return high, low


@functools.lru_cache(maxsize=None)
def fourier_tables():
    degree_a = np.arange(32).reshape(4, 1, 8)
    part = np.arange(2).reshape(1, 2, 1)
    first = np.arange(SIDE)
    spin = np.arange(2).reshape(2, 1, 1, 1, 1, 1, 1)
    order = SIDE * degree_a[None] + np.arange(SIDE).reshape(SIDE, 1, 1, 1)
    angle = (
        (2 * first.reshape(1, 1, 1, SIDE, 1, 1, 1) + spin)
        * order.reshape(1, SIDE, 1, 1, 4, 1, 8)
        % (2 * NPIX)
        * (math.pi / NPIX)
    )
    cosine, sine = np.cos(angle), np.sin(angle)
    row_part = np.arange(2).reshape(1, 1, 2, 1, 1, 1, 1)
    col_part = part.reshape(1, 1, 1, 1, 1, 2, 1)
    same = (row_part == col_part).astype(np.float64)
    cross = np.where(row_part == 1, 1.0, -1.0) * (row_part != col_part)
    doubling = np.where(order == 0, 1.0, 2.0).reshape(1, SIDE, 1, 1, 4, 1, 8)
    spread = (doubling * (same * cosine + cross * sine)).reshape(2, SIDE, 2 * SIDE, SIDE)
    gather = (same * cosine + cross * sine).reshape(2, SIDE, 2 * SIDE, SIDE)
    gather = np.swapaxes(gather, 2, 3)
    spread_parts = np.concatenate(split_table(spread), axis=3)
    gather_parts = np.concatenate(split_table(gather), axis=2)
    square = first[:, None] * first[None, :] % SIDE * (2.0 * math.pi / SIDE)
    pixel = np.concatenate(split_table(np.concatenate([np.cos(square), -np.sin(square)], axis=1)), axis=0)
    back_high, back_low = split_table(np.concatenate([np.cos(square), -np.sin(square)], axis=0))
    back = np.concatenate([back_high, back_high, back_low], axis=1)
    return spread_parts, pixel, back, gather_parts


def two_parts(value):
    high = value.astype(BF16)
    low = (value - high.astype(F32)).astype(BF16)
    return high, low


def synth_kernel(
    jb_here,
    first_step,
    info_ref,
    row_ref,
    node_ref,
    coeffs_ref,
    alpha_ref,
    beta_ref,
    legendre_ref,
    keep_ref,
    send_ref,
    filter_scr,
    weight_scr,
    legendre_scr,
    terms_scr,
    sums_scr,
    sems,
):
    step = pl.program_id(0)
    row = row_ref[0]
    radii = node_ref.shape[0]
    degrees = coeffs_ref.shape[2]
    cycles = legendre_ref.shape[1]
    owners = cycles // 4
    slots = legendre_scr.shape[0]

    def fetch(which):
        slot = lax.rem(which, slots)

        def one(place, carry):
            source = info_ref[(first_step + which) * 32 + place] >> 12
            pltpu.make_async_copy(
                legendre_ref.at[source], legendre_scr.at[slot, place], sems.at[slot]
            ).start()
            return carry

        lax.fori_loop(0, 32, one, 0)

    @pl.when(step == 0)
    def _():
        for ahead in range(min(slots - 1, jb_here)):
            fetch(ahead)
        for radius in range(radii):
            node = node_ref[radius]
            filter_scr[pl.ds(radius, 1), :] = alpha_ref[pl.ds(node, 1), :]
            filter_scr[pl.ds(radii + radius, 1), :] = beta_ref[pl.ds(node, 1), :]
        high, low = two_parts(filter_scr[...].T)
        weight_scr[:, : 2 * radii] = high
        weight_scr[:, 2 * radii :] = low

    @pl.when(step + slots - 1 < jb_here)
    def _():
        fetch(step + slots - 1)

    slot = lax.rem(step, slots)
    pltpu.make_async_copy(
        legendre_ref.at[pl.ds(0, 32)], legendre_scr.at[slot], sems.at[slot]
    ).wait()
    degree = row * degrees + lax.broadcasted_iota(jnp.int32, (1, degrees), 1)
    for group in range(4):
        half = group % 2
        for place in range(8):
            entry = info_ref[(first_step + step) * 32 + group * 8 + place]
            source = entry >> 12
            live = degree >= (entry & 4095)
            values = legendre_scr[slot, group * 8 + place].astype(F32)
            for part in range(2):
                coeff = jnp.where(live, coeffs_ref[part, pl.ds(source, 1), :], 0.0)
                high, low = two_parts(values * coeff)
                start = (part * 8 + place) * cycles
                terms_scr[half, 0, start : start + cycles, :] = high
                terms_scr[half, 1, start : start + cycles, :] = low
        both = jnp.dot(terms_scr[half, 0], weight_scr[...], preferred_element_type=F32)
        rest = jnp.dot(
            terms_scr[half, 1], weight_scr[:, : 2 * radii], preferred_element_type=F32
        )
        sums_scr[half] = both[:, : 2 * radii] + both[:, 2 * radii :] + rest
        for owner in range(owners):
            for away in range(4):
                cycle = 4 * owner + (row ^ away)
                piece = sums_scr[half, pl.ds(cycle, 16, stride=cycles), :]
                target = send_ref if away % 2 else keep_ref
                target[away // 2, owner, 0, group * 16 : group * 16 + 16, :] = piece


def synth(chunk, chunks, info, row, radius_index, coeffs, alpha_table, beta_table, legendre):
    orders_here, cycles, degrees = legendre.shape
    jb_here = orders_here // 32 // chunks
    owners = cycles // 4
    radii = radius_index.shape[0]
    out = jax.ShapeDtypeStruct((2, owners, jb_here, 64, 2 * radii), F32)
    out_spec = pl.BlockSpec((2, owners, 1, 64, 2 * radii), lambda t, *_: (0, 0, t, 0, 0))
    whole = lambda shape: pl.BlockSpec(shape, lambda t, *_: (0,) * len(shape))
    slots = min(3, jb_here)
    return pl.pallas_call(
        functools.partial(synth_kernel, jb_here, chunk * jb_here),
        grid_spec=pltpu.PrefetchScalarGridSpec(
            num_scalar_prefetch=3,
            grid=(jb_here,),
            in_specs=[
                whole(coeffs.shape),
                whole(alpha_table.shape),
                whole(beta_table.shape),
                pl.BlockSpec(memory_space=pl.ANY),
            ],
            out_specs=[out_spec, out_spec],
            scratch_shapes=[
                pltpu.VMEM((2 * radii, degrees), F32),
                pltpu.VMEM((degrees, 4 * radii), BF16),
                pltpu.VMEM((slots, 32, cycles, degrees), BF16),
                pltpu.VMEM((2, 2, 16 * cycles, degrees), BF16),
                pltpu.VMEM((2, 16 * cycles, 2 * radii), F32),
                pltpu.SemaphoreType.DMA((slots,)),
            ],
        ),
        out_shape=[out, out],
        compiler_params=pltpu.CompilerParams(vmem_limit_bytes=48 * MIB),
        cost_estimate=pl.CostEstimate(
            flops=16 * jb_here * 4 * cycles * degrees * 2 * radii * 2 * 4,
            bytes_accessed=jb_here * (32 * cycles * degrees * 2 + 2 * 2 * owners * 64 * 2 * radii * 4),
            transcendentals=0,
        ),
        name="synth",
    )(info, row, radius_index, coeffs, alpha_table, beta_table, legendre)


def cycle_kernel(device_count, chunks, offset_ref, row_ref, weight_ref, *refs):
    pieces = refs[:chunks]
    place_ref, spread_ref, pixel_ref, back_ref, gather_ref = refs[chunks : chunks + 5]
    outs = refs[chunks + 5 : 2 * chunks + 5]
    middle_scr, product_scr, back_scr = refs[2 * chunks + 5 :]
    jb_here = pieces[0].shape[1]
    scale = weight_ref[row_ref[0]]
    lane = lax.broadcasted_iota(jnp.int32, (SIDE, 128), 1)

    for chunk in range(chunks):

        def spread_step(step, carry, chunk=chunk):
            block = chunk * jb_here + step
            for spot in range(device_count):
                picked = jnp.zeros((SIDE, 128), BF16)
                for peer in range(device_count):
                    picked = jnp.where(
                        place_ref[peer, block] == spot, pieces[chunk][peer, step], picked
                    )
                low_order = block * device_count + spot
                stage = jnp.dot(
                    spread_ref[0, low_order],
                    jnp.concatenate([picked, picked], axis=0),
                    preferred_element_type=F32,
                )
                middle_scr[pl.ds(low_order * PADDED, 128), :] = stage
            return carry

        lax.fori_loop(0, jb_here, spread_step, 0)

    def pixel_step(step, total):
        for inner in range(8):
            first = step * 8 + inner
            column = jnp.concatenate(
                [
                    middle_scr[pl.ds(first, SIDE, stride=PADDED), :],
                    middle_scr[pl.ds(first + SIDE, SIDE, stride=PADDED), :],
                ],
                axis=0,
            )
            high, low = two_parts(column)
            stage = jnp.dot(
                pixel_ref[...], jnp.concatenate([high, low], axis=1), preferred_element_type=F32
            )
            field = stage[:SIDE, :128] + stage[:SIDE, 128:] + stage[SIDE:, :128]
            other = pltpu.roll(field, 64, 1)
            product = other * jnp.where(lane < 64, other, field)
            product_scr[first] = product
            total = total + jnp.sum(product.reshape(8, 8, 128), axis=0)
        return total

    total = lax.fori_loop(0, SIDE // 8, pixel_step, jnp.zeros((8, 128), F32))
    mean = jnp.sum(total, axis=0, keepdims=True) * (1.0 / NPIX)

    def back_step(step, carry):
        for inner in range(8):
            first = step * 8 + inner
            high, low = two_parts(product_scr[first] - mean)
            back_scr[pl.ds(first * PADDED, 128), :] = jnp.dot(
                back_ref[...],
                jnp.concatenate([high, low, high], axis=0),
                preferred_element_type=F32,
            )
        return carry

    lax.fori_loop(0, SIDE // 8, back_step, 0)

    for chunk in range(chunks):

        def gather_step(step, carry, chunk=chunk):
            block = chunk * jb_here + step
            found = []
            for spot in range(device_count):
                low_order = block * device_count + spot
                column = jnp.concatenate(
                    [
                        back_scr[pl.ds(low_order, SIDE, stride=PADDED), :],
                        back_scr[pl.ds(low_order + SIDE, SIDE, stride=PADDED), :],
                    ],
                    axis=0,
                )
                high, low = two_parts(column)
                stage = jnp.dot(
                    gather_ref[0, low_order],
                    jnp.concatenate([high, low], axis=1),
                    preferred_element_type=F32,
                )
                value = stage[:SIDE, :128] + stage[:SIDE, 128:] + stage[SIDE:, :128]
                found.append((value * scale).astype(BF16))
            for peer in range(device_count):
                place = place_ref[peer, block]
                picked = found[0]
                for spot in range(1, device_count):
                    picked = jnp.where(place == spot, found[spot], picked)
                outs[chunk][peer, step] = picked
            return carry

        lax.fori_loop(0, jb_here, gather_step, 0)


def cycle_work(pieces, places, offset, row, cycle_weight):
    chunks = len(pieces)
    device_count, jb_here = pieces[0].shape[:2]
    spread, pixel, back, gather = [jnp.asarray(table) for table in fourier_tables()]
    whole = lambda shape: pl.BlockSpec(shape, lambda t, *_: (0,) * len(shape))
    chosen = pl.BlockSpec((1,) + spread.shape[1:], lambda t, off, row: (off[row[0]], 0, 0, 0))
    chosen_back = pl.BlockSpec((1,) + gather.shape[1:], lambda t, off, row: (off[row[0]], 0, 0, 0))
    return pl.pallas_call(
        functools.partial(cycle_kernel, device_count, chunks),
        grid_spec=pltpu.PrefetchScalarGridSpec(
            num_scalar_prefetch=2,
            grid=(1,),
            in_specs=[pl.BlockSpec(memory_space=pltpu.SMEM)]
            + [whole(piece.shape) for piece in pieces]
            + [whole(places.shape), chosen, whole(pixel.shape), whole(back.shape), chosen_back],
            out_specs=[whole(piece.shape) for piece in pieces],
            scratch_shapes=[
                pltpu.VMEM((SIDE * PADDED, 128), F32),
                pltpu.VMEM((SIDE, SIDE, 128), F32),
                pltpu.VMEM((SIDE * PADDED, 128), F32),
            ],
        ),
        out_shape=[jax.ShapeDtypeStruct(piece.shape, BF16) for piece in pieces],
        compiler_params=pltpu.CompilerParams(vmem_limit_bytes=48 * MIB),
        cost_estimate=pl.CostEstimate(
            flops=4 * SIDE * 128 * 256 * 256 * 2, bytes_accessed=8 * MIB, transcendentals=0
        ),
        name="cycle_work",
    )(offset, row, cycle_weight, *pieces, places, spread, pixel, back, gather)


def adjoint_kernel(
    jb_here,
    first_step,
    info_ref,
    row_ref,
    node_ref,
    radial_ref,
    alpha_ref,
    beta_ref,
    own_ref,
    core_ref,
    far_ref,
    corner_ref,
    legendre_ref,
    earlier_ref,
    out_ref,
    filter_scr,
    weight_scr,
    legendre_scr,
    rows_scr,
    terms_scr,
    sems,
):
    step = pl.program_id(0)
    row = row_ref[0]
    radii = node_ref.shape[0]
    degrees = out_ref.shape[2]
    cycles = legendre_ref.shape[1]
    owners = cycles // 4
    slots = legendre_scr.shape[0]

    def fetch(which):
        slot = lax.rem(which, slots)

        def one(place, carry):
            source = info_ref[(first_step + which) * 32 + place] >> 12
            pltpu.make_async_copy(
                legendre_ref.at[source], legendre_scr.at[slot, place], sems.at[slot]
            ).start()
            return carry

        lax.fori_loop(0, 32, one, 0)

    @pl.when(step == 0)
    def _():
        for ahead in range(min(slots - 1, jb_here)):
            fetch(ahead)
        if earlier_ref is not None:
            out_ref[...] = earlier_ref[...]
        for radius in range(radii):
            node = node_ref[radius]
            scale = radial_ref[node]
            filter_scr[pl.ds(radius, 1), :] = scale * alpha_ref[pl.ds(node, 1), :]
            filter_scr[pl.ds(radii + radius, 1), :] = (2.0 * scale) * beta_ref[pl.ds(node, 1), :]
        high, low = two_parts(filter_scr[...])
        weight_scr[: 2 * radii, :] = high
        weight_scr[2 * radii :, :] = low

    @pl.when(step + slots - 1 < jb_here)
    def _():
        fetch(step + slots - 1)

    slot = lax.rem(step, slots)
    pltpu.make_async_copy(
        legendre_ref.at[pl.ds(0, 32)], legendre_scr.at[slot], sems.at[slot]
    ).wait()
    degree = row * degrees + lax.broadcasted_iota(jnp.int32, (1, degrees), 1)
    sources = (own_ref, core_ref, far_ref, corner_ref)
    for group in range(4):
        half = group % 2
        for owner in range(owners):
            for away in range(4):
                cycle = 4 * owner + (row ^ away)
                piece = sources[away][owner, 0, group * 16 : group * 16 + 16, :]
                rows_scr[half, pl.ds(cycle, 16, stride=cycles), :] = piece.astype(F32)
        rows = rows_scr[half].astype(BF16)
        terms_scr[half] = jnp.dot(
            jnp.concatenate([rows, rows], axis=1), weight_scr[...], preferred_element_type=F32
        )
        for place in range(8):
            entry = info_ref[(first_step + step) * 32 + group * 8 + place]
            target = entry >> 12
            live = degree >= (entry & 4095)
            values = legendre_scr[slot, group * 8 + place].astype(F32)
            for part in range(2):
                start = (part * 8 + place) * cycles
                summed = jnp.sum(
                    terms_scr[half, start : start + cycles, :] * values, axis=0, keepdims=True
                )
                out_ref[part, pl.ds(target, 1), :] = jnp.where(live, summed, 0.0)


def adjoint(
    chunk, chunks, info, row, radius_index, radial_weight, alpha_table, beta_table, pieces, legendre, earlier
):
    orders_here, cycles, degrees = legendre.shape
    jb_here = orders_here // 32 // chunks
    owners = cycles // 4
    radii = radius_index.shape[0]
    out = jax.ShapeDtypeStruct((2, orders_here, degrees), F32)
    whole = lambda shape: pl.BlockSpec(shape, lambda t, *_: (0,) * len(shape))
    piece_spec = pl.BlockSpec((owners, 1, 64, 2 * radii), lambda t, *_: (0, t, 0, 0))
    slots = min(3, jb_here)
    body = functools.partial(adjoint_kernel, jb_here, chunk * jb_here)
    operands = [info, row, radius_index, radial_weight, alpha_table, beta_table, *pieces, legendre]
    in_specs = [
        pl.BlockSpec(memory_space=pltpu.SMEM),
        whole(alpha_table.shape),
        whole(beta_table.shape),
        piece_spec,
        piece_spec,
        piece_spec,
        piece_spec,
        pl.BlockSpec(memory_space=pl.ANY),
    ]
    if earlier is None:
        kernel = lambda *refs: body(*refs[:11], None, *refs[11:])
    else:
        kernel = body
        operands.append(earlier)
        in_specs.append(whole(earlier.shape))
    return pl.pallas_call(
        kernel,
        grid_spec=pltpu.PrefetchScalarGridSpec(
            num_scalar_prefetch=3,
            grid=(jb_here,),
            in_specs=in_specs,
            out_specs=whole(out.shape),
            scratch_shapes=[
                pltpu.VMEM((2 * radii, degrees), F32),
                pltpu.VMEM((4 * radii, degrees), BF16),
                pltpu.VMEM((slots, 32, cycles, degrees), BF16),
                pltpu.VMEM((2, 16 * cycles, 2 * radii), F32),
                pltpu.VMEM((2, 16 * cycles, degrees), F32),
                pltpu.SemaphoreType.DMA((slots,)),
            ],
        ),
        out_shape=out,
        compiler_params=pltpu.CompilerParams(vmem_limit_bytes=56 * MIB),
        cost_estimate=pl.CostEstimate(
            flops=16 * jb_here * 4 * cycles * degrees * 2 * radii * 2 * 2,
            bytes_accessed=jb_here * (32 * cycles * degrees * 2 + 4 * owners * 64 * 2 * radii * 2),
            transcendentals=0,
        ),
        name="adjoint",
    )(*operands)


def slot_tables(orders, device_count, ma_id):
    local_orders = orders.shape[0] // device_count
    blocks = local_orders // 32
    position = jnp.arange(local_orders, dtype=jnp.int32)
    wanted = blocks * (position % 32) + position // 32
    by_device = orders.reshape(device_count, local_orders)
    mine = lax.dynamic_slice_in_dim(orders, ma_id * local_orders, local_orders)
    info = jnp.sum(
        jnp.where(mine[None, :] // device_count == wanted[:, None], position[None, :] * 4096 + mine[None, :], 0),
        axis=1,
    )
    place = jnp.sum(
        jnp.where(
            by_device[:, None, :] // device_count == wanted[None, :, None],
            by_device[:, None, :] % device_count,
            0,
        ),
        axis=2,
    )
    place = place.reshape(device_count, blocks, 4, 1, 8, 1)
    place = jnp.broadcast_to(place, (device_count, blocks, 4, 2, 8, 128))
    return info, place.reshape(device_count, blocks, 64, 128).astype(BF16)


def body(
    coeffs,
    legendre,
    alpha_table,
    beta_table,
    radial_weight,
    radius_index,
    orders,
    cycle_offset,
    cycle_weight,
):
    row_id = lax.axis_index("row")
    ma_id = lax.axis_index("ma")
    device_count = lax.axis_size("ma")
    row_count = lax.axis_size("row")
    row = row_id.reshape(1).astype(jnp.int32)
    info, places = slot_tables(orders, device_count, ma_id)
    core_pairs = [(i, i ^ 1) for i in range(row_count)]
    far_pairs = [(i, i ^ 2) for i in range(row_count)]
    chunks = min(CHUNKS, coeffs.shape[1] // 32)
    arrived = []
    for chunk in range(chunks):
        keep, send = synth(
            chunk, chunks, info, row, radius_index, coeffs, alpha_table, beta_table, legendre
        )
        other = lax.ppermute(send, "row", core_pairs)
        outgoing = (keep[1] + other[1]).astype(BF16)
        incoming = lax.ppermute(outgoing, "row", far_pairs)
        summed = (keep[0] + other[0] + incoming.astype(F32)).astype(BF16)
        arrived.append(lax.all_to_all(summed, "ma", split_axis=0, concat_axis=0, tiled=True))
    analysed = cycle_work(arrived, places, cycle_offset, row, cycle_weight)
    gradient = None
    for chunk in range(chunks):
        own = lax.all_to_all(analysed[chunk], "ma", split_axis=0, concat_axis=0, tiled=True)
        far = lax.ppermute(own, "row", far_pairs)
        core = lax.ppermute(own, "row", core_pairs)
        corner = lax.ppermute(far, "row", core_pairs)
        gradient = adjoint(
            chunk,
            chunks,
            info,
            row,
            radius_index,
            radial_weight,
            alpha_table,
            beta_table,
            (own, core, far, corner),
            legendre,
            gradient,
        )
    return gradient


def solution(mesh):
    in_specs = (
        P(None, "ma", "row"),
        P("ma", None, "row"),
        P(None, "row"),
        P(None, "row"),
        P(),
        P(),
        P(),
        P("ma"),
        P("ma"),
    )
    out_specs = P(None, "ma", "row")
    return jax.shard_map(body, mesh=mesh, in_specs=in_specs, out_specs=out_specs, check_vma=False)
```

time: 1830 us -> 175 us (0.10)
  matrix products: 709 us -> 0 us
  local copies, waits for them, and re-layouts: 582 us -> 7.86 us
  waiting for transfers between devices: 367 us -> 57.4 us
  other arithmetic: 76.8 us -> 6.28 us
  Pallas kernels: 0 us -> 60.5 us
  loops' own time: 26.5 us -> 0 us
  starting transfers between devices: 5.89 us -> 24.4 us
    dot_general x34 -> x0, matrix products: 709 us -> none  [the longest x8 156 us: block_step(): lax.dot_general(products, cos_table, contract, precision=lax.Precision.HI...]
    psum x1 -> x0, waiting for transfers between devices: 291 us -> none  [body(): lax.psum(synth_rows(radius_count, coeff_rows, alpha_table, beta_table, ra...]
    mul x9 -> x0, local copies, waits for them, and re-layouts: 201 us -> none  [the longest x4 197 us: synth_rows(): filters[None, :, :, None, :] * coeff_rows[:, None, None, :, :]]
    reshape x22 -> x0, local copies, waits for them, and re-layouts: 192 us -> none  [the longest x1 153 us: adjoint_rows(): adjoint_terms.reshape(local_orders, row_count, 2, 2, local_degrees)]
    reduce_sum x9 -> x2, other arithmetic: 65 us -> 0.61 us  [the longest x1 0.43 us: slot_tables(): jnp.sum(jnp.where(by_device[:, None, :] // device_count == wanted[None, :...]
    pallas_call x0 -> x5, Pallas kernels: none -> 60.5 us  [the longest x2 23.1 us: adjoint(): pl.pallas_call(kernel, grid_spec=pltpu.PrefetchScalarGridSpec(num_scalar_...]
    slice x3 -> x0, local copies, waits for them, and re-layouts: 54.4 us -> none  [the longest x2 36.9 us: cycle_work(): real_part = separated[..., 0]]
    ppermute x0 -> x10, waiting for transfers between devices: none -> 33.4 us  [the longest x2 23.3 us: body(): incoming = lax.ppermute(outgoing, 'row', far_pairs)]
  transfers between devices with their start and end apart: 3 -> 13, of which waited for: 3 -> 5; matrix products, arithmetic and copies ran while one was open for 0% -> 3% of each run, Pallas kernels for 0% -> 13%
where the time goes in v1:
time: 175 us; the launch traced here: 174 us
  Pallas kernels  60.5 us (35%)
  waiting for transfers between devices  57.4 us (33%)
  starting transfers between devices  24.4 us (14%)
  blocking collectives  16.8 us (10%)
  local copies, waits for them, and re-layouts  7.86 us (4%)
  other arithmetic  6.28 us (4%)
    ppermute x2, waiting for transfers between devices, body(): incoming = lax.ppermute(outgoing, 'row', far_pairs)  23.3 us
    pallas_call x2, Pallas kernels, adjoint(): pl.pallas_call(kernel, grid_spec=pltpu.PrefetchScalarGridSpec(num_scalar_...  23.1 us
    pallas_call x2, Pallas kernels, synth(): pl.pallas_call(functools.partial(synth_kernel, jb_here, chunk * jb_here),...  22.6 us
    all_to_all x1, blocking collectives, body(): lax.all_to_all(analysed[chunk], 'ma', split_axis=0, concat_axis=0, tiled=...  16.8 us
    pallas_call x1, Pallas kernels, cycle_work(): pl.pallas_call(functools.partial(cycle_kernel, device_count, chunks), gri...  14.9 us
    all_to_all x1, waiting for transfers between devices, body(): lax.all_to_all(analysed[chunk], 'ma', split_axis=0, concat_axis=0, tiled=...  12.4 us
    all_to_all x2, starting transfers between devices, body(): lax.all_to_all(summed, 'ma', split_axis=0, concat_axis=0, tiled=True)  11.8 us
    all_to_all x2, waiting for transfers between devices, body(): lax.all_to_all(summed, 'ma', split_axis=0, concat_axis=0, tiled=True)  11.5 us
  transfers between devices with their start and end apart: 13, of which 5 were waited for; matrix products, arithmetic and copies ran while one was open for 3% of the time, Pallas kernels for 13%

profile of v1, /device:TPU:0, one launch (start us, length us, event | category | flops | bytes accessed | tf_op | source)
XLA Modules:
  0.0 173.6 jit_solution(4451760727243705339)
XLA Ops:
  1.0 0.9 copy-done
  1.9 0.9 copy-done.1
  3.4 1.2 copy-done.4
  4.7 11.0 %synth.3 = (f32[2,8,4,64,128]{4,3,2,1,0:T(8,128)S(1)}, f32[2,8,4,64,128]{4,3,2,1,0:T(8,128)S(1)}) custom-call(s32[256]{0:T(256)S(1)} %select_reduce_fusion.1.info_ref.refs_0_, s32[1]{0:T(128)} %bitcast.row_ref.refs_1_, s32[64]{0:T(128)S(1)} %copy-done.3, f32[2,256,512]{2,1,0:T(8,128)S(1)} %copy-done.4, f32[64,512]{1,0:T(8,128)S(1)} %copy-done, ...), custom_call_target="tpu_custom_call" | custom-call | flops 4294967296 | bytes 8388608 | tf_op jit(solution)/shard_map/synth/pallas_call | solution.py:159
  16.2 11.6 %synth.2 = (f32[2,8,4,64,128]{4,3,2,1,0:T(8,128)S(1)}, f32[2,8,4,64,128]{4,3,2,1,0:T(8,128)}) custom-call(s32[256]{0:T(256)S(1)} %select_reduce_fusion.1.info_ref.refs_0_, s32[1]{0:T(128)} %bitcast.row_ref.refs_1_, s32[64]{0:T(128)S(1)} %copy-done.3, f32[2,256,512]{2,1,0:T(8,128)S(1)} %copy-done.4, f32[64,512]{1,0:T(8,128)S(1)} %copy-done, ...), custom_call_target="tpu_custom_call" | custom-call | flops 4294967296 | bytes 8388608 | tf_op jit(solution)/shard_map/synth/pallas_call | solution.py:159
  28.1 3.0 %collective-permute-start.3 = (bf16[8,4,64,128]{3,2,1,0:T(8,128)(2,1)S(1)}, bf16[8,4,64,128]{3,2,1,0:T(8,128)(2,1)S(1)}, u32[]{:S(2)}, u32[]{:S(2)}) collective-permute-start(bf16[8,4,64,128]{3,2,1,0:T(8,128)(2,1)S(1)} %fusion.9), channel_id=1, source_target_pairs={{0,16},{8,24},{16,0},{24,8},{1,17},{9,25},{17,1},{25,9},{2,18},{10... | collective-permute-start | bytes 1572872 | tf_op jit(solution)/shard_map/ppermute | solution.py:521
  31.1 12.1 %collective-permute-done.3 = bf16[8,4,64,128]{3,2,1,0:T(8,128)(2,1)S(1)} collective-permute-done((bf16[8,4,64,128]{3,2,1,0:T(8,128)(2,1)S(1)}, bf16[8,4,64,128]{3,2,1,0:T(8,128)(2,1)S(1)}, u32[]{:S(2)}, u32[]{:S(2)}) %collective-permute-start.3) | collective-permute-done | bytes 524320 | tf_op jit(solution)/shard_map/ppermute | solution.py:521
  43.2 1.1 fusion.3
  44.3 6.0 %all-to-all-start.1 = ((bf16[8,4,64,128]{3,2,1,0:T(8,128)(2,1)}), bf16[8,4,64,128]{3,2,1,0:T(8,128)(2,1)S(1)}, u32[]{:S(2)}, u32[]{:S(2)}) async-start(bf16[8,4,64,128]{3,2,1,0:T(8,128)(2,1)} %fusion.3), calls=%async_computation.1 | async-start | bytes 1048576 | tf_op jit(solution)/shard_map/all_to_all | solution.py:523
  50.3 1.4 fusion.8
  51.8 1.6 collective-permute-start.1
  53.3 11.2 %collective-permute-done.1 = bf16[8,4,64,128]{3,2,1,0:T(8,128)(2,1)S(1)} collective-permute-done((bf16[8,4,64,128]{3,2,1,0:T(8,128)(2,1)S(1)}, bf16[8,4,64,128]{3,2,1,0:T(8,128)(2,1)S(1)}, u32[]{:S(2)}, u32[]{:S(2)}) %collective-permute-start.1) | collective-permute-done | bytes 524320 | tf_op jit(solution)/shard_map/ppermute | solution.py:521
  64.6 2.3 %fusion.7 = bf16[8,4,64,128]{3,2,1,0:T(8,128)(2,1)} fusion(f32[2,8,4,64,128]{4,3,2,1,0:T(8,128)} %collective-permute-done, bf16[8,4,64,128]{3,2,1,0:T(8,128)(2,1)S(1)} %collective-permute-done.1, f32[2,8,4,64,128]{4,3,2,1,0:T(8,128)S(1)} %get-tuple-element.11), kind=kLoop, calls=%fused_computation.12 | loop fusion | flops 1048576 | bytes 3145728 | tf_op jit(solution)/shard_map/convert_element_type | solution.py:522
  66.8 5.7 %all-to-all-start = ((bf16[8,4,64,128]{3,2,1,0:T(8,128)(2,1)}), bf16[8,4,64,128]{3,2,1,0:T(8,128)(2,1)S(1)}, u32[]{:S(2)}, u32[]{:S(2)}) async-start(bf16[8,4,64,128]{3,2,1,0:T(8,128)(2,1)} %fusion.7), calls=%async_computation | async-start | bytes 1048576 | tf_op jit(solution)/shard_map/all_to_all | solution.py:523
  73.4 11.5 %all-to-all-done.refs_0_ = bf16[8,4,64,128]{3,2,1,0:T(8,128)(2,1)S(1)} async-done(((bf16[8,4,64,128]{3,2,1,0:T(8,128)(2,1)}), bf16[8,4,64,128]{3,2,1,0:T(8,128)(2,1)S(1)}, u32[]{:S(2)}, u32[]{:S(2)}) %all-to-all-start) | async-done | bytes 524320 | tf_op jit(solution)/shard_map/all_to_all | solution.py:523
  85.6 14.9 %cycle_work.1 = (bf16[8,4,64,128]{3,2,1,0:T(8,128)(2,1)S(1)}, bf16[8,4,64,128]{3,2,1,0:T(8,128)(2,1)}) custom-call(s32[4]{0:T(128)S(1)} %copy-done.5, s32[1]{0:T(128)} %bitcast.row_ref.refs_1_, f32[4]{0:T(128)S(1)} %copy-done.6, bf16[8,4,64,128]{3,2,1,0:T(8,128)(2,1)S(1)} %all-to-all-done.refs_0_, bf16[8,4,64,128]{3,2,1,0:T(8,128)(2,1)S(1)} %all-to-all-done.1.refs_1_, ...), custom_call_target="tpu_custom_call" | custom-call | flops 4294967296 | bytes 8388608 | tf_op jit(solution)/shard_map/cycle_work/pallas_call | solution.py:298
  100.4 16.8 %all_to_all.20.refs_6_ = bf16[8,4,64,128]{3,2,1,0:T(8,128)(2,1)S(1)} all-to-all(bf16[8,4,64,128]{3,2,1,0:T(8,128)(2,1)S(1)} %get-tuple-element.16), channel_id=1, replica_groups=mesh['row'=4,'ma'=8] {'ma'}, dimensions={0} | all-to-all | bytes 1048576 | tf_op jit(solution)/shard_map/all_to_all | solution.py:527
  117.2 3.7 %all-to-all-start.2 = ((bf16[8,4,64,128]{3,2,1,0:T(8,128)(2,1)}), bf16[8,4,64,128]{3,2,1,0:T(8,128)(2,1)S(1)}, u32[]{:S(2)}, u32[]{:S(2)}) async-start(bf16[8,4,64,128]{3,2,1,0:T(8,128)(2,1)} %get-tuple-element.15), calls=%async_computation.2 | async-start | bytes 1048576 | tf_op jit(solution)/shard_map/all_to_all | solution.py:527
  120.9 1.6 collective-permute-start.8
  122.5 12.4 %all-to-all-done.2.own_ref = bf16[8,4,64,128]{3,2,1,0:T(8,128)(2,1)S(1)} async-done(((bf16[8,4,64,128]{3,2,1,0:T(8,128)(2,1)}), bf16[8,4,64,128]{3,2,1,0:T(8,128)(2,1)S(1)}, u32[]{:S(2)}, u32[]{:S(2)}) %all-to-all-start.2) | async-done | bytes 524320 | tf_op jit(solution)/shard_map/all_to_all | solution.py:527
  134.9 1.5 collective-permute-start.5
  137.0 10.1 %collective-permute-done.5.far_ref = bf16[8,4,64,128]{3,2,1,0:T(8,128)(2,1)S(1)} collective-permute-done((bf16[8,4,64,128]{3,2,1,0:T(8,128)(2,1)S(1)}, bf16[8,4,64,128]{3,2,1,0:T(8,128)(2,1)S(1)}, u32[]{:S(2)}, u32[]{:S(2)}) %collective-permute-start.5) | collective-permute-done | bytes 524320 | tf_op jit(solution)/shard_map/ppermute | solution.py:528
  148.7 11.3 %adjoint.2.earlier_ref = f32[2,256,512]{2,1,0:T(8,128)} custom-call(s32[256]{0:T(256)} %copy-done.2, s32[1]{0:T(128)} %bitcast.row_ref.refs_1_, s32[64]{0:T(128)} %node_ref.5, f32[64]{0:T(128)} %radial_ref.1, f32[64,512]{1,0:T(8,128)} %alpha_ref.5, f32[64,512]{1,0:T(8,128)} %beta_ref.5, bf16[8,4,64,128]{3,2,1,0:T(8,128)(2,1)} %copy-done.10, ...), custom_call_target="tpu_custom_call" | custom-call | flops 2147483648 | bytes 6291456 | tf_op jit(solution)/shard_map/adjoint/pallas_call | solution.py:443
  161.6 11.8 %adjoint.3 = f32[2,256,512]{2,1,0:T(8,128)} custom-call(s32[256]{0:T(256)} %copy-done.2, s32[1]{0:T(128)} %bitcast.row_ref.refs_1_, s32[64]{0:T(128)} %node_ref.5, f32[64]{0:T(128)} %radial_ref.1, f32[64,512]{1,0:T(8,128)} %alpha_ref.5, f32[64,512]{1,0:T(8,128)} %beta_ref.5, bf16[8,4,64,128]{3,2,1,0:T(8,128)(2,1)} %copy-done.9, ...), custom_call_target="tpu_custom_call" | custom-call | flops 2147483648 | bytes 6291456 | tf_op jit(solution)/shard_map/adjoint/pallas_call | solution.py:443
  (58 shorter events, 7.6 us)
Async XLA Ops:
  0.9 15.2 %copy-start.2 = (s32[256]{0:T(256)}, s32[256]{0:T(256)S(1)}, u32[]{:S(2)}) copy-start(s32[256]{0:T(256)S(1)} %select_reduce_fusion.1.info_ref.refs_0_) | copy-start | bytes 3076
  3.4 1.2 copy-start.4
  15.6 12.2 %collective-permute-start.2 = (f32[2,8,4,64,128]{4,3,2,1,0:T(8,128)S(1)}, f32[2,8,4,64,128]{4,3,2,1,0:T(8,128)S(1)}, u32[]{:S(2)}, u32[]{:S(2)}) collective-permute-start(f32[2,8,4,64,128]{4,3,2,1,0:T(8,128)S(1)} %get-tuple-element.14), channel_id=1, source_target_pairs={{0,8},{8,0},{16,24},{24,16},{1,9},{9,1},{17,25},{25,17},{2,10},{10... | collective-permute-start | bytes 6291464 | tf_op jit(solution)/shard_map/ppermute | solution.py:519
  27.8 22.5 %collective-permute-start = (f32[2,8,4,64,128]{4,3,2,1,0:T(8,128)}, f32[2,8,4,64,128]{4,3,2,1,0:T(8,128)}, u32[]{:S(2)}, u32[]{:S(2)}) collective-permute-start(f32[2,8,4,64,128]{4,3,2,1,0:T(8,128)} %get-tuple-element.12), channel_id=1, source_target_pairs={{0,8},{8,0},{16,24},{24,16},{1,9},{9,1},{17,25},{25,17},{2,10},{10... | collective-permute-start | bytes 6291464 | tf_op jit(solution)/shard_map/ppermute | solution.py:519
  28.1 15.1 %collective-permute-start.3 = (bf16[8,4,64,128]{3,2,1,0:T(8,128)(2,1)S(1)}, bf16[8,4,64,128]{3,2,1,0:T(8,128)(2,1)S(1)}, u32[]{:S(2)}, u32[]{:S(2)}) collective-permute-start(bf16[8,4,64,128]{3,2,1,0:T(8,128)(2,1)S(1)} %fusion.9), channel_id=1, source_target_pairs={{0,16},{8,24},{16,0},{24,8},{1,17},{9,25},{17,1},{25,9},{2,18},{10... | collective-permute-start | bytes 1572872 | tf_op jit(solution)/shard_map/ppermute | solution.py:521
  44.3 22.6 %all-to-all-start.1 = ((bf16[8,4,64,128]{3,2,1,0:T(8,128)(2,1)}), bf16[8,4,64,128]{3,2,1,0:T(8,128)(2,1)S(1)}, u32[]{:S(2)}, u32[]{:S(2)}) async-start(bf16[8,4,64,128]{3,2,1,0:T(8,128)(2,1)} %fusion.3), calls=%async_computation.1 | async-start | bytes 1048576 | tf_op jit(solution)/shard_map/all_to_all | solution.py:523
  51.7 20.9 %copy-start.17 = (s32[2048]{0:T(1024)S(1)}, s32[2048]{0:T(1024)}, u32[]{:S(2)}) copy-start(s32[2048]{0:T(1024)} %param.19) | copy-start | bytes 24580
  51.7 33.8 %copy-start.5 = (s32[4]{0:T(128)S(1)}, s32[4]{0:T(128)}, u32[]{:S(2)}) copy-start(s32[4]{0:T(128)} %offset_ref.1) | copy-start | bytes 52
  51.7 33.8 %copy-start.6 = (f32[4]{0:T(128)S(1)}, f32[4]{0:T(128)}, u32[]{:S(2)}) copy-start(f32[4]{0:T(128)} %weight_ref.1) | copy-start | bytes 52
  51.7 33.8 %copy-start.7 = (bf16[128,192]{1,0:T(8,128)(2,1)S(1)}, bf16[128,192]{1,0:T(8,128)(2,1)}, u32[]{:S(2)}) copy-start(bf16[128,192]{1,0:T(8,128)(2,1)} %constant.96.clone.refs_5_) | copy-start | bytes 147460
  51.7 33.8 %copy-start.8 = (bf16[128,128]{1,0:T(8,128)(2,1)S(1)}, bf16[128,128]{1,0:T(8,128)(2,1)}, u32[]{:S(2)}) copy-start(bf16[128,128]{1,0:T(8,128)(2,1)} %constant.95.clone.refs_4_) | copy-start | bytes 98308
  51.8 12.8 %collective-permute-start.1 = (bf16[8,4,64,128]{3,2,1,0:T(8,128)(2,1)S(1)}, bf16[8,4,64,128]{3,2,1,0:T(8,128)(2,1)S(1)}, u32[]{:S(2)}, u32[]{:S(2)}) collective-permute-start(bf16[8,4,64,128]{3,2,1,0:T(8,128)(2,1)S(1)} %fusion.8), channel_id=1, source_target_pairs={{0,16},{8,24},{16,0},{24,8},{1,17},{9,25},{17,1},{25,9},{2,18},{10... | collective-permute-start | bytes 1572872 | tf_op jit(solution)/shard_map/ppermute | solution.py:521
  66.8 18.1 %all-to-all-start = ((bf16[8,4,64,128]{3,2,1,0:T(8,128)(2,1)}), bf16[8,4,64,128]{3,2,1,0:T(8,128)(2,1)S(1)}, u32[]{:S(2)}, u32[]{:S(2)}) async-start(bf16[8,4,64,128]{3,2,1,0:T(8,128)(2,1)} %fusion.7), calls=%async_computation | async-start | bytes 1048576 | tf_op jit(solution)/shard_map/all_to_all | solution.py:523
  117.2 29.9 %copy-start.10 = (bf16[8,4,64,128]{3,2,1,0:T(8,128)(2,1)}, bf16[8,4,64,128]{3,2,1,0:T(8,128)(2,1)S(1)}, u32[]{:S(2)}) copy-start(bf16[8,4,64,128]{3,2,1,0:T(8,128)(2,1)S(1)} %all_to_all.20.refs_6_) | copy-start | bytes 1572868
  117.2 17.7 %all-to-all-start.2 = ((bf16[8,4,64,128]{3,2,1,0:T(8,128)(2,1)}), bf16[8,4,64,128]{3,2,1,0:T(8,128)(2,1)S(1)}, u32[]{:S(2)}, u32[]{:S(2)}) async-start(bf16[8,4,64,128]{3,2,1,0:T(8,128)(2,1)} %get-tuple-element.15), calls=%async_computation.2 | async-start | bytes 1048576 | tf_op jit(solution)/shard_map/all_to_all | solution.py:527
  120.9 15.5 %collective-permute-start.8 = (bf16[8,4,64,128]{3,2,1,0:T(8,128)(2,1)S(1)}, bf16[8,4,64,128]{3,2,1,0:T(8,128)(2,1)S(1)}, u32[]{:S(2)}, u32[]{:S(2)}) collective-permute-start(bf16[8,4,64,128]{3,2,1,0:T(8,128)(2,1)S(1)} %all_to_all.20.refs_6_), channel_id=1, source_target_pairs={{0,16},{8,24},{16,0},{24,8},{1,17},{9,25},{17,1},{25,9},{2,18},{10... | collective-permute-start | bytes 1572872 | tf_op jit(solution)/shard_map/ppermute | solution.py:528
  134.9 25.1 %copy-start.9 = (bf16[8,4,64,128]{3,2,1,0:T(8,128)(2,1)}, bf16[8,4,64,128]{3,2,1,0:T(8,128)(2,1)S(1)}, u32[]{:S(2)}) copy-start(bf16[8,4,64,128]{3,2,1,0:T(8,128)(2,1)S(1)} %all-to-all-done.2.own_ref) | copy-start | bytes 1572868
  134.9 12.2 %collective-permute-start.5 = (bf16[8,4,64,128]{3,2,1,0:T(8,128)(2,1)S(1)}, bf16[8,4,64,128]{3,2,1,0:T(8,128)(2,1)S(1)}, u32[]{:S(2)}, u32[]{:S(2)}) collective-permute-start(bf16[8,4,64,128]{3,2,1,0:T(8,128)(2,1)S(1)} %all-to-all-done.2.own_ref), channel_id=1, source_target_pairs={{0,16},{8,24},{16,0},{24,8},{1,17},{9,25},{17,1},{25,9},{2,18},{10... | collective-permute-start | bytes 1572872 | tf_op jit(solution)/shard_map/ppermute | solution.py:528
  136.4 10.7 %collective-permute-start.7 = (bf16[8,4,64,128]{3,2,1,0:T(8,128)(2,1)S(1)}, bf16[8,4,64,128]{3,2,1,0:T(8,128)(2,1)S(1)}, u32[]{:S(2)}, u32[]{:S(2)}) collective-permute-start(bf16[8,4,64,128]{3,2,1,0:T(8,128)(2,1)S(1)} %all_to_all.20.refs_6_), channel_id=1, source_target_pairs={{0,8},{8,0},{16,24},{24,16},{1,9},{9,1},{17,25},{25,17},{2,10},{10... | collective-permute-start | bytes 1572872 | tf_op jit(solution)/shard_map/ppermute | solution.py:529
  136.4 10.7 %copy-start.12 = (bf16[8,4,64,128]{3,2,1,0:T(8,128)(2,1)}, bf16[8,4,64,128]{3,2,1,0:T(8,128)(2,1)S(1)}, u32[]{:S(2)}) copy-start(bf16[8,4,64,128]{3,2,1,0:T(8,128)(2,1)S(1)} %collective-permute-done.8.refs_8_) | copy-start | bytes 1572868
  136.4 10.7 %collective-permute-start.9 = (bf16[8,4,64,128]{3,2,1,0:T(8,128)(2,1)S(1)}, bf16[8,4,64,128]{3,2,1,0:T(8,128)(2,1)S(1)}, u32[]{:S(2)}, u32[]{:S(2)}) collective-permute-start(bf16[8,4,64,128]{3,2,1,0:T(8,128)(2,1)S(1)} %collective-permute-done.8.refs_8_), channel_id=1, source_target_pairs={{0,8},{8,0},{16,24},{24,16},{1,9},{9,1},{17,25},{25,17},{2,10},{10... | collective-permute-start | bytes 1572872 | tf_op jit(solution)/shard_map/ppermute | solution.py:530
  136.9 23.1 %collective-permute-start.4 = (bf16[8,4,64,128]{3,2,1,0:T(8,128)(2,1)S(1)}, bf16[8,4,64,128]{3,2,1,0:T(8,128)(2,1)S(1)}, u32[]{:S(2)}, u32[]{:S(2)}) collective-permute-start(bf16[8,4,64,128]{3,2,1,0:T(8,128)(2,1)S(1)} %all-to-all-done.2.own_ref), channel_id=1, source_target_pairs={{0,8},{8,0},{16,24},{24,16},{1,9},{9,1},{17,25},{25,17},{2,10},{10... | collective-permute-start | bytes 1572872 | tf_op jit(solution)/shard_map/ppermute | solution.py:529
  147.0 13.0 %copy-start.11 = (bf16[8,4,64,128]{3,2,1,0:T(8,128)(2,1)}, bf16[8,4,64,128]{3,2,1,0:T(8,128)(2,1)S(1)}, u32[]{:S(2)}) copy-start(bf16[8,4,64,128]{3,2,1,0:T(8,128)(2,1)S(1)} %collective-permute-done.5.far_ref) | copy-start | bytes 1572868
  147.1 13.0 %collective-permute-start.6 = (bf16[8,4,64,128]{3,2,1,0:T(8,128)(2,1)S(1)}, bf16[8,4,64,128]{3,2,1,0:T(8,128)(2,1)S(1)}, u32[]{:S(2)}, u32[]{:S(2)}) collective-permute-start(bf16[8,4,64,128]{3,2,1,0:T(8,128)(2,1)S(1)} %collective-permute-done.5.far_ref), channel_id=1, source_target_pairs={{0,8},{8,0},{16,24},{24,16},{1,9},{9,1},{17,25},{25,17},{2,10},{10... | collective-permute-start | bytes 1572872 | tf_op jit(solution)/shard_map/ppermute | solution.py:530
  (7 other events, 5.7 us)

commit v2 on v1

v2 whole, which is shorter than its diff:
```python
import functools
import math

import jax
import jax.numpy as jnp
import numpy as np
from jax import lax
from jax.experimental import pallas as pl
from jax.experimental.pallas import tpu as pltpu
from jax.sharding import PartitionSpec as P

NPIX = 4096
SIDE = 64
PADDED = 136
CHUNKS = 4
MIB = 1 << 20
F32 = jnp.float32
BF16 = jnp.bfloat16


def split_table(table):
    high = table.astype(jnp.bfloat16)
    low = (table - high.astype(np.float64)).astype(jnp.bfloat16)
    return high, low


@functools.lru_cache(maxsize=None)
def fourier_tables():
    degree_a = np.arange(32).reshape(4, 1, 8)
    part = np.arange(2).reshape(1, 2, 1)
    first = np.arange(SIDE)
    spin = np.arange(2).reshape(2, 1, 1, 1, 1, 1, 1)
    order = SIDE * degree_a[None] + np.arange(SIDE).reshape(SIDE, 1, 1, 1)
    angle = (
        (2 * first.reshape(1, 1, 1, SIDE, 1, 1, 1) + spin)
        * order.reshape(1, SIDE, 1, 1, 4, 1, 8)
        % (2 * NPIX)
        * (math.pi / NPIX)
    )
    cosine, sine = np.cos(angle), np.sin(angle)
    row_part = np.arange(2).reshape(1, 1, 2, 1, 1, 1, 1)
    col_part = part.reshape(1, 1, 1, 1, 1, 2, 1)
    same = (row_part == col_part).astype(np.float64)
    cross = np.where(row_part == 1, 1.0, -1.0) * (row_part != col_part)
    doubling = np.where(order == 0, 1.0, 2.0).reshape(1, SIDE, 1, 1, 4, 1, 8)
    spread = (doubling * (same * cosine + cross * sine)).reshape(2, SIDE, 2 * SIDE, SIDE)
    gather = (same * cosine + cross * sine).reshape(2, SIDE, 2 * SIDE, SIDE)
    gather = np.swapaxes(gather, 2, 3)
    spread_parts = np.concatenate(split_table(spread), axis=3)
    gather_parts = np.concatenate(split_table(gather), axis=2)
    square = first[:, None] * first[None, :] % SIDE * (2.0 * math.pi / SIDE)
    pixel = np.concatenate(split_table(np.concatenate([np.cos(square), -np.sin(square)], axis=1)), axis=0)
    back_high, back_low = split_table(np.concatenate([np.cos(square), -np.sin(square)], axis=0))
    back = np.concatenate([back_high, back_high, back_low], axis=1)
    return spread_parts, pixel, back, gather_parts


def two_parts(value):
    high = value.astype(BF16)
    low = (value - high.astype(F32)).astype(BF16)
    return high, low


def whole(shape):
    return pl.BlockSpec(shape, lambda t, *_: (0,) * len(shape))


def anywhere():
    return pl.BlockSpec(memory_space=pl.ANY)


def fetch_group(first, legendre_ref, legendre_scr, sems, info_ref, step, group):
    for place in range(8):
        source = info_ref[(first + step) * 32 + group * 8 + place] >> 12
        pltpu.make_async_copy(
            legendre_ref.at[source], legendre_scr.at[step, group * 8 + place], sems.at[step, group]
        ).start()


def await_group(legendre_ref, legendre_scr, sems, step, group):
    pltpu.make_async_copy(
        legendre_ref.at[pl.ds(0, 8)],
        legendre_scr.at[step, pl.ds(group * 8, 8)],
        sems.at[step, group],
    ).wait()


def weights_kernel(
    node_ref, radial_ref, alpha_ref, beta_ref, synth_ref, adjoint_ref, filter_scr, weighted_scr
):
    radii = node_ref.shape[0]
    for radius in range(radii):
        node = node_ref[radius]
        scale = radial_ref[node]
        alpha = alpha_ref[pl.ds(node, 1), :]
        beta = beta_ref[pl.ds(node, 1), :]
        filter_scr[pl.ds(radius, 1), :] = alpha
        filter_scr[pl.ds(radii + radius, 1), :] = beta
        weighted_scr[pl.ds(radius, 1), :] = scale * alpha
        weighted_scr[pl.ds(radii + radius, 1), :] = (2.0 * scale) * beta
    high, low = two_parts(filter_scr[...].T)
    synth_ref[:, : 2 * radii] = high
    synth_ref[:, 2 * radii :] = low
    high, low = two_parts(weighted_scr[...])
    adjoint_ref[: 2 * radii, :] = high
    adjoint_ref[2 * radii :, :] = low


def filter_weights(radius_index, radial_weight, alpha_table, beta_table):
    radii = radius_index.shape[0]
    degrees = alpha_table.shape[1]
    return pl.pallas_call(
        weights_kernel,
        grid_spec=pltpu.PrefetchScalarGridSpec(
            num_scalar_prefetch=1,
            grid=(1,),
            in_specs=[
                pl.BlockSpec(memory_space=pltpu.SMEM),
                whole(alpha_table.shape),
                whole(beta_table.shape),
            ],
            out_specs=[whole((degrees, 4 * radii)), whole((4 * radii, degrees))],
            scratch_shapes=[pltpu.VMEM((2 * radii, degrees), F32)] * 2,
        ),
        out_shape=[
            jax.ShapeDtypeStruct((degrees, 4 * radii), BF16),
            jax.ShapeDtypeStruct((4 * radii, degrees), BF16),
        ],
        compiler_params=pltpu.CompilerParams(vmem_limit_bytes=16 * MIB),
        name="filter_weights",
    )(radius_index, radial_weight, alpha_table, beta_table)


def synth_kernel(
    jb_here,
    first,
    info_ref,
    where_ref,
    coeffs_ref,
    weight_ref,
    legendre_ref,
    order_ref,
    keep_ref,
    send_ref,
    coeffs_scr,
    weight_scr,
    legendre_scr,
    terms_even,
    terms_odd,
    sums_even,
    sums_odd,
    sems,
    input_sems,
):
    step = pl.program_id(0)
    row = where_ref[0]
    device = where_ref[1]
    degrees = coeffs_ref.shape[2]
    cycles = legendre_ref.shape[1]
    owners = cycles // 4
    lanes = weight_ref.shape[1] // 2
    coeffs_copy = pltpu.make_async_copy(coeffs_ref, coeffs_scr, input_sems.at[0])
    weight_copy = pltpu.make_async_copy(weight_ref, weight_scr, input_sems.at[1])

    @pl.when(step == 0)
    def _():
        coeffs_copy.start()
        for group in range(4):
            fetch_group(first, legendre_ref, legendre_scr, sems, info_ref, step, group)
        weight_copy.start()
        coeffs_copy.wait()
        weight_copy.wait()

    degree = row * degrees + lax.broadcasted_iota(jnp.int32, (1, degrees), 1)

    def build(group, terms):
        await_group(legendre_ref, legendre_scr, sems, step, group)
        for place in range(8):
            entry = info_ref[(first + step) * 32 + group * 8 + place]
            source = entry >> 12
            live = degree >= (entry & 4095)
            values = legendre_scr[step, group * 8 + place].astype(F32)
            for part in range(2):
                coeff = jnp.where(live, coeffs_scr[part, pl.ds(source, 1), :], 0.0)
                high, low = two_parts(values * coeff)
                start = (part * 8 + place) * cycles
                terms[0, start : start + cycles, :] = high
                terms[1, start : start + cycles, :] = low

    terms = (terms_even, terms_odd)
    sums = (sums_even, sums_odd)
    build(0, terms[0])
    for group in range(4):
        half = group % 2
        if group < 3:
            build(group + 1, terms[1 - half])

        @pl.when(step + 1 < jb_here)
        def _():
            fetch_group(first, legendre_ref, legendre_scr, sems, info_ref, step + 1, group)

        both = jnp.dot(terms[half][0], weight_scr[...], preferred_element_type=F32)
        rest = jnp.dot(terms[half][1], weight_scr[:, :lanes], preferred_element_type=F32)
        sums[half][...] = both[:, :lanes] + both[:, lanes:] + rest
        for distance in range(owners):
            owner = device ^ distance
            for away in range(4):
                cycle = 4 * owner + (row ^ away)
                piece = sums[half][pl.ds(cycle, 16, stride=cycles), :]
                target = send_ref if away % 2 else keep_ref
                target[away // 2, distance, 0, group * 16 : group * 16 + 16, :] = piece


def synth(chunk, chunks, info, where, coeffs, weight, legendre, order):
    orders_here, cycles, degrees = legendre.shape
    jb_here = orders_here // 32 // chunks
    owners = cycles // 4
    lanes = weight.shape[1] // 2
    out = jax.ShapeDtypeStruct((2, owners, jb_here, 64, lanes), F32)
    out_spec = pl.BlockSpec((2, owners, 1, 64, lanes), lambda t, *_: (0, 0, t, 0, 0))
    return pl.pallas_call(
        functools.partial(synth_kernel, jb_here, chunk * jb_here),
        grid_spec=pltpu.PrefetchScalarGridSpec(
            num_scalar_prefetch=2,
            grid=(jb_here,),
            in_specs=[anywhere(), anywhere(), anywhere(), anywhere()],
            out_specs=[out_spec, out_spec],
            scratch_shapes=[
                pltpu.VMEM(coeffs.shape, F32),
                pltpu.VMEM(weight.shape, BF16),
                pltpu.VMEM((jb_here, 32, cycles, degrees), BF16),
                pltpu.VMEM((2, 16 * cycles, degrees), BF16),
                pltpu.VMEM((2, 16 * cycles, degrees), BF16),
                pltpu.VMEM((16 * cycles, lanes), F32),
                pltpu.VMEM((16 * cycles, lanes), F32),
                pltpu.SemaphoreType.DMA((jb_here, 4)),
                pltpu.SemaphoreType.DMA((2,)),
            ],
        ),
        out_shape=[out, out],
        compiler_params=pltpu.CompilerParams(vmem_limit_bytes=48 * MIB),
        cost_estimate=pl.CostEstimate(
            flops=16 * jb_here * 4 * cycles * degrees * lanes * 2 * 4,
            bytes_accessed=jb_here * (32 * cycles * degrees * 2 + 2 * 2 * owners * 64 * lanes * 4),
            transcendentals=0,
        ),
        name="synth",
    )(info, where, coeffs, weight, legendre, order)


def core_sum_kernel(keep_ref, other_ref, order_ref, out_ref):
    out_ref[...] = (keep_ref[0] + other_ref[0]).astype(BF16)


def core_sum(keep, other, order):
    shape = keep.shape[1:]
    half = pl.BlockSpec((1,) + shape, lambda t: (1,) + (0,) * len(shape))
    return pl.pallas_call(
        core_sum_kernel,
        grid=(1,),
        in_specs=[half, half, anywhere()],
        out_specs=pl.BlockSpec(shape, lambda t: (0,) * len(shape)),
        out_shape=jax.ShapeDtypeStruct(shape, BF16),
        compiler_params=pltpu.CompilerParams(vmem_limit_bytes=16 * MIB),
        name="core_sum",
    )(keep, other, order)


def full_sum_kernel(keep_ref, other_ref, incoming_ref, order_ref, *outs):
    for distance, out in enumerate(outs):
        total = keep_ref[0, distance] + other_ref[0, distance]
        out[...] = (total + incoming_ref[distance].astype(F32)).astype(BF16)


def full_sum(keep, other, incoming, order):
    shape = keep.shape[1:]
    half = pl.BlockSpec((1,) + shape, lambda t: (0,) * (1 + len(shape)))
    piece = pl.BlockSpec(shape[1:], lambda t: (0,) * len(shape[1:]))
    return pl.pallas_call(
        full_sum_kernel,
        grid=(1,),
        in_specs=[half, half, pl.BlockSpec(shape, lambda t: (0,) * len(shape)), anywhere()],
        out_specs=[piece] * shape[0],
        out_shape=[jax.ShapeDtypeStruct(shape[1:], BF16)] * shape[0],
        compiler_params=pltpu.CompilerParams(vmem_limit_bytes=16 * MIB),
        name="full_sum",
    )(keep, other, incoming, order)


def join_kernel(order_ref, *refs):
    for distance, piece in enumerate(refs[:-1]):
        refs[-1][distance] = piece[...]


def join(pieces, order):
    shape = pieces[0].shape
    full = (len(pieces),) + shape
    piece = pl.BlockSpec(shape, lambda t: (0,) * len(shape))
    return pl.pallas_call(
        join_kernel,
        grid=(1,),
        in_specs=[anywhere()] + [piece] * len(pieces),
        out_specs=pl.BlockSpec(full, lambda t: (0,) * len(full)),
        out_shape=jax.ShapeDtypeStruct(full, BF16),
        compiler_params=pltpu.CompilerParams(vmem_limit_bytes=16 * MIB),
        name="join",
    )(order, *pieces)


def cycle_kernel(device_count, chunks, offset_ref, where_ref, weight_ref, *refs):
    pieces = [refs[c * device_count : (c + 1) * device_count] for c in range(chunks)]
    count = chunks * device_count
    place_ref, spread_ref, pixel_ref, back_ref, gather_ref = refs[count : count + 5]
    outs = refs[count + 5 : 2 * count + 5]
    outs = [outs[c * device_count : (c + 1) * device_count] for c in range(chunks)]
    spread_scr, gather_scr, middle_scr, product_scr, back_scr, sems = refs[2 * count + 5 :]
    jb_here = pieces[0][0].shape[0]
    turned = offset_ref[where_ref[0]]
    scale = weight_ref[where_ref[0]]
    lane = lax.broadcasted_iota(jnp.int32, (SIDE, 128), 1)

    def spread_copy(block):
        rows = pl.ds(block * device_count, device_count)
        return pltpu.make_async_copy(
            spread_ref.at[turned, rows], spread_scr.at[rows], sems.at[block]
        )

    gather_copy = pltpu.make_async_copy(
        gather_ref.at[turned], gather_scr, sems.at[chunks * jb_here]
    )
    for block in range(chunks * jb_here):
        spread_copy(block).start()
    gather_copy.start()

    for chunk in range(chunks):

        def spread_step(step, carry, chunk=chunk):
            block = chunk * jb_here + step
            spread_copy(block).wait()

            def one(spot):
                picked = jnp.zeros((SIDE, 128), BF16)
                for peer in range(device_count):
                    picked = jnp.where(
                        place_ref[peer, block] == lax.convert_element_type(spot, BF16),
                        pieces[chunk][peer][step],
                        picked,
                    )
                low_order = block * device_count + spot
                stage = jnp.dot(
                    spread_scr[low_order],
                    jnp.concatenate([picked, picked], axis=0),
                    preferred_element_type=F32,
                )
                middle_scr[pl.ds(low_order * PADDED, 128), :] = stage

            if device_count <= 8:
                for spot in range(device_count):
                    one(spot)
            else:
                lax.fori_loop(0, device_count, lambda s, x: (one(s), x)[1], 0)
            return carry

        lax.fori_loop(0, jb_here, spread_step, 0)

    def pixel_step(step, total):
        for inner in range(8):
            first = step * 8 + inner
            column = jnp.concatenate(
                [
                    middle_scr[pl.ds(first, SIDE, stride=PADDED), :],
                    middle_scr[pl.ds(first + SIDE, SIDE, stride=PADDED), :],
                ],
                axis=0,
            )
            high, low = two_parts(column)
            stage = jnp.dot(
                pixel_ref[...], jnp.concatenate([high, low], axis=1), preferred_element_type=F32
            )
            field = stage[:SIDE, :128] + stage[:SIDE, 128:] + stage[SIDE:, :128]
            other = pltpu.roll(field, 64, 1)
            product = other * jnp.where(lane < 64, other, field)
            product_scr[first] = product
            total = total + jnp.sum(product.reshape(8, 8, 128), axis=0)
        return total

    total = lax.fori_loop(0, SIDE // 8, pixel_step, jnp.zeros((8, 128), F32))
    mean = jnp.sum(total, axis=0, keepdims=True) * (1.0 / NPIX)

    def back_step(step, carry):
        for inner in range(8):
            first = step * 8 + inner
            high, low = two_parts(product_scr[first] - mean)
            back_scr[pl.ds(first * PADDED, 128), :] = jnp.dot(
                back_ref[...],
                jnp.concatenate([high, low, high], axis=0),
                preferred_element_type=F32,
            )
        return carry

    lax.fori_loop(0, SIDE // 8, back_step, 0)
    gather_copy.wait()

    for chunk in range(chunks):

        def gather_step(step, carry, chunk=chunk):
            block = chunk * jb_here + step

            def one(spot):
                low_order = block * device_count + spot
                column = jnp.concatenate(
                    [
                        back_scr[pl.ds(low_order, SIDE, stride=PADDED), :],
                        back_scr[pl.ds(low_order + SIDE, SIDE, stride=PADDED), :],
                    ],
                    axis=0,
                )
                high, low = two_parts(column)
                stage = jnp.dot(
                    gather_scr[low_order],
                    jnp.concatenate([high, low], axis=1),
                    preferred_element_type=F32,
                )
                value = stage[:SIDE, :128] + stage[:SIDE, 128:] + stage[SIDE:, :128]
                return (value * scale).astype(BF16)

            if device_count <= 8:
                found = [one(spot) for spot in range(device_count)]
                for peer in range(device_count):
                    place = place_ref[peer, block]
                    picked = found[0]
                    for spot in range(1, device_count):
                        picked = jnp.where(place == spot, found[spot], picked)
                    outs[chunk][peer][step] = picked
            else:

                def spot_step(spot, carry):
                    value = one(spot)
                    for peer in range(device_count):
                        outs[chunk][peer][step] = jnp.where(
                            place_ref[peer, block] == lax.convert_element_type(spot, BF16),
                            value,
                            outs[chunk][peer][step],
                        )
                    return carry

                lax.fori_loop(0, device_count, spot_step, 0)
            return carry

        lax.fori_loop(0, jb_here, gather_step, 0)


def cycle_work(pieces, places, offset, where, cycle_weight):
    chunks = len(pieces)
    device_count = len(pieces[0])
    shape = pieces[0][0].shape
    flat = [piece for chunk in pieces for piece in chunk]
    spread, pixel, back, gather = [jnp.asarray(table) for table in fourier_tables()]
    result = pl.pallas_call(
        functools.partial(cycle_kernel, device_count, chunks),
        grid_spec=pltpu.PrefetchScalarGridSpec(
            num_scalar_prefetch=2,
            grid=(1,),
            in_specs=[pl.BlockSpec(memory_space=pltpu.SMEM)]
            + [whole(shape)] * len(flat)
            + [whole(places.shape), anywhere(), whole(pixel.shape), whole(back.shape), anywhere()],
            out_specs=[whole(shape)] * len(flat),
            scratch_shapes=[
                pltpu.VMEM(spread.shape[1:], BF16),
                pltpu.VMEM(gather.shape[1:], BF16),
                pltpu.VMEM((SIDE * PADDED, 128), F32),
                pltpu.VMEM((SIDE, SIDE, 128), F32),
                pltpu.VMEM((SIDE * PADDED, 128), F32),
                pltpu.SemaphoreType.DMA((chunks * shape[0] + 1,)),
            ],
        ),
        out_shape=[jax.ShapeDtypeStruct(shape, BF16)] * len(flat),
        compiler_params=pltpu.CompilerParams(vmem_limit_bytes=48 * MIB),
        cost_estimate=pl.CostEstimate(
            flops=4 * SIDE * 128 * 256 * 256 * 2, bytes_accessed=8 * MIB, transcendentals=0
        ),
        name="cycle_work",
    )(offset, where, cycle_weight, *flat, places, spread, pixel, back, gather)
    return [result[c * device_count : (c + 1) * device_count] for c in range(chunks)]


def adjoint_kernel(jb_here, first, earlier_count, info_ref, where_ref, *refs):
    own_ref, core_ref, far_ref, corner_ref, weight_ref, legendre_ref, order_ref = refs[:7]
    earlier = refs[7 : 7 + earlier_count]
    out_ref = refs[7 + earlier_count]
    (
        weight_scr,
        legendre_scr,
        values_even,
        values_odd,
        terms_even,
        terms_odd,
        sorted_scr,
        sems,
        input_sem,
    ) = refs[8 + earlier_count :]
    step = pl.program_id(0)
    row = where_ref[0]
    device = where_ref[1]
    degrees = weight_ref.shape[1]
    cycles = legendre_ref.shape[1]
    owners = cycles // 4
    last = earlier_count > 0
    weight_copy = pltpu.make_async_copy(weight_ref, weight_scr, input_sem.at[0])

    def scatter(base, rows_ref, count):
        for place in range(count):
            target = info_ref[base + place] >> 12
            for part in range(2):
                out_ref[part, pl.ds(target, 1), :] = rows_ref[part, place : place + 1, :]

    @pl.when(step == 0)
    def _():
        weight_copy.start()
        for group in range(4):
            fetch_group(first, legendre_ref, legendre_scr, sems, info_ref, step, group)
        for index, rows_ref in enumerate(earlier):
            scatter(index * jb_here * 32, rows_ref, jb_here * 32)
        weight_copy.wait()

    degree = row * degrees + lax.broadcasted_iota(jnp.int32, (8, degrees), 1)
    sublane = lax.broadcasted_iota(jnp.int32, (8, degrees), 0)
    sources = (own_ref, core_ref, far_ref, corner_ref)
    values = (values_even, values_odd)
    terms = (terms_even, terms_odd)

    def multiply(group, out):
        rows = jnp.concatenate(
            [
                source[:, 0, group * 16 : group * 16 + 16, :].reshape(owners * 16, source.shape[3])
                for source in sources
            ],
            axis=0,
        )
        out[...] = jnp.dot(
            jnp.concatenate([rows, rows], axis=1), weight_scr[...], preferred_element_type=F32
        )

    def widen(group, out):
        await_group(legendre_ref, legendre_scr, sems, step, group)
        for place in range(8):
            start = place * (cycles + 8)
            wide = legendre_scr[step, group * 8 + place].astype(F32)
            for tile in range(degrees // 128):
                out[tile, start : start + cycles, :] = wide[:, tile * 128 : tile * 128 + 128]

    multiply(0, terms[0])
    widen(0, values[0])
    for group in range(4):
        half = group % 2
        if group < 3:
            multiply(group + 1, terms[1 - half])
            widen(group + 1, values[1 - half])

        @pl.when(step + 1 < jb_here)
        def _():
            fetch_group(first, legendre_ref, legendre_scr, sems, info_ref, step + 1, group)

        total = [jnp.zeros((8, degrees), F32), jnp.zeros((8, degrees), F32)]
        for away in range(4):
            for distance in range(owners):
                cycle = 4 * (device ^ distance) + (row ^ away)
                factor = jnp.concatenate(
                    [
                        values[half][tile, pl.ds(cycle, 8, stride=cycles + 8), :]
                        for tile in range(degrees // 128)
                    ],
                    axis=1,
                )
                start = (away * owners + distance) * 16
                for part in range(2):
                    at = start + part * 8
                    total[part] = total[part] + terms[half][at : at + 8, :] * factor
        lowest = jnp.zeros((8, degrees), jnp.int32)
        for place in range(8):
            entry = info_ref[(first + step) * 32 + group * 8 + place]
            lowest = jnp.where(sublane == place, entry & 4095, lowest)
        for part in range(2):
            masked = jnp.where(degree >= lowest, total[part], 0.0)
            if last:
                sorted_scr[part, group * 8 : group * 8 + 8, :] = masked
            else:
                out_ref[part, group * 8 : group * 8 + 8, :] = masked
    if last:
        scatter((first + step) * 32, sorted_scr, 32)


def adjoint(chunk, chunks, info, where, weight, pieces, legendre, earlier, order):
    orders_here, cycles, degrees = legendre.shape
    jb_here = orders_here // 32 // chunks
    owners = cycles // 4
    lanes = weight.shape[0] // 2
    piece_spec = pl.BlockSpec((owners, 1, 64, lanes), lambda t, *_: (0, t, 0, 0))
    if earlier:
        out = jax.ShapeDtypeStruct((2, orders_here, degrees), F32)
        out_spec = whole(out.shape)
    else:
        out = jax.ShapeDtypeStruct((2, 32 * jb_here, degrees), F32)
        out_spec = pl.BlockSpec((2, 32, degrees), lambda t, *_: (0, t, 0))
    return pl.pallas_call(
        functools.partial(adjoint_kernel, jb_here, chunk * jb_here, len(earlier)),
        grid_spec=pltpu.PrefetchScalarGridSpec(
            num_scalar_prefetch=2,
            grid=(jb_here,),
            in_specs=[piece_spec] * 4
            + [anywhere()] * 3
            + [whole((2, 32 * jb_here, degrees))] * len(earlier),
            out_specs=out_spec,
            scratch_shapes=[
                pltpu.VMEM(weight.shape, BF16),
                pltpu.VMEM((jb_here, 32, cycles, degrees), BF16),
                pltpu.VMEM((degrees // 128, 8 * (cycles + 8), 128), F32),
                pltpu.VMEM((degrees // 128, 8 * (cycles + 8), 128), F32),
                pltpu.VMEM((16 * cycles, degrees), F32),
                pltpu.VMEM((16 * cycles, degrees), F32),
                pltpu.VMEM((2, 32, degrees), F32),
                pltpu.SemaphoreType.DMA((jb_here, 4)),
                pltpu.SemaphoreType.DMA((1,)),
            ],
        ),
        out_shape=out,
        compiler_params=pltpu.CompilerParams(vmem_limit_bytes=48 * MIB),
        cost_estimate=pl.CostEstimate(
            flops=16 * jb_here * 4 * cycles * degrees * lanes * 2 * 2,
            bytes_accessed=jb_here * (32 * cycles * degrees * 2 + 4 * owners * 64 * lanes * 2),
            transcendentals=0,
        ),
        name="adjoint",
    )(info, where, *pieces, weight, legendre, order, *earlier)


def slot_tables(orders, device_count, ma_id):
    local_orders = orders.shape[0] // device_count
    blocks = local_orders // 32
    position = jnp.arange(local_orders, dtype=jnp.int32)
    wanted = blocks * (position % 32) + position // 32
    by_device = orders.reshape(device_count, local_orders)
    by_device = by_device[jnp.arange(device_count, dtype=jnp.int32) ^ ma_id]
    mine = lax.dynamic_slice_in_dim(orders, ma_id * local_orders, local_orders)
    info = jnp.sum(
        jnp.where(mine[None, :] // device_count == wanted[:, None], position[None, :] * 4096 + mine[None, :], 0),
        axis=1,
    )
    place = jnp.sum(
        jnp.where(
            by_device[:, None, :] // device_count == wanted[None, :, None],
            by_device[:, None, :] % device_count,
            0,
        ),
        axis=2,
    )
    place = place.reshape(device_count, blocks, 4, 1, 8, 1)
    place = jnp.broadcast_to(place, (device_count, blocks, 4, 2, 8, 128))
    return info, place.reshape(device_count, blocks, 64, 128).astype(BF16)


def body(
    coeffs,
    legendre,
    alpha_table,
    beta_table,
    radial_weight,
    radius_index,
    orders,
    cycle_offset,
    cycle_weight,
):
    row_id = lax.axis_index("row")
    ma_id = lax.axis_index("ma")
    device_count = lax.axis_size("ma")
    row_count = lax.axis_size("row")
    where = jnp.stack([row_id, ma_id]).astype(jnp.int32)
    info, places = slot_tables(orders, device_count, ma_id)
    synth_weight, adjoint_weight = filter_weights(
        radius_index, radial_weight, alpha_table, beta_table
    )
    core_pairs = [(i, i ^ 1) for i in range(row_count)]
    far_pairs = [(i, i ^ 2) for i in range(row_count)]
    chunks = min(CHUNKS, coeffs.shape[1] // 32)

    def exchange(pieces):
        return [pieces[0]] + [
            lax.ppermute(pieces[d], "ma", [(i, i ^ d) for i in range(device_count)])
            for d in range(1, device_count)
        ]

    kept, others, outgoing = [], [], []
    for chunk in range(chunks):
        order = outgoing[chunk - 2] if chunk >= 2 else info
        keep, send = synth(chunk, chunks, info, where, coeffs, synth_weight, legendre, order)
        kept.append(keep)
        others.append(lax.ppermute(send, "row", core_pairs))
        if chunk >= 1:
            outgoing.append(core_sum(kept[chunk - 1], others[chunk - 1], keep))
    outgoing.append(core_sum(kept[-1], others[-1], info))
    arrived = []
    for chunk in range(chunks):
        incoming = lax.ppermute(outgoing[chunk], "row", far_pairs)
        order = kept[-1] if chunk == 0 else outgoing[-1]
        arrived.append(exchange(full_sum(kept[chunk], others[chunk], incoming, order)))
    analysed = cycle_work(arrived, places, cycle_offset, where, cycle_weight)
    owned = []
    returned = [exchange(pieces) for pieces in analysed]
    for chunk in range(chunks):
        owned.append(join(returned[chunk], info if chunk == 0 else owned[-1]))
    gradient = []
    for chunk in range(chunks):
        own = owned[chunk]
        far = lax.ppermute(own, "row", far_pairs)
        core = lax.ppermute(own, "row", core_pairs)
        corner = lax.ppermute(far, "row", core_pairs)
        last = chunk == chunks - 1
        result = adjoint(
            chunk,
            chunks,
            info,
            where,
            adjoint_weight,
            (own, core, far, corner),
            legendre,
            gradient if last else [],
            owned[min(chunk + 2, chunks - 1)],
        )
        gradient.append(result)
    return gradient[-1]


def solution(mesh):
    in_specs = (
        P(None, "ma", "row"),
        P("ma", None, "row"),
        P(None, "row"),
        P(None, "row"),
        P(),
        P(),
        P(),
        P("ma"),
        P("ma"),
    )
    out_specs = P(None, "ma", "row")
    return jax.shard_map(body, mesh=mesh, in_specs=in_specs, out_specs=out_specs, check_vma=False)
```

time: 175 us -> 222 us (1.27)
  starting transfers between devices: 24.4 us -> 101 us
  waiting for transfers between devices: 57.4 us -> 31.2 us
  blocking collectives: 16.8 us -> 0 us
  Pallas kernels: 60.5 us -> 72.7 us
  local copies, waits for them, and re-layouts: 7.86 us -> 12.5 us
  other arithmetic: 6.28 us -> 2.67 us
    ppermute x4 -> x64, starting transfers between devices: 5.25 us -> 96.2 us  [the longest x56 89.7 us: exchange(): lax.ppermute(pieces[d], 'ma', [(i, i ^ d) for i in range(device_count)])]
    all_to_all x3 -> x0, waiting for transfers between devices: 23.9 us -> none  [the longest x1 12.4 us: body(): lax.all_to_all(analysed[chunk], 'ma', split_axis=0, concat_axis=0, tiled=...]
    all_to_all x1 -> x0, blocking collectives: 16.8 us -> none  [body(): lax.all_to_all(analysed[chunk], 'ma', split_axis=0, concat_axis=0, tiled=...]
    all_to_all x3 -> x0, starting transfers between devices: 15.4 us -> none  [the longest x2 11.8 us: body(): lax.all_to_all(summed, 'ma', split_axis=0, concat_axis=0, tiled=True)]
    pallas_call x2 -> x4, Pallas kernels: 22.6 us -> 34.1 us  [synth(): pl.pallas_call(functools.partial(synth_kernel, jb_here, chunk * jb_here),...]
    ppermute x4 -> x64, waiting for transfers between devices: 23.3 us -> 18.1 us  [the longest x56 11.5 us: exchange(): lax.ppermute(pieces[d], 'ma', [(i, i ^ d) for i in range(device_count)])]
    convert_element_type x4 -> x0, other arithmetic: 4.89 us -> none  [the longest x2 3.32 us: body(): summed = (keep[0] + other[0] + incoming.astype(F32)).astype(BF16)]
    ppermute x2 -> x4, waiting for transfers between devices: 10.1 us -> 13 us  [body(): far = lax.ppermute(own, 'row', far_pairs)]
  transfers between devices with their start and end apart: 13 -> 76, of which waited for: 5 -> 12; matrix products, arithmetic and copies ran while one was open for 3% -> 2% of each run, Pallas kernels for 13% -> 19%
where the time goes in v2:
time: 222 us; the launch traced here: 221 us
  starting transfers between devices  101 us (45%)
  Pallas kernels  72.7 us (33%)
  waiting for transfers between devices  31.2 us (14%)
  local copies, waits for them, and re-layouts  12.5 us (6%)
  other arithmetic  2.67 us (1%)
    ppermute x56, starting transfers between devices, exchange(): lax.ppermute(pieces[d], 'ma', [(i, i ^ d) for i in range(device_count)])  89.7 us
    pallas_call x4, Pallas kernels, synth(): pl.pallas_call(functools.partial(synth_kernel, jb_here, chunk * jb_here),...  34.1 us
    pallas_call x4, Pallas kernels, adjoint(): pl.pallas_call(functools.partial(adjoint_kernel, jb_here, chunk * jb_here...  20.9 us
    pallas_call x1, Pallas kernels, cycle_work(): pl.pallas_call(functools.partial(cycle_kernel, device_count, chunks), gri...  13.9 us
    ppermute x4, waiting for transfers between devices, body(): far = lax.ppermute(own, 'row', far_pairs)  13 us
    ppermute x56, waiting for transfers between devices, exchange(): lax.ppermute(pieces[d], 'ma', [(i, i ^ d) for i in range(device_count)])  11.5 us
    unnamed x38, local copies, waits for them, and re-layouts  9.56 us
    ppermute x4, waiting for transfers between devices, body(): incoming = lax.ppermute(outgoing[chunk], 'row', far_pairs)  6.64 us
  transfers between devices with their start and end apart: 76, of which 12 were waited for; matrix products, arithmetic and copies ran while one was open for 2% of the time, Pallas kernels for 19%

profile of v2, /device:TPU:0, one launch (start us, length us, event | category | flops | bytes accessed | tf_op | source)
XLA Modules:
  0.0 221.1 jit_solution(7604626384546775893)
XLA Ops:
  7.3 8.5 %synth.4 = (f32[2,8,2,64,128]{4,3,2,1,0:T(8,128)S(1)}, f32[2,8,2,64,128]{4,3,2,1,0:T(8,128)S(1)}) custom-call(s32[256]{0:T(256)S(1)} %select_reduce_fusion.1.info_ref.order_ref, s32[2]{0:T(128)S(1)} %pad_add_fusion.where_ref, f32[2,256,512]{2,1,0:T(8,128)S(1)} %copy-done, bf16[512,256]{1,0:T(8,128)(2,1)S(1)} %get-tuple-element.79.weight_ref, ...), custom_call_target="tpu_custom_call" | custom-call | flops 2147483648 | bytes 4194304 | tf_op jit(solution)/shard_map/synth/pallas_call | solution.py:221
  16.3 8.5 %synth.5 = (f32[2,8,2,64,128]{4,3,2,1,0:T(8,128)S(1)}, f32[2,8,2,64,128]{4,3,2,1,0:T(8,128)S(1)}) custom-call(s32[256]{0:T(256)S(1)} %select_reduce_fusion.1.info_ref.order_ref, s32[2]{0:T(128)S(1)} %pad_add_fusion.where_ref, f32[2,256,512]{2,1,0:T(8,128)S(1)} %copy-done, bf16[512,256]{1,0:T(8,128)(2,1)S(1)} %get-tuple-element.79.weight_ref, ...), custom_call_target="tpu_custom_call" | custom-call | flops 2147483648 | bytes 4194304 | tf_op jit(solution)/shard_map/synth/pallas_call | solution.py:221
  24.9 8.5 %synth.6 = (f32[2,8,2,64,128]{4,3,2,1,0:T(8,128)S(1)}, f32[2,8,2,64,128]{4,3,2,1,0:T(8,128)S(1)}) custom-call(s32[256]{0:T(256)S(1)} %select_reduce_fusion.1.info_ref.order_ref, s32[2]{0:T(128)S(1)} %pad_add_fusion.where_ref, f32[2,256,512]{2,1,0:T(8,128)S(1)} %copy-done, bf16[512,256]{1,0:T(8,128)(2,1)S(1)} %get-tuple-element.79.weight_ref, ...), custom_call_target="tpu_custom_call" | custom-call | flops 2147483648 | bytes 4194304 | tf_op jit(solution)/shard_map/synth/pallas_call | solution.py:221
  34.0 8.7 %synth.7 = (f32[2,8,2,64,128]{4,3,2,1,0:T(8,128)S(1)}, f32[2,8,2,64,128]{4,3,2,1,0:T(8,128)S(1)}) custom-call(s32[256]{0:T(256)S(1)} %select_reduce_fusion.1.info_ref.order_ref, s32[2]{0:T(128)S(1)} %pad_add_fusion.where_ref, f32[2,256,512]{2,1,0:T(8,128)S(1)} %copy-done, bf16[512,256]{1,0:T(8,128)(2,1)S(1)} %get-tuple-element.79.weight_ref, ...), custom_call_target="tpu_custom_call" | custom-call | flops 2147483648 | bytes 4194304 | tf_op jit(solution)/shard_map/synth/pallas_call | solution.py:221
  42.8 3.0 %collective-permute-start.1 = (bf16[8,2,64,128]{3,2,1,0:T(8,128)(2,1)S(1)}, bf16[8,2,64,128]{3,2,1,0:T(8,128)(2,1)S(1)}, u32[]{:S(2)}, u32[]{:S(2)}) collective-permute-start(bf16[8,2,64,128]{3,2,1,0:T(8,128)(2,1)S(1)} %core_sum.4.order_ref), channel_id=1, source_target_pairs={{0,16},{8,24},{16,0},{24,8},{1,17},{9,25},{17,1},{25,9},{2,18},{10... | collective-permute-start | bytes 786440 | tf_op jit(solution)/shard_map/ppermute | solution.py:703
  48.2 4.7 %collective-permute-done.1.incoming_ref = bf16[8,2,64,128]{3,2,1,0:T(8,128)(2,1)S(1)} collective-permute-done((bf16[8,2,64,128]{3,2,1,0:T(8,128)(2,1)S(1)}, bf16[8,2,64,128]{3,2,1,0:T(8,128)(2,1)S(1)}, u32[]{:S(2)}, u32[]{:S(2)}) %collective-permute-start.1) | collective-permute-done | bytes 262176 | tf_op jit(solution)/shard_map/ppermute | solution.py:703
  58.5 3.0 %collective-permute-start.5 = (bf16[2,64,128]{2,1,0:T(8,128)(2,1)S(1)}, bf16[2,64,128]{2,1,0:T(8,128)(2,1)S(1)}, u32[]{:S(2)}, u32[]{:S(2)}) collective-permute-start(bf16[2,64,128]{2,1,0:T(8,128)(2,1)S(1)} %get-tuple-element.89), channel_id=1, source_target_pairs={{0,3},{1,2},{2,1},{3,0},{4,7},{5,6},{6,5},{7,4},{8,11},{9,10},{10,... | collective-permute-start | bytes 98312 | tf_op jit(solution)/shard_map/ppermute | solution.py:688
  61.5 2.6 %collective-permute-start.6 = (bf16[2,64,128]{2,1,0:T(8,128)(2,1)S(1)}, bf16[2,64,128]{2,1,0:T(8,128)(2,1)S(1)}, u32[]{:S(2)}, u32[]{:S(2)}) collective-permute-start(bf16[2,64,128]{2,1,0:T(8,128)(2,1)S(1)} %get-tuple-element.90), channel_id=1, source_target_pairs={{0,4},{1,5},{2,6},{3,7},{4,0},{5,1},{6,2},{7,3},{8,12},{9,13},{10,... | collective-permute-start | bytes 98312 | tf_op jit(solution)/shard_map/ppermute | solution.py:688
  64.4 3.2 %collective-permute-start.8 = (bf16[2,64,128]{2,1,0:T(8,128)(2,1)S(1)}, bf16[2,64,128]{2,1,0:T(8,128)(2,1)S(1)}, u32[]{:S(2)}, u32[]{:S(2)}) collective-permute-start(bf16[2,64,128]{2,1,0:T(8,128)(2,1)S(1)} %get-tuple-element.92), channel_id=1, source_target_pairs={{0,6},{1,7},{2,4},{3,5},{4,2},{5,3},{6,0},{7,1},{8,14},{9,15},{10,... | collective-permute-start | bytes 98312 | tf_op jit(solution)/shard_map/ppermute | solution.py:688
  71.1 3.8 %collective-permute-done.9.refs_7_ = bf16[2,64,128]{2,1,0:T(8,128)(2,1)S(1)} collective-permute-done((bf16[2,64,128]{2,1,0:T(8,128)(2,1)S(1)}, bf16[2,64,128]{2,1,0:T(8,128)(2,1)S(1)}, u32[]{:S(2)}, u32[]{:S(2)}) %collective-permute-start.9) | collective-permute-done | bytes 32800 | tf_op jit(solution)/shard_map/ppermute | solution.py:688
  93.5 2.8 %collective-permute-start.25 = (bf16[2,64,128]{2,1,0:T(8,128)(2,1)S(1)}, bf16[2,64,128]{2,1,0:T(8,128)(2,1)S(1)}, u32[]{:S(2)}, u32[]{:S(2)}) collective-permute-start(bf16[2,64,128]{2,1,0:T(8,128)(2,1)S(1)} %copy-done.12), channel_id=1, source_target_pairs={{0,5},{1,4},{2,7},{3,6},{4,1},{5,0},{6,3},{7,2},{8,13},{9,12},{10,... | collective-permute-start | bytes 98312 | tf_op jit(solution)/shard_map/ppermute | solution.py:688
  104.7 2.9 %collective-permute-start.33 = (bf16[2,64,128]{2,1,0:T(8,128)(2,1)}, bf16[2,64,128]{2,1,0:T(8,128)(2,1)S(1)}, u32[]{:S(2)}, u32[]{:S(2)}) collective-permute-start(bf16[2,64,128]{2,1,0:T(8,128)(2,1)} %get-tuple-element.117), channel_id=1, source_target_pairs={{0,5},{1,4},{2,7},{3,6},{4,1},{5,0},{6,3},{7,2},{8,13},{9,12},{10,... | collective-permute-start | bytes 98312 | tf_op jit(solution)/shard_map/ppermute | solution.py:688
  113.5 2.5 %collective-permute-done.35.refs_31_ = bf16[2,64,128]{2,1,0:T(8,128)(2,1)S(1)} collective-permute-done((bf16[2,64,128]{2,1,0:T(8,128)(2,1)}, bf16[2,64,128]{2,1,0:T(8,128)(2,1)S(1)}, u32[]{:S(2)}, u32[]{:S(2)}) %collective-permute-start.35) | collective-permute-done | bytes 32800 | tf_op jit(solution)/shard_map/ppermute | solution.py:688
  118.9 13.9 %cycle_work.1 = (bf16[2,64,128]{2,1,0:T(8,128)(2,1)S(1)}, bf16[2,64,128]{2,1,0:T(8,128)(2,1)S(1)}, bf16[2,64,128]{2,1,0:T(8,128)(2,1)S(1)}, bf16[2,64,128]{2,1,0...) custom-call(s32[4]{0:T(128)S(1)} %copy-done.13, ...), custom_call_target="tpu_custom_call" | custom-call | flops 4294967296 | bytes 8388608 | tf_op jit(solution)/shard_map/cycle_work/pallas_call | solution.py:459
  137.1 3.0 %collective-permute-start.40 = (bf16[2,64,128]{2,1,0:T(8,128)(2,1)S(1)}, bf16[2,64,128]{2,1,0:T(8,128)(2,1)S(1)}, u32[]{:S(2)}, u32[]{:S(2)}) collective-permute-start(bf16[2,64,128]{2,1,0:T(8,128)(2,1)S(1)} %get-tuple-element.125), channel_id=1, source_target_pairs={{0,5},{1,4},{2,7},{3,6},{4,1},{5,0},{6,3},{7,2},{8,13},{9,12},{10,... | collective-permute-start | bytes 98312 | tf_op jit(solution)/shard_map/ppermute | solution.py:688
  148.4 2.9 %collective-permute-start.47 = (bf16[2,64,128]{2,1,0:T(8,128)(2,1)S(1)}, bf16[2,64,128]{2,1,0:T(8,128)(2,1)S(1)}, u32[]{:S(2)}, u32[]{:S(2)}) collective-permute-start(bf16[2,64,128]{2,1,0:T(8,128)(2,1)S(1)} %get-tuple-element.133), channel_id=1, source_target_pairs={{0,5},{1,4},{2,7},{3,6},{4,1},{5,0},{6,3},{7,2},{8,13},{9,12},{10,... | collective-permute-start | bytes 98312 | tf_op jit(solution)/shard_map/ppermute | solution.py:688
  159.5 2.9 %collective-permute-start.54 = (bf16[2,64,128]{2,1,0:T(8,128)(2,1)S(1)}, bf16[2,64,128]{2,1,0:T(8,128)(2,1)S(1)}, u32[]{:S(2)}, u32[]{:S(2)}) collective-permute-start(bf16[2,64,128]{2,1,0:T(8,128)(2,1)S(1)} %get-tuple-element.141), channel_id=1, source_target_pairs={{0,5},{1,4},{2,7},{3,6},{4,1},{5,0},{6,3},{7,2},{8,13},{9,12},{10,... | collective-permute-start | bytes 98312 | tf_op jit(solution)/shard_map/ppermute | solution.py:688
  170.7 2.9 %collective-permute-start.61 = (bf16[2,64,128]{2,1,0:T(8,128)(2,1)S(1)}, bf16[2,64,128]{2,1,0:T(8,128)(2,1)S(1)}, u32[]{:S(2)}, u32[]{:S(2)}) collective-permute-start(bf16[2,64,128]{2,1,0:T(8,128)(2,1)S(1)} %get-tuple-element.149), channel_id=1, source_target_pairs={{0,5},{1,4},{2,7},{3,6},{4,1},{5,0},{6,3},{7,2},{8,13},{9,12},{10,... | collective-permute-start | bytes 98312 | tf_op jit(solution)/shard_map/ppermute | solution.py:688
  188.1 5.3 %collective-permute-done.68.refs_2_ = bf16[8,2,64,128]{3,2,1,0:T(8,128)(2,1)S(1)} collective-permute-done((bf16[8,2,64,128]{3,2,1,0:T(8,128)(2,1)S(1)}, bf16[8,2,64,128]{3,2,1,0:T(8,128)(2,1)S(1)}, u32[]{:S(2)}, u32[]{:S(2)}) %collective-permute-start.68) | collective-permute-done | bytes 262176 | tf_op jit(solution)/shard_map/ppermute | solution.py:714
  193.4 3.2 %collective-permute-done.71.refs_2_ = bf16[8,2,64,128]{3,2,1,0:T(8,128)(2,1)S(1)} collective-permute-done((bf16[8,2,64,128]{3,2,1,0:T(8,128)(2,1)S(1)}, bf16[8,2,64,128]{3,2,1,0:T(8,128)(2,1)S(1)}, u32[]{:S(2)}, u32[]{:S(2)}) %collective-permute-start.71) | collective-permute-done | bytes 262176 | tf_op jit(solution)/shard_map/ppermute | solution.py:714
  199.9 4.9 %adjoint.4.refs_7_ = f32[2,64,512]{2,1,0:T(8,128)S(1)} custom-call(s32[256]{0:T(256)S(1)} %select_reduce_fusion.1.info_ref.order_ref, s32[2]{0:T(128)S(1)} %pad_add_fusion.where_ref, bf16[8,2,64,128]{3,2,1,0:T(8,128)(2,1)S(1)} %join.4.order_ref.refs_0_, bf16[8,2,64,128]{3,2,1,0:T(8,128)(2,1)S(1)} %collective-permute-done.67.refs_1_, ...), custom_call_target="tpu_custom_call" | custom-call | flops 1073741824 | bytes 3145728 | tf_op jit(solution)/shard_map/adjoint/pallas_call | solution.py:605
  204.8 4.9 %adjoint.5.refs_8_ = f32[2,64,512]{2,1,0:T(8,128)S(1)} custom-call(s32[256]{0:T(256)S(1)} %select_reduce_fusion.1.info_ref.order_ref, s32[2]{0:T(128)S(1)} %pad_add_fusion.where_ref, bf16[8,2,64,128]{3,2,1,0:T(8,128)(2,1)S(1)} %join.5.order_ref.refs_0_, bf16[8,2,64,128]{3,2,1,0:T(8,128)(2,1)S(1)} %collective-permute-done.70.refs_1_, ...), custom_call_target="tpu_custom_call" | custom-call | flops 1073741824 | bytes 3145728 | tf_op jit(solution)/shard_map/adjoint/pallas_call | solution.py:605
  209.8 4.9 %adjoint.6.refs_9_ = f32[2,64,512]{2,1,0:T(8,128)S(1)} custom-call(s32[256]{0:T(256)S(1)} %select_reduce_fusion.1.info_ref.order_ref, s32[2]{0:T(128)S(1)} %pad_add_fusion.where_ref, bf16[8,2,64,128]{3,2,1,0:T(8,128)(2,1)S(1)} %join.6.order_ref.refs_6_.refs_0_, bf16[8,2,64,128]{3,2,1,0:T(8,128)(2,1)S(1)} %collective-permute-done.73.refs_1_, ...), custom_call_target="tpu_custom_call" | custom-call | flops 1073741824 | bytes 3145728 | tf_op jit(solution)/shard_map/adjoint/pallas_call | solution.py:605
  214.7 6.3 %adjoint.7 = f32[2,256,512]{2,1,0:T(8,128)} custom-call(s32[256]{0:T(256)S(1)} %select_reduce_fusion.1.info_ref.order_ref, s32[2]{0:T(128)S(1)} %pad_add_fusion.where_ref, bf16[8,2,64,128]{3,2,1,0:T(8,128)(2,1)S(1)} %join.7.refs_6_.refs_0_, bf16[8,2,64,128]{3,2,1,0:T(8,128)(2,1)S(1)} %collective-permute-done.64.refs_1_, ...), custom_call_target="tpu_custom_call" | custom-call | flops 1073741824 | bytes 3145728 | tf_op jit(solution)/shard_map/adjoint/pallas_call | solution.py:605
  (202 shorter events, 103.1 us)
Async XLA Ops:
  33.4 12.4 %collective-permute-start.19 = (f32[2,8,2,64,128]{4,3,2,1,0:T(8,128)S(1)}, f32[2,8,2,64,128]{4,3,2,1,0:T(8,128)S(1)}, u32[]{:S(2)}, u32[]{:S(2)}) collective-permute-start(f32[2,8,2,64,128]{4,3,2,1,0:T(8,128)S(1)} %get-tuple-element.103), channel_id=1, source_target_pairs={{0,8},{8,0},{16,24},{24,16},{1,9},{9,1},{17,25},{25,17},{2,10},{10... | collective-permute-start | bytes 3145736 | tf_op jit(solution)/shard_map/ppermute | solution.py:697
  42.8 10.1 %collective-permute-start.1 = (bf16[8,2,64,128]{3,2,1,0:T(8,128)(2,1)S(1)}, bf16[8,2,64,128]{3,2,1,0:T(8,128)(2,1)S(1)}, u32[]{:S(2)}, u32[]{:S(2)}) collective-permute-start(bf16[8,2,64,128]{3,2,1,0:T(8,128)(2,1)S(1)} %core_sum.4.order_ref), channel_id=1, source_target_pairs={{0,16},{8,24},{16,0},{24,8},{1,17},{9,25},{17,1},{25,9},{2,18},{10... | collective-permute-start | bytes 786440 | tf_op jit(solution)/shard_map/ppermute | solution.py:703
  45.8 12.7 %collective-permute-start.10 = (bf16[8,2,64,128]{3,2,1,0:T(8,128)(2,1)S(1)}, bf16[8,2,64,128]{3,2,1,0:T(8,128)(2,1)S(1)}, u32[]{:S(2)}, u32[]{:S(2)}) collective-permute-start(bf16[8,2,64,128]{3,2,1,0:T(8,128)(2,1)S(1)} %core_sum.5.order_ref), channel_id=1, source_target_pairs={{0,16},{8,24},{16,0},{24,8},{1,17},{9,25},{17,1},{25,9},{2,18},{10... | collective-permute-start | bytes 786440 | tf_op jit(solution)/shard_map/ppermute | solution.py:703
  45.9 32.8 %collective-permute-start.20 = (bf16[8,2,64,128]{3,2,1,0:T(8,128)(2,1)S(1)}, bf16[8,2,64,128]{3,2,1,0:T(8,128)(2,1)S(1)}, u32[]{:S(2)}, u32[]{:S(2)}) collective-permute-start(bf16[8,2,64,128]{3,2,1,0:T(8,128)(2,1)S(1)} %core_sum.7), channel_id=1, source_target_pairs={{0,16},{8,24},{16,0},{24,8},{1,17},{9,25},{17,1},{25,9},{2,18},{10... | collective-permute-start | bytes 786440 | tf_op jit(solution)/shard_map/ppermute | solution.py:703
  48.0 40.6 %collective-permute-start.28 = (bf16[8,2,64,128]{3,2,1,0:T(8,128)(2,1)S(1)}, bf16[8,2,64,128]{3,2,1,0:T(8,128)(2,1)S(1)}, u32[]{:S(2)}, u32[]{:S(2)}) collective-permute-start(bf16[8,2,64,128]{3,2,1,0:T(8,128)(2,1)S(1)} %core_sum.6.order_ref), channel_id=1, source_target_pairs={{0,16},{8,24},{16,0},{24,8},{1,17},{9,25},{17,1},{25,9},{2,18},{10... | collective-permute-start | bytes 786440 | tf_op jit(solution)/shard_map/ppermute | solution.py:703
  74.9 10.2 %collective-permute-start.15 = (bf16[2,64,128]{2,1,0:T(8,128)(2,1)S(1)}, bf16[2,64,128]{2,1,0:T(8,128)(2,1)S(1)}, u32[]{:S(2)}, u32[]{:S(2)}) collective-permute-start(bf16[2,64,128]{2,1,0:T(8,128)(2,1)S(1)} %get-tuple-element.99), channel_id=1, source_target_pairs={{0,4},{1,5},{2,6},{3,7},{4,0},{5,1},{6,2},{7,3},{8,12},{9,13},{10,... | collective-permute-start | bytes 98312 | tf_op jit(solution)/shard_map/ppermute | solution.py:688
  82.7 10.7 %collective-permute-start.18 = (bf16[2,64,128]{2,1,0:T(8,128)(2,1)}, bf16[2,64,128]{2,1,0:T(8,128)(2,1)S(1)}, u32[]{:S(2)}, u32[]{:S(2)}) collective-permute-start(bf16[2,64,128]{2,1,0:T(8,128)(2,1)} %get-tuple-element.102), channel_id=1, source_target_pairs={{0,7},{1,6},{2,5},{3,4},{4,3},{5,2},{6,1},{7,0},{8,15},{9,14},{10,... | collective-permute-start | bytes 98312 | tf_op jit(solution)/shard_map/ppermute | solution.py:688
  85.0 11.2 %collective-permute-start.21 = (bf16[2,64,128]{2,1,0:T(8,128)(2,1)}, bf16[2,64,128]{2,1,0:T(8,128)(2,1)S(1)}, u32[]{:S(2)}, u32[]{:S(2)}) collective-permute-start(bf16[2,64,128]{2,1,0:T(8,128)(2,1)} %get-tuple-element.105), channel_id=1, source_target_pairs={{0,1},{1,0},{2,3},{3,2},{4,5},{5,4},{6,7},{7,6},{8,9},{9,8},{10,11... | collective-permute-start | bytes 98312 | tf_op jit(solution)/shard_map/ppermute | solution.py:688
  86.5 11.3 %collective-permute-start.22 = (bf16[2,64,128]{2,1,0:T(8,128)(2,1)}, bf16[2,64,128]{2,1,0:T(8,128)(2,1)S(1)}, u32[]{:S(2)}, u32[]{:S(2)}) collective-permute-start(bf16[2,64,128]{2,1,0:T(8,128)(2,1)} %get-tuple-element.106), channel_id=1, source_target_pairs={{0,2},{1,3},{2,0},{3,1},{4,6},{5,7},{6,4},{7,5},{8,10},{9,11},{10,... | collective-permute-start | bytes 98312 | tf_op jit(solution)/shard_map/ppermute | solution.py:688
  86.7 13.4 %collective-permute-start.23 = (bf16[2,64,128]{2,1,0:T(8,128)(2,1)}, bf16[2,64,128]{2,1,0:T(8,128)(2,1)S(1)}, u32[]{:S(2)}, u32[]{:S(2)}) collective-permute-start(bf16[2,64,128]{2,1,0:T(8,128)(2,1)} %get-tuple-element.107), channel_id=1, source_target_pairs={{0,3},{1,2},{2,1},{3,0},{4,7},{5,6},{6,5},{7,4},{8,11},{9,10},{10,... | collective-permute-start | bytes 98312 | tf_op jit(solution)/shard_map/ppermute | solution.py:688
  88.5 13.0 %collective-permute-start.24 = (bf16[2,64,128]{2,1,0:T(8,128)(2,1)}, bf16[2,64,128]{2,1,0:T(8,128)(2,1)}, u32[]{:S(2)}, u32[]{:S(2)}) collective-permute-start(bf16[2,64,128]{2,1,0:T(8,128)(2,1)} %get-tuple-element.108), channel_id=1, source_target_pairs={{0,4},{1,5},{2,6},{3,7},{4,0},{5,1},{6,2},{7,3},{8,12},{9,13},{10,... | collective-permute-start | bytes 98312 | tf_op jit(solution)/shard_map/ppermute | solution.py:688
  101.6 11.2 %collective-permute-start.31 = (bf16[2,64,128]{2,1,0:T(8,128)(2,1)}, bf16[2,64,128]{2,1,0:T(8,128)(2,1)S(1)}, u32[]{:S(2)}, u32[]{:S(2)}) collective-permute-start(bf16[2,64,128]{2,1,0:T(8,128)(2,1)} %get-tuple-element.115), channel_id=1, source_target_pairs={{0,3},{1,2},{2,1},{3,0},{4,7},{5,6},{6,5},{7,4},{8,11},{9,10},{10,... | collective-permute-start | bytes 98312 | tf_op jit(solution)/shard_map/ppermute | solution.py:688
  145.4 9.7 %collective-permute-start.45 = (bf16[2,64,128]{2,1,0:T(8,128)(2,1)S(1)}, bf16[2,64,128]{2,1,0:T(8,128)(2,1)S(1)}, u32[]{:S(2)}, u32[]{:S(2)}) collective-permute-start(bf16[2,64,128]{2,1,0:T(8,128)(2,1)S(1)} %get-tuple-element.131), channel_id=1, source_target_pairs={{0,3},{1,2},{2,1},{3,0},{4,7},{5,6},{6,5},{7,4},{8,11},{9,10},{10,... | collective-permute-start | bytes 98312 | tf_op jit(solution)/shard_map/ppermute | solution.py:688
  156.6 9.7 %collective-permute-start.52 = (bf16[2,64,128]{2,1,0:T(8,128)(2,1)S(1)}, bf16[2,64,128]{2,1,0:T(8,128)(2,1)S(1)}, u32[]{:S(2)}, u32[]{:S(2)}) collective-permute-start(bf16[2,64,128]{2,1,0:T(8,128)(2,1)S(1)} %get-tuple-element.139), channel_id=1, source_target_pairs={{0,3},{1,2},{2,1},{3,0},{4,7},{5,6},{6,5},{7,4},{8,11},{9,10},{10,... | collective-permute-start | bytes 98312 | tf_op jit(solution)/shard_map/ppermute | solution.py:688
  167.8 9.8 %collective-permute-start.59 = (bf16[2,64,128]{2,1,0:T(8,128)(2,1)S(1)}, bf16[2,64,128]{2,1,0:T(8,128)(2,1)S(1)}, u32[]{:S(2)}, u32[]{:S(2)}) collective-permute-start(bf16[2,64,128]{2,1,0:T(8,128)(2,1)S(1)} %get-tuple-element.147), channel_id=1, source_target_pairs={{0,3},{1,2},{2,1},{3,0},{4,7},{5,6},{6,5},{7,4},{8,11},{9,10},{10,... | collective-permute-start | bytes 98312 | tf_op jit(solution)/shard_map/ppermute | solution.py:688
  183.3 10.1 %collective-permute-start.68 = (bf16[8,2,64,128]{3,2,1,0:T(8,128)(2,1)S(1)}, bf16[8,2,64,128]{3,2,1,0:T(8,128)(2,1)S(1)}, u32[]{:S(2)}, u32[]{:S(2)}) collective-permute-start(bf16[8,2,64,128]{3,2,1,0:T(8,128)(2,1)S(1)} %join.4.order_ref.refs_0_), channel_id=1, source_target_pairs={{0,16},{8,24},{16,0},{24,8},{1,17},{9,25},{17,1},{25,9},{2,18},{10... | collective-permute-start | bytes 786440 | tf_op jit(solution)/shard_map/ppermute | solution.py:714
  183.8 12.8 %collective-permute-start.71 = (bf16[8,2,64,128]{3,2,1,0:T(8,128)(2,1)S(1)}, bf16[8,2,64,128]{3,2,1,0:T(8,128)(2,1)S(1)}, u32[]{:S(2)}, u32[]{:S(2)}) collective-permute-start(bf16[8,2,64,128]{3,2,1,0:T(8,128)(2,1)S(1)} %join.5.order_ref.refs_0_), channel_id=1, source_target_pairs={{0,16},{8,24},{16,0},{24,8},{1,17},{9,25},{17,1},{25,9},{2,18},{10... | collective-permute-start | bytes 786440 | tf_op jit(solution)/shard_map/ppermute | solution.py:714
  185.3 11.3 %collective-permute-start.67 = (bf16[8,2,64,128]{3,2,1,0:T(8,128)(2,1)S(1)}, bf16[8,2,64,128]{3,2,1,0:T(8,128)(2,1)S(1)}, u32[]{:S(2)}, u32[]{:S(2)}) collective-permute-start(bf16[8,2,64,128]{3,2,1,0:T(8,128)(2,1)S(1)} %join.4.order_ref.refs_0_), channel_id=1, source_target_pairs={{0,8},{8,0},{16,24},{24,16},{1,9},{9,1},{17,25},{25,17},{2,10},{10... | collective-permute-start | bytes 786440 | tf_op jit(solution)/shard_map/ppermute | solution.py:715
  185.3 14.1 %collective-permute-start.74 = (bf16[8,2,64,128]{3,2,1,0:T(8,128)(2,1)S(1)}, bf16[8,2,64,128]{3,2,1,0:T(8,128)(2,1)S(1)}, u32[]{:S(2)}, u32[]{:S(2)}) collective-permute-start(bf16[8,2,64,128]{3,2,1,0:T(8,128)(2,1)S(1)} %join.6.order_ref.refs_6_.refs_0_), channel_id=1, source_target_pairs={{0,16},{8,24},{16,0},{24,8},{1,17},{9,25},{17,1},{25,9},{2,18},{10... | collective-permute-start | bytes 786440 | tf_op jit(solution)/shard_map/ppermute | solution.py:714
  188.1 11.2 %collective-permute-start.70 = (bf16[8,2,64,128]{3,2,1,0:T(8,128)(2,1)S(1)}, bf16[8,2,64,128]{3,2,1,0:T(8,128)(2,1)S(1)}, u32[]{:S(2)}, u32[]{:S(2)}) collective-permute-start(bf16[8,2,64,128]{3,2,1,0:T(8,128)(2,1)S(1)} %join.5.order_ref.refs_0_), channel_id=1, source_target_pairs={{0,8},{8,0},{16,24},{24,16},{1,9},{9,1},{17,25},{25,17},{2,10},{10... | collective-permute-start | bytes 786440 | tf_op jit(solution)/shard_map/ppermute | solution.py:715
  196.5 13.2 %collective-permute-start.73 = (bf16[8,2,64,128]{3,2,1,0:T(8,128)(2,1)S(1)}, bf16[8,2,64,128]{3,2,1,0:T(8,128)(2,1)S(1)}, u32[]{:S(2)}, u32[]{:S(2)}) collective-permute-start(bf16[8,2,64,128]{3,2,1,0:T(8,128)(2,1)S(1)} %join.6.order_ref.refs_6_.refs_0_), channel_id=1, source_target_pairs={{0,8},{8,0},{16,24},{24,16},{1,9},{9,1},{17,25},{25,17},{2,10},{10... | collective-permute-start | bytes 786440 | tf_op jit(solution)/shard_map/ppermute | solution.py:715
  199.3 10.4 %collective-permute-start.75 = (bf16[8,2,64,128]{3,2,1,0:T(8,128)(2,1)S(1)}, bf16[8,2,64,128]{3,2,1,0:T(8,128)(2,1)S(1)}, u32[]{:S(2)}, u32[]{:S(2)}) collective-permute-start(bf16[8,2,64,128]{3,2,1,0:T(8,128)(2,1)S(1)} %collective-permute-done.74.refs_2_), channel_id=1, source_target_pairs={{0,8},{8,0},{16,24},{24,16},{1,9},{9,1},{17,25},{25,17},{2,10},{10... | collective-permute-start | bytes 786440 | tf_op jit(solution)/shard_map/ppermute | solution.py:716
  199.4 15.3 %collective-permute-start.64 = (bf16[8,2,64,128]{3,2,1,0:T(8,128)(2,1)S(1)}, bf16[8,2,64,128]{3,2,1,0:T(8,128)(2,1)S(1)}, u32[]{:S(2)}, u32[]{:S(2)}) collective-permute-start(bf16[8,2,64,128]{3,2,1,0:T(8,128)(2,1)S(1)} %join.7.refs_6_.refs_0_), channel_id=1, source_target_pairs={{0,8},{8,0},{16,24},{24,16},{1,9},{9,1},{17,25},{25,17},{2,10},{10... | collective-permute-start | bytes 786440 | tf_op jit(solution)/shard_map/ppermute | solution.py:715
  199.9 14.8 %collective-permute-start.66 = (bf16[8,2,64,128]{3,2,1,0:T(8,128)(2,1)S(1)}, bf16[8,2,64,128]{3,2,1,0:T(8,128)(2,1)S(1)}, u32[]{:S(2)}, u32[]{:S(2)}) collective-permute-start(bf16[8,2,64,128]{3,2,1,0:T(8,128)(2,1)S(1)} %collective-permute-done.65.refs_2_), channel_id=1, source_target_pairs={{0,8},{8,0},{16,24},{24,16},{1,9},{9,1},{17,25},{25,17},{2,10},{10... | collective-permute-start | bytes 786440 | tf_op jit(solution)/shard_map/ppermute | solution.py:716
  (71 other events, 466.5 us)

commit v3 on v2

--- a/solution.py
+++ b/solution.py
@@ -13,6 +13,7 @@
 SIDE = 64
 PADDED = 136
 CHUNKS = 4
+GROUPS = 2
 MIB = 1 << 20
 F32 = jnp.float32
 BF16 = jnp.bfloat16
@@ -51,7 +52,7 @@
     square = first[:, None] * first[None, :] % SIDE * (2.0 * math.pi / SIDE)
     pixel = np.concatenate(split_table(np.concatenate([np.cos(square), -np.sin(square)], axis=1)), axis=0)
     back_high, back_low = split_table(np.concatenate([np.cos(square), -np.sin(square)], axis=0))
-    back = np.concatenate([back_high, back_high, back_low], axis=1)
+    back = np.concatenate([back_high, back_high, back_low, back_low], axis=1)
     return spread_parts, pixel, back, gather_parts
 
 
@@ -69,12 +70,20 @@
     return pl.BlockSpec(memory_space=pl.ANY)
 
 
-def fetch_group(first, legendre_ref, legendre_scr, sems, info_ref, step, group):
-    for place in range(8):
-        source = info_ref[(first + step) * 32 + group * 8 + place] >> 12
-        pltpu.make_async_copy(
-            legendre_ref.at[source], legendre_scr.at[step, group * 8 + place], sems.at[step, group]
-        ).start()
+def fetch_all(first, jb_here, legendre_ref, legendre_scr, sems, info_ref):
+    def fetch_group(index, carry):
+        step = index // 4
+        group = lax.rem(index, 4)
+        for place in range(8):
+            source = info_ref[first * 32 + index * 8 + place] >> 12
+            pltpu.make_async_copy(
+                legendre_ref.at[source],
+                legendre_scr.at[step, group * 8 + place],
+                sems.at[step, group],
+            ).start()
+        return carry
+
+    lax.fori_loop(0, 4 * jb_here, fetch_group, 0)
 
 
 def await_group(legendre_ref, legendre_scr, sems, step, group):
@@ -85,22 +94,17 @@
     ).wait()
 
 
-def weights_kernel(
-    node_ref, radial_ref, alpha_ref, beta_ref, synth_ref, adjoint_ref, filter_scr, weighted_scr
-):
+def weights_kernel(node_ref, radial_ref, alpha_ref, beta_ref, filter_ref, adjoint_ref, weighted_scr):
     radii = node_ref.shape[0]
     for radius in range(radii):
         node = node_ref[radius]
         scale = radial_ref[node]
         alpha = alpha_ref[pl.ds(node, 1), :]
         beta = beta_ref[pl.ds(node, 1), :]
-        filter_scr[pl.ds(radius, 1), :] = alpha
-        filter_scr[pl.ds(radii + radius, 1), :] = beta
+        filter_ref[pl.ds(radius, 1), :] = alpha
+        filter_ref[pl.ds(radii + radius, 1), :] = beta
         weighted_scr[pl.ds(radius, 1), :] = scale * alpha
         weighted_scr[pl.ds(radii + radius, 1), :] = (2.0 * scale) * beta
-    high, low = two_parts(filter_scr[...].T)
-    synth_ref[:, : 2 * radii] = high
-    synth_ref[:, 2 * radii :] = low
     high, low = two_parts(weighted_scr[...])
     adjoint_ref[: 2 * radii, :] = high
     adjoint_ref[2 * radii :, :] = low
@@ -119,11 +123,11 @@
                 whole(alpha_table.shape),
                 whole(beta_table.shape),
             ],
-            out_specs=[whole((degrees, 4 * radii)), whole((4 * radii, degrees))],
-            scratch_shapes=[pltpu.VMEM((2 * radii, degrees), F32)] * 2,
+            out_specs=[whole((2 * radii, degrees)), whole((4 * radii, degrees))],
+            scratch_shapes=[pltpu.VMEM((2 * radii, degrees), F32)],
         ),
         out_shape=[
-            jax.ShapeDtypeStruct((degrees, 4 * radii), BF16),
+            jax.ShapeDtypeStruct((2 * radii, degrees), F32),
             jax.ShapeDtypeStruct((4 * radii, degrees), BF16),
         ],
         compiler_params=pltpu.CompilerParams(vmem_limit_bytes=16 * MIB),
@@ -137,119 +141,113 @@
     info_ref,
     where_ref,
     coeffs_ref,
-    weight_ref,
+    filter_ref,
     legendre_ref,
-    order_ref,
-    keep_ref,
-    send_ref,
-    coeffs_scr,
-    weight_scr,
-    legendre_scr,
-    terms_even,
-    terms_odd,
-    sums_even,
-    sums_odd,
-    sems,
-    input_sems,
+    *refs,
 ):
+    (
+        keep_ref,
+        send_ref,
+        coeffs_scr,
+        filter_scr,
+        legendre_scr,
+        sums_scr,
+        sems,
+        input_sems,
+    ) = refs[-8:]
     step = pl.program_id(0)
     row = where_ref[0]
-    device = where_ref[1]
     degrees = coeffs_ref.shape[2]
     cycles = legendre_ref.shape[1]
     owners = cycles // 4
-    lanes = weight_ref.shape[1] // 2
+    lanes = filter_ref.shape[0]
     coeffs_copy = pltpu.make_async_copy(coeffs_ref, coeffs_scr, input_sems.at[0])
-    weight_copy = pltpu.make_async_copy(weight_ref, weight_scr, input_sems.at[1])
+    filter_copy = pltpu.make_async_copy(filter_ref, filter_scr, input_sems.at[1])
 
     @pl.when(step == 0)
     def _():
+        filter_copy.start()
         coeffs_copy.start()
-        for group in range(4):
-            fetch_group(first, legendre_ref, legendre_scr, sems, info_ref, step, group)
-        weight_copy.start()
+        fetch_all(first, jb_here, legendre_ref, legendre_scr, sems, info_ref)
+        filter_copy.wait()
         coeffs_copy.wait()
-        weight_copy.wait()
 
     degree = row * degrees + lax.broadcasted_iota(jnp.int32, (1, degrees), 1)
 
-    def build(group, terms):
+    def one_group(group, carry):
         await_group(legendre_ref, legendre_scr, sems, step, group)
         for place in range(8):
             entry = info_ref[(first + step) * 32 + group * 8 + place]
             source = entry >> 12
             live = degree >= (entry & 4095)
-            values = legendre_scr[step, group * 8 + place].astype(F32)
+            filtered = jnp.concatenate(
+                [
+                    (
+                        filter_scr[...]
+                        * jnp.where(live, coeffs_scr[part, pl.ds(source, 1), :], 0.0)
+                    ).astype(BF16)
+                    for part in range(2)
+                ],
+                axis=0,
+            )
+            summed = lax.dot_general(
+                legendre_scr[step, group * 8 + place],
+                filtered,
+                (((1,), (1,)), ((), ())),
+                preferred_element_type=F32,
+            )
             for part in range(2):
-                coeff = jnp.where(live, coeffs_scr[part, pl.ds(source, 1), :], 0.0)
-                high, low = two_parts(values * coeff)
                 start = (part * 8 + place) * cycles
-                terms[0, start : start + cycles, :] = high
-                terms[1, start : start + cycles, :] = low
-
-    terms = (terms_even, terms_odd)
-    sums = (sums_even, sums_odd)
-    build(0, terms[0])
-    for group in range(4):
-        half = group % 2
-        if group < 3:
-            build(group + 1, terms[1 - half])
-
-        @pl.when(step + 1 < jb_here)
-        def _():
-            fetch_group(first, legendre_ref, legendre_scr, sems, info_ref, step + 1, group)
-
-        both = jnp.dot(terms[half][0], weight_scr[...], preferred_element_type=F32)
-        rest = jnp.dot(terms[half][1], weight_scr[:, :lanes], preferred_element_type=F32)
-        sums[half][...] = both[:, :lanes] + both[:, lanes:] + rest
-        for distance in range(owners):
-            owner = device ^ distance
+                sums_scr[start : start + cycles, :] = summed[:, part * lanes : (part + 1) * lanes]
+        for owner in range(owners):
             for away in range(4):
                 cycle = 4 * owner + (row ^ away)
-                piece = sums[half][pl.ds(cycle, 16, stride=cycles), :]
+                piece = sums_scr[pl.ds(cycle, 16, stride=cycles), :]
                 target = send_ref if away % 2 else keep_ref
-                target[away // 2, distance, 0, group * 16 : group * 16 + 16, :] = piece
-
-
-def synth(chunk, chunks, info, where, coeffs, weight, legendre, order):
+                target[away // 2, owner, 0, pl.ds(pl.multiple_of(group * 16, 16), 16), :] = (
+                    piece.astype(target.dtype)
+                )
+        return carry
+
+    lax.fori_loop(0, 4, one_group, 0)
+
+
+def synth(chunk, chunks, info, where, coeffs, filters, legendre, order):
     orders_here, cycles, degrees = legendre.shape
     jb_here = orders_here // 32 // chunks
     owners = cycles // 4
-    lanes = weight.shape[1] // 2
-    out = jax.ShapeDtypeStruct((2, owners, jb_here, 64, lanes), F32)
+    lanes = filters.shape[0]
+    shape = (2, owners, jb_here, 64, lanes)
     out_spec = pl.BlockSpec((2, owners, 1, 64, lanes), lambda t, *_: (0, 0, t, 0, 0))
     return pl.pallas_call(
         functools.partial(synth_kernel, jb_here, chunk * jb_here),
         grid_spec=pltpu.PrefetchScalarGridSpec(
             num_scalar_prefetch=2,
             grid=(jb_here,),
-            in_specs=[anywhere(), anywhere(), anywhere(), anywhere()],
+            in_specs=[anywhere()] * (3 + len(order)),
             out_specs=[out_spec, out_spec],
             scratch_shapes=[
                 pltpu.VMEM(coeffs.shape, F32),
-                pltpu.VMEM(weight.shape, BF16),
+                pltpu.VMEM(filters.shape, F32),
                 pltpu.VMEM((jb_here, 32, cycles, degrees), BF16),
-                pltpu.VMEM((2, 16 * cycles, degrees), BF16),
-                pltpu.VMEM((2, 16 * cycles, degrees), BF16),
-                pltpu.VMEM((16 * cycles, lanes), F32),
                 pltpu.VMEM((16 * cycles, lanes), F32),
                 pltpu.SemaphoreType.DMA((jb_here, 4)),
                 pltpu.SemaphoreType.DMA((2,)),
             ],
         ),
-        out_shape=[out, out],
-        compiler_params=pltpu.CompilerParams(vmem_limit_bytes=48 * MIB),
+        out_shape=[jax.ShapeDtypeStruct(shape, F32), jax.ShapeDtypeStruct(shape, BF16)],
+        compiler_params=pltpu.CompilerParams(vmem_limit_bytes=32 * MIB),
         cost_estimate=pl.CostEstimate(
             flops=16 * jb_here * 4 * cycles * degrees * lanes * 2 * 4,
-            bytes_accessed=jb_here * (32 * cycles * degrees * 2 + 2 * 2 * owners * 64 * lanes * 4),
+            bytes_accessed=jb_here * (32 * cycles * degrees * 2 + 2 * 2 * owners * 64 * lanes * 3),
             transcendentals=0,
         ),
         name="synth",
-    )(info, where, coeffs, weight, legendre, order)
+    )(info, where, coeffs, filters, legendre, *order)
 
 
 def core_sum_kernel(keep_ref, other_ref, order_ref, out_ref):
-    out_ref[...] = (keep_ref[0] + other_ref[0]).astype(BF16)
+    out_ref[...] = (keep_ref[0] + other_ref[0].astype(F32)).astype(BF16)
 
 
 def core_sum(keep, other, order):
@@ -262,59 +260,50 @@
         out_specs=pl.BlockSpec(shape, lambda t: (0,) * len(shape)),
         out_shape=jax.ShapeDtypeStruct(shape, BF16),
         compiler_params=pltpu.CompilerParams(vmem_limit_bytes=16 * MIB),
+        cost_estimate=pl.CostEstimate(flops=10**10, bytes_accessed=MIB, transcendentals=0),
         name="core_sum",
     )(keep, other, order)
 
 
-def full_sum_kernel(keep_ref, other_ref, incoming_ref, order_ref, *outs):
-    for distance, out in enumerate(outs):
-        total = keep_ref[0, distance] + other_ref[0, distance]
-        out[...] = (total + incoming_ref[distance].astype(F32)).astype(BF16)
-
-
-def full_sum(keep, other, incoming, order):
-    shape = keep.shape[1:]
-    half = pl.BlockSpec((1,) + shape, lambda t: (0,) * (1 + len(shape)))
-    piece = pl.BlockSpec(shape[1:], lambda t: (0,) * len(shape[1:]))
+def full_sum_kernel(order_ref, *refs):
+    out_ref = refs[-1]
+    start = 0
+    for index in range(0, len(refs) - 1, 3):
+        keep_ref, other_ref, incoming_ref = refs[index : index + 3]
+        count = incoming_ref.shape[1]
+        total = keep_ref[0] + other_ref[0].astype(F32) + incoming_ref[...].astype(F32)
+        out_ref[:, start : start + count] = total.astype(BF16)
+        start += count
+
+
+def full_sum(chunks, order):
+    operands, specs, count = [], [anywhere()], 0
+    for keep, other, incoming in chunks:
+        shape = incoming.shape
+        half = pl.BlockSpec((1,) + shape, lambda t: (0, 0, 0, 0, 0))
+        operands += [keep, other, incoming]
+        specs += [half, half, pl.BlockSpec(shape, lambda t: (0, 0, 0, 0))]
+        count += shape[1]
+    full = (shape[0], count) + shape[2:]
     return pl.pallas_call(
         full_sum_kernel,
         grid=(1,),
-        in_specs=[half, half, pl.BlockSpec(shape, lambda t: (0,) * len(shape)), anywhere()],
-        out_specs=[piece] * shape[0],
-        out_shape=[jax.ShapeDtypeStruct(shape[1:], BF16)] * shape[0],
-        compiler_params=pltpu.CompilerParams(vmem_limit_bytes=16 * MIB),
+        in_specs=specs,
+        out_specs=pl.BlockSpec(full, lambda t: (0, 0, 0, 0)),
+        out_shape=jax.ShapeDtypeStruct(full, BF16),
+        compiler_params=pltpu.CompilerParams(vmem_limit_bytes=24 * MIB),
+        cost_estimate=pl.CostEstimate(flops=10**10, bytes_accessed=MIB, transcendentals=0),
         name="full_sum",
-    )(keep, other, incoming, order)
-
-
-def join_kernel(order_ref, *refs):
-    for distance, piece in enumerate(refs[:-1]):
-        refs[-1][distance] = piece[...]
-
-
-def join(pieces, order):
-    shape = pieces[0].shape
-    full = (len(pieces),) + shape
-    piece = pl.BlockSpec(shape, lambda t: (0,) * len(shape))
-    return pl.pallas_call(
-        join_kernel,
-        grid=(1,),
-        in_specs=[anywhere()] + [piece] * len(pieces),
-        out_specs=pl.BlockSpec(full, lambda t: (0,) * len(full)),
-        out_shape=jax.ShapeDtypeStruct(full, BF16),
-        compiler_params=pltpu.CompilerParams(vmem_limit_bytes=16 * MIB),
-        name="join",
-    )(order, *pieces)
+    )(order, *operands)
 
 
 def cycle_kernel(device_count, chunks, offset_ref, where_ref, weight_ref, *refs):
-    pieces = [refs[c * device_count : (c + 1) * device_count] for c in range(chunks)]
-    count = chunks * device_count
+    pieces = refs[:chunks]
+    count = chunks
     place_ref, spread_ref, pixel_ref, back_ref, gather_ref = refs[count : count + 5]
     outs = refs[count + 5 : 2 * count + 5]
-    outs = [outs[c * device_count : (c + 1) * device_count] for c in range(chunks)]
     spread_scr, gather_scr, middle_scr, product_scr, back_scr, sems = refs[2 * count + 5 :]
-    jb_here = pieces[0][0].shape[0]
+    jb_here = pieces[0].shape[1]
     turned = offset_ref[where_ref[0]]
     scale = weight_ref[where_ref[0]]
     lane = lax.broadcasted_iota(jnp.int32, (SIDE, 128), 1)
@@ -343,7 +332,7 @@
                 for peer in range(device_count):
                     picked = jnp.where(
                         place_ref[peer, block] == lax.convert_element_type(spot, BF16),
-                        pieces[chunk][peer][step],
+                        pieces[chunk][peer, step],
                         picked,
                     )
                 low_order = block * device_count + spot
@@ -393,7 +382,7 @@
             high, low = two_parts(product_scr[first] - mean)
             back_scr[pl.ds(first * PADDED, 128), :] = jnp.dot(
                 back_ref[...],
-                jnp.concatenate([high, low, high], axis=0),
+                jnp.concatenate([high, low, high, low], axis=0),
                 preferred_element_type=F32,
             )
         return carry
@@ -431,16 +420,16 @@
                     picked = found[0]
                     for spot in range(1, device_count):
                         picked = jnp.where(place == spot, found[spot], picked)
-                    outs[chunk][peer][step] = picked
+                    outs[chunk][peer, step] = picked
             else:
 
                 def spot_step(spot, carry):
                     value = one(spot)
                     for peer in range(device_count):
-                        outs[chunk][peer][step] = jnp.where(
+                        outs[chunk][peer, step] = jnp.where(
                             place_ref[peer, block] == lax.convert_element_type(spot, BF16),
                             value,
-                            outs[chunk][peer][step],
+                            outs[chunk][peer, step],
                         )
                     return carry
 
@@ -452,11 +441,11 @@
 
 def cycle_work(pieces, places, offset, where, cycle_weight):
     chunks = len(pieces)
-    device_count = len(pieces[0])
-    shape = pieces[0][0].shape
-    flat = [piece for chunk in pieces for piece in chunk]
+    shape = pieces[0].shape
+    device_count = shape[0]
+    flat = list(pieces)
     spread, pixel, back, gather = [jnp.asarray(table) for table in fourier_tables()]
-    result = pl.pallas_call(
+    return pl.pallas_call(
         functools.partial(cycle_kernel, device_count, chunks),
         grid_spec=pltpu.PrefetchScalarGridSpec(
             num_scalar_prefetch=2,
@@ -471,7 +460,7 @@
                 pltpu.VMEM((SIDE * PADDED, 128), F32),
                 pltpu.VMEM((SIDE, SIDE, 128), F32),
                 pltpu.VMEM((SIDE * PADDED, 128), F32),
-                pltpu.SemaphoreType.DMA((chunks * shape[0] + 1,)),
+                pltpu.SemaphoreType.DMA((chunks * shape[1] + 1,)),
             ],
         ),
         out_shape=[jax.ShapeDtypeStruct(shape, BF16)] * len(flat),
@@ -481,7 +470,6 @@
         ),
         name="cycle_work",
     )(offset, where, cycle_weight, *flat, places, spread, pixel, back, gather)
-    return [result[c * device_count : (c + 1) * device_count] for c in range(chunks)]
 
 
 def adjoint_kernel(jb_here, first, earlier_count, info_ref, where_ref, *refs):
@@ -501,7 +489,6 @@
     ) = refs[8 + earlier_count :]
     step = pl.program_id(0)
     row = where_ref[0]
-    device = where_ref[1]
     degrees = weight_ref.shape[1]
     cycles = legendre_ref.shape[1]
     owners = cycles // 4
@@ -509,16 +496,21 @@
     weight_copy = pltpu.make_async_copy(weight_ref, weight_scr, input_sem.at[0])
 
     def scatter(base, rows_ref, count):
-        for place in range(count):
-            target = info_ref[base + place] >> 12
-            for part in range(2):
-                out_ref[part, pl.ds(target, 1), :] = rows_ref[part, place : place + 1, :]
+        def eight(block, carry):
+            start = pl.multiple_of(block * 8, 8)
+            rows = [rows_ref[part, pl.ds(start, 8), :] for part in range(2)]
+            for place in range(8):
+                target = info_ref[base + start + place] >> 12
+                for part in range(2):
+                    out_ref[part, pl.ds(target, 1), :] = rows[part][place : place + 1, :]
+            return carry
+
+        lax.fori_loop(0, count // 8, eight, 0)
 
     @pl.when(step == 0)
     def _():
         weight_copy.start()
-        for group in range(4):
-            fetch_group(first, legendre_ref, legendre_scr, sems, info_ref, step, group)
+        fetch_all(first, jb_here, legendre_ref, legendre_scr, sems, info_ref)
         for index, rows_ref in enumerate(earlier):
             scatter(index * jb_here * 32, rows_ref, jb_here * 32)
         weight_copy.wait()
@@ -557,14 +549,10 @@
             multiply(group + 1, terms[1 - half])
             widen(group + 1, values[1 - half])
 
-        @pl.when(step + 1 < jb_here)
-        def _():
-            fetch_group(first, legendre_ref, legendre_scr, sems, info_ref, step + 1, group)
-
         total = [jnp.zeros((8, degrees), F32), jnp.zeros((8, degrees), F32)]
         for away in range(4):
-            for distance in range(owners):
-                cycle = 4 * (device ^ distance) + (row ^ away)
+            for owner in range(owners):
+                cycle = 4 * owner + (row ^ away)
                 factor = jnp.concatenate(
                     [
                         values[half][tile, pl.ds(cycle, 8, stride=cycles + 8), :]
@@ -572,7 +560,7 @@
                     ],
                     axis=1,
                 )
-                start = (away * owners + distance) * 16
+                start = (away * owners + owner) * 16
                 for part in range(2):
                     at = start + part * 8
                     total[part] = total[part] + terms[half][at : at + 8, :] * factor
@@ -640,7 +628,6 @@
     position = jnp.arange(local_orders, dtype=jnp.int32)
     wanted = blocks * (position % 32) + position // 32
     by_device = orders.reshape(device_count, local_orders)
-    by_device = by_device[jnp.arange(device_count, dtype=jnp.int32) ^ ma_id]
     mine = lax.dynamic_slice_in_dim(orders, ma_id * local_orders, local_orders)
     info = jnp.sum(
         jnp.where(mine[None, :] // device_count == wanted[:, None], position[None, :] * 4096 + mine[None, :], 0),
@@ -683,50 +670,71 @@
     far_pairs = [(i, i ^ 2) for i in range(row_count)]
     chunks = min(CHUNKS, coeffs.shape[1] // 32)
 
-    def exchange(pieces):
-        return [pieces[0]] + [
-            lax.ppermute(pieces[d], "ma", [(i, i ^ d) for i in range(device_count)])
-            for d in range(1, device_count)
-        ]
-
-    kept, others, outgoing = [], [], []
-    for chunk in range(chunks):
-        order = outgoing[chunk - 2] if chunk >= 2 else info
+    groups = min(GROUPS, chunks)
+    size = chunks // groups
+    kept, others, outgoing, incoming, arrived = [], [], [], [], []
+
+    def launch(chunk, order):
         keep, send = synth(chunk, chunks, info, where, coeffs, synth_weight, legendre, order)
         kept.append(keep)
         others.append(lax.ppermute(send, "row", core_pairs))
-        if chunk >= 1:
-            outgoing.append(core_sum(kept[chunk - 1], others[chunk - 1], keep))
-    outgoing.append(core_sum(kept[-1], others[-1], info))
-    arrived = []
-    for chunk in range(chunks):
-        incoming = lax.ppermute(outgoing[chunk], "row", far_pairs)
-        order = kept[-1] if chunk == 0 else outgoing[-1]
-        arrived.append(exchange(full_sum(kept[chunk], others[chunk], incoming, order)))
+
+    def pass_on(chunk, order):
+        outgoing.append(core_sum(kept[chunk], others[chunk], order))
+        incoming.append(lax.ppermute(outgoing[chunk], "row", far_pairs))
+
+    def deliver(group, order):
+        own = slice(group * size, (group + 1) * size)
+        summed = full_sum(list(zip(kept[own], others[own], incoming[own])), order)
+        arrived.append(lax.all_to_all(summed, "ma", split_axis=0, concat_axis=0, tiled=True))
+        return summed
+
+    if chunks == 4:
+        launch(0, [])
+        launch(1, [])
+        pass_on(0, kept[1])
+        info, places = lax.optimization_barrier((info, places))
+        launch(2, [outgoing[0]])
+        pass_on(1, kept[2])
+        pass_on(2, outgoing[1])
+        launch(3, [outgoing[2], incoming[0]])
+        summed = deliver(0, kept[3])
+        pass_on(3, summed)
+        deliver(1, outgoing[3])
+    else:
+        for chunk in range(chunks):
+            launch(chunk, [])
+        for chunk in range(chunks):
+            pass_on(chunk, kept[-1])
+        for group in range(groups):
+            deliver(group, outgoing[-1])
     analysed = cycle_work(arrived, places, cycle_offset, where, cycle_weight)
-    owned = []
-    returned = [exchange(pieces) for pieces in analysed]
-    for chunk in range(chunks):
-        owned.append(join(returned[chunk], info if chunk == 0 else owned[-1]))
-    gradient = []
-    for chunk in range(chunks):
-        own = owned[chunk]
-        far = lax.ppermute(own, "row", far_pairs)
-        core = lax.ppermute(own, "row", core_pairs)
-        corner = lax.ppermute(far, "row", core_pairs)
-        last = chunk == chunks - 1
-        result = adjoint(
-            chunk,
-            chunks,
-            info,
-            where,
-            adjoint_weight,
-            (own, core, far, corner),
-            legendre,
-            gradient if last else [],
-            owned[min(chunk + 2, chunks - 1)],
+    own = [
+        lax.all_to_all(piece, "ma", split_axis=0, concat_axis=0, tiled=True) for piece in analysed
+    ]
+    far, gradient = [], []
+    for group in range(groups):
+        far.append(lax.ppermute(own[group], "row", far_pairs))
+        if group + 1 < groups:
+            far[group], own[group + 1] = lax.optimization_barrier((far[group], own[group + 1]))
+    for group in range(groups):
+        if gradient:
+            far[group], gradient[-1] = lax.optimization_barrier((far[group], gradient[-1]))
+        core = lax.ppermute(own[group], "row", core_pairs)
+        corner = lax.ppermute(far[group], "row", core_pairs)
+        gradient.append(
+            adjoint(
+                group,
+                groups,
+                info,
+                where,
+                adjoint_weight,
+                (own[group], core, far[group], corner),
+                legendre,
+                gradient if group == groups - 1 else [],
+                info,
+            )
         )
-        gradient.append(result)
     return gradient[-1]
 
 

time: 222 us -> 189 us (0.85)
  starting transfers between devices: 101 us -> 19.3 us
  blocking collectives: 0 us -> 35.7 us
  Pallas kernels: 72.7 us -> 83.6 us
  local copies, waits for them, and re-layouts: 12.5 us -> 17.9 us
    ppermute x76 -> x14, starting transfers between devices: 101 us -> 9.65 us  [the longest x4 7.46 us: pass_on(): incoming.append(lax.ppermute(outgoing[chunk], 'row', far_pairs))]
    all_to_all x0 -> x2, blocking collectives: none -> 35.7 us  [the longest x1 18.1 us: deliver(): lax.all_to_all(summed, 'ma', split_axis=0, concat_axis=0, tiled=True)]
    ppermute x76 -> x14, waiting for transfers between devices: 31.2 us -> 7.9 us  [the longest x2 3.82 us: body(): far.append(lax.ppermute(own[group], 'row', far_pairs))]
    all_to_all x0 -> x2, waiting for transfers between devices: none -> 21.6 us  [the longest x1 13.3 us: body(): lax.all_to_all(piece, 'ma', split_axis=0, concat_axis=0, tiled=True)]
    pallas_call x4, Pallas kernels: 34.1 us -> 45.8 us  [synth(): pl.pallas_call(functools.partial(synth_kernel, jb_here, chunk * jb_here),...]
    all_to_all x0 -> x2, starting transfers between devices: none -> 9.63 us  [the longest x1 5.95 us: deliver(): lax.all_to_all(summed, 'ma', split_axis=0, concat_axis=0, tiled=True)]
    unnamed x38 -> x58, local copies, waits for them, and re-layouts: 9.56 us -> 16.9 us
    pallas_call x4 -> x2, Pallas kernels: 20.9 us -> 18.7 us  [adjoint(): pl.pallas_call(functools.partial(adjoint_kernel, jb_here, chunk * jb_here...]
  transfers between devices with their start and end apart: 76 -> 16, of which waited for: 12 -> 6; matrix products, arithmetic and copies ran while one was open for 2% -> 1% of each run, Pallas kernels for 19% -> 25%
where the time goes in v3:
time: 189 us; the launch traced here: 188 us
  Pallas kernels  83.6 us (44%)
  blocking collectives  35.7 us (19%)
  waiting for transfers between devices  29.5 us (16%)
  starting transfers between devices  19.3 us (10%)
  local copies, waits for them, and re-layouts  17.9 us (9%)
    pallas_call x4, Pallas kernels, synth(): pl.pallas_call(functools.partial(synth_kernel, jb_here, chunk * jb_here),...  45.8 us
    pallas_call x2, Pallas kernels, adjoint(): pl.pallas_call(functools.partial(adjoint_kernel, jb_here, chunk * jb_here...  18.7 us
    all_to_all x1, blocking collectives, deliver(): lax.all_to_all(summed, 'ma', split_axis=0, concat_axis=0, tiled=True)  18.1 us
    all_to_all x1, blocking collectives, body(): lax.all_to_all(piece, 'ma', split_axis=0, concat_axis=0, tiled=True)  17.6 us
    unnamed x58, local copies, waits for them, and re-layouts  16.9 us
    pallas_call x1, Pallas kernels, cycle_work(): pl.pallas_call(functools.partial(cycle_kernel, device_count, chunks), gri...  14.1 us
    all_to_all x1, waiting for transfers between devices, body(): lax.all_to_all(piece, 'ma', split_axis=0, concat_axis=0, tiled=True)  13.3 us
    all_to_all x1, waiting for transfers between devices, deliver(): lax.all_to_all(summed, 'ma', split_axis=0, concat_axis=0, tiled=True)  8.22 us
  transfers between devices with their start and end apart: 16, of which 6 were waited for; matrix products, arithmetic and copies ran while one was open for 1% of the time, Pallas kernels for 25%

profile of v3, /device:TPU:0, one launch (start us, length us, event | category | flops | bytes accessed | tf_op | source)
XLA Modules:
  0.0 187.8 jit_solution(10777305658866543655)
XLA Ops:
  4.2 1.3 filter_weights.1
  5.5 3.4 %copy-done = bf16[256,32,512]{2,1,0:T(8,128)(2,1)S(1)} copy-done((bf16[256,32,512]{2,1,0:T(8,128)(2,1)S(1)}, bf16[256,32,512]{2,1,0:T(8,128)(2,1)}, u32[]{:S(2)}) %copy-start) | copy-done | bytes 8388632
  10.1 11.8 %synth.4 = (f32[2,8,2,64,128]{4,3,2,1,0:T(8,128)S(1)}, bf16[2,8,2,64,128]{4,3,2,1,0:T(8,128)(2,1)}) custom-call(s32[256]{0:T(256)S(1)} %select_reduce_fusion.1.info_ref.refs_6_, s32[2]{0:T(128)S(1)} %pad_add_fusion.where_ref, f32[2,256,512]{2,1,0:T(8,128)S(1)} %copy-done.1, f32[128,512]{1,0:T(8,128)S(1)} %get-tuple-element.24.filter_ref, ...), custom_call_target="tpu_custom_call" | custom-call | flops 2147483648 | bytes 3670016 | tf_op jit(solution)/shard_map/synth/pallas_call | solution.py:222
  22.4 11.8 %synth.5 = (f32[2,8,2,64,128]{4,3,2,1,0:T(8,128)S(1)}, bf16[2,8,2,64,128]{4,3,2,1,0:T(8,128)(2,1)}) custom-call(s32[256]{0:T(256)S(1)} %select_reduce_fusion.1.info_ref.refs_6_, s32[2]{0:T(128)S(1)} %pad_add_fusion.where_ref, f32[2,256,512]{2,1,0:T(8,128)S(1)} %copy-done.1, f32[128,512]{1,0:T(8,128)S(1)} %get-tuple-element.24.filter_ref, ...), custom_call_target="tpu_custom_call" | custom-call | flops 2147483648 | bytes 3670016 | tf_op jit(solution)/shard_map/synth/pallas_call | solution.py:222
  36.7 1.5 copy-done.10
  38.3 3.0 %collective-permute-start.3 = (bf16[8,2,64,128]{3,2,1,0:T(8,128)(2,1)S(1)}, bf16[8,2,64,128]{3,2,1,0:T(8,128)(2,1)S(1)}, u32[]{:S(2)}, u32[]{:S(2)}) collective-permute-start(bf16[8,2,64,128]{3,2,1,0:T(8,128)(2,1)S(1)} %core_sum.4.refs_0_), channel_id=1, source_target_pairs={{0,16},{8,24},{16,0},{24,8},{1,17},{9,25},{17,1},{25,9},{2,18},{10... | collective-permute-start | bytes 786440 | tf_op jit(solution)/shard_map/ppermute | solution.py:684
  41.3 11.1 %synth.6 = (f32[2,8,2,64,128]{4,3,2,1,0:T(8,128)S(1)}, bf16[2,8,2,64,128]{4,3,2,1,0:T(8,128)(2,1)S(1)}) custom-call(s32[256]{0:T(256)S(1)} %select_reduce_fusion.1.info_ref.refs_6_, s32[2]{0:T(128)S(1)} %pad_add_fusion.where_ref, f32[2,256,512]{2,1,0:T(8,128)S(1)} %copy-done.2, f32[128,512]{1,0:T(8,128)S(1)} %get-tuple-element.24.filter_ref, ...), custom_call_target="tpu_custom_call" | custom-call | flops 2147483648 | bytes 3670016 | tf_op jit(solution)/shard_map/synth/pallas_call | solution.py:222
  52.6 1.2 core_sum.5.order_ref
  53.8 2.4 %collective-permute-start.4 = (bf16[8,2,64,128]{3,2,1,0:T(8,128)(2,1)S(1)}, bf16[8,2,64,128]{3,2,1,0:T(8,128)(2,1)S(1)}, u32[]{:S(2)}, u32[]{:S(2)}) collective-permute-start(bf16[8,2,64,128]{3,2,1,0:T(8,128)(2,1)S(1)} %core_sum.5.order_ref), channel_id=1, source_target_pairs={{0,16},{8,24},{16,0},{24,8},{1,17},{9,25},{17,1},{25,9},{2,18},{10... | collective-permute-start | bytes 786440 | tf_op jit(solution)/shard_map/ppermute | solution.py:684
  57.6 11.1 %synth.7 = (f32[2,8,2,64,128]{4,3,2,1,0:T(8,128)S(1)}, bf16[2,8,2,64,128]{4,3,2,1,0:T(8,128)(2,1)S(1)}) custom-call(s32[256]{0:T(256)S(1)} %select_reduce_fusion.1.info_ref.refs_6_, s32[2]{0:T(128)S(1)} %pad_add_fusion.where_ref, f32[2,256,512]{2,1,0:T(8,128)S(1)} %copy-done.2, f32[128,512]{1,0:T(8,128)S(1)} %get-tuple-element.24.filter_ref, ...), custom_call_target="tpu_custom_call" | custom-call | flops 2147483648 | bytes 3670016 | tf_op jit(solution)/shard_map/synth/pallas_call | solution.py:222
  68.8 2.1 %full_sum.2.order_ref = bf16[8,4,64,128]{3,2,1,0:T(8,128)(2,1)} custom-call(f32[2,8,2,64,128]{4,3,2,1,0:T(8,128)S(1)} %get-tuple-element.31.order_ref.keep_ref.refs_3_, f32[2,8,2,64,128]{4,3,2,1,0:T(8,128)S(1)} %copy-done.8, bf16[2,8,2,64,128]{4,3,2,1,0:T(8,128)(2,1)S(1)} %collective-permute-done.other_ref.refs_1_, ...), custom_call_target="tpu_custom_call" | custom-call | flops 10000000000 | bytes 1048576 | tf_op jit(solution)/shard_map/full_sum/pallas_call | solution.py:288
  71.8 1.4 collective-permute-start.7
  73.2 6.0 %all-to-all-start = ((bf16[8,4,64,128]{3,2,1,0:T(8,128)(2,1)}), bf16[8,4,64,128]{3,2,1,0:T(8,128)(2,1)S(1)}, u32[]{:S(2)}, u32[]{:S(2)}) async-start(bf16[8,4,64,128]{3,2,1,0:T(8,128)(2,1)} %full_sum.2.order_ref), calls=%async_computation | async-start | bytes 1048576 | tf_op jit(solution)/shard_map/all_to_all | solution.py:689
  81.0 1.2 copy-done.13
  85.6 8.2 %all-to-all-done.refs_0_ = bf16[8,4,64,128]{3,2,1,0:T(8,128)(2,1)S(1)} async-done(((bf16[8,4,64,128]{3,2,1,0:T(8,128)(2,1)}), bf16[8,4,64,128]{3,2,1,0:T(8,128)(2,1)S(1)}, u32[]{:S(2)}, u32[]{:S(2)}) %all-to-all-start) | async-done | bytes 524320 | tf_op jit(solution)/shard_map/all_to_all | solution.py:689
  93.8 18.1 %all_to_all.20.refs_1_ = bf16[8,4,64,128]{3,2,1,0:T(8,128)(2,1)S(1)} all-to-all(bf16[8,4,64,128]{3,2,1,0:T(8,128)(2,1)S(1)} %full_sum.3), channel_id=1, replica_groups=mesh['row'=4,'ma'=8] {'ma'}, dimensions={0} | all-to-all | bytes 1048576 | tf_op jit(solution)/shard_map/all_to_all | solution.py:689
  111.9 14.1 %cycle_work.1 = (bf16[8,4,64,128]{3,2,1,0:T(8,128)(2,1)S(1)}, bf16[8,4,64,128]{3,2,1,0:T(8,128)(2,1)}) custom-call(s32[4]{0:T(128)S(1)} %copy-done.22, s32[2]{0:T(128)S(1)} %pad_add_fusion.where_ref, f32[4]{0:T(128)S(1)} %copy-done.23, bf16[8,4,64,128]{3,2,1,0:T(8,128)(2,1)S(1)} %all-to-all-done.refs_0_, bf16[8,4,64,128]{3,2,1,0:T(8,128)(2,1)S(1)} %all_to_all.20.refs_1_, ...), custom_call_target="tpu_custom_call" | custom-call | flops 4294967296 | bytes 8388608 | tf_op jit(solution)/shard_map/cycle_work/pallas_call | solution.py:448
  126.0 17.6 %all_to_all.21.refs_0_ = bf16[8,4,64,128]{3,2,1,0:T(8,128)(2,1)S(1)} all-to-all(bf16[8,4,64,128]{3,2,1,0:T(8,128)(2,1)S(1)} %get-tuple-element.34), channel_id=1, replica_groups=mesh['row'=4,'ma'=8] {'ma'}, dimensions={0} | all-to-all | bytes 1048576 | tf_op jit(solution)/shard_map/all_to_all | solution.py:713
  143.6 3.7 %all-to-all-start.3 = ((bf16[8,4,64,128]{3,2,1,0:T(8,128)(2,1)}), bf16[8,4,64,128]{3,2,1,0:T(8,128)(2,1)S(1)}, u32[]{:S(2)}, u32[]{:S(2)}) async-start(bf16[8,4,64,128]{3,2,1,0:T(8,128)(2,1)} %get-tuple-element.35), calls=%async_computation.3 | async-start | bytes 1048576 | tf_op jit(solution)/shard_map/all_to_all | solution.py:713
  147.9 13.3 %all-to-all-done.3.refs_0_ = bf16[8,4,64,128]{3,2,1,0:T(8,128)(2,1)S(1)} async-done(((bf16[8,4,64,128]{3,2,1,0:T(8,128)(2,1)}), bf16[8,4,64,128]{3,2,1,0:T(8,128)(2,1)S(1)}, u32[]{:S(2)}, u32[]{:S(2)}) %all-to-all-start.3) | async-done | bytes 524320 | tf_op jit(solution)/shard_map/all_to_all | solution.py:713
  163.2 8.6 %adjoint.2.refs_7_ = f32[2,128,512]{2,1,0:T(8,128)S(1)} custom-call(s32[256]{0:T(256)S(1)} %select_reduce_fusion.1.info_ref.refs_6_, s32[2]{0:T(128)S(1)} %pad_add_fusion.where_ref, bf16[8,4,64,128]{3,2,1,0:T(8,128)(2,1)S(1)} %all_to_all.21.refs_0_, bf16[8,4,64,128]{3,2,1,0:T(8,128)(2,1)S(1)} %collective-permute-done.11.refs_1_, ...), custom_call_target="tpu_custom_call" | custom-call | flops 2147483648 | bytes 6291456 | tf_op jit(solution)/shard_map/adjoint/pallas_call | solution.py:593
  171.8 3.8 %collective-permute-done.10.refs_2_ = bf16[8,4,64,128]{3,2,1,0:T(8,128)(2,1)S(1)} collective-permute-done((bf16[8,4,64,128]{3,2,1,0:T(8,128)(2,1)S(1)}, bf16[8,4,64,128]{3,2,1,0:T(8,128)(2,1)S(1)}, u32[]{:S(2)}, u32[]{:S(2)}) %collective-permute-start.10) | collective-permute-done | bytes 524320 | tf_op jit(solution)/shard_map/ppermute | solution.py:717
  175.6 1.9 %collective-permute-done.13.refs_3_ = bf16[8,4,64,128]{3,2,1,0:T(8,128)(2,1)S(1)} collective-permute-done((bf16[8,4,64,128]{3,2,1,0:T(8,128)(2,1)S(1)}, bf16[8,4,64,128]{3,2,1,0:T(8,128)(2,1)S(1)}, u32[]{:S(2)}, u32[]{:S(2)}) %collective-permute-start.13) | collective-permute-done | bytes 524320 | tf_op jit(solution)/shard_map/ppermute | solution.py:724
  177.5 10.1 %adjoint.3 = f32[2,256,512]{2,1,0:T(8,128)} custom-call(s32[256]{0:T(256)S(1)} %select_reduce_fusion.1.info_ref.refs_6_, s32[2]{0:T(128)S(1)} %pad_add_fusion.where_ref, bf16[8,4,64,128]{3,2,1,0:T(8,128)(2,1)S(1)} %all-to-all-done.3.refs_0_, bf16[8,4,64,128]{3,2,1,0:T(8,128)(2,1)S(1)} %collective-permute-done.9.refs_1_, ...), custom_call_target="tpu_custom_call" | custom-call | flops 2147483648 | bytes 6291456 | tf_op jit(solution)/shard_map/adjoint/pallas_call | solution.py:593
  (94 shorter events, 18.5 us)
Async XLA Ops:
  21.8 14.8 %copy-start.7 = (f32[2,8,2,64,128]{4,3,2,1,0:T(8,128)}, f32[2,8,2,64,128]{4,3,2,1,0:T(8,128)S(1)}, u32[]{:S(2)}) copy-start(f32[2,8,2,64,128]{4,3,2,1,0:T(8,128)S(1)} %get-tuple-element.25.keep_ref.refs_0_) | copy-start | bytes 3145732
  21.9 13.4 %copy-start.26 = (s32[2048]{0:T(1024)S(1)}, s32[2048]{0:T(1024)}, u32[]{:S(2)}) copy-start(s32[2048]{0:T(1024)} %param.19) | copy-start | bytes 24580
  21.9 14.8 %collective-permute-start = (bf16[2,8,2,64,128]{4,3,2,1,0:T(8,128)(2,1)}, bf16[2,8,2,64,128]{4,3,2,1,0:T(8,128)(2,1)S(1)}, u32[]{:S(2)}, u32[]{:S(2)}) collective-permute-start(bf16[2,8,2,64,128]{4,3,2,1,0:T(8,128)(2,1)} %get-tuple-element.26), channel_id=1, source_target_pairs={{0,8},{8,0},{16,24},{24,16},{1,9},{9,1},{17,25},{25,17},{2,10},{10... | collective-permute-start | bytes 1572872 | tf_op jit(solution)/shard_map/ppermute | solution.py:680
  35.2 17.4 %collective-permute-start.2 = (bf16[2,8,2,64,128]{4,3,2,1,0:T(8,128)(2,1)}, bf16[2,8,2,64,128]{4,3,2,1,0:T(8,128)(2,1)}, u32[]{:S(2)}, u32[]{:S(2)}) collective-permute-start(bf16[2,8,2,64,128]{4,3,2,1,0:T(8,128)(2,1)} %get-tuple-element.30), channel_id=1, source_target_pairs={{0,8},{8,0},{16,24},{24,16},{1,9},{9,1},{17,25},{25,17},{2,10},{10... | collective-permute-start | bytes 1572872 | tf_op jit(solution)/shard_map/ppermute | solution.py:680
  38.3 14.3 %copy-start.11 = (f32[2,8,2,64,128]{4,3,2,1,0:T(8,128)S(1)}, f32[2,8,2,64,128]{4,3,2,1,0:T(8,128)}, u32[]{:S(2)}) copy-start(f32[2,8,2,64,128]{4,3,2,1,0:T(8,128)} %copy-done.9) | copy-start | bytes 3145732
  38.3 19.3 %collective-permute-start.3 = (bf16[8,2,64,128]{3,2,1,0:T(8,128)(2,1)S(1)}, bf16[8,2,64,128]{3,2,1,0:T(8,128)(2,1)S(1)}, u32[]{:S(2)}, u32[]{:S(2)}) collective-permute-start(bf16[8,2,64,128]{3,2,1,0:T(8,128)(2,1)S(1)} %core_sum.4.refs_0_), channel_id=1, source_target_pairs={{0,16},{8,24},{16,0},{24,8},{1,17},{9,25},{17,1},{25,9},{2,18},{10... | collective-permute-start | bytes 786440 | tf_op jit(solution)/shard_map/ppermute | solution.py:684
  52.5 3.7 %collective-permute-start.1 = (bf16[2,8,2,64,128]{4,3,2,1,0:T(8,128)(2,1)S(1)}, bf16[2,8,2,64,128]{4,3,2,1,0:T(8,128)(2,1)S(1)}, u32[]{:S(2)}, u32[]{:S(2)}) collective-permute-start(bf16[2,8,2,64,128]{4,3,2,1,0:T(8,128)(2,1)S(1)} %get-tuple-element.29), channel_id=1, source_target_pairs={{0,8},{8,0},{16,24},{24,16},{1,9},{9,1},{17,25},{25,17},{2,10},{10... | collective-permute-start | bytes 1572872 | tf_op jit(solution)/shard_map/ppermute | solution.py:680
  53.8 15.0 %collective-permute-start.4 = (bf16[8,2,64,128]{3,2,1,0:T(8,128)(2,1)S(1)}, bf16[8,2,64,128]{3,2,1,0:T(8,128)(2,1)S(1)}, u32[]{:S(2)}, u32[]{:S(2)}) collective-permute-start(bf16[8,2,64,128]{3,2,1,0:T(8,128)(2,1)S(1)} %core_sum.5.order_ref), channel_id=1, source_target_pairs={{0,16},{8,24},{16,0},{24,8},{1,17},{9,25},{17,1},{25,9},{2,18},{10... | collective-permute-start | bytes 786440 | tf_op jit(solution)/shard_map/ppermute | solution.py:684
  57.0 11.8 %copy-start.8 = (f32[2,8,2,64,128]{4,3,2,1,0:T(8,128)S(1)}, f32[2,8,2,64,128]{4,3,2,1,0:T(8,128)}, u32[]{:S(2)}) copy-start(f32[2,8,2,64,128]{4,3,2,1,0:T(8,128)} %copy-done.7) | copy-start | bytes 3145732
  57.0 22.2 %collective-permute-start.6 = (bf16[8,2,64,128]{3,2,1,0:T(8,128)(2,1)S(1)}, bf16[8,2,64,128]{3,2,1,0:T(8,128)(2,1)S(1)}, u32[]{:S(2)}, u32[]{:S(2)}) collective-permute-start(bf16[8,2,64,128]{3,2,1,0:T(8,128)(2,1)S(1)} %core_sum.6.refs_0_), channel_id=1, source_target_pairs={{0,16},{8,24},{16,0},{24,8},{1,17},{9,25},{17,1},{25,9},{2,18},{10... | collective-permute-start | bytes 786440 | tf_op jit(solution)/shard_map/ppermute | solution.py:684
  68.7 2.3 %collective-permute-start.5 = (bf16[2,8,2,64,128]{4,3,2,1,0:T(8,128)(2,1)S(1)}, bf16[2,8,2,64,128]{4,3,2,1,0:T(8,128)(2,1)S(1)}, u32[]{:S(2)}, u32[]{:S(2)}) collective-permute-start(bf16[2,8,2,64,128]{4,3,2,1,0:T(8,128)(2,1)S(1)} %get-tuple-element.32), channel_id=1, source_target_pairs={{0,8},{8,0},{16,24},{24,16},{1,9},{9,1},{17,25},{25,17},{2,10},{10... | collective-permute-start | bytes 1572872 | tf_op jit(solution)/shard_map/ppermute | solution.py:680
  71.8 8.5 %collective-permute-start.7 = (bf16[8,2,64,128]{3,2,1,0:T(8,128)(2,1)S(1)}, bf16[8,2,64,128]{3,2,1,0:T(8,128)(2,1)S(1)}, u32[]{:S(2)}, u32[]{:S(2)}) collective-permute-start(bf16[8,2,64,128]{3,2,1,0:T(8,128)(2,1)S(1)} %core_sum.7.order_ref), channel_id=1, source_target_pairs={{0,16},{8,24},{16,0},{24,8},{1,17},{9,25},{17,1},{25,9},{2,18},{10... | collective-permute-start | bytes 786440 | tf_op jit(solution)/shard_map/ppermute | solution.py:684
  73.2 38.7 %copy-start.22 = (s32[4]{0:T(128)S(1)}, s32[4]{0:T(128)}, u32[]{:S(2)}) copy-start(s32[4]{0:T(128)} %offset_ref.1) | copy-start | bytes 52
  73.2 38.7 %copy-start.23 = (f32[4]{0:T(128)S(1)}, f32[4]{0:T(128)}, u32[]{:S(2)}) copy-start(f32[4]{0:T(128)} %weight_ref.1) | copy-start | bytes 52
  73.2 38.7 %copy-start.24 = (bf16[128,256]{1,0:T(8,128)(2,1)S(1)}, bf16[128,256]{1,0:T(8,128)(2,1)}, u32[]{:S(2)}) copy-start(bf16[128,256]{1,0:T(8,128)(2,1)} %constant.96.clone.refs_5_) | copy-start | bytes 196612
  73.2 38.7 %copy-start.25 = (bf16[128,128]{1,0:T(8,128)(2,1)S(1)}, bf16[128,128]{1,0:T(8,128)(2,1)}, u32[]{:S(2)}) copy-start(bf16[128,128]{1,0:T(8,128)(2,1)} %constant.95.clone.refs_4_) | copy-start | bytes 98308
  73.2 20.6 %all-to-all-start = ((bf16[8,4,64,128]{3,2,1,0:T(8,128)(2,1)}), bf16[8,4,64,128]{3,2,1,0:T(8,128)(2,1)S(1)}, u32[]{:S(2)}, u32[]{:S(2)}) async-start(bf16[8,4,64,128]{3,2,1,0:T(8,128)(2,1)} %full_sum.2.order_ref), calls=%async_computation | async-start | bytes 1048576 | tf_op jit(solution)/shard_map/all_to_all | solution.py:689
  143.6 17.7 %all-to-all-start.3 = ((bf16[8,4,64,128]{3,2,1,0:T(8,128)(2,1)}), bf16[8,4,64,128]{3,2,1,0:T(8,128)(2,1)S(1)}, u32[]{:S(2)}, u32[]{:S(2)}) async-start(bf16[8,4,64,128]{3,2,1,0:T(8,128)(2,1)} %get-tuple-element.35), calls=%async_computation.3 | async-start | bytes 1048576 | tf_op jit(solution)/shard_map/all_to_all | solution.py:713
  147.3 14.0 %collective-permute-start.8 = (bf16[8,4,64,128]{3,2,1,0:T(8,128)(2,1)S(1)}, bf16[8,4,64,128]{3,2,1,0:T(8,128)(2,1)S(1)}, u32[]{:S(2)}, u32[]{:S(2)}) collective-permute-start(bf16[8,4,64,128]{3,2,1,0:T(8,128)(2,1)S(1)} %all_to_all.21.refs_0_), channel_id=1, source_target_pairs={{0,16},{8,24},{16,0},{24,8},{1,17},{9,25},{17,1},{25,9},{2,18},{10... | collective-permute-start | bytes 1572872 | tf_op jit(solution)/shard_map/ppermute | solution.py:717
  147.9 14.2 %collective-permute-start.11 = (bf16[8,4,64,128]{3,2,1,0:T(8,128)(2,1)S(1)}, bf16[8,4,64,128]{3,2,1,0:T(8,128)(2,1)S(1)}, u32[]{:S(2)}, u32[]{:S(2)}) collective-permute-start(bf16[8,4,64,128]{3,2,1,0:T(8,128)(2,1)S(1)} %all_to_all.21.refs_0_), channel_id=1, source_target_pairs={{0,8},{8,0},{16,24},{24,16},{1,9},{9,1},{17,25},{25,17},{2,10},{10... | collective-permute-start | bytes 1572872 | tf_op jit(solution)/shard_map/ppermute | solution.py:723
  161.3 1.9 %collective-permute-start.12 = (bf16[8,4,64,128]{3,2,1,0:T(8,128)(2,1)S(1)}, bf16[8,4,64,128]{3,2,1,0:T(8,128)(2,1)S(1)}, u32[]{:S(2)}, u32[]{:S(2)}) collective-permute-start(bf16[8,4,64,128]{3,2,1,0:T(8,128)(2,1)S(1)} %collective-permute-done.8.refs_2_), channel_id=1, source_target_pairs={{0,8},{8,0},{16,24},{24,16},{1,9},{9,1},{17,25},{25,17},{2,10},{10... | collective-permute-start | bytes 1572872 | tf_op jit(solution)/shard_map/ppermute | solution.py:724
  161.3 14.3 %collective-permute-start.10 = (bf16[8,4,64,128]{3,2,1,0:T(8,128)(2,1)S(1)}, bf16[8,4,64,128]{3,2,1,0:T(8,128)(2,1)S(1)}, u32[]{:S(2)}, u32[]{:S(2)}) collective-permute-start(bf16[8,4,64,128]{3,2,1,0:T(8,128)(2,1)S(1)} %all-to-all-done.3.refs_0_), channel_id=1, source_target_pairs={{0,16},{8,24},{16,0},{24,8},{1,17},{9,25},{17,1},{25,9},{2,18},{10... | collective-permute-start | bytes 1572872 | tf_op jit(solution)/shard_map/ppermute | solution.py:717
  161.9 13.8 %collective-permute-start.9 = (bf16[8,4,64,128]{3,2,1,0:T(8,128)(2,1)S(1)}, bf16[8,4,64,128]{3,2,1,0:T(8,128)(2,1)S(1)}, u32[]{:S(2)}, u32[]{:S(2)}) collective-permute-start(bf16[8,4,64,128]{3,2,1,0:T(8,128)(2,1)S(1)} %all-to-all-done.3.refs_0_), channel_id=1, source_target_pairs={{0,8},{8,0},{16,24},{24,16},{1,9},{9,1},{17,25},{25,17},{2,10},{10... | collective-permute-start | bytes 1572872 | tf_op jit(solution)/shard_map/ppermute | solution.py:723
  175.6 1.9 %collective-permute-start.13 = (bf16[8,4,64,128]{3,2,1,0:T(8,128)(2,1)S(1)}, bf16[8,4,64,128]{3,2,1,0:T(8,128)(2,1)S(1)}, u32[]{:S(2)}, u32[]{:S(2)}) collective-permute-start(bf16[8,4,64,128]{3,2,1,0:T(8,128)(2,1)S(1)} %collective-permute-done.10.refs_2_), channel_id=1, source_target_pairs={{0,8},{8,0},{16,24},{24,16},{1,9},{9,1},{17,25},{25,17},{2,10},{10... | collective-permute-start | bytes 1572872 | tf_op jit(solution)/shard_map/ppermute | solution.py:724
  (21 other events, 44.6 us)

commit v4 on v3

v4 whole, which is shorter than its diff:
```python
import functools
import math

import jax
import jax.numpy as jnp
import numpy as np
from jax import lax
from jax.experimental import pallas as pl
from jax.experimental.pallas import tpu as pltpu
from jax.sharding import PartitionSpec as P

NPIX = 4096
SIDE = 64
PADDED = 136
CHUNKS = 4
GROUPS = 2
BLOCK = 16
MIB = 1 << 20
F32 = jnp.float32
BF16 = jnp.bfloat16


def split_table(table):
    high = table.astype(jnp.bfloat16)
    low = (table - high.astype(np.float64)).astype(jnp.bfloat16)
    return high, low


@functools.lru_cache(maxsize=None)
def fourier_tables():
    first = np.arange(SIDE)
    spin = np.arange(2).reshape(2, 1, 1, 1, 1, 1)
    order = SIDE * np.arange(32)[None, :] + np.arange(SIDE)[:, None]
    order = order.reshape(1, SIDE, 1, 1, 1, 32)
    angle = (2 * first.reshape(1, 1, 1, SIDE, 1, 1) + spin) * order % (2 * NPIX) * (math.pi / NPIX)
    cosine, sine = np.cos(angle), np.sin(angle)
    row_part = np.arange(2).reshape(1, 1, 2, 1, 1, 1)
    col_part = np.arange(2).reshape(1, 1, 1, 1, 2, 1)
    same = (row_part == col_part).astype(np.float64)
    cross = np.where(row_part == 1, 1.0, -1.0) * (row_part != col_part)
    doubling = np.where(order == 0, 1.0, 2.0)
    spread = (doubling * (same * cosine + cross * sine)).reshape(2, SIDE, 2 * SIDE, SIDE)
    gather = (same * cosine + cross * sine).reshape(2, SIDE, 2 * SIDE, SIDE)
    gather = np.swapaxes(gather, 2, 3)
    spread_parts = np.concatenate(split_table(spread), axis=3)
    gather_parts = np.concatenate(split_table(gather), axis=2)
    square = first[:, None] * first[None, :] % SIDE * (2.0 * math.pi / SIDE)
    pixel = np.concatenate(split_table(np.concatenate([np.cos(square), -np.sin(square)], axis=1)), axis=0)
    back_high, back_low = split_table(np.concatenate([np.cos(square), -np.sin(square)], axis=0))
    back = np.concatenate([back_high, back_high, back_low, back_low], axis=1)
    return spread_parts, pixel, back, gather_parts


def two_parts(value):
    high = value.astype(BF16)
    low = (value - high.astype(F32)).astype(BF16)
    return high, low


def whole(shape):
    return pl.BlockSpec(shape, lambda t, *_: (0,) * len(shape))


def anywhere():
    return pl.BlockSpec(memory_space=pl.ANY)


def hbm():
    return pl.BlockSpec(memory_space=pltpu.HBM)


def weights_kernel(
    node_ref,
    radial_ref,
    alpha_ref,
    beta_ref,
    synth_ref,
    adjoint_ref,
    alpha_scr,
    beta_scr,
    filter_scr,
    weighted_scr,
    sems,
):
    copies = [
        pltpu.make_async_copy(alpha_ref, alpha_scr, sems.at[0]),
        pltpu.make_async_copy(beta_ref, beta_scr, sems.at[1]),
    ]
    for copy in copies:
        copy.start()
    for copy in copies:
        copy.wait()
    radii = node_ref.shape[0]

    def gather(radius, carry):
        node = node_ref[radius]
        scale = radial_ref[node]
        alpha = alpha_scr[pl.ds(node, 1), :]
        beta = beta_scr[pl.ds(node, 1), :]
        filter_scr[pl.ds(radius, 1), :] = alpha
        filter_scr[pl.ds(radii + radius, 1), :] = beta
        weighted_scr[pl.ds(radius, 1), :] = scale * alpha
        weighted_scr[pl.ds(radii + radius, 1), :] = (2.0 * scale) * beta
        return carry

    lax.fori_loop(0, radii, gather, 0, unroll=8)
    high, low = two_parts(filter_scr[...].T)
    synth_ref[:, : 2 * radii] = high
    synth_ref[:, 2 * radii :] = low
    high, low = two_parts(weighted_scr[...])
    adjoint_ref[: 2 * radii, :] = high
    adjoint_ref[2 * radii :, :] = low


def filter_weights(radius_index, radial_weight, alpha_table, beta_table):
    radii = radius_index.shape[0]
    degrees = alpha_table.shape[1]
    return pl.pallas_call(
        weights_kernel,
        grid_spec=pltpu.PrefetchScalarGridSpec(
            num_scalar_prefetch=2,
            grid=(1,),
            in_specs=[hbm(), hbm()],
            out_specs=[whole((degrees, 4 * radii)), whole((4 * radii, degrees))],
            scratch_shapes=[pltpu.VMEM(alpha_table.shape, F32)] * 2
            + [pltpu.VMEM((2 * radii, degrees), F32)] * 2
            + [pltpu.SemaphoreType.DMA((2,))],
        ),
        out_shape=[
            jax.ShapeDtypeStruct((degrees, 4 * radii), BF16),
            jax.ShapeDtypeStruct((4 * radii, degrees), BF16),
        ],
        compiler_params=pltpu.CompilerParams(vmem_limit_bytes=56 * MIB),
        name="filter_weights",
    )(radius_index, radial_weight, alpha_table, beta_table)


def synth_kernel(
    first, order_ref, where_ref, coeffs_ref, weight_ref, legendre_ref, *refs
):
    keep_ref, send_ref, terms_scr, sums_scr = refs[-4:]
    step = pl.program_id(0)
    row = where_ref[0]
    base = where_ref[1] + first + step * BLOCK
    degrees = coeffs_ref.shape[2]
    cycles = legendre_ref.shape[1]
    owners = cycles // 4
    lanes = weight_ref.shape[1] // 2
    degree = row * degrees + lax.broadcasted_iota(jnp.int32, (1, degrees), 1)
    for slot in range(BLOCK):
        live = degree >= order_ref[base + slot]
        values = legendre_ref[slot].astype(F32)
        for part in range(2):
            coeff = jnp.where(live, coeffs_ref[part, slot : slot + 1, :], 0.0)
            high, low = two_parts(values * coeff)
            start = (part * BLOCK + slot) * cycles
            terms_scr[0, start : start + cycles, :] = high
            terms_scr[1, start : start + cycles, :] = low
    for part in range(2):
        rows = slice(part * BLOCK * cycles, (part + 1) * BLOCK * cycles)
        both = jnp.dot(terms_scr[0, rows], weight_ref[...], preferred_element_type=F32)
        rest = jnp.dot(terms_scr[1, rows], weight_ref[:, :lanes], preferred_element_type=F32)
        sums_scr[rows, :] = both[:, :lanes] + both[:, lanes:] + rest
    for part in range(2):
        for owner in range(owners):
            for away in range(4):
                cycle = 4 * owner + (row ^ away)
                piece = sums_scr[pl.ds(part * BLOCK * cycles + cycle, BLOCK, stride=cycles), :]
                target = send_ref if away % 2 else keep_ref
                target[away // 2, owner, :, part * lanes : (part + 1) * lanes] = piece


def synth(chunk, chunks, orders, where, coeffs, weight, legendre, order):
    orders_here, cycles, degrees = legendre.shape
    count = orders_here // chunks
    steps = count // BLOCK
    start = chunk * steps
    owners = cycles // 4
    lanes = weight.shape[1] // 2
    out = jax.ShapeDtypeStruct((2, owners, count, 2 * lanes), F32)
    out_spec = pl.BlockSpec((2, owners, BLOCK, 2 * lanes), lambda t, *_: (0, 0, t, 0))
    return pl.pallas_call(
        functools.partial(synth_kernel, chunk * count),
        grid_spec=pltpu.PrefetchScalarGridSpec(
            num_scalar_prefetch=2,
            grid=(steps,),
            in_specs=[
                pl.BlockSpec((2, BLOCK, degrees), lambda t, *_: (0, start + t, 0)),
                whole(weight.shape),
                pl.BlockSpec((BLOCK, cycles, degrees), lambda t, *_: (start + t, 0, 0)),
            ]
            + [anywhere()] * len(order),
            out_specs=[out_spec, out_spec],
            scratch_shapes=[
                pltpu.VMEM((2, 2 * BLOCK * cycles, degrees), BF16),
                pltpu.VMEM((2 * BLOCK * cycles, lanes), F32),
            ],
        ),
        out_shape=[out, out],
        compiler_params=pltpu.CompilerParams(vmem_limit_bytes=56 * MIB),
        cost_estimate=pl.CostEstimate(
            flops=2 * count * cycles * degrees * lanes * 2 * 4,
            bytes_accessed=count * (cycles * degrees * 2 + 2 * cycles * lanes * 4),
            transcendentals=0,
        ),
        name="synth",
    )(orders, where, coeffs, weight, legendre, *order)


def core_sum_kernel(keep_ref, other_ref, order_ref, out_ref):
    out_ref[...] = (keep_ref[0] + other_ref[0]).astype(BF16)


def core_sum(keep, other, order):
    shape = keep.shape[1:]
    half = pl.BlockSpec((1,) + shape, lambda t: (1, 0, 0, 0))
    return pl.pallas_call(
        core_sum_kernel,
        grid=(1,),
        in_specs=[half, half, anywhere()],
        out_specs=pl.BlockSpec(shape, lambda t: (0, 0, 0)),
        out_shape=jax.ShapeDtypeStruct(shape, BF16),
        compiler_params=pltpu.CompilerParams(vmem_limit_bytes=16 * MIB),
        cost_estimate=pl.CostEstimate(flops=4 * 10**10, bytes_accessed=MIB, transcendentals=0),
        name="core_sum",
    )(keep, other, order)


def full_sum_kernel(order_ref, *refs):
    out_ref = refs[-1]
    start = 0
    for index in range(0, len(refs) - 1, 3):
        keep_ref, other_ref, incoming_ref = refs[index : index + 3]
        count = incoming_ref.shape[1]
        total = keep_ref[0] + other_ref[0] + incoming_ref[...].astype(F32)
        out_ref[:, start : start + count] = total.astype(BF16)
        start += count


def full_sum(chunks, order):
    operands, specs, count = [], [anywhere()], 0
    for keep, other, incoming in chunks:
        shape = incoming.shape
        half = pl.BlockSpec((1,) + shape, lambda t: (0, 0, 0, 0))
        operands += [keep, other, incoming]
        specs += [half, half, pl.BlockSpec(shape, lambda t: (0, 0, 0))]
        count += shape[1]
    full = (shape[0], count, shape[2])
    return pl.pallas_call(
        full_sum_kernel,
        grid=(1,),
        in_specs=specs,
        out_specs=pl.BlockSpec(full, lambda t: (0, 0, 0)),
        out_shape=jax.ShapeDtypeStruct(full, BF16),
        compiler_params=pltpu.CompilerParams(vmem_limit_bytes=24 * MIB),
        cost_estimate=pl.CostEstimate(flops=4 * 10**10, bytes_accessed=MIB, transcendentals=0),
        name="full_sum",
    )(order, *operands)


def cycle_kernel(device_count, groups, offset_ref, where_ref, weight_ref, *refs):
    pieces = refs[:groups]
    place_ref, sort_ref, unsort_ref, spread_ref, pixel_ref, back_ref, gather_ref = refs[
        groups : groups + 7
    ]
    outs = refs[groups + 7 : 2 * groups + 7]
    spread_scr, gather_scr, sorted_scr, middle_scr, product_scr, back_scr, sems = refs[
        2 * groups + 7 :
    ]
    blocks = place_ref.shape[1]
    count = pieces[0].shape[1]
    lanes = pieces[0].shape[2] // 2
    turned = offset_ref[where_ref[0]]
    scale = weight_ref[where_ref[0]]
    lane = lax.broadcasted_iota(jnp.int32, (SIDE, lanes), 1)

    def spread_copy(block):
        rows = pl.ds(block * device_count, device_count)
        return pltpu.make_async_copy(
            spread_ref.at[turned, rows], spread_scr.at[rows], sems.at[block]
        )

    gather_copy = pltpu.make_async_copy(gather_ref.at[turned], gather_scr, sems.at[blocks])
    for block in range(blocks):
        spread_copy(block).start()
    gather_copy.start()

    def sort_step(peer, carry):
        slots = jnp.concatenate([piece[peer] for piece in pieces], axis=0)
        sorted_scr[peer] = jnp.dot(
            sort_ref[peer], slots, preferred_element_type=F32
        ).astype(BF16)
        return carry

    lax.fori_loop(0, device_count, sort_step, 0, unroll=2)

    def spread_step(block, carry):
        spread_copy(block).wait()
        rows = pl.ds(pl.multiple_of(block * 32, 32), 32)

        def one(spot):
            picked = jnp.zeros((32, 2 * lanes), BF16)
            for peer in range(device_count):
                place = place_ref[peer, block]
                picked = jnp.where(
                    place == lax.convert_element_type(spot, BF16),
                    sorted_scr[peer, rows, :],
                    picked,
                )
            low_order = block * device_count + spot
            column = jnp.concatenate([picked[:, :lanes], picked[:, lanes:]], axis=0)
            stage = jnp.dot(
                spread_scr[low_order],
                jnp.concatenate([column, column], axis=0),
                preferred_element_type=F32,
            )
            middle_scr[pl.ds(low_order * PADDED, 2 * SIDE), :] = stage

        if device_count <= 8:
            for spot in range(device_count):
                one(spot)
        else:
            lax.fori_loop(0, device_count, lambda s, x: (one(s), x)[1], 0)
        return carry

    lax.fori_loop(0, blocks, spread_step, 0)

    def pixel_step(step, total):
        for inner in range(8):
            first = step * 8 + inner
            column = jnp.concatenate(
                [
                    middle_scr[pl.ds(first, SIDE, stride=PADDED), :],
                    middle_scr[pl.ds(first + SIDE, SIDE, stride=PADDED), :],
                ],
                axis=0,
            )
            high, low = two_parts(column)
            stage = jnp.dot(
                pixel_ref[...], jnp.concatenate([high, low], axis=1), preferred_element_type=F32
            )
            field = stage[:SIDE, :lanes] + stage[:SIDE, lanes:] + stage[SIDE:, :lanes]
            other = pltpu.roll(field, lanes // 2, 1)
            product = other * jnp.where(lane < lanes // 2, other, field)
            product_scr[first] = product
            total = total + jnp.sum(product.reshape(8, 8, lanes), axis=0)
        return total

    total = lax.fori_loop(0, SIDE // 8, pixel_step, jnp.zeros((8, lanes), F32))
    mean = jnp.sum(total, axis=0, keepdims=True) * (1.0 / NPIX)

    def back_step(step, carry):
        for inner in range(8):
            first = step * 8 + inner
            high, low = two_parts(product_scr[first] - mean)
            back_scr[pl.ds(first * PADDED, 2 * SIDE), :] = jnp.dot(
                back_ref[...],
                jnp.concatenate([high, low, high, low], axis=0),
                preferred_element_type=F32,
            )
        return carry

    lax.fori_loop(0, SIDE // 8, back_step, 0)
    gather_copy.wait()

    def gather_step(block, carry):
        rows = pl.ds(pl.multiple_of(block * 32, 32), 32)

        def one(spot):
            low_order = block * device_count + spot
            column = jnp.concatenate(
                [
                    back_scr[pl.ds(low_order, SIDE, stride=PADDED), :],
                    back_scr[pl.ds(low_order + SIDE, SIDE, stride=PADDED), :],
                ],
                axis=0,
            )
            high, low = two_parts(column)
            stage = jnp.dot(
                gather_scr[low_order],
                jnp.concatenate([high, low], axis=1),
                preferred_element_type=F32,
            )
            value = stage[:SIDE, :lanes] + stage[:SIDE, lanes:] + stage[SIDE:, :lanes]
            value = (value * scale).astype(BF16)
            return jnp.concatenate([value[:32], value[32:]], axis=1)

        if device_count <= 8:
            found = [one(spot) for spot in range(device_count)]
            for peer in range(device_count):
                place = place_ref[peer, block]
                picked = found[0]
                for spot in range(1, device_count):
                    picked = jnp.where(place == spot, found[spot], picked)
                sorted_scr[peer, rows, :] = picked
        else:

            def spot_step(spot, carry):
                value = one(spot)
                for peer in range(device_count):
                    sorted_scr[peer, rows, :] = jnp.where(
                        place_ref[peer, block] == lax.convert_element_type(spot, BF16),
                        value,
                        sorted_scr[peer, rows, :],
                    )
                return carry

            lax.fori_loop(0, device_count, spot_step, 0)
        return carry

    lax.fori_loop(0, blocks, gather_step, 0)

    def unsort_step(peer, carry):
        slots = jnp.dot(
            unsort_ref[peer], sorted_scr[peer], preferred_element_type=F32
        ).astype(BF16)
        for group in range(groups):
            outs[group][peer] = slots[group * count : (group + 1) * count]
        return carry

    lax.fori_loop(0, device_count, unsort_step, 0, unroll=2)


def cycle_work(pieces, places, sort, unsort, offset, where, cycle_weight):
    groups = len(pieces)
    device_count, count, lanes = pieces[0].shape
    spread, pixel, back, gather = [jnp.asarray(table) for table in fourier_tables()]
    tables = [places, sort, unsort]
    return pl.pallas_call(
        functools.partial(cycle_kernel, device_count, groups),
        grid_spec=pltpu.PrefetchScalarGridSpec(
            num_scalar_prefetch=2,
            grid=(1,),
            in_specs=[pl.BlockSpec(memory_space=pltpu.SMEM)]
            + [whole(piece.shape) for piece in pieces]
            + [whole(table.shape) for table in tables]
            + [hbm(), whole(pixel.shape), whole(back.shape), hbm()],
            out_specs=[whole(piece.shape) for piece in pieces],
            scratch_shapes=[
                pltpu.VMEM(spread.shape[1:], BF16),
                pltpu.VMEM(gather.shape[1:], BF16),
                pltpu.VMEM((device_count, groups * count, lanes), BF16),
                pltpu.VMEM((SIDE * PADDED, lanes // 2), F32),
                pltpu.VMEM((SIDE, SIDE, lanes // 2), F32),
                pltpu.VMEM((SIDE * PADDED, lanes // 2), F32),
                pltpu.SemaphoreType.DMA((places.shape[1] + 1,)),
            ],
        ),
        out_shape=[jax.ShapeDtypeStruct(piece.shape, BF16) for piece in pieces],
        compiler_params=pltpu.CompilerParams(vmem_limit_bytes=48 * MIB),
        cost_estimate=pl.CostEstimate(
            flops=4 * SIDE * 128 * 256 * 256 * 2, bytes_accessed=8 * MIB, transcendentals=0
        ),
        name="cycle_work",
    )(offset, where, cycle_weight, *pieces, *tables, spread, pixel, back, gather)


def adjoint_kernel(
    first, order_ref, where_ref, own_ref, core_ref, far_ref, corner_ref, weight_ref, legendre_ref, *refs
):
    out_ref, values_scr, terms_scr = refs[-3:]
    step = pl.program_id(0)
    row = where_ref[0]
    base = where_ref[1] + first + step * BLOCK
    degrees = weight_ref.shape[1]
    cycles = legendre_ref.shape[1]
    owners = cycles // 4
    lanes = weight_ref.shape[0] // 2
    pitch = cycles + 8
    tiles = degrees // 128
    degree = row * degrees + lax.broadcasted_iota(jnp.int32, (8, degrees), 1)
    sublane = lax.broadcasted_iota(jnp.int32, (8, degrees), 0)
    for slot in range(BLOCK):
        wide = legendre_ref[slot].astype(F32)
        for tile in range(tiles):
            values_scr[tile, slot * pitch : slot * pitch + cycles, :] = wide[
                :, tile * 128 : tile * 128 + 128
            ]
    sources = (own_ref, core_ref, far_ref, corner_ref)
    quarter = owners * BLOCK
    for part in range(2):
        for away in range(4):
            rows = sources[away][:, :, part * lanes : (part + 1) * lanes].reshape(quarter, lanes)
            start = (part * 4 + away) * quarter
            terms_scr[start : start + quarter, :] = jnp.dot(
                jnp.concatenate([rows, rows], axis=1), weight_ref[...], preferred_element_type=F32
            )
    for half in range(BLOCK // 8):
        total = [jnp.zeros((8, degrees), F32), jnp.zeros((8, degrees), F32)]
        for away in range(4):
            for owner in range(owners):
                cycle = 4 * owner + (row ^ away)
                factor = jnp.concatenate(
                    [
                        values_scr[tile, pl.ds(half * 8 * pitch + cycle, 8, stride=pitch), :]
                        for tile in range(tiles)
                    ],
                    axis=1,
                )
                for part in range(2):
                    at = (part * 4 + away) * quarter + owner * BLOCK + half * 8
                    total[part] = total[part] + terms_scr[at : at + 8, :] * factor
        lowest = jnp.zeros((8, degrees), jnp.int32)
        for slot in range(8):
            lowest = jnp.where(sublane == slot, order_ref[base + half * 8 + slot], lowest)
        for part in range(2):
            out_ref[part, half * 8 : half * 8 + 8, :] = jnp.where(
                degree >= lowest, total[part], 0.0
            )


def adjoint(chunk, chunks, orders, where, weight, pieces, legendre, earlier):
    orders_here, cycles, degrees = legendre.shape
    count = orders_here // chunks
    steps = count // BLOCK
    start = chunk * steps
    owners = cycles // 4
    lanes = weight.shape[0] // 2
    piece_spec = pl.BlockSpec((owners, BLOCK, 2 * lanes), lambda t, *_: (0, t, 0))
    out = jax.ShapeDtypeStruct((2, orders_here, degrees), F32)
    return pl.pallas_call(
        functools.partial(adjoint_kernel, chunk * count),
        grid_spec=pltpu.PrefetchScalarGridSpec(
            num_scalar_prefetch=2,
            grid=(steps,),
            in_specs=[piece_spec] * 4
            + [
                whole(weight.shape),
                pl.BlockSpec((BLOCK, cycles, degrees), lambda t, *_: (start + t, 0, 0)),
            ]
            + [anywhere()] * len(earlier),
            out_specs=pl.BlockSpec((2, BLOCK, degrees), lambda t, *_: (0, start + t, 0)),
            scratch_shapes=[
                pltpu.VMEM((degrees // 128, BLOCK * (cycles + 8), 128), F32),
                pltpu.VMEM((2 * BLOCK * cycles, degrees), F32),
            ],
        ),
        out_shape=out,
        input_output_aliases={8: 0} if earlier else {},
        compiler_params=pltpu.CompilerParams(vmem_limit_bytes=48 * MIB),
        cost_estimate=pl.CostEstimate(
            flops=2 * count * cycles * degrees * lanes * 2 * 2,
            bytes_accessed=count * (cycles * degrees * 2 + 2 * cycles * lanes * 2),
            transcendentals=0,
        ),
        name="adjoint",
    )(orders, where, *pieces, weight, legendre, *earlier)


def slot_tables(orders, device_count):
    local_orders = orders.shape[0] // device_count
    blocks = local_orders // 32
    by_device = orders.reshape(device_count, local_orders)
    block = by_device // device_count
    position = 32 * (block % blocks) + block // blocks
    wanted = jnp.arange(local_orders, dtype=jnp.int32)
    sort = position[:, None, :] == wanted[None, :, None]
    unsort = position[:, :, None] == wanted[None, None, :]
    place = jnp.sum(jnp.where(sort, (by_device % device_count)[:, None, :], 0), axis=2)
    place = place.reshape(device_count, blocks, 32, 1)
    place = jnp.broadcast_to(place, (device_count, blocks, 32, 256))
    return place.astype(BF16), sort.astype(BF16), unsort.astype(BF16)


def body(
    coeffs,
    legendre,
    alpha_table,
    beta_table,
    radial_weight,
    radius_index,
    orders,
    cycle_offset,
    cycle_weight,
):
    row_id = lax.axis_index("row")
    ma_id = lax.axis_index("ma")
    device_count = lax.axis_size("ma")
    row_count = lax.axis_size("row")
    local_orders = coeffs.shape[1]
    where = jnp.stack([row_id, ma_id * local_orders]).astype(jnp.int32)
    places, sort, unsort = slot_tables(orders, device_count)
    synth_weight, adjoint_weight = filter_weights(
        radius_index, radial_weight, alpha_table, beta_table
    )
    core_pairs = [(i, i ^ 1) for i in range(row_count)]
    far_pairs = [(i, i ^ 2) for i in range(row_count)]
    chunks = min(CHUNKS, local_orders // 32)
    groups = min(GROUPS, chunks)
    size = chunks // groups
    kept, others, outgoing, incoming, arrived = [], [], [], [], []

    def launch(chunk, order):
        keep, send = synth(chunk, chunks, orders, where, coeffs, synth_weight, legendre, order)
        kept.append(keep)
        others.append(lax.ppermute(send, "row", core_pairs))

    def pass_on(chunk, order):
        outgoing.append(core_sum(kept[chunk], others[chunk], order))
        incoming.append(lax.ppermute(outgoing[chunk], "row", far_pairs))

    def deliver(group, order):
        own = slice(group * size, (group + 1) * size)
        summed = full_sum(list(zip(kept[own], others[own], incoming[own])), order)
        arrived.append(lax.all_to_all(summed, "ma", split_axis=0, concat_axis=0, tiled=True))
        return summed

    if chunks == 4:
        launch(0, [])
        launch(1, [])
        pass_on(0, kept[1])
        places, sort, unsort, ready = lax.optimization_barrier(
            (places, sort, unsort, outgoing[0])
        )
        launch(2, [ready])
        pass_on(1, kept[2])
        pass_on(2, outgoing[1])
        launch(3, [outgoing[2], incoming[0]])
        summed = deliver(0, kept[3])
        pass_on(3, summed)
        deliver(1, outgoing[3])
    else:
        for chunk in range(chunks):
            launch(chunk, [])
        for chunk in range(chunks):
            pass_on(chunk, kept[-1])
        for group in range(groups):
            deliver(group, outgoing[-1])
    analysed = cycle_work(arrived, places, sort, unsort, cycle_offset, where, cycle_weight)
    own = [
        lax.all_to_all(piece, "ma", split_axis=0, concat_axis=0, tiled=True) for piece in analysed
    ]
    far, gradient = [], []
    for group in range(groups):
        far.append(lax.ppermute(own[group], "row", far_pairs))
        if group + 1 < groups:
            far[group], own[group + 1] = lax.optimization_barrier((far[group], own[group + 1]))
    for group in range(groups):
        if gradient:
            far[group], gradient[-1] = lax.optimization_barrier((far[group], gradient[-1]))
        core = lax.ppermute(own[group], "row", core_pairs)
        corner = lax.ppermute(far[group], "row", core_pairs)
        gradient.append(
            adjoint(
                group,
                groups,
                orders,
                where,
                adjoint_weight,
                (own[group], core, far[group], corner),
                legendre,
                gradient[-1:],
            )
        )
    return gradient[-1]


def solution(mesh):
    in_specs = (
        P(None, "ma", "row"),
        P("ma", None, "row"),
        P(None, "row"),
        P(None, "row"),
        P(),
        P(),
        P(),
        P("ma"),
        P("ma"),
    )
    out_specs = P(None, "ma", "row")
    return jax.shard_map(body, mesh=mesh, in_specs=in_specs, out_specs=out_specs, check_vma=False)
```

time: 189 us -> 166 us (0.88)
  Pallas kernels: 83.6 us -> 68.7 us
  local copies, waits for them, and re-layouts: 17.9 us -> 12.1 us
  waiting for transfers between devices: 29.5 us -> 26.6 us
    pallas_call x7, Pallas kernels: 78.6 us -> 60.1 us  [the longest x4 29 us: synth(): pl.pallas_call(functools.partial(synth_kernel, chunk * count), grid_spec=...]
    unnamed x58 -> x52, local copies, waits for them, and re-layouts: 16.9 us -> 11.7 us
    all_to_all x1, waiting for transfers between devices: 8.22 us -> 5.74 us  [deliver(): lax.all_to_all(summed, 'ma', split_axis=0, concat_axis=0, tiled=True)]
  transfers between devices with their start and end apart: 16 -> 16, of which waited for: 6 -> 7; matrix products, arithmetic and copies ran while one was open for 1% -> 1% of each run, Pallas kernels for 25% -> 22%
where the time goes in v4:
time: 166 us; the launch traced here: 164 us
  Pallas kernels  68.7 us (41%)
  blocking collectives  36 us (22%)
  waiting for transfers between devices  26.6 us (16%)
  starting transfers between devices  18.9 us (11%)
  local copies, waits for them, and re-layouts  12.1 us (7%)
  other arithmetic  1.75 us (1%)
    pallas_call x4, Pallas kernels, synth(): pl.pallas_call(functools.partial(synth_kernel, chunk * count), grid_spec=...  29 us
    all_to_all x1, blocking collectives, deliver(): lax.all_to_all(summed, 'ma', split_axis=0, concat_axis=0, tiled=True)  18.3 us
    pallas_call x2, Pallas kernels, adjoint(): pl.pallas_call(functools.partial(adjoint_kernel, chunk * count), grid_spe...  17.7 us
    all_to_all x1, blocking collectives, body(): lax.all_to_all(piece, 'ma', split_axis=0, concat_axis=0, tiled=True)  17.7 us
    pallas_call x1, Pallas kernels, cycle_work(): pl.pallas_call(functools.partial(cycle_kernel, device_count, groups), gri...  13.4 us
    all_to_all x1, waiting for transfers between devices, body(): lax.all_to_all(piece, 'ma', split_axis=0, concat_axis=0, tiled=True)  12.7 us
    unnamed x52, local copies, waits for them, and re-layouts  11.7 us
    all_to_all x1, starting transfers between devices, deliver(): lax.all_to_all(summed, 'ma', split_axis=0, concat_axis=0, tiled=True)  5.94 us
  transfers between devices with their start and end apart: 16, of which 7 were waited for; matrix products, arithmetic and copies ran while one was open for 1% of the time, Pallas kernels for 22%

profile of v4, /device:TPU:0, one launch (start us, length us, event | category | flops | bytes accessed | tf_op | source)
XLA Modules:
  0.0 164.2 jit_solution(12737118606029649396)
XLA Ops:
  0.6 3.0 %filter_weights.1 = (bf16[512,256]{1,0:T(8,128)(2,1)}, bf16[256,512]{1,0:T(8,128)(2,1)}) custom-call(s32[64]{0:T(128)} %node_ref.1, f32[64]{0:T(128)} %radial_ref.1, f32[64,512]{1,0:T(8,128)} %alpha_ref.1, f32[64,512]{1,0:T(8,128)} %beta_ref.1), custom_call_target="tpu_custom_call" | custom-call | tf_op jit(solution)/shard_map/filter_weights/pallas_call | solution.py:118
  3.6 7.2 %synth.4 = (f32[2,8,64,256]{3,2,1,0:T(8,128)}, f32[2,8,64,256]{3,2,1,0:T(8,128)}) custom-call(s32[2048]{0:T(1024)} %order_ref.11, s32[2]{0:T(128)} %pad_add_fusion.where_ref, f32[2,256,512]{2,1,0:T(8,128)} %coeffs_ref.7, bf16[512,256]{1,0:T(8,128)(2,1)} %get-tuple-element.25.weight_ref, bf16[256,32,512]{2,1,0:T(8,128)(2,1)} %legendre_ref.11), custom_call_target="tpu_custom_call" | custom-call | flops 2147483648 | bytes 4194304 | tf_op jit(solution)/shard_map/synth/pallas_call | solution.py:182
  11.3 7.3 %synth.5 = (f32[2,8,64,256]{3,2,1,0:T(8,128)}, f32[2,8,64,256]{3,2,1,0:T(8,128)}) custom-call(s32[2048]{0:T(1024)} %order_ref.11, s32[2]{0:T(128)} %pad_add_fusion.where_ref, f32[2,256,512]{2,1,0:T(8,128)} %coeffs_ref.7, bf16[512,256]{1,0:T(8,128)(2,1)} %get-tuple-element.25.weight_ref, bf16[256,32,512]{2,1,0:T(8,128)(2,1)} %legendre_ref.11), custom_call_target="tpu_custom_call" | custom-call | flops 2147483648 | bytes 4194304 | tf_op jit(solution)/shard_map/synth/pallas_call | solution.py:182
  21.6 3.0 %collective-permute-start.3 = (bf16[8,64,256]{2,1,0:T(8,128)(2,1)S(1)}, bf16[8,64,256]{2,1,0:T(8,128)(2,1)S(1)}, u32[]{:S(2)}, u32[]{:S(2)}) collective-permute-start(bf16[8,64,256]{2,1,0:T(8,128)(2,1)S(1)} %core_sum.4.refs_0_), channel_id=1, source_target_pairs={{0,16},{8,24},{16,0},{24,8},{1,17},{9,25},{17,1},{25,9},{2,18},{10... | collective-permute-start | bytes 786440 | tf_op jit(solution)/shard_map/ppermute | solution.py:600
  24.9 7.2 %synth.6 = (f32[2,8,64,256]{3,2,1,0:T(8,128)}, f32[2,8,64,256]{3,2,1,0:T(8,128)}) custom-call(s32[2048]{0:T(1024)} %order_ref.11, s32[2]{0:T(128)} %pad_add_fusion.where_ref, f32[2,256,512]{2,1,0:T(8,128)} %coeffs_ref.7, bf16[512,256]{1,0:T(8,128)(2,1)} %get-tuple-element.25.weight_ref, bf16[256,32,512]{2,1,0:T(8,128)(2,1)} %legendre_ref.11, ...), custom_call_target="tpu_custom_call" | custom-call | flops 2147483648 | bytes 4194304 | tf_op jit(solution)/shard_map/synth/pallas_call | solution.py:182
  36.0 1.6 collective-permute-start.6
  38.3 7.2 %synth.7 = (f32[2,8,64,256]{3,2,1,0:T(8,128)}, f32[2,8,64,256]{3,2,1,0:T(8,128)}) custom-call(s32[2048]{0:T(1024)} %order_ref.11, s32[2]{0:T(128)} %pad_add_fusion.where_ref, f32[2,256,512]{2,1,0:T(8,128)} %coeffs_ref.7, bf16[512,256]{1,0:T(8,128)(2,1)} %get-tuple-element.25.weight_ref, bf16[256,32,512]{2,1,0:T(8,128)(2,1)} %legendre_ref.11, ...), custom_call_target="tpu_custom_call" | custom-call | flops 2147483648 | bytes 4194304 | tf_op jit(solution)/shard_map/synth/pallas_call | solution.py:182
  46.5 1.2 copy-done.18
  47.8 1.3 full_sum.2.order_ref
  51.2 5.9 %all-to-all-start = ((bf16[8,128,256]{2,1,0:T(8,128)(2,1)}), bf16[8,128,256]{2,1,0:T(8,128)(2,1)}, u32[]{:S(2)}, u32[]{:S(2)}) async-start(bf16[8,128,256]{2,1,0:T(8,128)(2,1)} %copy-done.1), calls=%async_computation | async-start | bytes 1048576 | tf_op jit(solution)/shard_map/all_to_all | solution.py:605
  57.2 2.2 %collective-permute-done.7.refs_5_ = bf16[8,64,256]{2,1,0:T(8,128)(2,1)} collective-permute-done((bf16[8,64,256]{2,1,0:T(8,128)(2,1)}, bf16[8,64,256]{2,1,0:T(8,128)(2,1)}, u32[]{:S(2)}, u32[]{:S(2)}) %collective-permute-start.7) | collective-permute-done | bytes 262176 | tf_op jit(solution)/shard_map/ppermute | solution.py:600
  59.3 1.2 copy-done.15
  66.2 5.7 %all-to-all-done.refs_0_ = bf16[8,128,256]{2,1,0:T(8,128)(2,1)} async-done(((bf16[8,128,256]{2,1,0:T(8,128)(2,1)}), bf16[8,128,256]{2,1,0:T(8,128)(2,1)}, u32[]{:S(2)}, u32[]{:S(2)}) %all-to-all-start) | async-done | bytes 524320 | tf_op jit(solution)/shard_map/all_to_all | solution.py:605
  71.9 18.3 %all_to_all.20.refs_1_ = bf16[8,128,256]{2,1,0:T(8,128)(2,1)S(1)} all-to-all(bf16[8,128,256]{2,1,0:T(8,128)(2,1)} %copy-done.3), channel_id=1, replica_groups=mesh['row'=4,'ma'=8] {'ma'}, dimensions={0} | all-to-all | bytes 1048576 | tf_op jit(solution)/shard_map/all_to_all | solution.py:605
  90.3 13.4 %cycle_work.1 = (bf16[8,128,256]{2,1,0:T(8,128)(2,1)S(1)}, bf16[8,128,256]{2,1,0:T(8,128)(2,1)S(1)}) custom-call(s32[4]{0:T(128)S(1)} %copy-done.22, s32[2]{0:T(128)S(1)} %copy-done.10, f32[4]{0:T(128)S(1)} %copy-done.23, bf16[8,128,256]{2,1,0:T(8,128)(2,1)} %all-to-all-done.refs_0_, bf16[8,128,256]{2,1,0:T(8,128)(2,1)S(1)} %all_to_all.20.refs_1_, ...), custom_call_target="tpu_custom_call" | custom-call | flops 4294967296 | bytes 8388608 | tf_op jit(solution)/shard_map/cycle_work/pallas_call | solution.py:429
  103.7 17.7 %all_to_all.21.own_ref = bf16[8,128,256]{2,1,0:T(8,128)(2,1)S(1)} all-to-all(bf16[8,128,256]{2,1,0:T(8,128)(2,1)S(1)} %get-tuple-element.38), channel_id=1, replica_groups=mesh['row'=4,'ma'=8] {'ma'}, dimensions={0} | all-to-all | bytes 1048576 | tf_op jit(solution)/shard_map/all_to_all | solution.py:631
  121.4 3.6 %all-to-all-start.3 = ((bf16[8,128,256]{2,1,0:T(8,128)(2,1)}), bf16[8,128,256]{2,1,0:T(8,128)(2,1)S(1)}, u32[]{:S(2)}, u32[]{:S(2)}) async-start(bf16[8,128,256]{2,1,0:T(8,128)(2,1)} %copy-done.2), calls=%async_computation.3 | async-start | bytes 1048576 | tf_op jit(solution)/shard_map/all_to_all | solution.py:631
  125.0 1.3 collective-permute-start.8
  126.4 12.7 %all-to-all-done.3.own_ref = bf16[8,128,256]{2,1,0:T(8,128)(2,1)S(1)} async-done(((bf16[8,128,256]{2,1,0:T(8,128)(2,1)}), bf16[8,128,256]{2,1,0:T(8,128)(2,1)S(1)}, u32[]{:S(2)}, u32[]{:S(2)}) %all-to-all-start.3) | async-done | bytes 524320 | tf_op jit(solution)/shard_map/all_to_all | solution.py:631
  139.1 1.3 collective-permute-start.10
  141.0 8.8 %adjoint.2.refs_0_ = f32[2,256,512]{2,1,0:T(8,128)} custom-call(s32[2048]{0:T(1024)S(1)} %copy-done.5, s32[2]{0:T(128)S(1)} %copy-done.10, bf16[8,128,256]{2,1,0:T(8,128)(2,1)S(1)} %all_to_all.21.own_ref, bf16[8,128,256]{2,1,0:T(8,128)(2,1)S(1)} %collective-permute-done.11.core_ref, bf16[8,128,256]{2,1,0:T(8,128)(2,1)S(1)} %collective-permute-done.8.far_ref, ...), custom_call_target="tpu_custom_call" | custom-call | flops 2147483648 | bytes 6291456 | tf_op jit(solution)/shard_map/adjoint/pallas_call | solution.py:521
  149.8 3.6 %collective-permute-done.10.far_ref = bf16[8,128,256]{2,1,0:T(8,128)(2,1)S(1)} collective-permute-done((bf16[8,128,256]{2,1,0:T(8,128)(2,1)S(1)}, bf16[8,128,256]{2,1,0:T(8,128)(2,1)S(1)}, u32[]{:S(2)}, u32[]{:S(2)}) %collective-permute-start.10) | collective-permute-done | bytes 524320 | tf_op jit(solution)/shard_map/ppermute | solution.py:635
  153.4 1.9 %collective-permute-done.13.corner_ref = bf16[8,128,256]{2,1,0:T(8,128)(2,1)S(1)} collective-permute-done((bf16[8,128,256]{2,1,0:T(8,128)(2,1)S(1)}, bf16[8,128,256]{2,1,0:T(8,128)(2,1)S(1)}, u32[]{:S(2)}, u32[]{:S(2)}) %collective-permute-start.13) | collective-permute-done | bytes 524320 | tf_op jit(solution)/shard_map/ppermute | solution.py:642
  155.3 8.9 %adjoint.3 = f32[2,256,512]{2,1,0:T(8,128)} custom-call(s32[2048]{0:T(1024)S(1)} %copy-done.5, s32[2]{0:T(128)S(1)} %copy-done.10, bf16[8,128,256]{2,1,0:T(8,128)(2,1)S(1)} %all-to-all-done.3.own_ref, bf16[8,128,256]{2,1,0:T(8,128)(2,1)S(1)} %collective-permute-done.9.core_ref, ...), custom_call_target="tpu_custom_call", output_to_operand_aliasing={{}: (8, {})} | custom-call | flops 2147483648 | bytes 6291456 | tf_op jit(solution)/shard_map/adjoint/pallas_call | solution.py:521
  (84 shorter events, 18.2 us)
Async XLA Ops:
  10.8 9.1 %collective-permute-start = (f32[2,8,64,256]{3,2,1,0:T(8,128)}, f32[2,8,64,256]{3,2,1,0:T(8,128)}, u32[]{:S(2)}, u32[]{:S(2)}) collective-permute-start(f32[2,8,64,256]{3,2,1,0:T(8,128)} %get-tuple-element.27), channel_id=1, source_target_pairs={{0,8},{8,0},{16,24},{24,16},{1,9},{9,1},{17,25},{25,17},{2,10},{10... | collective-permute-start | bytes 3145736 | tf_op jit(solution)/shard_map/ppermute | solution.py:596
  18.6 13.6 %collective-permute-start.2 = (f32[2,8,64,256]{3,2,1,0:T(8,128)}, f32[2,8,64,256]{3,2,1,0:T(8,128)}, u32[]{:S(2)}, u32[]{:S(2)}) collective-permute-start(f32[2,8,64,256]{3,2,1,0:T(8,128)} %get-tuple-element.32), channel_id=1, source_target_pairs={{0,8},{8,0},{16,24},{24,16},{1,9},{9,1},{17,25},{25,17},{2,10},{10... | collective-permute-start | bytes 3145736 | tf_op jit(solution)/shard_map/ppermute | solution.py:596
  21.6 16.0 %collective-permute-start.3 = (bf16[8,64,256]{2,1,0:T(8,128)(2,1)S(1)}, bf16[8,64,256]{2,1,0:T(8,128)(2,1)S(1)}, u32[]{:S(2)}, u32[]{:S(2)}) collective-permute-start(bf16[8,64,256]{2,1,0:T(8,128)(2,1)S(1)} %core_sum.4.refs_0_), channel_id=1, source_target_pairs={{0,16},{8,24},{16,0},{24,8},{1,17},{9,25},{17,1},{25,9},{2,18},{10... | collective-permute-start | bytes 786440 | tf_op jit(solution)/shard_map/ppermute | solution.py:600
  32.2 2.9 %collective-permute-start.1 = (f32[2,8,64,256]{3,2,1,0:T(8,128)}, f32[2,8,64,256]{3,2,1,0:T(8,128)S(1)}, u32[]{:S(2)}, u32[]{:S(2)}) collective-permute-start(f32[2,8,64,256]{3,2,1,0:T(8,128)} %get-tuple-element.31), channel_id=1, source_target_pairs={{0,8},{8,0},{16,24},{24,16},{1,9},{9,1},{17,25},{25,17},{2,10},{10... | collective-permute-start | bytes 3145736 | tf_op jit(solution)/shard_map/ppermute | solution.py:596
  34.5 11.1 %collective-permute-start.4 = (bf16[8,64,256]{2,1,0:T(8,128)(2,1)S(1)}, bf16[8,64,256]{2,1,0:T(8,128)(2,1)S(1)}, u32[]{:S(2)}, u32[]{:S(2)}) collective-permute-start(bf16[8,64,256]{2,1,0:T(8,128)(2,1)S(1)} %core_sum.5.order_ref), channel_id=1, source_target_pairs={{0,16},{8,24},{16,0},{24,8},{1,17},{9,25},{17,1},{25,9},{2,18},{10... | collective-permute-start | bytes 786440 | tf_op jit(solution)/shard_map/ppermute | solution.py:600
  36.0 21.1 %collective-permute-start.6 = (bf16[8,64,256]{2,1,0:T(8,128)(2,1)S(1)}, bf16[8,64,256]{2,1,0:T(8,128)(2,1)}, u32[]{:S(2)}, u32[]{:S(2)}) collective-permute-start(bf16[8,64,256]{2,1,0:T(8,128)(2,1)S(1)} %core_sum.6.refs_0_), channel_id=1, source_target_pairs={{0,16},{8,24},{16,0},{24,8},{1,17},{9,25},{17,1},{25,9},{2,18},{10... | collective-permute-start | bytes 786440 | tf_op jit(solution)/shard_map/ppermute | solution.py:600
  45.6 3.5 %collective-permute-start.5 = (f32[2,8,64,256]{3,2,1,0:T(8,128)}, f32[2,8,64,256]{3,2,1,0:T(8,128)S(1)}, u32[]{:S(2)}, u32[]{:S(2)}) collective-permute-start(f32[2,8,64,256]{3,2,1,0:T(8,128)} %get-tuple-element.34), channel_id=1, source_target_pairs={{0,8},{8,0},{16,24},{24,16},{1,9},{9,1},{17,25},{25,17},{2,10},{10... | collective-permute-start | bytes 3145736 | tf_op jit(solution)/shard_map/ppermute | solution.py:596
  50.3 9.0 %collective-permute-start.7 = (bf16[8,64,256]{2,1,0:T(8,128)(2,1)}, bf16[8,64,256]{2,1,0:T(8,128)(2,1)}, u32[]{:S(2)}, u32[]{:S(2)}) collective-permute-start(bf16[8,64,256]{2,1,0:T(8,128)(2,1)} %core_sum.7.order_ref), channel_id=1, source_target_pairs={{0,16},{8,24},{16,0},{24,8},{1,17},{9,25},{17,1},{25,9},{2,18},{10... | collective-permute-start | bytes 786440 | tf_op jit(solution)/shard_map/ppermute | solution.py:600
  51.2 39.0 %copy-start.22 = (s32[4]{0:T(128)S(1)}, s32[4]{0:T(128)}, u32[]{:S(2)}) copy-start(s32[4]{0:T(128)} %offset_ref.1) | copy-start | bytes 52
  51.2 39.0 %copy-start.23 = (f32[4]{0:T(128)S(1)}, f32[4]{0:T(128)}, u32[]{:S(2)}) copy-start(f32[4]{0:T(128)} %weight_ref.1) | copy-start | bytes 52
  51.2 39.0 %copy-start.24 = (bf16[128,256]{1,0:T(8,128)(2,1)S(1)}, bf16[128,256]{1,0:T(8,128)(2,1)}, u32[]{:S(2)}) copy-start(bf16[128,256]{1,0:T(8,128)(2,1)} %constant.65.clone.refs_7_) | copy-start | bytes 196612
  51.2 39.0 %copy-start.25 = (bf16[128,128]{1,0:T(8,128)(2,1)S(1)}, bf16[128,128]{1,0:T(8,128)(2,1)}, u32[]{:S(2)}) copy-start(bf16[128,128]{1,0:T(8,128)(2,1)} %constant.64.clone.refs_6_) | copy-start | bytes 98308
  51.2 20.7 %all-to-all-start = ((bf16[8,128,256]{2,1,0:T(8,128)(2,1)}), bf16[8,128,256]{2,1,0:T(8,128)(2,1)}, u32[]{:S(2)}, u32[]{:S(2)}) async-start(bf16[8,128,256]{2,1,0:T(8,128)(2,1)} %copy-done.1), calls=%async_computation | async-start | bytes 1048576 | tf_op jit(solution)/shard_map/all_to_all | solution.py:605
  57.2 33.1 %copy-start.10 = (s32[2]{0:T(128)S(1)}, s32[2]{0:T(128)}, u32[]{:S(2)}) copy-start(s32[2]{0:T(128)} %pad_add_fusion.where_ref) | copy-start | bytes 28
  103.7 17.7 %copy-start.2 = (bf16[8,128,256]{2,1,0:T(8,128)(2,1)}, bf16[8,128,256]{2,1,0:T(8,128)(2,1)S(1)}, u32[]{:S(2)}) copy-start(bf16[8,128,256]{2,1,0:T(8,128)(2,1)S(1)} %get-tuple-element.39) | copy-start | bytes 1572868
  103.7 37.3 %copy-start = (bf16[256,512]{1,0:T(8,128)(2,1)S(1)}, bf16[256,512]{1,0:T(8,128)(2,1)}, u32[]{:S(2)}) copy-start(bf16[256,512]{1,0:T(8,128)(2,1)} %get-tuple-element.42.weight_ref) | copy-start | bytes 786436
  103.7 37.3 %copy-start.5 = (s32[2048]{0:T(1024)S(1)}, s32[2048]{0:T(1024)}, u32[]{:S(2)}) copy-start(s32[2048]{0:T(1024)} %order_ref.11) | copy-start | bytes 24580
  121.4 17.7 %all-to-all-start.3 = ((bf16[8,128,256]{2,1,0:T(8,128)(2,1)}), bf16[8,128,256]{2,1,0:T(8,128)(2,1)S(1)}, u32[]{:S(2)}, u32[]{:S(2)}) async-start(bf16[8,128,256]{2,1,0:T(8,128)(2,1)} %copy-done.2), calls=%async_computation.3 | async-start | bytes 1048576 | tf_op jit(solution)/shard_map/all_to_all | solution.py:631
  125.0 14.0 %collective-permute-start.8 = (bf16[8,128,256]{2,1,0:T(8,128)(2,1)S(1)}, bf16[8,128,256]{2,1,0:T(8,128)(2,1)S(1)}, u32[]{:S(2)}, u32[]{:S(2)}) collective-permute-start(bf16[8,128,256]{2,1,0:T(8,128)(2,1)S(1)} %all_to_all.21.own_ref), channel_id=1, source_target_pairs={{0,16},{8,24},{16,0},{24,8},{1,17},{9,25},{17,1},{25,9},{2,18},{10... | collective-permute-start | bytes 1572872 | tf_op jit(solution)/shard_map/ppermute | solution.py:635
  126.4 14.3 %collective-permute-start.11 = (bf16[8,128,256]{2,1,0:T(8,128)(2,1)S(1)}, bf16[8,128,256]{2,1,0:T(8,128)(2,1)S(1)}, u32[]{:S(2)}, u32[]{:S(2)}) collective-permute-start(bf16[8,128,256]{2,1,0:T(8,128)(2,1)S(1)} %all_to_all.21.own_ref), channel_id=1, source_target_pairs={{0,8},{8,0},{16,24},{24,16},{1,9},{9,1},{17,25},{25,17},{2,10},{10... | collective-permute-start | bytes 1572872 | tf_op jit(solution)/shard_map/ppermute | solution.py:641
  139.1 1.9 %collective-permute-start.12 = (bf16[8,128,256]{2,1,0:T(8,128)(2,1)S(1)}, bf16[8,128,256]{2,1,0:T(8,128)(2,1)S(1)}, u32[]{:S(2)}, u32[]{:S(2)}) collective-permute-start(bf16[8,128,256]{2,1,0:T(8,128)(2,1)S(1)} %collective-permute-done.8.far_ref), channel_id=1, source_target_pairs={{0,8},{8,0},{16,24},{24,16},{1,9},{9,1},{17,25},{25,17},{2,10},{10... | collective-permute-start | bytes 1572872 | tf_op jit(solution)/shard_map/ppermute | solution.py:642
  139.1 14.3 %collective-permute-start.10 = (bf16[8,128,256]{2,1,0:T(8,128)(2,1)S(1)}, bf16[8,128,256]{2,1,0:T(8,128)(2,1)S(1)}, u32[]{:S(2)}, u32[]{:S(2)}) collective-permute-start(bf16[8,128,256]{2,1,0:T(8,128)(2,1)S(1)} %all-to-all-done.3.own_ref), channel_id=1, source_target_pairs={{0,16},{8,24},{16,0},{24,8},{1,17},{9,25},{17,1},{25,9},{2,18},{10... | collective-permute-start | bytes 1572872 | tf_op jit(solution)/shard_map/ppermute | solution.py:635
  140.4 13.0 %collective-permute-start.9 = (bf16[8,128,256]{2,1,0:T(8,128)(2,1)S(1)}, bf16[8,128,256]{2,1,0:T(8,128)(2,1)S(1)}, u32[]{:S(2)}, u32[]{:S(2)}) collective-permute-start(bf16[8,128,256]{2,1,0:T(8,128)(2,1)S(1)} %all-to-all-done.3.own_ref), channel_id=1, source_target_pairs={{0,8},{8,0},{16,24},{24,16},{1,9},{9,1},{17,25},{25,17},{2,10},{10... | collective-permute-start | bytes 1572872 | tf_op jit(solution)/shard_map/ppermute | solution.py:641
  153.4 1.9 %collective-permute-start.13 = (bf16[8,128,256]{2,1,0:T(8,128)(2,1)S(1)}, bf16[8,128,256]{2,1,0:T(8,128)(2,1)S(1)}, u32[]{:S(2)}, u32[]{:S(2)}) collective-permute-start(bf16[8,128,256]{2,1,0:T(8,128)(2,1)S(1)} %collective-permute-done.10.far_ref), channel_id=1, source_target_pairs={{0,8},{8,0},{16,24},{24,16},{1,9},{9,1},{17,25},{25,17},{2,10},{10... | collective-permute-start | bytes 1572872 | tf_op jit(solution)/shard_map/ppermute | solution.py:642
  (18 other events, 37.8 us)

commit v5 on v4

--- a/solution.py
+++ b/solution.py
@@ -14,7 +14,8 @@
 PADDED = 136
 CHUNKS = 4
 GROUPS = 2
-BLOCK = 16
+SYNTH_BLOCK = 16
+BLOCK = 32
 MIB = 1 << 20
 F32 = jnp.float32
 BF16 = jnp.bfloat16
@@ -138,76 +139,84 @@
 def synth_kernel(
     first, order_ref, where_ref, coeffs_ref, weight_ref, legendre_ref, *refs
 ):
-    keep_ref, send_ref, terms_scr, sums_scr = refs[-4:]
+    keep_ref, send_ref, terms_even, terms_odd, sums_even, sums_odd = refs[-6:]
     step = pl.program_id(0)
     row = where_ref[0]
-    base = where_ref[1] + first + step * BLOCK
+    base = where_ref[1] + first + step * SYNTH_BLOCK
     degrees = coeffs_ref.shape[2]
     cycles = legendre_ref.shape[1]
     owners = cycles // 4
     lanes = weight_ref.shape[1] // 2
     degree = row * degrees + lax.broadcasted_iota(jnp.int32, (1, degrees), 1)
-    for slot in range(BLOCK):
-        live = degree >= order_ref[base + slot]
-        values = legendre_ref[slot].astype(F32)
+    for group in range(SYNTH_BLOCK // 8):
+        terms = terms_odd if group % 2 else terms_even
+        sums = sums_odd if group % 2 else sums_even
+        for place in range(8):
+            slot = group * 8 + place
+            live = degree >= order_ref[base + slot]
+            values = legendre_ref[slot].astype(F32)
+            for part in range(2):
+                coeff = jnp.where(live, coeffs_ref[part, slot : slot + 1, :], 0.0)
+                high, low = two_parts(values * coeff)
+                start = (part * 8 + place) * cycles
+                terms[0, start : start + cycles, :] = high
+                terms[1, start : start + cycles, :] = low
+        both = jnp.dot(terms[0], weight_ref[...], preferred_element_type=F32)
+        rest = jnp.dot(terms[1], weight_ref[:, :lanes], preferred_element_type=F32)
+        sums[...] = both[:, :lanes] + both[:, lanes:] + rest
         for part in range(2):
-            coeff = jnp.where(live, coeffs_ref[part, slot : slot + 1, :], 0.0)
-            high, low = two_parts(values * coeff)
-            start = (part * BLOCK + slot) * cycles
-            terms_scr[0, start : start + cycles, :] = high
-            terms_scr[1, start : start + cycles, :] = low
-    for part in range(2):
-        rows = slice(part * BLOCK * cycles, (part + 1) * BLOCK * cycles)
-        both = jnp.dot(terms_scr[0, rows], weight_ref[...], preferred_element_type=F32)
-        rest = jnp.dot(terms_scr[1, rows], weight_ref[:, :lanes], preferred_element_type=F32)
-        sums_scr[rows, :] = both[:, :lanes] + both[:, lanes:] + rest
-    for part in range(2):
-        for owner in range(owners):
-            for away in range(4):
-                cycle = 4 * owner + (row ^ away)
-                piece = sums_scr[pl.ds(part * BLOCK * cycles + cycle, BLOCK, stride=cycles), :]
-                target = send_ref if away % 2 else keep_ref
-                target[away // 2, owner, :, part * lanes : (part + 1) * lanes] = piece
-
-
-def synth(chunk, chunks, orders, where, coeffs, weight, legendre, order):
+            for owner in range(owners):
+                for away in range(4):
+                    cycle = 4 * owner + (row ^ away)
+                    piece = sums[pl.ds(part * 8 * cycles + cycle, 8, stride=cycles), :]
+                    target = send_ref if away % 2 else keep_ref
+                    target[
+                        away // 2,
+                        owner,
+                        group * 8 : group * 8 + 8,
+                        part * lanes : (part + 1) * lanes,
+                    ] = piece
+
+
+def synth(chunk, chunks, orders, where, coeffs, weight, legendre):
     orders_here, cycles, degrees = legendre.shape
     count = orders_here // chunks
-    steps = count // BLOCK
+    steps = count // SYNTH_BLOCK
     start = chunk * steps
     owners = cycles // 4
     lanes = weight.shape[1] // 2
     out = jax.ShapeDtypeStruct((2, owners, count, 2 * lanes), F32)
-    out_spec = pl.BlockSpec((2, owners, BLOCK, 2 * lanes), lambda t, *_: (0, 0, t, 0))
+    out_spec = pl.BlockSpec((2, owners, SYNTH_BLOCK, 2 * lanes), lambda t, *_: (0, 0, t, 0))
     return pl.pallas_call(
         functools.partial(synth_kernel, chunk * count),
         grid_spec=pltpu.PrefetchScalarGridSpec(
             num_scalar_prefetch=2,
             grid=(steps,),
             in_specs=[
-                pl.BlockSpec((2, BLOCK, degrees), lambda t, *_: (0, start + t, 0)),
+                pl.BlockSpec((2, SYNTH_BLOCK, degrees), lambda t, *_: (0, start + t, 0)),
                 whole(weight.shape),
-                pl.BlockSpec((BLOCK, cycles, degrees), lambda t, *_: (start + t, 0, 0)),
-            ]
-            + [anywhere()] * len(order),
+                pl.BlockSpec((SYNTH_BLOCK, cycles, degrees), lambda t, *_: (start + t, 0, 0)),
+            ],
             out_specs=[out_spec, out_spec],
             scratch_shapes=[
-                pltpu.VMEM((2, 2 * BLOCK * cycles, degrees), BF16),
-                pltpu.VMEM((2 * BLOCK * cycles, lanes), F32),
+                pltpu.VMEM((2, 16 * cycles, degrees), BF16),
+                pltpu.VMEM((2, 16 * cycles, degrees), BF16),
+                pltpu.VMEM((16 * cycles, lanes), F32),
+                pltpu.VMEM((16 * cycles, lanes), F32),
             ],
         ),
         out_shape=[out, out],
-        compiler_params=pltpu.CompilerParams(vmem_limit_bytes=56 * MIB),
+        compiler_params=pltpu.CompilerParams(vmem_limit_bytes=50 * MIB),
         cost_estimate=pl.CostEstimate(
             flops=2 * count * cycles * degrees * lanes * 2 * 4,
             bytes_accessed=count * (cycles * degrees * 2 + 2 * cycles * lanes * 4),
             transcendentals=0,
         ),
         name="synth",
-    )(orders, where, coeffs, weight, legendre, *order)
-
-
-def core_sum_kernel(keep_ref, other_ref, order_ref, out_ref):
+    )(orders, where, coeffs, weight, legendre)
+
+
+def core_sum_kernel(keep_ref, other_ref, token_ref, out_ref):
     out_ref[...] = (keep_ref[0] + other_ref[0]).astype(BF16)
 
 
@@ -217,7 +226,7 @@
     return pl.pallas_call(
         core_sum_kernel,
         grid=(1,),
-        in_specs=[half, half, anywhere()],
+        in_specs=[half, half, pl.BlockSpec(memory_space=pltpu.SMEM)],
         out_specs=pl.BlockSpec(shape, lambda t: (0, 0, 0)),
         out_shape=jax.ShapeDtypeStruct(shape, BF16),
         compiler_params=pltpu.CompilerParams(vmem_limit_bytes=16 * MIB),
@@ -226,7 +235,7 @@
     )(keep, other, order)
 
 
-def full_sum_kernel(order_ref, *refs):
+def full_sum_kernel(token_ref, *refs):
     out_ref = refs[-1]
     start = 0
     for index in range(0, len(refs) - 1, 3):
@@ -238,7 +247,7 @@
 
 
 def full_sum(chunks, order):
-    operands, specs, count = [], [anywhere()], 0
+    operands, specs, count = [], [pl.BlockSpec(memory_space=pltpu.SMEM)], 0
     for keep, other, incoming in chunks:
         shape = incoming.shape
         half = pl.BlockSpec((1,) + shape, lambda t: (0, 0, 0, 0))
@@ -252,23 +261,20 @@
         in_specs=specs,
         out_specs=pl.BlockSpec(full, lambda t: (0, 0, 0)),
         out_shape=jax.ShapeDtypeStruct(full, BF16),
-        compiler_params=pltpu.CompilerParams(vmem_limit_bytes=24 * MIB),
+        compiler_params=pltpu.CompilerParams(vmem_limit_bytes=16 * MIB),
         cost_estimate=pl.CostEstimate(flops=4 * 10**10, bytes_accessed=MIB, transcendentals=0),
         name="full_sum",
     )(order, *operands)
 
 
-def cycle_kernel(device_count, groups, offset_ref, where_ref, weight_ref, *refs):
+def cycle_kernel(groups, sizes, offset_ref, where_ref, weight_ref, *refs):
     pieces = refs[:groups]
     place_ref, sort_ref, unsort_ref, spread_ref, pixel_ref, back_ref, gather_ref = refs[
         groups : groups + 7
     ]
-    outs = refs[groups + 7 : 2 * groups + 7]
-    spread_scr, gather_scr, sorted_scr, middle_scr, product_scr, back_scr, sems = refs[
-        2 * groups + 7 :
-    ]
-    blocks = place_ref.shape[1]
-    count = pieces[0].shape[1]
+    outs = refs[groups + 7 : groups + 7 + len(sizes)]
+    spread_scr, gather_scr, sorted_scr, middle_scr, product_scr, back_scr, sems = refs[-7:]
+    device_count, blocks = place_ref.shape[:2]
     lanes = pieces[0].shape[2] // 2
     turned = offset_ref[where_ref[0]]
     scale = weight_ref[where_ref[0]]
@@ -414,20 +420,23 @@
         slots = jnp.dot(
             unsort_ref[peer], sorted_scr[peer], preferred_element_type=F32
         ).astype(BF16)
-        for group in range(groups):
-            outs[group][peer] = slots[group * count : (group + 1) * count]
+        start = 0
+        for out, size in zip(outs, sizes):
+            out[peer] = slots[start : start + size]
+            start += size
         return carry
 
     lax.fori_loop(0, device_count, unsort_step, 0, unroll=2)
 
 
-def cycle_work(pieces, places, sort, unsort, offset, where, cycle_weight):
+def cycle_work(pieces, sizes, places, sort, unsort, offset, where, cycle_weight):
     groups = len(pieces)
     device_count, count, lanes = pieces[0].shape
+    out_shapes = [(device_count, size, lanes) for size in sizes]
     spread, pixel, back, gather = [jnp.asarray(table) for table in fourier_tables()]
     tables = [places, sort, unsort]
     return pl.pallas_call(
-        functools.partial(cycle_kernel, device_count, groups),
+        functools.partial(cycle_kernel, groups, sizes),
         grid_spec=pltpu.PrefetchScalarGridSpec(
             num_scalar_prefetch=2,
             grid=(1,),
@@ -435,7 +444,7 @@
             + [whole(piece.shape) for piece in pieces]
             + [whole(table.shape) for table in tables]
             + [hbm(), whole(pixel.shape), whole(back.shape), hbm()],
-            out_specs=[whole(piece.shape) for piece in pieces],
+            out_specs=[whole(shape) for shape in out_shapes],
             scratch_shapes=[
                 pltpu.VMEM(spread.shape[1:], BF16),
                 pltpu.VMEM(gather.shape[1:], BF16),
@@ -446,8 +455,8 @@
                 pltpu.SemaphoreType.DMA((places.shape[1] + 1,)),
             ],
         ),
-        out_shape=[jax.ShapeDtypeStruct(piece.shape, BF16) for piece in pieces],
-        compiler_params=pltpu.CompilerParams(vmem_limit_bytes=48 * MIB),
+        out_shape=[jax.ShapeDtypeStruct(shape, BF16) for shape in out_shapes],
+        compiler_params=pltpu.CompilerParams(vmem_limit_bytes=40 * MIB),
         cost_estimate=pl.CostEstimate(
             flops=4 * SIDE * 128 * 256 * 256 * 2, bytes_accessed=8 * MIB, transcendentals=0
         ),
@@ -458,7 +467,7 @@
 def adjoint_kernel(
     first, order_ref, where_ref, own_ref, core_ref, far_ref, corner_ref, weight_ref, legendre_ref, *refs
 ):
-    out_ref, values_scr, terms_scr = refs[-3:]
+    out_ref, values_even, values_odd, terms_even, terms_odd = refs[-5:]
     step = pl.program_id(0)
     row = where_ref[0]
     base = where_ref[1] + first + step * BLOCK
@@ -468,58 +477,66 @@
     lanes = weight_ref.shape[0] // 2
     pitch = cycles + 8
     tiles = degrees // 128
+    quarter = owners * 16
     degree = row * degrees + lax.broadcasted_iota(jnp.int32, (8, degrees), 1)
     sublane = lax.broadcasted_iota(jnp.int32, (8, degrees), 0)
-    for slot in range(BLOCK):
-        wide = legendre_ref[slot].astype(F32)
-        for tile in range(tiles):
-            values_scr[tile, slot * pitch : slot * pitch + cycles, :] = wide[
-                :, tile * 128 : tile * 128 + 128
-            ]
     sources = (own_ref, core_ref, far_ref, corner_ref)
-    quarter = owners * BLOCK
-    for part in range(2):
-        for away in range(4):
-            rows = sources[away][:, :, part * lanes : (part + 1) * lanes].reshape(quarter, lanes)
-            start = (part * 4 + away) * quarter
-            terms_scr[start : start + quarter, :] = jnp.dot(
-                jnp.concatenate([rows, rows], axis=1), weight_ref[...], preferred_element_type=F32
-            )
-    for half in range(BLOCK // 8):
-        total = [jnp.zeros((8, degrees), F32), jnp.zeros((8, degrees), F32)]
-        for away in range(4):
-            for owner in range(owners):
-                cycle = 4 * owner + (row ^ away)
-                factor = jnp.concatenate(
-                    [
-                        values_scr[tile, pl.ds(half * 8 * pitch + cycle, 8, stride=pitch), :]
-                        for tile in range(tiles)
-                    ],
-                    axis=1,
+    for group in range(BLOCK // 16):
+        values_scr = values_odd if group % 2 else values_even
+        terms_scr = terms_odd if group % 2 else terms_even
+        for place in range(16):
+            wide = legendre_ref[group * 16 + place].astype(F32)
+            for tile in range(tiles):
+                values_scr[tile, place * pitch : place * pitch + cycles, :] = wide[
+                    :, tile * 128 : tile * 128 + 128
+                ]
+        for part in range(2):
+            for away in range(4):
+                rows = sources[away][
+                    :, group * 16 : group * 16 + 16, part * lanes : (part + 1) * lanes
+                ].reshape(quarter, lanes)
+                start = (part * 4 + away) * quarter
+                terms_scr[start : start + quarter, :] = jnp.dot(
+                    jnp.concatenate([rows, rows], axis=1),
+                    weight_ref[...],
+                    preferred_element_type=F32,
                 )
-                for part in range(2):
-                    at = (part * 4 + away) * quarter + owner * BLOCK + half * 8
-                    total[part] = total[part] + terms_scr[at : at + 8, :] * factor
-        lowest = jnp.zeros((8, degrees), jnp.int32)
-        for slot in range(8):
-            lowest = jnp.where(sublane == slot, order_ref[base + half * 8 + slot], lowest)
-        for part in range(2):
-            out_ref[part, half * 8 : half * 8 + 8, :] = jnp.where(
-                degree >= lowest, total[part], 0.0
-            )
-
-
-def adjoint(chunk, chunks, orders, where, weight, pieces, legendre, earlier):
+        for half in range(2):
+            total = [jnp.zeros((8, degrees), F32), jnp.zeros((8, degrees), F32)]
+            for away in range(4):
+                for owner in range(owners):
+                    cycle = 4 * owner + (row ^ away)
+                    factor = jnp.concatenate(
+                        [
+                            values_scr[tile, pl.ds(half * 8 * pitch + cycle, 8, stride=pitch), :]
+                            for tile in range(tiles)
+                        ],
+                        axis=1,
+                    )
+                    for part in range(2):
+                        at = (part * 4 + away) * quarter + owner * 16 + half * 8
+                        total[part] = total[part] + terms_scr[at : at + 8, :] * factor
+            lowest = jnp.zeros((8, degrees), jnp.int32)
+            first_slot = group * 16 + half * 8
+            for place in range(8):
+                lowest = jnp.where(sublane == place, order_ref[base + first_slot + place], lowest)
+            for part in range(2):
+                out_ref[part, first_slot : first_slot + 8, :] = jnp.where(
+                    degree >= lowest, total[part], 0.0
+                )
+
+
+def adjoint(first, orders, where, weight, pieces, legendre, earlier):
     orders_here, cycles, degrees = legendre.shape
-    count = orders_here // chunks
+    count = pieces[0].shape[1]
     steps = count // BLOCK
-    start = chunk * steps
+    start = first // BLOCK
     owners = cycles // 4
     lanes = weight.shape[0] // 2
     piece_spec = pl.BlockSpec((owners, BLOCK, 2 * lanes), lambda t, *_: (0, t, 0))
     out = jax.ShapeDtypeStruct((2, orders_here, degrees), F32)
     return pl.pallas_call(
-        functools.partial(adjoint_kernel, chunk * count),
+        functools.partial(adjoint_kernel, first),
         grid_spec=pltpu.PrefetchScalarGridSpec(
             num_scalar_prefetch=2,
             grid=(steps,),
@@ -531,13 +548,15 @@
             + [anywhere()] * len(earlier),
             out_specs=pl.BlockSpec((2, BLOCK, degrees), lambda t, *_: (0, start + t, 0)),
             scratch_shapes=[
-                pltpu.VMEM((degrees // 128, BLOCK * (cycles + 8), 128), F32),
-                pltpu.VMEM((2 * BLOCK * cycles, degrees), F32),
+                pltpu.VMEM((degrees // 128, 16 * (cycles + 8), 128), F32),
+                pltpu.VMEM((degrees // 128, 16 * (cycles + 8), 128), F32),
+                pltpu.VMEM((32 * cycles, degrees), F32),
+                pltpu.VMEM((32 * cycles, degrees), F32),
             ],
         ),
         out_shape=out,
         input_output_aliases={8: 0} if earlier else {},
-        compiler_params=pltpu.CompilerParams(vmem_limit_bytes=48 * MIB),
+        compiler_params=pltpu.CompilerParams(vmem_limit_bytes=40 * MIB),
         cost_estimate=pl.CostEstimate(
             flops=2 * count * cycles * degrees * lanes * 2 * 2,
             bytes_accessed=count * (cycles * degrees * 2 + 2 * cycles * lanes * 2),
@@ -590,68 +609,74 @@
     size = chunks // groups
     kept, others, outgoing, incoming, arrived = [], [], [], [], []
 
-    def launch(chunk, order):
-        keep, send = synth(chunk, chunks, orders, where, coeffs, synth_weight, legendre, order)
+    def after(*values):
+        return lax.optimization_barrier((where, *values))[0]
+
+    def launch(chunk, token):
+        keep, send = synth(chunk, chunks, orders, token, coeffs, synth_weight, legendre)
         kept.append(keep)
         others.append(lax.ppermute(send, "row", core_pairs))
 
-    def pass_on(chunk, order):
-        outgoing.append(core_sum(kept[chunk], others[chunk], order))
+    def pass_on(chunk, token):
+        outgoing.append(core_sum(kept[chunk], others[chunk], token))
         incoming.append(lax.ppermute(outgoing[chunk], "row", far_pairs))
 
-    def deliver(group, order):
+    def deliver(group, token):
         own = slice(group * size, (group + 1) * size)
-        summed = full_sum(list(zip(kept[own], others[own], incoming[own])), order)
+        summed = full_sum(list(zip(kept[own], others[own], incoming[own])), token)
         arrived.append(lax.all_to_all(summed, "ma", split_axis=0, concat_axis=0, tiled=True))
         return summed
 
     if chunks == 4:
-        launch(0, [])
-        launch(1, [])
-        pass_on(0, kept[1])
-        places, sort, unsort, ready = lax.optimization_barrier(
-            (places, sort, unsort, outgoing[0])
-        )
-        launch(2, [ready])
-        pass_on(1, kept[2])
-        pass_on(2, outgoing[1])
-        launch(3, [outgoing[2], incoming[0]])
-        summed = deliver(0, kept[3])
-        pass_on(3, summed)
-        deliver(1, outgoing[3])
+        launch(0, where)
+        launch(1, where)
+        pass_on(0, after(kept[1]))
+        places, sort, unsort, token = lax.optimization_barrier((places, sort, unsort, where))
+        launch(2, lax.optimization_barrier((token, outgoing[0]))[0])
+        pass_on(1, after(kept[2]))
+        pass_on(2, after(outgoing[1]))
+        launch(3, after(outgoing[2], incoming[0]))
+        summed = deliver(0, after(kept[3]))
+        pass_on(3, after(summed))
+        deliver(1, after(outgoing[3]))
     else:
         for chunk in range(chunks):
-            launch(chunk, [])
+            launch(chunk, where)
         for chunk in range(chunks):
-            pass_on(chunk, kept[-1])
+            pass_on(chunk, after(kept[-1]))
         for group in range(groups):
-            deliver(group, outgoing[-1])
-    analysed = cycle_work(arrived, places, sort, unsort, cycle_offset, where, cycle_weight)
+            deliver(group, after(outgoing[-1]))
+    units = local_orders // 32
+    early = 32 * ((5 * units) // 8)
+    sizes = (early, local_orders - early)
+    analysed = cycle_work(
+        arrived, sizes, places, sort, unsort, cycle_offset, where, cycle_weight
+    )
     own = [
         lax.all_to_all(piece, "ma", split_axis=0, concat_axis=0, tiled=True) for piece in analysed
     ]
-    far, gradient = [], []
-    for group in range(groups):
-        far.append(lax.ppermute(own[group], "row", far_pairs))
-        if group + 1 < groups:
-            far[group], own[group + 1] = lax.optimization_barrier((far[group], own[group + 1]))
-    for group in range(groups):
+    far = lax.ppermute(own[0], "row", far_pairs)
+    far, second = lax.optimization_barrier((far, own[1]))
+    gradient, first = [], 0
+    for own_part, far_part in ((own[0], far), (second, None)):
+        if far_part is None:
+            far_part = lax.ppermute(own_part, "row", far_pairs)
         if gradient:
-            far[group], gradient[-1] = lax.optimization_barrier((far[group], gradient[-1]))
-        core = lax.ppermute(own[group], "row", core_pairs)
-        corner = lax.ppermute(far[group], "row", core_pairs)
+            far_part, gradient[-1] = lax.optimization_barrier((far_part, gradient[-1]))
+        core = lax.ppermute(own_part, "row", core_pairs)
+        corner = lax.ppermute(far_part, "row", core_pairs)
         gradient.append(
             adjoint(
-                group,
-                groups,
+                first,
                 orders,
                 where,
                 adjoint_weight,
-                (own[group], core, far[group], corner),
+                (own_part, core, far_part, corner),
                 legendre,
                 gradient[-1:],
             )
         )
+        first += own_part.shape[1]
     return gradient[-1]
 
 

time: 166 us -> 170 us (1.024)
  local copies, waits for them, and re-layouts: 12.1 us -> 20 us
  Pallas kernels: 68.7 us -> 63.1 us
  blocking collectives: 36 us -> 39.2 us
    unnamed x52 -> x58, local copies, waits for them, and re-layouts: 11.7 us -> 19.5 us
    all_to_all x1, blocking collectives: 17.7 us -> 20.9 us  [body(): lax.all_to_all(piece, 'ma', split_axis=0, concat_axis=0, tiled=True)]
    pallas_call x7, Pallas kernels: 34.2 us -> 31.1 us  [the longest x1 14.4 us: cycle_work(): pl.pallas_call(functools.partial(cycle_kernel, groups, sizes), grid_spec=...]
    pallas_call x4, Pallas kernels: 29 us -> 26.2 us  [synth(): pl.pallas_call(functools.partial(synth_kernel, chunk * count), grid_spec=...]
    all_to_all x1, waiting for transfers between devices: 12.7 us -> 10 us  [body(): lax.all_to_all(piece, 'ma', split_axis=0, concat_axis=0, tiled=True)]
    ppermute x4, waiting for transfers between devices: 0.11 us -> 2.05 us  [launch(): others.append(lax.ppermute(send, 'row', core_pairs))]
  transfers between devices with their start and end apart: 16 -> 16, of which waited for: 7 -> 8; matrix products, arithmetic and copies ran while one was open for 1% -> 1% of each run, Pallas kernels for 22% -> 20%
where the time goes in v5:
time: 170 us; the launch traced here: 168 us
  Pallas kernels  63.1 us (37%)
  blocking collectives  39.2 us (23%)
  waiting for transfers between devices  27 us (16%)
  local copies, waits for them, and re-layouts  20 us (12%)
  starting transfers between devices  17.5 us (10%)
    pallas_call x4, Pallas kernels, synth(): pl.pallas_call(functools.partial(synth_kernel, chunk * count), grid_spec=...  26.2 us
    all_to_all x1, blocking collectives, body(): lax.all_to_all(piece, 'ma', split_axis=0, concat_axis=0, tiled=True)  20.9 us
    unnamed x58, local copies, waits for them, and re-layouts  19.5 us
    all_to_all x1, blocking collectives, deliver(): lax.all_to_all(summed, 'ma', split_axis=0, concat_axis=0, tiled=True)  18.3 us
    pallas_call x1, Pallas kernels, cycle_work(): pl.pallas_call(functools.partial(cycle_kernel, groups, sizes), grid_spec=...  14.4 us
    pallas_call x2, Pallas kernels, adjoint(): pl.pallas_call(functools.partial(adjoint_kernel, first), grid_spec=pltpu....  11.6 us
    all_to_all x1, waiting for transfers between devices, body(): lax.all_to_all(piece, 'ma', split_axis=0, concat_axis=0, tiled=True)  10 us
    all_to_all x1, waiting for transfers between devices, deliver(): lax.all_to_all(summed, 'ma', split_axis=0, concat_axis=0, tiled=True)  6.3 us
  transfers between devices with their start and end apart: 16, of which 8 were waited for; matrix products, arithmetic and copies ran while one was open for 1% of the time, Pallas kernels for 20%

profile of v5, /device:TPU:0, one launch (start us, length us, event | category | flops | bytes accessed | tf_op | source)
XLA Modules:
  0.0 168.2 jit_solution(16745586242460065256)
XLA Ops:
  0.1 3.1 %filter_weights.1 = (bf16[512,256]{1,0:T(8,128)(2,1)}, bf16[256,512]{1,0:T(8,128)(2,1)}) custom-call(s32[64]{0:T(128)} %node_ref.1, f32[64]{0:T(128)} %radial_ref.1, f32[64,512]{1,0:T(8,128)} %alpha_ref.1, f32[64,512]{1,0:T(8,128)} %beta_ref.1), custom_call_target="tpu_custom_call" | custom-call | tf_op jit(solution)/shard_map/filter_weights/pallas_call | solution.py:119
  6.0 6.9 %synth.4 = (f32[2,8,64,256]{3,2,1,0:T(8,128)S(1)}, f32[2,8,64,256]{3,2,1,0:T(8,128)}) custom-call(s32[2048]{0:T(1024)S(1)} %copy-done.8, s32[2]{0:T(128)S(1)} %pad_add_fusion.where_ref.token_ref, f32[2,256,512]{2,1,0:T(8,128)S(1)} %copy-done.1, bf16[512,256]{1,0:T(8,128)(2,1)S(1)} %copy-done.3, bf16[256,32,512]{2,1,0:T(8,128)(2,1)} %legendre_ref.11), custom_call_target="tpu_custom_call" | custom-call | flops 2147483648 | bytes 4194304 | tf_op jit(solution)/shard_map/synth/pallas_call | solution.py:190
  14.3 6.9 %synth.5 = (f32[2,8,64,256]{3,2,1,0:T(8,128)S(1)}, f32[2,8,64,256]{3,2,1,0:T(8,128)}) custom-call(s32[2048]{0:T(1024)S(1)} %copy-done.8, s32[2]{0:T(128)S(1)} %pad_add_fusion.where_ref.token_ref, f32[2,256,512]{2,1,0:T(8,128)S(1)} %copy-done.1, bf16[512,256]{1,0:T(8,128)(2,1)S(1)} %copy-done.3, bf16[256,32,512]{2,1,0:T(8,128)(2,1)} %legendre_ref.11), custom_call_target="tpu_custom_call" | custom-call | flops 2147483648 | bytes 4194304 | tf_op jit(solution)/shard_map/synth/pallas_call | solution.py:190
  26.3 3.0 %collective-permute-start.3 = (bf16[8,64,256]{2,1,0:T(8,128)(2,1)S(1)}, bf16[8,64,256]{2,1,0:T(8,128)(2,1)S(1)}, u32[]{:S(2)}, u32[]{:S(2)}) collective-permute-start(bf16[8,64,256]{2,1,0:T(8,128)(2,1)S(1)} %core_sum.4), channel_id=1, source_target_pairs={{0,16},{8,24},{16,0},{24,8},{1,17},{9,25},{17,1},{25,9},{2,18},{10... | collective-permute-start | bytes 786440 | tf_op jit(solution)/shard_map/ppermute | solution.py:622
  29.4 6.2 %synth.6 = (f32[2,8,64,256]{3,2,1,0:T(8,128)S(1)}, f32[2,8,64,256]{3,2,1,0:T(8,128)S(1)}) custom-call(s32[2048]{0:T(1024)S(1)} %copy-done.9, s32[2]{0:T(128)S(1)} %pad_add_fusion.where_ref.token_ref, f32[2,256,512]{2,1,0:T(8,128)S(1)} %copy-done.2, bf16[512,256]{1,0:T(8,128)(2,1)S(1)} %copy-done.4, bf16[256,32,512]{2,1,0:T(8,128)(2,1)} %legendre_ref.11), custom_call_target="tpu_custom_call" | custom-call | flops 2147483648 | bytes 4194304 | tf_op jit(solution)/shard_map/synth/pallas_call | solution.py:190
  35.7 1.4 core_sum.5
  38.3 1.3 core_sum.6
  40.5 6.2 %synth.7 = (f32[2,8,64,256]{3,2,1,0:T(8,128)S(1)}, f32[2,8,64,256]{3,2,1,0:T(8,128)S(1)}) custom-call(s32[2048]{0:T(1024)S(1)} %copy-done.9, s32[2]{0:T(128)S(1)} %pad_add_fusion.where_ref.token_ref, f32[2,256,512]{2,1,0:T(8,128)S(1)} %copy-done.2, bf16[512,256]{1,0:T(8,128)(2,1)S(1)} %copy-done.4, bf16[256,32,512]{2,1,0:T(8,128)(2,1)} %legendre_ref.11), custom_call_target="tpu_custom_call" | custom-call | flops 2147483648 | bytes 4194304 | tf_op jit(solution)/shard_map/synth/pallas_call | solution.py:190
  46.8 1.6 full_sum.2
  51.9 6.0 %all-to-all-start = ((bf16[8,128,256]{2,1,0:T(8,128)(2,1)}), bf16[8,128,256]{2,1,0:T(8,128)(2,1)}, u32[]{:S(2)}, u32[]{:S(2)}) async-start(bf16[8,128,256]{2,1,0:T(8,128)(2,1)} %copy-done.6), calls=%async_computation | async-start | bytes 1048576 | tf_op jit(solution)/shard_map/all_to_all | solution.py:627
  57.9 1.5 collective-permute-done.7.refs_5_
  66.2 6.3 %all-to-all-done.refs_0_ = bf16[8,128,256]{2,1,0:T(8,128)(2,1)} async-done(((bf16[8,128,256]{2,1,0:T(8,128)(2,1)}), bf16[8,128,256]{2,1,0:T(8,128)(2,1)}, u32[]{:S(2)}, u32[]{:S(2)}) %all-to-all-start) | async-done | bytes 524320 | tf_op jit(solution)/shard_map/all_to_all | solution.py:627
  72.5 18.3 %all_to_all.20.refs_1_ = bf16[8,128,256]{2,1,0:T(8,128)(2,1)S(1)} all-to-all(bf16[8,128,256]{2,1,0:T(8,128)(2,1)} %copy-done.7), channel_id=1, replica_groups=mesh['row'=4,'ma'=8] {'ma'}, dimensions={0} | all-to-all | bytes 1048576 | tf_op jit(solution)/shard_map/all_to_all | solution.py:627
  90.8 2.2 %copy-done.25 = bf16[2,64,128,128]{3,2,1,0:T(8,128)(2,1)S(1)} copy-done((bf16[2,64,128,128]{3,2,1,0:T(8,128)(2,1)S(1)}, bf16[2,64,128,128]{3,2,1,0:T(8,128)(2,1)}, u32[]{:S(2)}) %copy-start.25) | copy-done | bytes 4194328
  93.0 2.2 %copy-done.26 = bf16[2,64,128,128]{3,2,1,0:T(8,128)(2,1)S(1)} copy-done((bf16[2,64,128,128]{3,2,1,0:T(8,128)(2,1)S(1)}, bf16[2,64,128,128]{3,2,1,0:T(8,128)(2,1)}, u32[]{:S(2)}) %copy-start.26) | copy-done | bytes 4194328
  95.2 14.4 %cycle_work.1 = (bf16[8,160,256]{2,1,0:T(8,128)(2,1)S(1)}, bf16[8,96,256]{2,1,0:T(8,128)(2,1)}) custom-call(s32[4]{0:T(128)S(1)} %copy-done.23, s32[2]{0:T(128)S(1)} %pad_add_fusion.where_ref.token_ref, f32[4]{0:T(128)S(1)} %copy-done.24, bf16[8,128,256]{2,1,0:T(8,128)(2,1)} %all-to-all-done.refs_0_, bf16[8,128,256]{2,1,0:T(8,128)(2,1)S(1)} %all_to_all.20.refs_1_, ...), custom_call_target="tpu_custom_call" | custom-call | flops 4294967296 | bytes 8388608 | tf_op jit(solution)/shard_map/cycle_work/pallas_call | solution.py:438
  109.6 20.9 %all_to_all.21.own_ref = bf16[8,160,256]{2,1,0:T(8,128)(2,1)S(1)} all-to-all(bf16[8,160,256]{2,1,0:T(8,128)(2,1)S(1)} %get-tuple-element.54), channel_id=1, replica_groups=mesh['row'=4,'ma'=8] {'ma'}, dimensions={0} | all-to-all | bytes 1310720 | tf_op jit(solution)/shard_map/all_to_all | solution.py:656
  130.5 3.5 %all-to-all-start.3 = ((bf16[8,96,256]{2,1,0:T(8,128)(2,1)}), bf16[8,96,256]{2,1,0:T(8,128)(2,1)S(1)}, u32[]{:S(2)}, u32[]{:S(2)}) async-start(bf16[8,96,256]{2,1,0:T(8,128)(2,1)} %get-tuple-element.55), calls=%async_computation.3 | async-start | bytes 786432 | tf_op jit(solution)/shard_map/all_to_all | solution.py:656
  134.9 10.0 %all-to-all-done.3.own_ref = bf16[8,96,256]{2,1,0:T(8,128)(2,1)S(1)} async-done(((bf16[8,96,256]{2,1,0:T(8,128)(2,1)}), bf16[8,96,256]{2,1,0:T(8,128)(2,1)S(1)}, u32[]{:S(2)}, u32[]{:S(2)}) %all-to-all-start.3) | async-done | bytes 393248 | tf_op jit(solution)/shard_map/all_to_all | solution.py:656
  145.0 4.5 %collective-permute-done.8.far_ref = bf16[8,160,256]{2,1,0:T(8,128)(2,1)S(1)} collective-permute-done((bf16[8,160,256]{2,1,0:T(8,128)(2,1)S(1)}, bf16[8,160,256]{2,1,0:T(8,128)(2,1)S(1)}, u32[]{:S(2)}, u32[]{:S(2)}) %collective-permute-start.8) | collective-permute-done | bytes 655392 | tf_op jit(solution)/shard_map/ppermute | solution.py:658
  151.6 3.4 %copy-done = bf16[256,32,512]{2,1,0:T(8,128)(2,1)S(1)} copy-done((bf16[256,32,512]{2,1,0:T(8,128)(2,1)S(1)}, bf16[256,32,512]{2,1,0:T(8,128)(2,1)}, u32[]{:S(2)}) %copy-start) | copy-done | bytes 8388632
  155.0 6.9 %adjoint.2.refs_0_ = f32[2,256,512]{2,1,0:T(8,128)} custom-call(s32[2048]{0:T(1024)S(1)} %copy-done.9, s32[2]{0:T(128)S(1)} %pad_add_fusion.where_ref.token_ref, bf16[8,160,256]{2,1,0:T(8,128)(2,1)S(1)} %all_to_all.21.own_ref, bf16[8,160,256]{2,1,0:T(8,128)(2,1)S(1)} %collective-permute-done.11.core_ref, ...), custom_call_target="tpu_custom_call" | custom-call | flops 2684354560 | bytes 7864320 | tf_op jit(solution)/shard_map/adjoint/pallas_call | solution.py:538
  162.0 1.6 collective-permute-done.13.corner_ref
  163.6 4.6 %adjoint.3 = f32[2,256,512]{2,1,0:T(8,128)} custom-call(s32[2048]{0:T(1024)S(1)} %copy-done.9, s32[2]{0:T(128)S(1)} %pad_add_fusion.where_ref.token_ref, bf16[8,96,256]{2,1,0:T(8,128)(2,1)S(1)} %all-to-all-done.3.own_ref, bf16[8,96,256]{2,1,0:T(8,128)(2,1)S(1)} %collective-permute-done.9.core_ref, ...), custom_call_target="tpu_custom_call", output_to_operand_aliasing={{}: (8, {})} | custom-call | flops 1610612736 | bytes 4718592 | tf_op jit(solution)/shard_map/adjoint/pallas_call | solution.py:538
  (90 shorter events, 25.1 us)
Async XLA Ops:
  13.9 8.4 %copy-start.9 = (s32[2048]{0:T(1024)S(1)}, s32[2048]{0:T(1024)}, u32[]{:S(2)}) copy-start(s32[2048]{0:T(1024)} %order_ref.11) | copy-start | bytes 24580
  13.9 10.0 %collective-permute-start = (f32[2,8,64,256]{3,2,1,0:T(8,128)}, f32[2,8,64,256]{3,2,1,0:T(8,128)}, u32[]{:S(2)}, u32[]{:S(2)}) collective-permute-start(f32[2,8,64,256]{3,2,1,0:T(8,128)} %get-tuple-element.36), channel_id=1, source_target_pairs={{0,8},{8,0},{16,24},{24,16},{1,9},{9,1},{17,25},{25,17},{2,10},{10... | collective-permute-start | bytes 3145736 | tf_op jit(solution)/shard_map/ppermute | solution.py:618
  22.2 13.5 %collective-permute-start.2 = (f32[2,8,64,256]{3,2,1,0:T(8,128)}, f32[2,8,64,256]{3,2,1,0:T(8,128)}, u32[]{:S(2)}, u32[]{:S(2)}) collective-permute-start(f32[2,8,64,256]{3,2,1,0:T(8,128)} %get-tuple-element.42), channel_id=1, source_target_pairs={{0,8},{8,0},{16,24},{24,16},{1,9},{9,1},{17,25},{25,17},{2,10},{10... | collective-permute-start | bytes 3145736 | tf_op jit(solution)/shard_map/ppermute | solution.py:618
  26.3 9.4 %copy-start.14 = (f32[2,8,64,256]{3,2,1,0:T(8,128)S(1)}, f32[2,8,64,256]{3,2,1,0:T(8,128)}, u32[]{:S(2)}) copy-start(f32[2,8,64,256]{3,2,1,0:T(8,128)} %copy-done.13) | copy-start | bytes 3145732
  26.3 14.2 %collective-permute-start.3 = (bf16[8,64,256]{2,1,0:T(8,128)(2,1)S(1)}, bf16[8,64,256]{2,1,0:T(8,128)(2,1)S(1)}, u32[]{:S(2)}, u32[]{:S(2)}) collective-permute-start(bf16[8,64,256]{2,1,0:T(8,128)(2,1)S(1)} %core_sum.4), channel_id=1, source_target_pairs={{0,16},{8,24},{16,0},{24,8},{1,17},{9,25},{17,1},{25,9},{2,18},{10... | collective-permute-start | bytes 786440 | tf_op jit(solution)/shard_map/ppermute | solution.py:622
  35.6 2.7 %collective-permute-start.1 = (f32[2,8,64,256]{3,2,1,0:T(8,128)S(1)}, f32[2,8,64,256]{3,2,1,0:T(8,128)S(1)}, u32[]{:S(2)}, u32[]{:S(2)}) collective-permute-start(f32[2,8,64,256]{3,2,1,0:T(8,128)S(1)} %get-tuple-element.41), channel_id=1, source_target_pairs={{0,8},{8,0},{16,24},{24,16},{1,9},{9,1},{17,25},{25,17},{2,10},{10... | collective-permute-start | bytes 3145736 | tf_op jit(solution)/shard_map/ppermute | solution.py:618
  37.1 9.7 %collective-permute-start.4 = (bf16[8,64,256]{2,1,0:T(8,128)(2,1)S(1)}, bf16[8,64,256]{2,1,0:T(8,128)(2,1)S(1)}, u32[]{:S(2)}, u32[]{:S(2)}) collective-permute-start(bf16[8,64,256]{2,1,0:T(8,128)(2,1)S(1)} %core_sum.5), channel_id=1, source_target_pairs={{0,16},{8,24},{16,0},{24,8},{1,17},{9,25},{17,1},{25,9},{2,18},{10... | collective-permute-start | bytes 786440 | tf_op jit(solution)/shard_map/ppermute | solution.py:622
  39.6 7.2 %copy-start.12 = (f32[2,8,64,256]{3,2,1,0:T(8,128)S(1)}, f32[2,8,64,256]{3,2,1,0:T(8,128)}, u32[]{:S(2)}) copy-start(f32[2,8,64,256]{3,2,1,0:T(8,128)} %copy-done.10) | copy-start | bytes 3145732
  39.6 18.3 %collective-permute-start.6 = (bf16[8,64,256]{2,1,0:T(8,128)(2,1)}, bf16[8,64,256]{2,1,0:T(8,128)(2,1)S(1)}, u32[]{:S(2)}, u32[]{:S(2)}) collective-permute-start(bf16[8,64,256]{2,1,0:T(8,128)(2,1)} %core_sum.6), channel_id=1, source_target_pairs={{0,16},{8,24},{16,0},{24,8},{1,17},{9,25},{17,1},{25,9},{2,18},{10... | collective-permute-start | bytes 786440 | tf_op jit(solution)/shard_map/ppermute | solution.py:622
  46.7 2.7 %collective-permute-start.5 = (f32[2,8,64,256]{3,2,1,0:T(8,128)S(1)}, f32[2,8,64,256]{3,2,1,0:T(8,128)S(1)}, u32[]{:S(2)}, u32[]{:S(2)}) collective-permute-start(f32[2,8,64,256]{3,2,1,0:T(8,128)S(1)} %get-tuple-element.48), channel_id=1, source_target_pairs={{0,8},{8,0},{16,24},{24,16},{1,9},{9,1},{17,25},{25,17},{2,10},{10... | collective-permute-start | bytes 3145736 | tf_op jit(solution)/shard_map/ppermute | solution.py:618
  50.7 8.7 %collective-permute-start.7 = (bf16[8,64,256]{2,1,0:T(8,128)(2,1)}, bf16[8,64,256]{2,1,0:T(8,128)(2,1)}, u32[]{:S(2)}, u32[]{:S(2)}) collective-permute-start(bf16[8,64,256]{2,1,0:T(8,128)(2,1)} %core_sum.7), channel_id=1, source_target_pairs={{0,16},{8,24},{16,0},{24,8},{1,17},{9,25},{17,1},{25,9},{2,18},{10... | collective-permute-start | bytes 786440 | tf_op jit(solution)/shard_map/ppermute | solution.py:622
  51.9 38.9 %copy-start.23 = (s32[4]{0:T(128)S(1)}, s32[4]{0:T(128)}, u32[]{:S(2)}) copy-start(s32[4]{0:T(128)} %offset_ref.1) | copy-start | bytes 52
  51.9 38.9 %copy-start.24 = (f32[4]{0:T(128)S(1)}, f32[4]{0:T(128)}, u32[]{:S(2)}) copy-start(f32[4]{0:T(128)} %weight_ref.1) | copy-start | bytes 52
  51.9 38.9 %copy-start.27 = (bf16[128,256]{1,0:T(8,128)(2,1)S(1)}, bf16[128,256]{1,0:T(8,128)(2,1)}, u32[]{:S(2)}) copy-start(bf16[128,256]{1,0:T(8,128)(2,1)} %constant.65.clone.refs_7_) | copy-start | bytes 196612
  51.9 38.9 %copy-start.28 = (bf16[128,128]{1,0:T(8,128)(2,1)S(1)}, bf16[128,128]{1,0:T(8,128)(2,1)}, u32[]{:S(2)}) copy-start(bf16[128,128]{1,0:T(8,128)(2,1)} %constant.64.clone.refs_6_) | copy-start | bytes 98308
  51.9 20.6 %all-to-all-start = ((bf16[8,128,256]{2,1,0:T(8,128)(2,1)}), bf16[8,128,256]{2,1,0:T(8,128)(2,1)}, u32[]{:S(2)}, u32[]{:S(2)}) async-start(bf16[8,128,256]{2,1,0:T(8,128)(2,1)} %copy-done.6), calls=%async_computation | async-start | bytes 1048576 | tf_op jit(solution)/shard_map/all_to_all | solution.py:627
  109.6 42.0 %copy-start.5 = (bf16[256,512]{1,0:T(8,128)(2,1)S(1)}, bf16[256,512]{1,0:T(8,128)(2,1)}, u32[]{:S(2)}) copy-start(bf16[256,512]{1,0:T(8,128)(2,1)} %get-tuple-element.58.weight_ref) | copy-start | bytes 786436
  130.5 14.4 %all-to-all-start.3 = ((bf16[8,96,256]{2,1,0:T(8,128)(2,1)}), bf16[8,96,256]{2,1,0:T(8,128)(2,1)S(1)}, u32[]{:S(2)}, u32[]{:S(2)}) async-start(bf16[8,96,256]{2,1,0:T(8,128)(2,1)} %get-tuple-element.55), calls=%async_computation.3 | async-start | bytes 786432 | tf_op jit(solution)/shard_map/all_to_all | solution.py:656
  134.0 15.5 %collective-permute-start.8 = (bf16[8,160,256]{2,1,0:T(8,128)(2,1)S(1)}, bf16[8,160,256]{2,1,0:T(8,128)(2,1)S(1)}, u32[]{:S(2)}, u32[]{:S(2)}) collective-permute-start(bf16[8,160,256]{2,1,0:T(8,128)(2,1)S(1)} %all_to_all.21.own_ref), channel_id=1, source_target_pairs={{0,16},{8,24},{16,0},{24,8},{1,17},{9,25},{17,1},{25,9},{2,18},{10... | collective-permute-start | bytes 1966088 | tf_op jit(solution)/shard_map/ppermute | solution.py:658
  134.9 15.6 %collective-permute-start.11 = (bf16[8,160,256]{2,1,0:T(8,128)(2,1)S(1)}, bf16[8,160,256]{2,1,0:T(8,128)(2,1)S(1)}, u32[]{:S(2)}, u32[]{:S(2)}) collective-permute-start(bf16[8,160,256]{2,1,0:T(8,128)(2,1)S(1)} %all_to_all.21.own_ref), channel_id=1, source_target_pairs={{0,8},{8,0},{16,24},{24,16},{1,9},{9,1},{17,25},{25,17},{2,10},{10... | collective-permute-start | bytes 1966088 | tf_op jit(solution)/shard_map/ppermute | solution.py:666
  149.5 2.1 %collective-permute-start.12 = (bf16[8,160,256]{2,1,0:T(8,128)(2,1)S(1)}, bf16[8,160,256]{2,1,0:T(8,128)(2,1)S(1)}, u32[]{:S(2)}, u32[]{:S(2)}) collective-permute-start(bf16[8,160,256]{2,1,0:T(8,128)(2,1)S(1)} %collective-permute-done.8.far_ref), channel_id=1, source_target_pairs={{0,8},{8,0},{16,24},{24,16},{1,9},{9,1},{17,25},{25,17},{2,10},{10... | collective-permute-start | bytes 1966088 | tf_op jit(solution)/shard_map/ppermute | solution.py:667
  149.5 12.4 %collective-permute-start.10 = (bf16[8,96,256]{2,1,0:T(8,128)(2,1)S(1)}, bf16[8,96,256]{2,1,0:T(8,128)(2,1)S(1)}, u32[]{:S(2)}, u32[]{:S(2)}) collective-permute-start(bf16[8,96,256]{2,1,0:T(8,128)(2,1)S(1)} %all-to-all-done.3.own_ref), channel_id=1, source_target_pairs={{0,16},{8,24},{16,0},{24,8},{1,17},{9,25},{17,1},{25,9},{2,18},{10... | collective-permute-start | bytes 1179656 | tf_op jit(solution)/shard_map/ppermute | solution.py:663
  150.3 11.7 %collective-permute-start.9 = (bf16[8,96,256]{2,1,0:T(8,128)(2,1)S(1)}, bf16[8,96,256]{2,1,0:T(8,128)(2,1)S(1)}, u32[]{:S(2)}, u32[]{:S(2)}) collective-permute-start(bf16[8,96,256]{2,1,0:T(8,128)(2,1)S(1)} %all-to-all-done.3.own_ref), channel_id=1, source_target_pairs={{0,8},{8,0},{16,24},{24,16},{1,9},{9,1},{17,25},{25,17},{2,10},{10... | collective-permute-start | bytes 1179656 | tf_op jit(solution)/shard_map/ppermute | solution.py:666
  161.9 1.7 %collective-permute-start.13 = (bf16[8,96,256]{2,1,0:T(8,128)(2,1)S(1)}, bf16[8,96,256]{2,1,0:T(8,128)(2,1)S(1)}, u32[]{:S(2)}, u32[]{:S(2)}) collective-permute-start(bf16[8,96,256]{2,1,0:T(8,128)(2,1)S(1)} %collective-permute-done.10.far_ref), channel_id=1, source_target_pairs={{0,8},{8,0},{16,24},{24,16},{1,9},{9,1},{17,25},{25,17},{2,10},{10... | collective-permute-start | bytes 1179656 | tf_op jit(solution)/shard_map/ppermute | solution.py:667
  (21 other events, 38.4 us)

commit v6 on v5

--- a/solution.py
+++ b/solution.py
@@ -12,8 +12,6 @@
 NPIX = 4096
 SIDE = 64
 PADDED = 136
-CHUNKS = 4
-GROUPS = 2
 SYNTH_BLOCK = 16
 BLOCK = 32
 MIB = 1 << 20
@@ -178,17 +176,16 @@
                     ] = piece
 
 
-def synth(chunk, chunks, orders, where, coeffs, weight, legendre):
-    orders_here, cycles, degrees = legendre.shape
-    count = orders_here // chunks
+def synth(first, count, orders, where, coeffs, weight, legendre):
+    cycles, degrees = legendre.shape[1:]
     steps = count // SYNTH_BLOCK
-    start = chunk * steps
+    start = first // SYNTH_BLOCK
     owners = cycles // 4
     lanes = weight.shape[1] // 2
     out = jax.ShapeDtypeStruct((2, owners, count, 2 * lanes), F32)
     out_spec = pl.BlockSpec((2, owners, SYNTH_BLOCK, 2 * lanes), lambda t, *_: (0, 0, t, 0))
     return pl.pallas_call(
-        functools.partial(synth_kernel, chunk * count),
+        functools.partial(synth_kernel, first),
         grid_spec=pltpu.PrefetchScalarGridSpec(
             num_scalar_prefetch=2,
             grid=(steps,),
@@ -206,7 +203,7 @@
             ],
         ),
         out_shape=[out, out],
-        compiler_params=pltpu.CompilerParams(vmem_limit_bytes=50 * MIB),
+        compiler_params=pltpu.CompilerParams(vmem_limit_bytes=48 * MIB),
         cost_estimate=pl.CostEstimate(
             flops=2 * count * cycles * degrees * lanes * 2 * 4,
             bytes_accessed=count * (cycles * degrees * 2 + 2 * cycles * lanes * 4),
@@ -268,14 +265,43 @@
 
 
 def cycle_kernel(groups, sizes, offset_ref, where_ref, weight_ref, *refs):
-    pieces = refs[:groups]
-    place_ref, sort_ref, unsort_ref, spread_ref, pixel_ref, back_ref, gather_ref = refs[
+    arrived = refs[:groups]
+    places_ref, sorts_ref, unsorts_ref, spread_ref, pixel_ref, back_ref, gather_ref = refs[
         groups : groups + 7
     ]
-    outs = refs[groups + 7 : groups + 7 + len(sizes)]
-    spread_scr, gather_scr, sorted_scr, middle_scr, product_scr, back_scr, sems = refs[-7:]
+    results = refs[groups + 7 : groups + 7 + len(sizes)]
+    scratch = refs[groups + 7 + len(sizes) :]
+    pieces = scratch[:groups]
+    outs = scratch[groups : groups + len(sizes)]
+    (
+        place_ref,
+        sort_ref,
+        unsort_ref,
+        spread_scr,
+        gather_scr,
+        sorted_scr,
+        middle_scr,
+        product_scr,
+        back_scr,
+        sems,
+        input_sems,
+        out_sems,
+    ) = scratch[groups + len(sizes) :]
     device_count, blocks = place_ref.shape[:2]
     lanes = pieces[0].shape[2] // 2
+    inputs = [
+        pltpu.make_async_copy(source, target, input_sems.at[index])
+        for index, (source, target) in enumerate(
+            [
+                *zip(arrived, pieces),
+                (sorts_ref, sort_ref),
+                (places_ref, place_ref),
+                (unsorts_ref, unsort_ref),
+            ]
+        )
+    ]
+    for copy in inputs[:-1]:
+        copy.start()
     turned = offset_ref[where_ref[0]]
     scale = weight_ref[where_ref[0]]
     lane = lax.broadcasted_iota(jnp.int32, (SIDE, lanes), 1)
@@ -290,6 +316,9 @@
     for block in range(blocks):
         spread_copy(block).start()
     gather_copy.start()
+    inputs[-1].start()
+    for copy in inputs[: groups + 1]:
+        copy.wait()
 
     def sort_step(peer, carry):
         slots = jnp.concatenate([piece[peer] for piece in pieces], axis=0)
@@ -299,6 +328,7 @@
         return carry
 
     lax.fori_loop(0, device_count, sort_step, 0, unroll=2)
+    inputs[groups + 1].wait()
 
     def spread_step(block, carry):
         spread_copy(block).wait()
@@ -415,18 +445,28 @@
         return carry
 
     lax.fori_loop(0, blocks, gather_step, 0)
+    inputs[-1].wait()
+
+    def result_copy(peer, index):
+        return pltpu.make_async_copy(
+            outs[index].at[peer], results[index].at[peer], out_sems.at[index, peer]
+        )
 
     def unsort_step(peer, carry):
         slots = jnp.dot(
             unsort_ref[peer], sorted_scr[peer], preferred_element_type=F32
         ).astype(BF16)
         start = 0
-        for out, size in zip(outs, sizes):
-            out[peer] = slots[start : start + size]
+        for index, size in enumerate(sizes):
+            outs[index][peer] = slots[start : start + size]
             start += size
+            result_copy(peer, index).start()
         return carry
 
     lax.fori_loop(0, device_count, unsort_step, 0, unroll=2)
+    for index in range(len(sizes)):
+        for peer in range(device_count):
+            result_copy(peer, index).wait()
 
 
 def cycle_work(pieces, sizes, places, sort, unsort, offset, where, cycle_weight):
@@ -441,11 +481,13 @@
             num_scalar_prefetch=2,
             grid=(1,),
             in_specs=[pl.BlockSpec(memory_space=pltpu.SMEM)]
-            + [whole(piece.shape) for piece in pieces]
-            + [whole(table.shape) for table in tables]
-            + [hbm(), whole(pixel.shape), whole(back.shape), hbm()],
-            out_specs=[whole(shape) for shape in out_shapes],
-            scratch_shapes=[
+            + [anywhere()] * (groups + 4)
+            + [whole(pixel.shape), whole(back.shape), anywhere()],
+            out_specs=[anywhere()] * len(sizes),
+            scratch_shapes=[pltpu.VMEM(piece.shape, BF16) for piece in pieces]
+            + [pltpu.VMEM(shape, BF16) for shape in out_shapes]
+            + [pltpu.VMEM(table.shape, BF16) for table in tables]
+            + [
                 pltpu.VMEM(spread.shape[1:], BF16),
                 pltpu.VMEM(gather.shape[1:], BF16),
                 pltpu.VMEM((device_count, groups * count, lanes), BF16),
@@ -453,10 +495,12 @@
                 pltpu.VMEM((SIDE, SIDE, lanes // 2), F32),
                 pltpu.VMEM((SIDE * PADDED, lanes // 2), F32),
                 pltpu.SemaphoreType.DMA((places.shape[1] + 1,)),
+                pltpu.SemaphoreType.DMA((groups + 3,)),
+                pltpu.SemaphoreType.DMA((len(sizes), device_count)),
             ],
         ),
         out_shape=[jax.ShapeDtypeStruct(shape, BF16) for shape in out_shapes],
-        compiler_params=pltpu.CompilerParams(vmem_limit_bytes=40 * MIB),
+        compiler_params=pltpu.CompilerParams(vmem_limit_bytes=48 * MIB),
         cost_estimate=pl.CostEstimate(
             flops=4 * SIDE * 128 * 256 * 256 * 2, bytes_accessed=8 * MIB, transcendentals=0
         ),
@@ -556,7 +600,7 @@
         ),
         out_shape=out,
         input_output_aliases={8: 0} if earlier else {},
-        compiler_params=pltpu.CompilerParams(vmem_limit_bytes=40 * MIB),
+        compiler_params=pltpu.CompilerParams(vmem_limit_bytes=48 * MIB),
         cost_estimate=pl.CostEstimate(
             flops=2 * count * cycles * degrees * lanes * 2 * 2,
             bytes_accessed=count * (cycles * degrees * 2 + 2 * cycles * lanes * 2),
@@ -604,16 +648,19 @@
     )
     core_pairs = [(i, i ^ 1) for i in range(row_count)]
     far_pairs = [(i, i ^ 2) for i in range(row_count)]
-    chunks = min(CHUNKS, local_orders // 32)
-    groups = min(GROUPS, chunks)
-    size = chunks // groups
+    units = local_orders // 32
+    counts = (units // 4, units // 4, units // 2) if units >= 4 else (units // 2, units // 2)
+    counts = [32 * count for count in counts]
     kept, others, outgoing, incoming, arrived = [], [], [], [], []
 
     def after(*values):
         return lax.optimization_barrier((where, *values))[0]
 
     def launch(chunk, token):
-        keep, send = synth(chunk, chunks, orders, token, coeffs, synth_weight, legendre)
+        first = sum(counts[:chunk])
+        keep, send = synth(
+            first, counts[chunk], orders, token, coeffs, synth_weight, legendre
+        )
         kept.append(keep)
         others.append(lax.ppermute(send, "row", core_pairs))
 
@@ -621,32 +668,25 @@
         outgoing.append(core_sum(kept[chunk], others[chunk], token))
         incoming.append(lax.ppermute(outgoing[chunk], "row", far_pairs))
 
-    def deliver(group, token):
-        own = slice(group * size, (group + 1) * size)
+    def deliver(own, token):
         summed = full_sum(list(zip(kept[own], others[own], incoming[own])), token)
         arrived.append(lax.all_to_all(summed, "ma", split_axis=0, concat_axis=0, tiled=True))
         return summed
 
-    if chunks == 4:
-        launch(0, where)
-        launch(1, where)
-        pass_on(0, after(kept[1]))
-        places, sort, unsort, token = lax.optimization_barrier((places, sort, unsort, where))
-        launch(2, lax.optimization_barrier((token, outgoing[0]))[0])
-        pass_on(1, after(kept[2]))
-        pass_on(2, after(outgoing[1]))
-        launch(3, after(outgoing[2], incoming[0]))
-        summed = deliver(0, after(kept[3]))
-        pass_on(3, after(summed))
-        deliver(1, after(outgoing[3]))
+    launch(0, where)
+    launch(1, where)
+    pass_on(0, after(kept[1]))
+    pass_on(1, after(outgoing[0]))
+    if len(counts) == 3:
+        launch(2, after(outgoing[1]))
+        places, sort, unsort, token = lax.optimization_barrier(
+            (places, sort, unsort, after(kept[2]))
+        )
+        pass_on(2, after(deliver(slice(0, 2), token)))
+        deliver(slice(2, 3), after(outgoing[2]))
     else:
-        for chunk in range(chunks):
-            launch(chunk, where)
-        for chunk in range(chunks):
-            pass_on(chunk, after(kept[-1]))
-        for group in range(groups):
-            deliver(group, after(outgoing[-1]))
-    units = local_orders // 32
+        deliver(slice(0, 1), after(outgoing[1]))
+        deliver(slice(1, 2), after(outgoing[1]))
     early = 32 * ((5 * units) // 8)
     sizes = (early, local_orders - early)
     analysed = cycle_work(

time: 170 us -> 162 us (0.953)
  local copies, waits for them, and re-layouts: 20 us -> 9.05 us
  waiting for transfers between devices: 27 us -> 30.4 us
  Pallas kernels: 63.1 us -> 64.9 us
    unnamed x58 -> x42, local copies, waits for them, and re-layouts: 19.5 us -> 8.63 us
    ppermute x4 -> x3, waiting for transfers between devices: 1.52 us -> 6.75 us  [pass_on(): incoming.append(lax.ppermute(outgoing[chunk], 'row', far_pairs))]
    all_to_all x1, waiting for transfers between devices: 6.3 us -> 2.67 us  [deliver(): lax.all_to_all(summed, 'ma', split_axis=0, concat_axis=0, tiled=True)]
    pallas_call x2, Pallas kernels: 11.6 us -> 14.5 us  [adjoint(): pl.pallas_call(functools.partial(adjoint_kernel, first), grid_spec=pltpu....]
    pallas_call x1, Pallas kernels: 14.4 us -> 16.3 us  [cycle_work(): pl.pallas_call(functools.partial(cycle_kernel, groups, sizes), grid_spec=...]
    pallas_call x4 -> x3, Pallas kernels: 26.2 us -> 24.5 us  [synth(): pl.pallas_call(functools.partial(synth_kernel, first), grid_spec=pltpu.Pr...]
    pallas_call x4 -> x3, Pallas kernels: 5.15 us -> 3.82 us  [core_sum(): pl.pallas_call(core_sum_kernel, grid=(1,), in_specs=[half, half, pl.Block...]
    ppermute x4 -> x3, starting transfers between devices: 5.26 us -> 5.12 us  [pass_on(): incoming.append(lax.ppermute(outgoing[chunk], 'row', far_pairs))]
  transfers between devices with their start and end apart: 16 -> 14, of which waited for: 8 -> 8; matrix products, arithmetic and copies ran while one was open for 1% -> 1% of each run, Pallas kernels for 20% -> 19%
where the time goes in v6:
time: 162 us; the launch traced here: 161 us
  Pallas kernels  64.9 us (40%)
  blocking collectives  39.2 us (24%)
  waiting for transfers between devices  30.4 us (19%)
  starting transfers between devices  16 us (10%)
  local copies, waits for them, and re-layouts  9.05 us (6%)
    pallas_call x3, Pallas kernels, synth(): pl.pallas_call(functools.partial(synth_kernel, first), grid_spec=pltpu.Pr...  24.5 us
    all_to_all x1, blocking collectives, body(): lax.all_to_all(piece, 'ma', split_axis=0, concat_axis=0, tiled=True)  20.9 us
    all_to_all x1, blocking collectives, deliver(): lax.all_to_all(summed, 'ma', split_axis=0, concat_axis=0, tiled=True)  18.3 us
    pallas_call x1, Pallas kernels, cycle_work(): pl.pallas_call(functools.partial(cycle_kernel, groups, sizes), grid_spec=...  16.3 us
    pallas_call x2, Pallas kernels, adjoint(): pl.pallas_call(functools.partial(adjoint_kernel, first), grid_spec=pltpu....  14.5 us
    all_to_all x1, waiting for transfers between devices, body(): lax.all_to_all(piece, 'ma', split_axis=0, concat_axis=0, tiled=True)  10.5 us
    unnamed x42, local copies, waits for them, and re-layouts  8.63 us
    ppermute x3, waiting for transfers between devices, pass_on(): incoming.append(lax.ppermute(outgoing[chunk], 'row', far_pairs))  6.75 us
  transfers between devices with their start and end apart: 14, of which 8 were waited for; matrix products, arithmetic and copies ran while one was open for 1% of the time, Pallas kernels for 19%

profile of v6, /device:TPU:0, one launch (start us, length us, event | category | flops | bytes accessed | tf_op | source)
XLA Modules:
  0.0 161.0 jit_solution(2913683770641167571)
XLA Ops:
  0.1 3.0 %filter_weights.1 = (bf16[512,256]{1,0:T(8,128)(2,1)}, bf16[256,512]{1,0:T(8,128)(2,1)}) custom-call(s32[64]{0:T(128)} %node_ref.1, f32[64]{0:T(128)} %radial_ref.1, f32[64,512]{1,0:T(8,128)} %alpha_ref.1, f32[64,512]{1,0:T(8,128)} %beta_ref.1), custom_call_target="tpu_custom_call" | custom-call | tf_op jit(solution)/shard_map/filter_weights/pallas_call | solution.py:117
  6.0 6.9 %synth.4 = (f32[2,8,64,256]{3,2,1,0:T(8,128)S(1)}, f32[2,8,64,256]{3,2,1,0:T(8,128)}) custom-call(s32[2048]{0:T(1024)S(1)} %copy-done.7, s32[2]{0:T(128)S(1)} %pad_add_fusion.where_ref.token_ref, f32[2,256,512]{2,1,0:T(8,128)S(1)} %copy-done, bf16[512,256]{1,0:T(8,128)(2,1)S(1)} %copy-done.3, bf16[256,32,512]{2,1,0:T(8,128)(2,1)} %legendre_ref.9), custom_call_target="tpu_custom_call" | custom-call | flops 2147483648 | bytes 4194304 | tf_op jit(solution)/shard_map/synth/pallas_call | solution.py:187
  13.3 6.9 %synth.3 = (f32[2,8,64,256]{3,2,1,0:T(8,128)S(1)}, f32[2,8,64,256]{3,2,1,0:T(8,128)}) custom-call(s32[2048]{0:T(1024)S(1)} %copy-done.7, s32[2]{0:T(128)S(1)} %pad_add_fusion.where_ref.token_ref, f32[2,256,512]{2,1,0:T(8,128)S(1)} %copy-done, bf16[512,256]{1,0:T(8,128)(2,1)S(1)} %copy-done.3, bf16[256,32,512]{2,1,0:T(8,128)(2,1)} %legendre_ref.9), custom_call_target="tpu_custom_call" | custom-call | flops 2147483648 | bytes 4194304 | tf_op jit(solution)/shard_map/synth/pallas_call | solution.py:187
  23.8 3.0 %collective-permute-start.2 = (bf16[8,64,256]{2,1,0:T(8,128)(2,1)S(1)}, bf16[8,64,256]{2,1,0:T(8,128)(2,1)S(1)}, u32[]{:S(2)}, u32[]{:S(2)}) collective-permute-start(bf16[8,64,256]{2,1,0:T(8,128)(2,1)S(1)} %core_sum.3), channel_id=1, source_target_pairs={{0,16},{8,24},{16,0},{24,8},{1,17},{9,25},{17,1},{25,9},{2,18},{10... | collective-permute-start | bytes 786440 | tf_op jit(solution)/shard_map/ppermute | solution.py:669
  28.2 10.7 %synth.5 = (f32[2,8,128,256]{3,2,1,0:T(8,128)S(1)}, f32[2,8,128,256]{3,2,1,0:T(8,128)S(1)}) custom-call(s32[2048]{0:T(1024)S(1)} %copy-done.8, s32[2]{0:T(128)S(1)} %pad_add_fusion.where_ref.token_ref, f32[2,256,512]{2,1,0:T(8,128)S(1)} %copy-done.1, bf16[512,256]{1,0:T(8,128)(2,1)S(1)} %copy-done.4, bf16[256,32,512]{2,1,0:T(8,128)(2,1)} %legendre_ref.9), custom_call_target="tpu_custom_call" | custom-call | flops 4294967296 | bytes 8388608 | tf_op jit(solution)/shard_map/synth/pallas_call | solution.py:187
  39.3 1.6 full_sum.2
  41.8 1.7 %collective-permute-done.4.other_ref.refs_1_ = f32[2,8,128,256]{3,2,1,0:T(8,128)S(1)} collective-permute-done((f32[2,8,128,256]{3,2,1,0:T(8,128)S(1)}, f32[2,8,128,256]{3,2,1,0:T(8,128)S(1)}, u32[]{:S(2)}, u32[]{:S(2)}) %collective-permute-start.4) | collective-permute-done | bytes 2097184 | tf_op jit(solution)/shard_map/ppermute | solution.py:665
  43.5 1.5 core_sum.5
  45.0 1.9 %collective-permute-start.5 = (bf16[8,128,256]{2,1,0:T(8,128)(2,1)}, bf16[8,128,256]{2,1,0:T(8,128)(2,1)}, u32[]{:S(2)}, u32[]{:S(2)}) collective-permute-start(bf16[8,128,256]{2,1,0:T(8,128)(2,1)} %core_sum.5), channel_id=1, source_target_pairs={{0,16},{8,24},{16,0},{24,8},{1,17},{9,25},{17,1},{25,9},{2,18},{10... | collective-permute-start | bytes 1572872 | tf_op jit(solution)/shard_map/ppermute | solution.py:669
  46.9 5.8 %all-to-all-start = ((bf16[8,128,256]{2,1,0:T(8,128)(2,1)}), bf16[8,128,256]{2,1,0:T(8,128)(2,1)}, u32[]{:S(2)}, u32[]{:S(2)}) async-start(bf16[8,128,256]{2,1,0:T(8,128)(2,1)} %copy-done.5), calls=%async_computation | async-start | bytes 1048576 | tf_op jit(solution)/shard_map/all_to_all | solution.py:673
  52.7 6.7 %collective-permute-done.5.refs_2_ = bf16[8,128,256]{2,1,0:T(8,128)(2,1)} collective-permute-done((bf16[8,128,256]{2,1,0:T(8,128)(2,1)}, bf16[8,128,256]{2,1,0:T(8,128)(2,1)}, u32[]{:S(2)}, u32[]{:S(2)}) %collective-permute-start.5) | collective-permute-done | bytes 524320 | tf_op jit(solution)/shard_map/ppermute | solution.py:669
  59.4 1.6 copy-done.10
  61.0 1.6 copy-done.20
  64.6 2.7 %all-to-all-done.refs_0_ = bf16[8,128,256]{2,1,0:T(8,128)(2,1)} async-done(((bf16[8,128,256]{2,1,0:T(8,128)(2,1)}), bf16[8,128,256]{2,1,0:T(8,128)(2,1)}, u32[]{:S(2)}, u32[]{:S(2)}) %all-to-all-start) | async-done | bytes 524320 | tf_op jit(solution)/shard_map/all_to_all | solution.py:673
  67.3 18.3 %all_to_all.20.refs_1_ = bf16[8,128,256]{2,1,0:T(8,128)(2,1)S(1)} all-to-all(bf16[8,128,256]{2,1,0:T(8,128)(2,1)} %copy-done.6), channel_id=1, replica_groups=mesh['row'=4,'ma'=8] {'ma'}, dimensions={0} | all-to-all | bytes 1048576 | tf_op jit(solution)/shard_map/all_to_all | solution.py:673
  85.6 16.3 %cycle_work.1 = (bf16[8,160,256]{2,1,0:T(8,128)(2,1)S(1)}, bf16[8,96,256]{2,1,0:T(8,128)(2,1)}) custom-call(s32[4]{0:T(128)S(1)} %copy-done.15, s32[2]{0:T(128)S(1)} %pad_add_fusion.where_ref.token_ref, f32[4]{0:T(128)S(1)} %copy-done.16, bf16[8,128,256]{2,1,0:T(8,128)(2,1)} %all-to-all-done.refs_0_, bf16[8,128,256]{2,1,0:T(8,128)(2,1)S(1)} %all_to_all.20.refs_1_, ...), custom_call_target="tpu_custom_call" | custom-call | flops 4294967296 | bytes 8388608 | tf_op jit(solution)/shard_map/cycle_work/pallas_call | solution.py:478
  101.9 20.9 %all_to_all.21.own_ref = bf16[8,160,256]{2,1,0:T(8,128)(2,1)S(1)} all-to-all(bf16[8,160,256]{2,1,0:T(8,128)(2,1)S(1)} %get-tuple-element.46), channel_id=1, replica_groups=mesh['row'=4,'ma'=8] {'ma'}, dimensions={0} | all-to-all | bytes 1310720 | tf_op jit(solution)/shard_map/all_to_all | solution.py:696
  122.8 3.5 %all-to-all-start.3 = ((bf16[8,96,256]{2,1,0:T(8,128)(2,1)}), bf16[8,96,256]{2,1,0:T(8,128)(2,1)S(1)}, u32[]{:S(2)}, u32[]{:S(2)}) async-start(bf16[8,96,256]{2,1,0:T(8,128)(2,1)} %get-tuple-element.47), calls=%async_computation.3 | async-start | bytes 786432 | tf_op jit(solution)/shard_map/all_to_all | solution.py:696
  126.7 10.5 %all-to-all-done.3.own_ref = bf16[8,96,256]{2,1,0:T(8,128)(2,1)S(1)} async-done(((bf16[8,96,256]{2,1,0:T(8,128)(2,1)}), bf16[8,96,256]{2,1,0:T(8,128)(2,1)S(1)}, u32[]{:S(2)}, u32[]{:S(2)}) %all-to-all-start.3) | async-done | bytes 393248 | tf_op jit(solution)/shard_map/all_to_all | solution.py:696
  137.2 4.5 %collective-permute-done.6.far_ref = bf16[8,160,256]{2,1,0:T(8,128)(2,1)S(1)} collective-permute-done((bf16[8,160,256]{2,1,0:T(8,128)(2,1)S(1)}, bf16[8,160,256]{2,1,0:T(8,128)(2,1)S(1)}, u32[]{:S(2)}, u32[]{:S(2)}) %collective-permute-start.6) | collective-permute-done | bytes 655392 | tf_op jit(solution)/shard_map/ppermute | solution.py:698
  142.4 1.5 collective-permute-done.10.corner_ref
  143.8 8.4 %adjoint.2.refs_0_ = f32[2,256,512]{2,1,0:T(8,128)} custom-call(s32[2048]{0:T(1024)S(1)} %copy-done.8, s32[2]{0:T(128)S(1)} %pad_add_fusion.where_ref.token_ref, bf16[8,160,256]{2,1,0:T(8,128)(2,1)S(1)} %all_to_all.21.own_ref, bf16[8,160,256]{2,1,0:T(8,128)(2,1)S(1)} %collective-permute-done.9.core_ref, ...), custom_call_target="tpu_custom_call" | custom-call | flops 2684354560 | bytes 7864320 | tf_op jit(solution)/shard_map/adjoint/pallas_call | solution.py:582
  153.3 1.7 %collective-permute-done.11.corner_ref = bf16[8,96,256]{2,1,0:T(8,128)(2,1)S(1)} collective-permute-done((bf16[8,96,256]{2,1,0:T(8,128)(2,1)S(1)}, bf16[8,96,256]{2,1,0:T(8,128)(2,1)S(1)}, u32[]{:S(2)}, u32[]{:S(2)}) %collective-permute-start.11) | collective-permute-done | bytes 393248 | tf_op jit(solution)/shard_map/ppermute | solution.py:707
  155.0 6.0 %adjoint.3 = f32[2,256,512]{2,1,0:T(8,128)} custom-call(s32[2048]{0:T(1024)S(1)} %copy-done.8, s32[2]{0:T(128)S(1)} %pad_add_fusion.where_ref.token_ref, bf16[8,96,256]{2,1,0:T(8,128)(2,1)S(1)} %all-to-all-done.3.own_ref, bf16[8,96,256]{2,1,0:T(8,128)(2,1)S(1)} %collective-permute-done.7.core_ref, ...), custom_call_target="tpu_custom_call", output_to_operand_aliasing={{}: (8, {})} | custom-call | flops 1610612736 | bytes 4718592 | tf_op jit(solution)/shard_map/adjoint/pallas_call | solution.py:582
  (68 shorter events, 13.5 us)
Async XLA Ops:
  12.9 9.7 %copy-start.11 = (f32[2,8,64,256]{3,2,1,0:T(8,128)}, f32[2,8,64,256]{3,2,1,0:T(8,128)S(1)}, u32[]{:S(2)}) copy-start(f32[2,8,64,256]{3,2,1,0:T(8,128)S(1)} %get-tuple-element.32.keep_ref.refs_0_) | copy-start | bytes 3145732
  12.9 8.4 %copy-start.8 = (s32[2048]{0:T(1024)S(1)}, s32[2048]{0:T(1024)}, u32[]{:S(2)}) copy-start(s32[2048]{0:T(1024)} %order_ref.9) | copy-start | bytes 24580
  12.9 9.6 %collective-permute-start.1 = (f32[2,8,64,256]{3,2,1,0:T(8,128)}, f32[2,8,64,256]{3,2,1,0:T(8,128)}, u32[]{:S(2)}, u32[]{:S(2)}) collective-permute-start(f32[2,8,64,256]{3,2,1,0:T(8,128)} %get-tuple-element.33), channel_id=1, source_target_pairs={{0,8},{8,0},{16,24},{24,16},{1,9},{9,1},{17,25},{25,17},{2,10},{10... | collective-permute-start | bytes 3145736 | tf_op jit(solution)/shard_map/ppermute | solution.py:665
  21.2 5.6 %collective-permute-start = (f32[2,8,64,256]{3,2,1,0:T(8,128)}, f32[2,8,64,256]{3,2,1,0:T(8,128)}, u32[]{:S(2)}, u32[]{:S(2)}) collective-permute-start(f32[2,8,64,256]{3,2,1,0:T(8,128)} %get-tuple-element.31), channel_id=1, source_target_pairs={{0,8},{8,0},{16,24},{24,16},{1,9},{9,1},{17,25},{25,17},{2,10},{10... | collective-permute-start | bytes 3145736 | tf_op jit(solution)/shard_map/ppermute | solution.py:665
  23.7 4.4 %copy-start.1 = (f32[2,256,512]{2,1,0:T(8,128)S(1)}, f32[2,256,512]{2,1,0:T(8,128)}, u32[]{:S(2)}) copy-start(f32[2,256,512]{2,1,0:T(8,128)} %coeffs_ref.5) | copy-start | bytes 3145732
  23.8 15.6 %collective-permute-start.2 = (bf16[8,64,256]{2,1,0:T(8,128)(2,1)S(1)}, bf16[8,64,256]{2,1,0:T(8,128)(2,1)S(1)}, u32[]{:S(2)}, u32[]{:S(2)}) collective-permute-start(bf16[8,64,256]{2,1,0:T(8,128)(2,1)S(1)} %core_sum.3), channel_id=1, source_target_pairs={{0,16},{8,24},{16,0},{24,8},{1,17},{9,25},{17,1},{25,9},{2,18},{10... | collective-permute-start | bytes 786440 | tf_op jit(solution)/shard_map/ppermute | solution.py:669
  27.9 11.4 %copy-start.12 = (f32[2,8,64,256]{3,2,1,0:T(8,128)S(1)}, f32[2,8,64,256]{3,2,1,0:T(8,128)}, u32[]{:S(2)}) copy-start(f32[2,8,64,256]{3,2,1,0:T(8,128)} %copy-done.11) | copy-start | bytes 3145732
  27.9 11.4 %collective-permute-start.3 = (bf16[8,64,256]{2,1,0:T(8,128)(2,1)S(1)}, bf16[8,64,256]{2,1,0:T(8,128)(2,1)S(1)}, u32[]{:S(2)}, u32[]{:S(2)}) collective-permute-start(bf16[8,64,256]{2,1,0:T(8,128)(2,1)S(1)} %core_sum.4), channel_id=1, source_target_pairs={{0,16},{8,24},{16,0},{24,8},{1,17},{9,25},{17,1},{25,9},{2,18},{10... | collective-permute-start | bytes 786440 | tf_op jit(solution)/shard_map/ppermute | solution.py:669
  38.9 4.6 %copy-start.19 = (f32[2,8,128,256]{3,2,1,0:T(8,128)}, f32[2,8,128,256]{3,2,1,0:T(8,128)S(1)}, u32[]{:S(2)}) copy-start(f32[2,8,128,256]{3,2,1,0:T(8,128)S(1)} %get-tuple-element.37.keep_ref.refs_0_) | copy-start | bytes 6291460
  39.2 4.2 %collective-permute-start.4 = (f32[2,8,128,256]{3,2,1,0:T(8,128)S(1)}, f32[2,8,128,256]{3,2,1,0:T(8,128)S(1)}, u32[]{:S(2)}, u32[]{:S(2)}) collective-permute-start(f32[2,8,128,256]{3,2,1,0:T(8,128)S(1)} %get-tuple-element.40), channel_id=1, source_target_pairs={{0,8},{8,0},{16,24},{24,16},{1,9},{9,1},{17,25},{25,17},{2,10},{10... | collective-permute-start | bytes 6291464 | tf_op jit(solution)/shard_map/ppermute | solution.py:665
  45.0 14.4 %collective-permute-start.5 = (bf16[8,128,256]{2,1,0:T(8,128)(2,1)}, bf16[8,128,256]{2,1,0:T(8,128)(2,1)}, u32[]{:S(2)}, u32[]{:S(2)}) collective-permute-start(bf16[8,128,256]{2,1,0:T(8,128)(2,1)} %core_sum.5), channel_id=1, source_target_pairs={{0,16},{8,24},{16,0},{24,8},{1,17},{9,25},{17,1},{25,9},{2,18},{10... | collective-permute-start | bytes 1572872 | tf_op jit(solution)/shard_map/ppermute | solution.py:669
  46.9 20.4 %all-to-all-start = ((bf16[8,128,256]{2,1,0:T(8,128)(2,1)}), bf16[8,128,256]{2,1,0:T(8,128)(2,1)}, u32[]{:S(2)}, u32[]{:S(2)}) async-start(bf16[8,128,256]{2,1,0:T(8,128)(2,1)} %copy-done.5), calls=%async_computation | async-start | bytes 1048576 | tf_op jit(solution)/shard_map/all_to_all | solution.py:673
  62.6 23.0 %copy-start.15 = (s32[4]{0:T(128)S(1)}, s32[4]{0:T(128)}, u32[]{:S(2)}) copy-start(s32[4]{0:T(128)} %offset_ref.1) | copy-start | bytes 52
  62.6 23.0 %copy-start.16 = (f32[4]{0:T(128)S(1)}, f32[4]{0:T(128)}, u32[]{:S(2)}) copy-start(f32[4]{0:T(128)} %weight_ref.1) | copy-start | bytes 52
  62.6 23.0 %copy-start.17 = (bf16[128,256]{1,0:T(8,128)(2,1)S(1)}, bf16[128,256]{1,0:T(8,128)(2,1)}, u32[]{:S(2)}) copy-start(bf16[128,256]{1,0:T(8,128)(2,1)} %constant.65.clone.refs_7_) | copy-start | bytes 196612
  62.6 23.0 %copy-start.18 = (bf16[128,128]{1,0:T(8,128)(2,1)S(1)}, bf16[128,128]{1,0:T(8,128)(2,1)}, u32[]{:S(2)}) copy-start(bf16[128,128]{1,0:T(8,128)(2,1)} %constant.64.clone.refs_6_) | copy-start | bytes 98308
  101.9 42.0 %copy-start.2 = (bf16[256,512]{1,0:T(8,128)(2,1)S(1)}, bf16[256,512]{1,0:T(8,128)(2,1)}, u32[]{:S(2)}) copy-start(bf16[256,512]{1,0:T(8,128)(2,1)} %get-tuple-element.50.weight_ref) | copy-start | bytes 786436
  122.8 14.4 %all-to-all-start.3 = ((bf16[8,96,256]{2,1,0:T(8,128)(2,1)}), bf16[8,96,256]{2,1,0:T(8,128)(2,1)S(1)}, u32[]{:S(2)}, u32[]{:S(2)}) async-start(bf16[8,96,256]{2,1,0:T(8,128)(2,1)} %get-tuple-element.47), calls=%async_computation.3 | async-start | bytes 786432 | tf_op jit(solution)/shard_map/all_to_all | solution.py:696
  126.3 15.5 %collective-permute-start.6 = (bf16[8,160,256]{2,1,0:T(8,128)(2,1)S(1)}, bf16[8,160,256]{2,1,0:T(8,128)(2,1)S(1)}, u32[]{:S(2)}, u32[]{:S(2)}) collective-permute-start(bf16[8,160,256]{2,1,0:T(8,128)(2,1)S(1)} %all_to_all.21.own_ref), channel_id=1, source_target_pairs={{0,16},{8,24},{16,0},{24,8},{1,17},{9,25},{17,1},{25,9},{2,18},{10... | collective-permute-start | bytes 1966088 | tf_op jit(solution)/shard_map/ppermute | solution.py:698
  126.7 15.6 %collective-permute-start.9 = (bf16[8,160,256]{2,1,0:T(8,128)(2,1)S(1)}, bf16[8,160,256]{2,1,0:T(8,128)(2,1)S(1)}, u32[]{:S(2)}, u32[]{:S(2)}) collective-permute-start(bf16[8,160,256]{2,1,0:T(8,128)(2,1)S(1)} %all_to_all.21.own_ref), channel_id=1, source_target_pairs={{0,8},{8,0},{16,24},{24,16},{1,9},{9,1},{17,25},{25,17},{2,10},{10... | collective-permute-start | bytes 1966088 | tf_op jit(solution)/shard_map/ppermute | solution.py:706
  141.7 2.1 %collective-permute-start.10 = (bf16[8,160,256]{2,1,0:T(8,128)(2,1)S(1)}, bf16[8,160,256]{2,1,0:T(8,128)(2,1)S(1)}, u32[]{:S(2)}, u32[]{:S(2)}) collective-permute-start(bf16[8,160,256]{2,1,0:T(8,128)(2,1)S(1)} %collective-permute-done.6.far_ref), channel_id=1, source_target_pairs={{0,8},{8,0},{16,24},{24,16},{1,9},{9,1},{17,25},{25,17},{2,10},{10... | collective-permute-start | bytes 1966088 | tf_op jit(solution)/shard_map/ppermute | solution.py:707
  141.7 11.5 %collective-permute-start.8 = (bf16[8,96,256]{2,1,0:T(8,128)(2,1)S(1)}, bf16[8,96,256]{2,1,0:T(8,128)(2,1)S(1)}, u32[]{:S(2)}, u32[]{:S(2)}) collective-permute-start(bf16[8,96,256]{2,1,0:T(8,128)(2,1)S(1)} %all-to-all-done.3.own_ref), channel_id=1, source_target_pairs={{0,16},{8,24},{16,0},{24,8},{1,17},{9,25},{17,1},{25,9},{2,18},{10... | collective-permute-start | bytes 1179656 | tf_op jit(solution)/shard_map/ppermute | solution.py:703
  142.1 11.1 %collective-permute-start.7 = (bf16[8,96,256]{2,1,0:T(8,128)(2,1)S(1)}, bf16[8,96,256]{2,1,0:T(8,128)(2,1)S(1)}, u32[]{:S(2)}, u32[]{:S(2)}) collective-permute-start(bf16[8,96,256]{2,1,0:T(8,128)(2,1)S(1)} %all-to-all-done.3.own_ref), channel_id=1, source_target_pairs={{0,8},{8,0},{16,24},{24,16},{1,9},{9,1},{17,25},{25,17},{2,10},{10... | collective-permute-start | bytes 1179656 | tf_op jit(solution)/shard_map/ppermute | solution.py:706
  153.3 1.7 %collective-permute-start.11 = (bf16[8,96,256]{2,1,0:T(8,128)(2,1)S(1)}, bf16[8,96,256]{2,1,0:T(8,128)(2,1)S(1)}, u32[]{:S(2)}, u32[]{:S(2)}) collective-permute-start(bf16[8,96,256]{2,1,0:T(8,128)(2,1)S(1)} %collective-permute-done.8.far_ref), channel_id=1, source_target_pairs={{0,8},{8,0},{16,24},{24,16},{1,9},{9,1},{17,25},{25,17},{2,10},{10... | collective-permute-start | bytes 1179656 | tf_op jit(solution)/shard_map/ppermute | solution.py:707
  (11 other events, 18.8 us)

commit v7 on v5

--- a/solution.py
+++ b/solution.py
@@ -12,8 +12,6 @@
 NPIX = 4096
 SIDE = 64
 PADDED = 136
-CHUNKS = 4
-GROUPS = 2
 SYNTH_BLOCK = 16
 BLOCK = 32
 MIB = 1 << 20
@@ -48,7 +46,7 @@
     square = first[:, None] * first[None, :] % SIDE * (2.0 * math.pi / SIDE)
     pixel = np.concatenate(split_table(np.concatenate([np.cos(square), -np.sin(square)], axis=1)), axis=0)
     back_high, back_low = split_table(np.concatenate([np.cos(square), -np.sin(square)], axis=0))
-    back = np.concatenate([back_high, back_high, back_low, back_low], axis=1)
+    back = np.concatenate([np.tile(back_high, (1, 2)), np.tile(back_low, (1, 2))], axis=0)
     return spread_parts, pixel, back, gather_parts
 
 
@@ -148,6 +146,7 @@
     owners = cycles // 4
     lanes = weight_ref.shape[1] // 2
     degree = row * degrees + lax.broadcasted_iota(jnp.int32, (1, degrees), 1)
+    half = 16 * cycles
     for group in range(SYNTH_BLOCK // 8):
         terms = terms_odd if group % 2 else terms_even
         sums = sums_odd if group % 2 else sums_even
@@ -159,11 +158,10 @@
                 coeff = jnp.where(live, coeffs_ref[part, slot : slot + 1, :], 0.0)
                 high, low = two_parts(values * coeff)
                 start = (part * 8 + place) * cycles
-                terms[0, start : start + cycles, :] = high
-                terms[1, start : start + cycles, :] = low
-        both = jnp.dot(terms[0], weight_ref[...], preferred_element_type=F32)
-        rest = jnp.dot(terms[1], weight_ref[:, :lanes], preferred_element_type=F32)
-        sums[...] = both[:, :lanes] + both[:, lanes:] + rest
+                terms[start : start + cycles, :] = high
+                terms[half + start : half + start + cycles, :] = low
+        both = jnp.dot(terms[...], weight_ref[...], preferred_element_type=F32)
+        sums[...] = both[:half, :lanes] + both[:half, lanes:] + both[half:, :lanes]
         for part in range(2):
             for owner in range(owners):
                 for away in range(4):
@@ -178,17 +176,16 @@
                     ] = piece
 
 
-def synth(chunk, chunks, orders, where, coeffs, weight, legendre):
-    orders_here, cycles, degrees = legendre.shape
-    count = orders_here // chunks
+def synth(first, count, orders, where, coeffs, weight, legendre):
+    cycles, degrees = legendre.shape[1:]
     steps = count // SYNTH_BLOCK
-    start = chunk * steps
+    start = first // SYNTH_BLOCK
     owners = cycles // 4
     lanes = weight.shape[1] // 2
     out = jax.ShapeDtypeStruct((2, owners, count, 2 * lanes), F32)
     out_spec = pl.BlockSpec((2, owners, SYNTH_BLOCK, 2 * lanes), lambda t, *_: (0, 0, t, 0))
     return pl.pallas_call(
-        functools.partial(synth_kernel, chunk * count),
+        functools.partial(synth_kernel, first),
         grid_spec=pltpu.PrefetchScalarGridSpec(
             num_scalar_prefetch=2,
             grid=(steps,),
@@ -199,14 +196,14 @@
             ],
             out_specs=[out_spec, out_spec],
             scratch_shapes=[
-                pltpu.VMEM((2, 16 * cycles, degrees), BF16),
-                pltpu.VMEM((2, 16 * cycles, degrees), BF16),
+                pltpu.VMEM((32 * cycles, degrees), BF16),
+                pltpu.VMEM((32 * cycles, degrees), BF16),
                 pltpu.VMEM((16 * cycles, lanes), F32),
                 pltpu.VMEM((16 * cycles, lanes), F32),
             ],
         ),
         out_shape=[out, out],
-        compiler_params=pltpu.CompilerParams(vmem_limit_bytes=50 * MIB),
+        compiler_params=pltpu.CompilerParams(vmem_limit_bytes=56 * MIB),
         cost_estimate=pl.CostEstimate(
             flops=2 * count * cycles * degrees * lanes * 2 * 4,
             bytes_accessed=count * (cycles * degrees * 2 + 2 * cycles * lanes * 4),
@@ -359,11 +356,10 @@
         for inner in range(8):
             first = step * 8 + inner
             high, low = two_parts(product_scr[first] - mean)
-            back_scr[pl.ds(first * PADDED, 2 * SIDE), :] = jnp.dot(
-                back_ref[...],
-                jnp.concatenate([high, low, high, low], axis=0),
-                preferred_element_type=F32,
+            stage = jnp.dot(
+                back_ref[...], jnp.concatenate([high, low], axis=0), preferred_element_type=F32
             )
+            back_scr[pl.ds(first * PADDED, 2 * SIDE), :] = stage[: 2 * SIDE] + stage[2 * SIDE :]
         return carry
 
     lax.fori_loop(0, SIDE // 8, back_step, 0)
@@ -456,7 +452,7 @@
             ],
         ),
         out_shape=[jax.ShapeDtypeStruct(shape, BF16) for shape in out_shapes],
-        compiler_params=pltpu.CompilerParams(vmem_limit_bytes=40 * MIB),
+        compiler_params=pltpu.CompilerParams(vmem_limit_bytes=48 * MIB),
         cost_estimate=pl.CostEstimate(
             flops=4 * SIDE * 128 * 256 * 256 * 2, bytes_accessed=8 * MIB, transcendentals=0
         ),
@@ -490,17 +486,19 @@
                 values_scr[tile, place * pitch : place * pitch + cycles, :] = wide[
                     :, tile * 128 : tile * 128 + 128
                 ]
-        for part in range(2):
-            for away in range(4):
-                rows = sources[away][
+        rows = jnp.concatenate(
+            [
+                source[
                     :, group * 16 : group * 16 + 16, part * lanes : (part + 1) * lanes
                 ].reshape(quarter, lanes)
-                start = (part * 4 + away) * quarter
-                terms_scr[start : start + quarter, :] = jnp.dot(
-                    jnp.concatenate([rows, rows], axis=1),
-                    weight_ref[...],
-                    preferred_element_type=F32,
-                )
+                for part in range(2)
+                for source in sources
+            ],
+            axis=0,
+        )
+        terms_scr[...] = jnp.dot(
+            jnp.concatenate([rows, rows], axis=1), weight_ref[...], preferred_element_type=F32
+        )
         for half in range(2):
             total = [jnp.zeros((8, degrees), F32), jnp.zeros((8, degrees), F32)]
             for away in range(4):
@@ -556,7 +554,7 @@
         ),
         out_shape=out,
         input_output_aliases={8: 0} if earlier else {},
-        compiler_params=pltpu.CompilerParams(vmem_limit_bytes=40 * MIB),
+        compiler_params=pltpu.CompilerParams(vmem_limit_bytes=48 * MIB),
         cost_estimate=pl.CostEstimate(
             flops=2 * count * cycles * degrees * lanes * 2 * 2,
             bytes_accessed=count * (cycles * degrees * 2 + 2 * cycles * lanes * 2),
@@ -598,22 +596,24 @@
     row_count = lax.axis_size("row")
     local_orders = coeffs.shape[1]
     where = jnp.stack([row_id, ma_id * local_orders]).astype(jnp.int32)
-    places, sort, unsort = slot_tables(orders, device_count)
     synth_weight, adjoint_weight = filter_weights(
         radius_index, radial_weight, alpha_table, beta_table
     )
     core_pairs = [(i, i ^ 1) for i in range(row_count)]
     far_pairs = [(i, i ^ 2) for i in range(row_count)]
-    chunks = min(CHUNKS, local_orders // 32)
-    groups = min(GROUPS, chunks)
-    size = chunks // groups
+    units = local_orders // 32
+    counts = (units // 4, units // 4, units // 2) if units >= 4 else (units // 2, units // 2)
+    counts = [32 * count for count in counts]
     kept, others, outgoing, incoming, arrived = [], [], [], [], []
 
     def after(*values):
         return lax.optimization_barrier((where, *values))[0]
 
     def launch(chunk, token):
-        keep, send = synth(chunk, chunks, orders, token, coeffs, synth_weight, legendre)
+        first = sum(counts[:chunk])
+        keep, send = synth(
+            first, counts[chunk], orders, token, coeffs, synth_weight, legendre
+        )
         kept.append(keep)
         others.append(lax.ppermute(send, "row", core_pairs))
 
@@ -621,33 +621,26 @@
         outgoing.append(core_sum(kept[chunk], others[chunk], token))
         incoming.append(lax.ppermute(outgoing[chunk], "row", far_pairs))
 
-    def deliver(group, token):
-        own = slice(group * size, (group + 1) * size)
+    def deliver(own, token):
         summed = full_sum(list(zip(kept[own], others[own], incoming[own])), token)
         arrived.append(lax.all_to_all(summed, "ma", split_axis=0, concat_axis=0, tiled=True))
         return summed
 
-    if chunks == 4:
-        launch(0, where)
-        launch(1, where)
-        pass_on(0, after(kept[1]))
-        places, sort, unsort, token = lax.optimization_barrier((places, sort, unsort, where))
-        launch(2, lax.optimization_barrier((token, outgoing[0]))[0])
-        pass_on(1, after(kept[2]))
-        pass_on(2, after(outgoing[1]))
-        launch(3, after(outgoing[2], incoming[0]))
-        summed = deliver(0, after(kept[3]))
-        pass_on(3, after(summed))
-        deliver(1, after(outgoing[3]))
+    launch(0, where)
+    launch(1, where)
+    pass_on(0, after(kept[1]))
+    pass_on(1, after(outgoing[0]))
+    if len(counts) == 3:
+        launch(2, after(outgoing[1]))
+        pass_on(2, after(deliver(slice(0, 2), after(kept[2]))))
+        tables = slot_tables(lax.optimization_barrier((orders, outgoing[2]))[0], device_count)
+        places, sort, unsort, token = lax.optimization_barrier((*tables, where))
+        deliver(slice(2, 3), token)
     else:
-        for chunk in range(chunks):
-            launch(chunk, where)
-        for chunk in range(chunks):
-            pass_on(chunk, after(kept[-1]))
-        for group in range(groups):
-            deliver(group, after(outgoing[-1]))
-    units = local_orders // 32
-    early = 32 * ((5 * units) // 8)
+        deliver(slice(0, 1), after(outgoing[1]))
+        deliver(slice(1, 2), after(outgoing[1]))
+        places, sort, unsort = slot_tables(orders, device_count)
+    early = 32 * (units // 2)
     sizes = (early, local_orders - early)
     analysed = cycle_work(
         arrived, sizes, places, sort, unsort, cycle_offset, where, cycle_weight

time: 170 us -> 158 us (0.929)
  local copies, waits for them, and re-layouts: 20 us -> 4.45 us
  waiting for transfers between devices: 27 us -> 34.3 us
  blocking collectives: 39.2 us -> 36.9 us
    unnamed x58 -> x32, local copies, waits for them, and re-layouts: 19.5 us -> 4.03 us
    ppermute x4 -> x3, waiting for transfers between devices: 1.52 us -> 12.1 us  [pass_on(): incoming.append(lax.ppermute(outgoing[chunk], 'row', far_pairs))]
    all_to_all x1, waiting for transfers between devices: 6.3 us -> 0.01 us  [deliver(): lax.all_to_all(summed, 'ma', split_axis=0, concat_axis=0, tiled=True)]
    ppermute x1, waiting for transfers between devices: 0.01 us -> 5.52 us  [body(): far_part = lax.ppermute(own_part, 'row', far_pairs)]
    ppermute x1, waiting for transfers between devices: 4.51 us -> 0.01 us  [body(): far = lax.ppermute(own[0], 'row', far_pairs)]
    all_to_all x1, waiting for transfers between devices: 10 us -> 13.5 us  [body(): lax.all_to_all(piece, 'ma', split_axis=0, concat_axis=0, tiled=True)]
    all_to_all x1, blocking collectives: 20.9 us -> 17.6 us  [body(): lax.all_to_all(piece, 'ma', split_axis=0, concat_axis=0, tiled=True)]
    pallas_call x4 -> x3, Pallas kernels: 5.15 us -> 2.7 us  [core_sum(): pl.pallas_call(core_sum_kernel, grid=(1,), in_specs=[half, half, pl.Block...]
  transfers between devices with their start and end apart: 16 -> 14, of which waited for: 8 -> 5; matrix products, arithmetic and copies ran while one was open for 1% -> 1% of each run, Pallas kernels for 20% -> 20%
where the time goes in v7:
time: 158 us; the launch traced here: 157 us
  Pallas kernels  62.3 us (39%)
  blocking collectives  36.9 us (23%)
  waiting for transfers between devices  34.3 us (22%)
  starting transfers between devices  16.8 us (11%)
  local copies, waits for them, and re-layouts  4.45 us (3%)
  other arithmetic  1.72 us (1%)
    pallas_call x3, Pallas kernels, synth(): pl.pallas_call(functools.partial(synth_kernel, first), grid_spec=pltpu.Pr...  26.7 us
    all_to_all x1, blocking collectives, deliver(): lax.all_to_all(summed, 'ma', split_axis=0, concat_axis=0, tiled=True)  19.4 us
    all_to_all x1, blocking collectives, body(): lax.all_to_all(piece, 'ma', split_axis=0, concat_axis=0, tiled=True)  17.6 us
    pallas_call x2, Pallas kernels, adjoint(): pl.pallas_call(functools.partial(adjoint_kernel, first), grid_spec=pltpu....  13.8 us
    all_to_all x1, waiting for transfers between devices, body(): lax.all_to_all(piece, 'ma', split_axis=0, concat_axis=0, tiled=True)  13.5 us
    pallas_call x1, Pallas kernels, cycle_work(): pl.pallas_call(functools.partial(cycle_kernel, groups, sizes), grid_spec=...  13.4 us
    ppermute x3, waiting for transfers between devices, pass_on(): incoming.append(lax.ppermute(outgoing[chunk], 'row', far_pairs))  12.1 us
    all_to_all x1, starting transfers between devices, deliver(): lax.all_to_all(summed, 'ma', split_axis=0, concat_axis=0, tiled=True)  5.8 us
  transfers between devices with their start and end apart: 14, of which 5 were waited for; matrix products, arithmetic and copies ran while one was open for 1% of the time, Pallas kernels for 20%

profile of v7, /device:TPU:0, one launch (start us, length us, event | category | flops | bytes accessed | tf_op | source)
XLA Modules:
  0.0 156.7 jit_solution(17110226508025852145)
XLA Ops:
  0.6 3.1 %filter_weights.1 = (bf16[512,256]{1,0:T(8,128)(2,1)}, bf16[256,512]{1,0:T(8,128)(2,1)}) custom-call(s32[64]{0:T(128)} %node_ref.1, f32[64]{0:T(128)} %radial_ref.1, f32[64,512]{1,0:T(8,128)} %alpha_ref.1, f32[64,512]{1,0:T(8,128)} %beta_ref.1), custom_call_target="tpu_custom_call" | custom-call | tf_op jit(solution)/shard_map/filter_weights/pallas_call | solution.py:117
  3.6 7.3 %synth.4 = (f32[2,8,64,256]{3,2,1,0:T(8,128)}, f32[2,8,64,256]{3,2,1,0:T(8,128)}) custom-call(s32[2048]{0:T(1024)} %order_ref.9, s32[2]{0:T(128)} %pad_add_fusion.where_ref.token_ref, f32[2,256,512]{2,1,0:T(8,128)} %coeffs_ref.5, bf16[512,256]{1,0:T(8,128)(2,1)} %get-tuple-element.29.weight_ref, bf16[256,32,512]{2,1,0:T(8,128)(2,1)} %legendre_ref.9), custom_call_target="tpu_custom_call" | custom-call | flops 2147483648 | bytes 4194304 | tf_op jit(solution)/shard_map/synth/pallas_call | solution.py:187
  11.5 7.3 %synth.3 = (f32[2,8,64,256]{3,2,1,0:T(8,128)}, f32[2,8,64,256]{3,2,1,0:T(8,128)}) custom-call(s32[2048]{0:T(1024)} %order_ref.9, s32[2]{0:T(128)} %pad_add_fusion.where_ref.token_ref, f32[2,256,512]{2,1,0:T(8,128)} %coeffs_ref.5, bf16[512,256]{1,0:T(8,128)(2,1)} %get-tuple-element.29.weight_ref, bf16[256,32,512]{2,1,0:T(8,128)(2,1)} %legendre_ref.9), custom_call_target="tpu_custom_call" | custom-call | flops 2147483648 | bytes 4194304 | tf_op jit(solution)/shard_map/synth/pallas_call | solution.py:187
  19.6 2.9 %collective-permute-start.2 = (bf16[8,64,256]{2,1,0:T(8,128)(2,1)S(1)}, bf16[8,64,256]{2,1,0:T(8,128)(2,1)S(1)}, u32[]{:S(2)}, u32[]{:S(2)}) collective-permute-start(bf16[8,64,256]{2,1,0:T(8,128)(2,1)S(1)} %core_sum.3), channel_id=1, source_target_pairs={{0,16},{8,24},{16,0},{24,8},{1,17},{9,25},{17,1},{25,9},{2,18},{10... | collective-permute-start | bytes 786440 | tf_op jit(solution)/shard_map/ppermute | solution.py:622
  23.1 1.9 %collective-permute-start.3 = (bf16[8,64,256]{2,1,0:T(8,128)(2,1)S(1)}, bf16[8,64,256]{2,1,0:T(8,128)(2,1)S(1)}, u32[]{:S(2)}, u32[]{:S(2)}) collective-permute-start(bf16[8,64,256]{2,1,0:T(8,128)(2,1)S(1)} %core_sum.4), channel_id=1, source_target_pairs={{0,16},{8,24},{16,0},{24,8},{1,17},{9,25},{17,1},{25,9},{2,18},{10... | collective-permute-start | bytes 786440 | tf_op jit(solution)/shard_map/ppermute | solution.py:622
  25.0 12.0 %synth.5 = (f32[2,8,128,256]{3,2,1,0:T(8,128)}, f32[2,8,128,256]{3,2,1,0:T(8,128)}) custom-call(s32[2048]{0:T(1024)} %order_ref.9, s32[2]{0:T(128)} %pad_add_fusion.where_ref.token_ref, f32[2,256,512]{2,1,0:T(8,128)} %coeffs_ref.5, bf16[512,256]{1,0:T(8,128)(2,1)} %get-tuple-element.29.weight_ref, bf16[256,32,512]{2,1,0:T(8,128)(2,1)} %legendre_ref.9), custom_call_target="tpu_custom_call" | custom-call | flops 4294967296 | bytes 8388608 | tf_op jit(solution)/shard_map/synth/pallas_call | solution.py:187
  37.1 1.5 full_sum.2
  38.6 5.8 %all-to-all-start = ((bf16[8,128,256]{2,1,0:T(8,128)(2,1)}), bf16[8,128,256]{2,1,0:T(8,128)(2,1)}, u32[]{:S(2)}, u32[]{:S(2)}) async-start(bf16[8,128,256]{2,1,0:T(8,128)(2,1)} %full_sum.2), calls=%async_computation | async-start | bytes 1048576 | tf_op jit(solution)/shard_map/all_to_all | solution.py:626
  44.4 1.6 %copy-done.14 = f32[2,8,128,256]{3,2,1,0:T(8,128)S(1)} copy-done((f32[2,8,128,256]{3,2,1,0:T(8,128)S(1)}, f32[2,8,128,256]{3,2,1,0:T(8,128)}, u32[]{:S(2)}) %copy-start.14) | copy-done | bytes 2097176
  46.0 1.5 core_sum.5
  49.7 12.1 %collective-permute-done.5.refs_2_ = bf16[8,128,256]{2,1,0:T(8,128)(2,1)} collective-permute-done((bf16[8,128,256]{2,1,0:T(8,128)(2,1)}, bf16[8,128,256]{2,1,0:T(8,128)(2,1)}, u32[]{:S(2)}, u32[]{:S(2)}) %collective-permute-start.5) | collective-permute-done | bytes 524320 | tf_op jit(solution)/shard_map/ppermute | solution.py:622
  61.9 1.6 %copy-done.15 = f32[2,8,128,256]{3,2,1,0:T(8,128)S(1)} copy-done((f32[2,8,128,256]{3,2,1,0:T(8,128)S(1)}, f32[2,8,128,256]{3,2,1,0:T(8,128)}, u32[]{:S(2)}) %copy-start.15) | copy-done | bytes 2097176
  63.4 1.2 full_sum.3
  64.7 0.8 copy-done.2
  65.4 19.4 %all_to_all.20.refs_1_ = bf16[8,128,256]{2,1,0:T(8,128)(2,1)S(1)} all-to-all(bf16[8,128,256]{2,1,0:T(8,128)(2,1)} %copy-done.2), channel_id=1, replica_groups=mesh['row'=4,'ma'=8] {'ma'}, dimensions={0} | all-to-all | bytes 1048576 | tf_op jit(solution)/shard_map/all_to_all | solution.py:626
  84.8 13.4 %cycle_work.1 = (bf16[8,128,256]{2,1,0:T(8,128)(2,1)S(1)}, bf16[8,128,256]{2,1,0:T(8,128)(2,1)S(1)}) custom-call(s32[4]{0:T(128)S(1)} %copy-done.10, s32[2]{0:T(128)S(1)} %copy-done.5, f32[4]{0:T(128)S(1)} %copy-done.11, bf16[8,128,256]{2,1,0:T(8,128)(2,1)} %all-to-all-done.refs_0_, bf16[8,128,256]{2,1,0:T(8,128)(2,1)S(1)} %all_to_all.20.refs_1_, ...), custom_call_target="tpu_custom_call" | custom-call | flops 4294967296 | bytes 8388608 | tf_op jit(solution)/shard_map/cycle_work/pallas_call | solution.py:434
  98.3 17.6 %all_to_all.21.own_ref = bf16[8,128,256]{2,1,0:T(8,128)(2,1)S(1)} all-to-all(bf16[8,128,256]{2,1,0:T(8,128)(2,1)S(1)} %get-tuple-element.46), channel_id=1, replica_groups=mesh['row'=4,'ma'=8] {'ma'}, dimensions={0} | all-to-all | bytes 1048576 | tf_op jit(solution)/shard_map/all_to_all | solution.py:649
  115.9 3.6 %all-to-all-start.3 = ((bf16[8,128,256]{2,1,0:T(8,128)(2,1)}), bf16[8,128,256]{2,1,0:T(8,128)(2,1)S(1)}, u32[]{:S(2)}, u32[]{:S(2)}) async-start(bf16[8,128,256]{2,1,0:T(8,128)(2,1)} %copy-done.1), calls=%async_computation.3 | async-start | bytes 1048576 | tf_op jit(solution)/shard_map/all_to_all | solution.py:649
  120.0 13.5 %all-to-all-done.3.own_ref = bf16[8,128,256]{2,1,0:T(8,128)(2,1)S(1)} async-done(((bf16[8,128,256]{2,1,0:T(8,128)(2,1)}), bf16[8,128,256]{2,1,0:T(8,128)(2,1)S(1)}, u32[]{:S(2)}, u32[]{:S(2)}) %all-to-all-start.3) | async-done | bytes 524320 | tf_op jit(solution)/shard_map/all_to_all | solution.py:649
  134.3 1.2 collective-permute-done.10.corner_ref
  135.5 6.9 %adjoint.2.refs_0_ = f32[2,256,512]{2,1,0:T(8,128)} custom-call(s32[2048]{0:T(1024)S(1)} %copy-done.3, s32[2]{0:T(128)S(1)} %copy-done.5, bf16[8,128,256]{2,1,0:T(8,128)(2,1)S(1)} %all_to_all.21.own_ref, bf16[8,128,256]{2,1,0:T(8,128)(2,1)S(1)} %collective-permute-done.9.core_ref, bf16[8,128,256]{2,1,0:T(8,128)(2,1)S(1)} %collective-permute-done.6.far_ref, ...), custom_call_target="tpu_custom_call" | custom-call | flops 2147483648 | bytes 6291456 | tf_op jit(solution)/shard_map/adjoint/pallas_call | solution.py:536
  142.4 5.5 %collective-permute-done.8.far_ref = bf16[8,128,256]{2,1,0:T(8,128)(2,1)S(1)} collective-permute-done((bf16[8,128,256]{2,1,0:T(8,128)(2,1)S(1)}, bf16[8,128,256]{2,1,0:T(8,128)(2,1)S(1)}, u32[]{:S(2)}, u32[]{:S(2)}) %collective-permute-start.8) | collective-permute-done | bytes 524320 | tf_op jit(solution)/shard_map/ppermute | solution.py:656
  147.9 1.9 %collective-permute-done.11.corner_ref = bf16[8,128,256]{2,1,0:T(8,128)(2,1)S(1)} collective-permute-done((bf16[8,128,256]{2,1,0:T(8,128)(2,1)S(1)}, bf16[8,128,256]{2,1,0:T(8,128)(2,1)S(1)}, u32[]{:S(2)}, u32[]{:S(2)}) %collective-permute-start.11) | collective-permute-done | bytes 524320 | tf_op jit(solution)/shard_map/ppermute | solution.py:660
  149.8 6.9 %adjoint.3 = f32[2,256,512]{2,1,0:T(8,128)} custom-call(s32[2048]{0:T(1024)S(1)} %copy-done.3, s32[2]{0:T(128)S(1)} %copy-done.5, bf16[8,128,256]{2,1,0:T(8,128)(2,1)S(1)} %all-to-all-done.3.own_ref, bf16[8,128,256]{2,1,0:T(8,128)(2,1)S(1)} %collective-permute-done.7.core_ref, ...), custom_call_target="tpu_custom_call", output_to_operand_aliasing={{}: (8, {})} | custom-call | flops 2147483648 | bytes 6291456 | tf_op jit(solution)/shard_map/adjoint/pallas_call | solution.py:536
  (58 shorter events, 6.0 us)
Async XLA Ops:
  10.9 8.0 %copy-start.4 = (s32[2]{0:T(128)S(1)}, s32[2]{0:T(128)}, u32[]{:S(2)}) copy-start(s32[2]{0:T(128)} %pad_add_fusion.where_ref.token_ref) | copy-start | bytes 28
  10.9 8.0 %copy-start.8 = (f32[2,8,64,256]{3,2,1,0:T(8,128)S(1)}, f32[2,8,64,256]{3,2,1,0:T(8,128)}, u32[]{:S(2)}) copy-start(f32[2,8,64,256]{3,2,1,0:T(8,128)} %get-tuple-element.32.keep_ref.refs_0_) | copy-start | bytes 3145732
  10.9 8.0 %collective-permute-start.1 = (f32[2,8,64,256]{3,2,1,0:T(8,128)}, f32[2,8,64,256]{3,2,1,0:T(8,128)S(1)}, u32[]{:S(2)}, u32[]{:S(2)}) collective-permute-start(f32[2,8,64,256]{3,2,1,0:T(8,128)} %get-tuple-element.33), channel_id=1, source_target_pairs={{0,8},{8,0},{16,24},{24,16},{1,9},{9,1},{17,25},{25,17},{2,10},{10... | collective-permute-start | bytes 3145736 | tf_op jit(solution)/shard_map/ppermute | solution.py:618
  18.8 3.7 %collective-permute-start = (f32[2,8,64,256]{3,2,1,0:T(8,128)}, f32[2,8,64,256]{3,2,1,0:T(8,128)S(1)}, u32[]{:S(2)}, u32[]{:S(2)}) collective-permute-start(f32[2,8,64,256]{3,2,1,0:T(8,128)} %get-tuple-element.31), channel_id=1, source_target_pairs={{0,8},{8,0},{16,24},{24,16},{1,9},{9,1},{17,25},{25,17},{2,10},{10... | collective-permute-start | bytes 3145736 | tf_op jit(solution)/shard_map/ppermute | solution.py:618
  19.6 17.5 %collective-permute-start.2 = (bf16[8,64,256]{2,1,0:T(8,128)(2,1)S(1)}, bf16[8,64,256]{2,1,0:T(8,128)(2,1)S(1)}, u32[]{:S(2)}, u32[]{:S(2)}) collective-permute-start(bf16[8,64,256]{2,1,0:T(8,128)(2,1)S(1)} %core_sum.3), channel_id=1, source_target_pairs={{0,16},{8,24},{16,0},{24,8},{1,17},{9,25},{17,1},{25,9},{2,18},{10... | collective-permute-start | bytes 786440 | tf_op jit(solution)/shard_map/ppermute | solution.py:622
  23.1 14.0 %copy-start.5 = (s32[2]{0:T(128)S(1)}, s32[2]{0:T(128)}, u32[]{:S(2)}) copy-start(s32[2]{0:T(128)} %pad_add_fusion.where_ref.token_ref) | copy-start | bytes 28
  23.1 14.0 %collective-permute-start.3 = (bf16[8,64,256]{2,1,0:T(8,128)(2,1)S(1)}, bf16[8,64,256]{2,1,0:T(8,128)(2,1)S(1)}, u32[]{:S(2)}, u32[]{:S(2)}) collective-permute-start(bf16[8,64,256]{2,1,0:T(8,128)(2,1)S(1)} %core_sum.4), channel_id=1, source_target_pairs={{0,16},{8,24},{16,0},{24,8},{1,17},{9,25},{17,1},{25,9},{2,18},{10... | collective-permute-start | bytes 786440 | tf_op jit(solution)/shard_map/ppermute | solution.py:622
  37.0 7.4 %collective-permute-start.4 = (f32[2,8,128,256]{3,2,1,0:T(8,128)}, f32[2,8,128,256]{3,2,1,0:T(8,128)S(1)}, u32[]{:S(2)}, u32[]{:S(2)}) collective-permute-start(f32[2,8,128,256]{3,2,1,0:T(8,128)} %get-tuple-element.39), channel_id=1, source_target_pairs={{0,8},{8,0},{16,24},{24,16},{1,9},{9,1},{17,25},{25,17},{2,10},{10... | collective-permute-start | bytes 6291464 | tf_op jit(solution)/shard_map/ppermute | solution.py:618
  38.6 26.8 %all-to-all-start = ((bf16[8,128,256]{2,1,0:T(8,128)(2,1)}), bf16[8,128,256]{2,1,0:T(8,128)(2,1)}, u32[]{:S(2)}, u32[]{:S(2)}) async-start(bf16[8,128,256]{2,1,0:T(8,128)(2,1)} %full_sum.2), calls=%async_computation | async-start | bytes 1048576 | tf_op jit(solution)/shard_map/all_to_all | solution.py:626
  47.6 14.3 %collective-permute-start.5 = (bf16[8,128,256]{2,1,0:T(8,128)(2,1)}, bf16[8,128,256]{2,1,0:T(8,128)(2,1)}, u32[]{:S(2)}, u32[]{:S(2)}) collective-permute-start(bf16[8,128,256]{2,1,0:T(8,128)(2,1)} %core_sum.5), channel_id=1, source_target_pairs={{0,16},{8,24},{16,0},{24,8},{1,17},{9,25},{17,1},{25,9},{2,18},{10... | collective-permute-start | bytes 1572872 | tf_op jit(solution)/shard_map/ppermute | solution.py:622
  48.6 13.2 %copy-start.7 = (f32[2,8,128,256]{3,2,1,0:T(8,128)S(1)}, f32[2,8,128,256]{3,2,1,0:T(8,128)}, u32[]{:S(2)}) copy-start(f32[2,8,128,256]{3,2,1,0:T(8,128)} %copy-done.6) | copy-start | bytes 6291460
  49.7 35.2 %copy-start.10 = (s32[4]{0:T(128)S(1)}, s32[4]{0:T(128)}, u32[]{:S(2)}) copy-start(s32[4]{0:T(128)} %offset_ref.1) | copy-start | bytes 52
  49.7 35.1 %copy-start.11 = (f32[4]{0:T(128)S(1)}, f32[4]{0:T(128)}, u32[]{:S(2)}) copy-start(f32[4]{0:T(128)} %weight_ref.1) | copy-start | bytes 52
  49.7 35.1 %copy-start.12 = (bf16[256,128]{1,0:T(8,128)(2,1)S(1)}, bf16[256,128]{1,0:T(8,128)(2,1)}, u32[]{:S(2)}) copy-start(bf16[256,128]{1,0:T(8,128)(2,1)} %constant.65.clone.refs_7_) | copy-start | bytes 196612
  49.7 35.1 %copy-start.13 = (bf16[128,128]{1,0:T(8,128)(2,1)S(1)}, bf16[128,128]{1,0:T(8,128)(2,1)}, u32[]{:S(2)}) copy-start(bf16[128,128]{1,0:T(8,128)(2,1)} %constant.64.clone.refs_6_) | copy-start | bytes 98308
  98.3 17.6 %copy-start.1 = (bf16[8,128,256]{2,1,0:T(8,128)(2,1)}, bf16[8,128,256]{2,1,0:T(8,128)(2,1)S(1)}, u32[]{:S(2)}) copy-start(bf16[8,128,256]{2,1,0:T(8,128)(2,1)S(1)} %get-tuple-element.47) | copy-start | bytes 1572868
  98.3 37.2 %copy-start = (bf16[256,512]{1,0:T(8,128)(2,1)S(1)}, bf16[256,512]{1,0:T(8,128)(2,1)}, u32[]{:S(2)}) copy-start(bf16[256,512]{1,0:T(8,128)(2,1)} %get-tuple-element.50.weight_ref) | copy-start | bytes 786436
  115.9 17.7 %all-to-all-start.3 = ((bf16[8,128,256]{2,1,0:T(8,128)(2,1)}), bf16[8,128,256]{2,1,0:T(8,128)(2,1)S(1)}, u32[]{:S(2)}, u32[]{:S(2)}) async-start(bf16[8,128,256]{2,1,0:T(8,128)(2,1)} %copy-done.1), calls=%async_computation.3 | async-start | bytes 1048576 | tf_op jit(solution)/shard_map/all_to_all | solution.py:649
  119.5 14.0 %collective-permute-start.6 = (bf16[8,128,256]{2,1,0:T(8,128)(2,1)S(1)}, bf16[8,128,256]{2,1,0:T(8,128)(2,1)S(1)}, u32[]{:S(2)}, u32[]{:S(2)}) collective-permute-start(bf16[8,128,256]{2,1,0:T(8,128)(2,1)S(1)} %all_to_all.21.own_ref), channel_id=1, source_target_pairs={{0,16},{8,24},{16,0},{24,8},{1,17},{9,25},{17,1},{25,9},{2,18},{10... | collective-permute-start | bytes 1572872 | tf_op jit(solution)/shard_map/ppermute | solution.py:651
  120.0 14.3 %collective-permute-start.9 = (bf16[8,128,256]{2,1,0:T(8,128)(2,1)S(1)}, bf16[8,128,256]{2,1,0:T(8,128)(2,1)S(1)}, u32[]{:S(2)}, u32[]{:S(2)}) collective-permute-start(bf16[8,128,256]{2,1,0:T(8,128)(2,1)S(1)} %all_to_all.21.own_ref), channel_id=1, source_target_pairs={{0,8},{8,0},{16,24},{24,16},{1,9},{9,1},{17,25},{25,17},{2,10},{10... | collective-permute-start | bytes 1572872 | tf_op jit(solution)/shard_map/ppermute | solution.py:659
  133.6 1.9 %collective-permute-start.10 = (bf16[8,128,256]{2,1,0:T(8,128)(2,1)S(1)}, bf16[8,128,256]{2,1,0:T(8,128)(2,1)S(1)}, u32[]{:S(2)}, u32[]{:S(2)}) collective-permute-start(bf16[8,128,256]{2,1,0:T(8,128)(2,1)S(1)} %collective-permute-done.6.far_ref), channel_id=1, source_target_pairs={{0,8},{8,0},{16,24},{24,16},{1,9},{9,1},{17,25},{25,17},{2,10},{10... | collective-permute-start | bytes 1572872 | tf_op jit(solution)/shard_map/ppermute | solution.py:660
  133.6 14.3 %collective-permute-start.8 = (bf16[8,128,256]{2,1,0:T(8,128)(2,1)S(1)}, bf16[8,128,256]{2,1,0:T(8,128)(2,1)S(1)}, u32[]{:S(2)}, u32[]{:S(2)}) collective-permute-start(bf16[8,128,256]{2,1,0:T(8,128)(2,1)S(1)} %all-to-all-done.3.own_ref), channel_id=1, source_target_pairs={{0,16},{8,24},{16,0},{24,8},{1,17},{9,25},{17,1},{25,9},{2,18},{10... | collective-permute-start | bytes 1572872 | tf_op jit(solution)/shard_map/ppermute | solution.py:656
  134.1 13.8 %collective-permute-start.7 = (bf16[8,128,256]{2,1,0:T(8,128)(2,1)S(1)}, bf16[8,128,256]{2,1,0:T(8,128)(2,1)S(1)}, u32[]{:S(2)}, u32[]{:S(2)}) collective-permute-start(bf16[8,128,256]{2,1,0:T(8,128)(2,1)S(1)} %all-to-all-done.3.own_ref), channel_id=1, source_target_pairs={{0,8},{8,0},{16,24},{24,16},{1,9},{9,1},{17,25},{25,17},{2,10},{10... | collective-permute-start | bytes 1572872 | tf_op jit(solution)/shard_map/ppermute | solution.py:659
  147.9 1.9 %collective-permute-start.11 = (bf16[8,128,256]{2,1,0:T(8,128)(2,1)S(1)}, bf16[8,128,256]{2,1,0:T(8,128)(2,1)S(1)}, u32[]{:S(2)}, u32[]{:S(2)}) collective-permute-start(bf16[8,128,256]{2,1,0:T(8,128)(2,1)S(1)} %collective-permute-done.8.far_ref), channel_id=1, source_target_pairs={{0,8},{8,0},{16,24},{24,16},{1,9},{9,1},{17,25},{25,17},{2,10},{10... | collective-permute-start | bytes 1572872 | tf_op jit(solution)/shard_map/ppermute | solution.py:660
  (6 other events, 12.7 us)

commit v8 on v7

--- a/solution.py
+++ b/solution.py
@@ -160,8 +160,9 @@
                 start = (part * 8 + place) * cycles
                 terms[start : start + cycles, :] = high
                 terms[half + start : half + start + cycles, :] = low
-        both = jnp.dot(terms[...], weight_ref[...], preferred_element_type=F32)
-        sums[...] = both[:half, :lanes] + both[:half, lanes:] + both[half:, :lanes]
+        both = jnp.dot(terms[:half], weight_ref[...], preferred_element_type=F32)
+        rest = jnp.dot(terms[half:], weight_ref[:, :lanes], preferred_element_type=F32)
+        sums[...] = both[:, :lanes] + both[:, lanes:] + rest
         for part in range(2):
             for owner in range(owners):
                 for away in range(4):
@@ -176,7 +177,7 @@
                     ] = piece
 
 
-def synth(first, count, orders, where, coeffs, weight, legendre):
+def synth(first, count, grant, orders, where, coeffs, weight, legendre):
     cycles, degrees = legendre.shape[1:]
     steps = count // SYNTH_BLOCK
     start = first // SYNTH_BLOCK
@@ -203,7 +204,7 @@
             ],
         ),
         out_shape=[out, out],
-        compiler_params=pltpu.CompilerParams(vmem_limit_bytes=56 * MIB),
+        compiler_params=pltpu.CompilerParams(vmem_limit_bytes=grant * MIB),
         cost_estimate=pl.CostEstimate(
             flops=2 * count * cycles * degrees * lanes * 2 * 4,
             bytes_accessed=count * (cycles * degrees * 2 + 2 * cycles * lanes * 4),
@@ -427,7 +428,8 @@
 
 def cycle_work(pieces, sizes, places, sort, unsort, offset, where, cycle_weight):
     groups = len(pieces)
-    device_count, count, lanes = pieces[0].shape
+    device_count, _, lanes = pieces[0].shape
+    count = sum(piece.shape[1] for piece in pieces)
     out_shapes = [(device_count, size, lanes) for size in sizes]
     spread, pixel, back, gather = [jnp.asarray(table) for table in fourier_tables()]
     tables = [places, sort, unsort]
@@ -444,7 +446,7 @@
             scratch_shapes=[
                 pltpu.VMEM(spread.shape[1:], BF16),
                 pltpu.VMEM(gather.shape[1:], BF16),
-                pltpu.VMEM((device_count, groups * count, lanes), BF16),
+                pltpu.VMEM((device_count, count, lanes), BF16),
                 pltpu.VMEM((SIDE * PADDED, lanes // 2), F32),
                 pltpu.VMEM((SIDE, SIDE, lanes // 2), F32),
                 pltpu.VMEM((SIDE * PADDED, lanes // 2), F32),
@@ -602,7 +604,7 @@
     core_pairs = [(i, i ^ 1) for i in range(row_count)]
     far_pairs = [(i, i ^ 2) for i in range(row_count)]
     units = local_orders // 32
-    counts = (units // 4, units // 4, units // 2) if units >= 4 else (units // 2, units // 2)
+    counts = (2, (units - 2) // 2, (units - 1) // 2) if units > 4 else (units // 2, units // 2)
     counts = [32 * count for count in counts]
     kept, others, outgoing, incoming, arrived = [], [], [], [], []
 
@@ -611,8 +613,9 @@
 
     def launch(chunk, token):
         first = sum(counts[:chunk])
+        grant = 44 if chunk == 2 else 56
         keep, send = synth(
-            first, counts[chunk], orders, token, coeffs, synth_weight, legendre
+            first, counts[chunk], grant, orders, token, coeffs, synth_weight, legendre
         )
         kept.append(keep)
         others.append(lax.ppermute(send, "row", core_pairs))
@@ -640,7 +643,7 @@
         deliver(slice(0, 1), after(outgoing[1]))
         deliver(slice(1, 2), after(outgoing[1]))
         places, sort, unsort = slot_tables(orders, device_count)
-    early = 32 * (units // 2)
+    early = 32 * ((5 * units) // 8)
     sizes = (early, local_orders - early)
     analysed = cycle_work(
         arrived, sizes, places, sort, unsort, cycle_offset, where, cycle_weight

time: 158 us -> 160 us (1.013)
  local copies, waits for them, and re-layouts: 4.45 us -> 9.08 us
  waiting for transfers between devices: 34.3 us -> 31.6 us
    ppermute x1, waiting for transfers between devices: 0.01 us -> 4.51 us  [body(): far = lax.ppermute(own[0], 'row', far_pairs)]
    ppermute x1, waiting for transfers between devices: 5.52 us -> 1.37 us  [body(): far_part = lax.ppermute(own_part, 'row', far_pairs)]
    all_to_all x1, waiting for transfers between devices: 13.5 us -> 9.4 us  [body(): lax.all_to_all(piece, 'ma', split_axis=0, concat_axis=0, tiled=True)]
    unnamed x32 -> x38, local copies, waits for them, and re-layouts: 4.03 us -> 8.05 us
    all_to_all x1, blocking collectives: 19.4 us -> 15.8 us  [deliver(): lax.all_to_all(summed, 'ma', split_axis=0, concat_axis=0, tiled=True)]
    ppermute x3, waiting for transfers between devices: 0.01 us -> 2.78 us  [launch(): others.append(lax.ppermute(send, 'row', core_pairs))]
    all_to_all x1, blocking collectives: 17.6 us -> 19.8 us  [body(): lax.all_to_all(piece, 'ma', split_axis=0, concat_axis=0, tiled=True)]
  transfers between devices with their start and end apart: 14 -> 14, of which waited for: 5 -> 8; matrix products, arithmetic and copies ran while one was open for 1% -> 1% of each run, Pallas kernels for 20% -> 20%
where the time goes in v8:
time: 160 us; the launch traced here: 158 us
  Pallas kernels  62.1 us (39%)
  blocking collectives  35.6 us (22%)
  waiting for transfers between devices  31.6 us (20%)
  starting transfers between devices  18 us (11%)
  local copies, waits for them, and re-layouts  9.08 us (6%)
  other arithmetic  1.74 us (1%)
    pallas_call x3, Pallas kernels, synth(): pl.pallas_call(functools.partial(synth_kernel, first), grid_spec=pltpu.Pr...  26.3 us
    all_to_all x1, blocking collectives, body(): lax.all_to_all(piece, 'ma', split_axis=0, concat_axis=0, tiled=True)  19.8 us
    all_to_all x1, blocking collectives, deliver(): lax.all_to_all(summed, 'ma', split_axis=0, concat_axis=0, tiled=True)  15.8 us
    pallas_call x1, Pallas kernels, cycle_work(): pl.pallas_call(functools.partial(cycle_kernel, groups, sizes), grid_spec=...  14.2 us
    pallas_call x2, Pallas kernels, adjoint(): pl.pallas_call(functools.partial(adjoint_kernel, first), grid_spec=pltpu....  13.8 us
    ppermute x3, waiting for transfers between devices, pass_on(): incoming.append(lax.ppermute(outgoing[chunk], 'row', far_pairs))  11.5 us
    all_to_all x1, waiting for transfers between devices, body(): lax.all_to_all(piece, 'ma', split_axis=0, concat_axis=0, tiled=True)  9.4 us
    unnamed x38, local copies, waits for them, and re-layouts  8.05 us
  transfers between devices with their start and end apart: 14, of which 8 were waited for; matrix products, arithmetic and copies ran while one was open for 1% of the time, Pallas kernels for 20%

profile of v8, /device:TPU:0, one launch (start us, length us, event | category | flops | bytes accessed | tf_op | source)
XLA Modules:
  0.0 158.3 jit_solution(18402142936737771023)
XLA Ops:
  0.6 3.1 %filter_weights.1 = (bf16[512,256]{1,0:T(8,128)(2,1)}, bf16[256,512]{1,0:T(8,128)(2,1)}) custom-call(s32[64]{0:T(128)} %node_ref.1, f32[64]{0:T(128)} %radial_ref.1, f32[64,512]{1,0:T(8,128)} %alpha_ref.1, f32[64,512]{1,0:T(8,128)} %beta_ref.1), custom_call_target="tpu_custom_call" | custom-call | tf_op jit(solution)/shard_map/filter_weights/pallas_call | solution.py:117
  3.7 7.4 %synth.4 = (f32[2,8,64,256]{3,2,1,0:T(8,128)}, f32[2,8,64,256]{3,2,1,0:T(8,128)}) custom-call(s32[2048]{0:T(1024)} %order_ref.9, s32[2]{0:T(128)} %pad_add_fusion.where_ref.token_ref, f32[2,256,512]{2,1,0:T(8,128)} %coeffs_ref.5, bf16[512,256]{1,0:T(8,128)(2,1)} %get-tuple-element.29.weight_ref, bf16[256,32,512]{2,1,0:T(8,128)(2,1)} %legendre_ref.9), custom_call_target="tpu_custom_call" | custom-call | flops 2147483648 | bytes 4194304 | tf_op jit(solution)/shard_map/synth/pallas_call | solution.py:188
  11.5 9.8 %synth.3 = (f32[2,8,96,256]{3,2,1,0:T(8,128)}, f32[2,8,96,256]{3,2,1,0:T(8,128)}) custom-call(s32[2048]{0:T(1024)} %order_ref.9, s32[2]{0:T(128)} %pad_add_fusion.where_ref.token_ref, f32[2,256,512]{2,1,0:T(8,128)} %coeffs_ref.5, bf16[512,256]{1,0:T(8,128)(2,1)} %get-tuple-element.29.weight_ref, bf16[256,32,512]{2,1,0:T(8,128)(2,1)} %legendre_ref.9), custom_call_target="tpu_custom_call" | custom-call | flops 3221225472 | bytes 6291456 | tf_op jit(solution)/shard_map/synth/pallas_call | solution.py:188
  22.1 2.8 %collective-permute-done.other_ref.refs_4_ = f32[2,8,96,256]{3,2,1,0:T(8,128)S(1)} collective-permute-done((f32[2,8,96,256]{3,2,1,0:T(8,128)}, f32[2,8,96,256]{3,2,1,0:T(8,128)S(1)}, u32[]{:S(2)}, u32[]{:S(2)}) %collective-permute-start) | collective-permute-done | bytes 1572896 | tf_op jit(solution)/shard_map/ppermute | solution.py:621
  25.5 2.7 %collective-permute-start.3 = (bf16[8,96,256]{2,1,0:T(8,128)(2,1)S(1)}, bf16[8,96,256]{2,1,0:T(8,128)(2,1)S(1)}, u32[]{:S(2)}, u32[]{:S(2)}) collective-permute-start(bf16[8,96,256]{2,1,0:T(8,128)(2,1)S(1)} %core_sum.4), channel_id=1, source_target_pairs={{0,16},{8,24},{16,0},{24,8},{1,17},{9,25},{17,1},{25,9},{2,18},{10... | collective-permute-start | bytes 1179656 | tf_op jit(solution)/shard_map/ppermute | solution.py:625
  28.4 9.2 %synth.5 = (f32[2,8,96,256]{3,2,1,0:T(8,128)S(1)}, f32[2,8,96,256]{3,2,1,0:T(8,128)}) custom-call(s32[2048]{0:T(1024)S(1)} %copy-done.3, s32[2]{0:T(128)S(1)} %copy-done.4, f32[2,256,512]{2,1,0:T(8,128)S(1)} %copy-done.1, bf16[512,256]{1,0:T(8,128)(2,1)S(1)} %copy-done.2, bf16[256,32,512]{2,1,0:T(8,128)(2,1)} %legendre_ref.9), custom_call_target="tpu_custom_call" | custom-call | flops 3221225472 | bytes 6291456 | tf_op jit(solution)/shard_map/synth/pallas_call | solution.py:188
  38.8 4.7 %collective-permute-done.2.refs_2_ = bf16[8,64,256]{2,1,0:T(8,128)(2,1)S(1)} collective-permute-done((bf16[8,64,256]{2,1,0:T(8,128)(2,1)S(1)}, bf16[8,64,256]{2,1,0:T(8,128)(2,1)S(1)}, u32[]{:S(2)}, u32[]{:S(2)}) %collective-permute-start.2) | collective-permute-done | bytes 262176 | tf_op jit(solution)/shard_map/ppermute | solution.py:625
  43.5 1.5 full_sum.2
  45.1 6.0 %all-to-all-start = ((bf16[8,160,256]{2,1,0:T(8,128)(2,1)}), bf16[8,160,256]{2,1,0:T(8,128)(2,1)}, u32[]{:S(2)}, u32[]{:S(2)}) async-start(bf16[8,160,256]{2,1,0:T(8,128)(2,1)} %full_sum.2), calls=%async_computation | async-start | bytes 1310720 | tf_op jit(solution)/shard_map/all_to_all | solution.py:629
  51.1 1.4 copy-done.15
  53.9 1.5 collective-permute-start.5
  57.6 6.8 %collective-permute-done.5.refs_2_ = bf16[8,96,256]{2,1,0:T(8,128)(2,1)S(1)} collective-permute-done((bf16[8,96,256]{2,1,0:T(8,128)(2,1)}, bf16[8,96,256]{2,1,0:T(8,128)(2,1)S(1)}, u32[]{:S(2)}, u32[]{:S(2)}) %collective-permute-start.5) | collective-permute-done | bytes 393248 | tf_op jit(solution)/shard_map/ppermute | solution.py:625
  66.1 1.4 copy-done.16
  68.2 15.8 %all_to_all.20.refs_1_ = bf16[8,96,256]{2,1,0:T(8,128)(2,1)S(1)} all-to-all(bf16[8,96,256]{2,1,0:T(8,128)(2,1)S(1)} %full_sum.3), channel_id=1, replica_groups=mesh['row'=4,'ma'=8] {'ma'}, dimensions={0} | all-to-all | bytes 786432 | tf_op jit(solution)/shard_map/all_to_all | solution.py:629
  86.3 14.2 %cycle_work.1 = (bf16[8,160,256]{2,1,0:T(8,128)(2,1)S(1)}, bf16[8,96,256]{2,1,0:T(8,128)(2,1)}) custom-call(s32[4]{0:T(128)S(1)} %copy-done.10, s32[2]{0:T(128)S(1)} %copy-done.4, f32[4]{0:T(128)S(1)} %copy-done.11, bf16[8,160,256]{2,1,0:T(8,128)(2,1)} %all-to-all-done.refs_0_, bf16[8,96,256]{2,1,0:T(8,128)(2,1)S(1)} %all_to_all.20.refs_1_, ...), custom_call_target="tpu_custom_call" | custom-call | flops 4294967296 | bytes 8388608 | tf_op jit(solution)/shard_map/cycle_work/pallas_call | solution.py:436
  100.5 19.8 %all_to_all.21.own_ref = bf16[8,160,256]{2,1,0:T(8,128)(2,1)S(1)} all-to-all(bf16[8,160,256]{2,1,0:T(8,128)(2,1)S(1)} %get-tuple-element.46), channel_id=1, replica_groups=mesh['row'=4,'ma'=8] {'ma'}, dimensions={0} | all-to-all | bytes 1310720 | tf_op jit(solution)/shard_map/all_to_all | solution.py:652
  120.3 3.5 %all-to-all-start.3 = ((bf16[8,96,256]{2,1,0:T(8,128)(2,1)}), bf16[8,96,256]{2,1,0:T(8,128)(2,1)S(1)}, u32[]{:S(2)}, u32[]{:S(2)}) async-start(bf16[8,96,256]{2,1,0:T(8,128)(2,1)} %get-tuple-element.47), calls=%async_computation.3 | async-start | bytes 786432 | tf_op jit(solution)/shard_map/all_to_all | solution.py:652
  123.8 1.6 %collective-permute-start.6 = (bf16[8,160,256]{2,1,0:T(8,128)(2,1)S(1)}, bf16[8,160,256]{2,1,0:T(8,128)(2,1)S(1)}, u32[]{:S(2)}, u32[]{:S(2)}) collective-permute-start(bf16[8,160,256]{2,1,0:T(8,128)(2,1)S(1)} %all_to_all.21.own_ref), channel_id=1, source_target_pairs={{0,16},{8,24},{16,0},{24,8},{1,17},{9,25},{17,1},{25,9},{2,18},{10... | collective-permute-start | bytes 1966088 | tf_op jit(solution)/shard_map/ppermute | solution.py:654
  125.3 9.4 %all-to-all-done.3.own_ref = bf16[8,96,256]{2,1,0:T(8,128)(2,1)S(1)} async-done(((bf16[8,96,256]{2,1,0:T(8,128)(2,1)}), bf16[8,96,256]{2,1,0:T(8,128)(2,1)S(1)}, u32[]{:S(2)}, u32[]{:S(2)}) %all-to-all-start.3) | async-done | bytes 393248 | tf_op jit(solution)/shard_map/all_to_all | solution.py:652
  134.7 4.5 %collective-permute-done.6.far_ref = bf16[8,160,256]{2,1,0:T(8,128)(2,1)S(1)} collective-permute-done((bf16[8,160,256]{2,1,0:T(8,128)(2,1)S(1)}, bf16[8,160,256]{2,1,0:T(8,128)(2,1)S(1)}, u32[]{:S(2)}, u32[]{:S(2)}) %collective-permute-start.6) | collective-permute-done | bytes 655392 | tf_op jit(solution)/shard_map/ppermute | solution.py:654
  139.3 1.5 collective-permute-start.8
  141.4 8.1 %adjoint.2.refs_0_ = f32[2,256,512]{2,1,0:T(8,128)} custom-call(s32[2048]{0:T(1024)S(1)} %copy-done.3, s32[2]{0:T(128)S(1)} %copy-done.4, bf16[8,160,256]{2,1,0:T(8,128)(2,1)S(1)} %all_to_all.21.own_ref, bf16[8,160,256]{2,1,0:T(8,128)(2,1)S(1)} %collective-permute-done.9.core_ref, bf16[8,160,256]{2,1,0:T(8,128)(2,1)S(1)} %collective-permute-done.6.far_ref, ...), custom_call_target="tpu_custom_call" | custom-call | flops 2684354560 | bytes 7864320 | tf_op jit(solution)/shard_map/adjoint/pallas_call | solution.py:538
  150.8 1.7 %collective-permute-done.11.corner_ref = bf16[8,96,256]{2,1,0:T(8,128)(2,1)S(1)} collective-permute-done((bf16[8,96,256]{2,1,0:T(8,128)(2,1)S(1)}, bf16[8,96,256]{2,1,0:T(8,128)(2,1)S(1)}, u32[]{:S(2)}, u32[]{:S(2)}) %collective-permute-start.11) | collective-permute-done | bytes 393248 | tf_op jit(solution)/shard_map/ppermute | solution.py:663
  152.5 5.8 %adjoint.3 = f32[2,256,512]{2,1,0:T(8,128)} custom-call(s32[2048]{0:T(1024)S(1)} %copy-done.3, s32[2]{0:T(128)S(1)} %copy-done.4, bf16[8,96,256]{2,1,0:T(8,128)(2,1)S(1)} %all-to-all-done.3.own_ref, bf16[8,96,256]{2,1,0:T(8,128)(2,1)S(1)} %collective-permute-done.7.core_ref, ...), custom_call_target="tpu_custom_call", output_to_operand_aliasing={{}: (8, {})} | custom-call | flops 1610612736 | bytes 4718592 | tf_op jit(solution)/shard_map/adjoint/pallas_call | solution.py:538
  (64 shorter events, 14.1 us)
Async XLA Ops:
  11.0 10.5 %copy-start.4 = (s32[2]{0:T(128)S(1)}, s32[2]{0:T(128)}, u32[]{:S(2)}) copy-start(s32[2]{0:T(128)} %pad_add_fusion.where_ref.token_ref) | copy-start | bytes 28
  11.0 10.5 %copy-start.7 = (f32[2,8,64,256]{3,2,1,0:T(8,128)S(1)}, f32[2,8,64,256]{3,2,1,0:T(8,128)}, u32[]{:S(2)}) copy-start(f32[2,8,64,256]{3,2,1,0:T(8,128)} %get-tuple-element.32.keep_ref.refs_0_) | copy-start | bytes 3145732
  11.0 10.5 %collective-permute-start.1 = (f32[2,8,64,256]{3,2,1,0:T(8,128)}, f32[2,8,64,256]{3,2,1,0:T(8,128)S(1)}, u32[]{:S(2)}, u32[]{:S(2)}) collective-permute-start(f32[2,8,64,256]{3,2,1,0:T(8,128)} %get-tuple-element.33), channel_id=1, source_target_pairs={{0,8},{8,0},{16,24},{24,16},{1,9},{9,1},{17,25},{25,17},{2,10},{10... | collective-permute-start | bytes 3145736 | tf_op jit(solution)/shard_map/ppermute | solution.py:621
  21.3 3.6 %collective-permute-start = (f32[2,8,96,256]{3,2,1,0:T(8,128)}, f32[2,8,96,256]{3,2,1,0:T(8,128)S(1)}, u32[]{:S(2)}, u32[]{:S(2)}) collective-permute-start(f32[2,8,96,256]{3,2,1,0:T(8,128)} %get-tuple-element.31), channel_id=1, source_target_pairs={{0,8},{8,0},{16,24},{24,16},{1,9},{9,1},{17,25},{25,17},{2,10},{10... | collective-permute-start | bytes 4718600 | tf_op jit(solution)/shard_map/ppermute | solution.py:621
  21.5 3.4 %copy-start.17 = (f32[2,8,96,256]{3,2,1,0:T(8,128)S(1)}, f32[2,8,96,256]{3,2,1,0:T(8,128)}, u32[]{:S(2)}) copy-start(f32[2,8,96,256]{3,2,1,0:T(8,128)} %get-tuple-element.30.keep_ref.refs_3_) | copy-start | bytes 4718596
  22.1 6.3 %copy-start.1 = (f32[2,256,512]{2,1,0:T(8,128)S(1)}, f32[2,256,512]{2,1,0:T(8,128)}, u32[]{:S(2)}) copy-start(f32[2,256,512]{2,1,0:T(8,128)} %coeffs_ref.5) | copy-start | bytes 3145732
  22.1 6.2 %copy-start.2 = (bf16[512,256]{1,0:T(8,128)(2,1)S(1)}, bf16[512,256]{1,0:T(8,128)(2,1)}, u32[]{:S(2)}) copy-start(bf16[512,256]{1,0:T(8,128)(2,1)} %get-tuple-element.29.weight_ref) | copy-start | bytes 786436
  22.1 6.2 %copy-start.3 = (s32[2048]{0:T(1024)S(1)}, s32[2048]{0:T(1024)}, u32[]{:S(2)}) copy-start(s32[2048]{0:T(1024)} %order_ref.9) | copy-start | bytes 24580
  25.5 18.0 %collective-permute-start.3 = (bf16[8,96,256]{2,1,0:T(8,128)(2,1)S(1)}, bf16[8,96,256]{2,1,0:T(8,128)(2,1)S(1)}, u32[]{:S(2)}, u32[]{:S(2)}) collective-permute-start(bf16[8,96,256]{2,1,0:T(8,128)(2,1)S(1)} %core_sum.4), channel_id=1, source_target_pairs={{0,16},{8,24},{16,0},{24,8},{1,17},{9,25},{17,1},{25,9},{2,18},{10... | collective-permute-start | bytes 1179656 | tf_op jit(solution)/shard_map/ppermute | solution.py:625
  28.3 15.2 %collective-permute-start.2 = (bf16[8,64,256]{2,1,0:T(8,128)(2,1)S(1)}, bf16[8,64,256]{2,1,0:T(8,128)(2,1)S(1)}, u32[]{:S(2)}, u32[]{:S(2)}) collective-permute-start(bf16[8,64,256]{2,1,0:T(8,128)(2,1)S(1)} %core_sum.3), channel_id=1, source_target_pairs={{0,16},{8,24},{16,0},{24,8},{1,17},{9,25},{17,1},{25,9},{2,18},{10... | collective-permute-start | bytes 786440 | tf_op jit(solution)/shard_map/ppermute | solution.py:625
  38.8 12.3 %collective-permute-start.4 = (f32[2,8,96,256]{3,2,1,0:T(8,128)}, f32[2,8,96,256]{3,2,1,0:T(8,128)S(1)}, u32[]{:S(2)}, u32[]{:S(2)}) collective-permute-start(f32[2,8,96,256]{3,2,1,0:T(8,128)} %get-tuple-element.39), channel_id=1, source_target_pairs={{0,8},{8,0},{16,24},{24,16},{1,9},{9,1},{17,25},{25,17},{2,10},{10... | collective-permute-start | bytes 4718600 | tf_op jit(solution)/shard_map/ppermute | solution.py:621
  45.1 23.2 %all-to-all-start = ((bf16[8,160,256]{2,1,0:T(8,128)(2,1)}), bf16[8,160,256]{2,1,0:T(8,128)(2,1)}, u32[]{:S(2)}, u32[]{:S(2)}) async-start(bf16[8,160,256]{2,1,0:T(8,128)(2,1)} %full_sum.2), calls=%async_computation | async-start | bytes 1310720 | tf_op jit(solution)/shard_map/all_to_all | solution.py:629
  51.1 1.4 copy-start.15
  53.9 10.5 %collective-permute-start.5 = (bf16[8,96,256]{2,1,0:T(8,128)(2,1)}, bf16[8,96,256]{2,1,0:T(8,128)(2,1)S(1)}, u32[]{:S(2)}, u32[]{:S(2)}) collective-permute-start(bf16[8,96,256]{2,1,0:T(8,128)(2,1)} %core_sum.5), channel_id=1, source_target_pairs={{0,16},{8,24},{16,0},{24,8},{1,17},{9,25},{17,1},{25,9},{2,18},{10... | collective-permute-start | bytes 1179656 | tf_op jit(solution)/shard_map/ppermute | solution.py:625
  56.6 8.6 %copy-start.6 = (f32[2,8,96,256]{3,2,1,0:T(8,128)S(1)}, f32[2,8,96,256]{3,2,1,0:T(8,128)}, u32[]{:S(2)}) copy-start(f32[2,8,96,256]{3,2,1,0:T(8,128)} %copy-done.5) | copy-start | bytes 4718596
  67.6 16.5 %copy-start.10 = (s32[4]{0:T(128)S(1)}, s32[4]{0:T(128)}, u32[]{:S(2)}) copy-start(s32[4]{0:T(128)} %offset_ref.1) | copy-start | bytes 52
  100.5 40.9 %copy-start = (bf16[256,512]{1,0:T(8,128)(2,1)S(1)}, bf16[256,512]{1,0:T(8,128)(2,1)}, u32[]{:S(2)}) copy-start(bf16[256,512]{1,0:T(8,128)(2,1)} %get-tuple-element.50.weight_ref) | copy-start | bytes 786436
  120.3 14.5 %all-to-all-start.3 = ((bf16[8,96,256]{2,1,0:T(8,128)(2,1)}), bf16[8,96,256]{2,1,0:T(8,128)(2,1)S(1)}, u32[]{:S(2)}, u32[]{:S(2)}) async-start(bf16[8,96,256]{2,1,0:T(8,128)(2,1)} %get-tuple-element.47), calls=%async_computation.3 | async-start | bytes 786432 | tf_op jit(solution)/shard_map/all_to_all | solution.py:652
  123.8 15.5 %collective-permute-start.6 = (bf16[8,160,256]{2,1,0:T(8,128)(2,1)S(1)}, bf16[8,160,256]{2,1,0:T(8,128)(2,1)S(1)}, u32[]{:S(2)}, u32[]{:S(2)}) collective-permute-start(bf16[8,160,256]{2,1,0:T(8,128)(2,1)S(1)} %all_to_all.21.own_ref), channel_id=1, source_target_pairs={{0,16},{8,24},{16,0},{24,8},{1,17},{9,25},{17,1},{25,9},{2,18},{10... | collective-permute-start | bytes 1966088 | tf_op jit(solution)/shard_map/ppermute | solution.py:654
  125.3 15.7 %collective-permute-start.9 = (bf16[8,160,256]{2,1,0:T(8,128)(2,1)S(1)}, bf16[8,160,256]{2,1,0:T(8,128)(2,1)S(1)}, u32[]{:S(2)}, u32[]{:S(2)}) collective-permute-start(bf16[8,160,256]{2,1,0:T(8,128)(2,1)S(1)} %all_to_all.21.own_ref), channel_id=1, source_target_pairs={{0,8},{8,0},{16,24},{24,16},{1,9},{9,1},{17,25},{25,17},{2,10},{10... | collective-permute-start | bytes 1966088 | tf_op jit(solution)/shard_map/ppermute | solution.py:662
  139.3 2.1 %collective-permute-start.10 = (bf16[8,160,256]{2,1,0:T(8,128)(2,1)S(1)}, bf16[8,160,256]{2,1,0:T(8,128)(2,1)S(1)}, u32[]{:S(2)}, u32[]{:S(2)}) collective-permute-start(bf16[8,160,256]{2,1,0:T(8,128)(2,1)S(1)} %collective-permute-done.6.far_ref), channel_id=1, source_target_pairs={{0,8},{8,0},{16,24},{24,16},{1,9},{9,1},{17,25},{25,17},{2,10},{10... | collective-permute-start | bytes 1966088 | tf_op jit(solution)/shard_map/ppermute | solution.py:663
  139.3 11.5 %collective-permute-start.8 = (bf16[8,96,256]{2,1,0:T(8,128)(2,1)S(1)}, bf16[8,96,256]{2,1,0:T(8,128)(2,1)S(1)}, u32[]{:S(2)}, u32[]{:S(2)}) collective-permute-start(bf16[8,96,256]{2,1,0:T(8,128)(2,1)S(1)} %all-to-all-done.3.own_ref), channel_id=1, source_target_pairs={{0,16},{8,24},{16,0},{24,8},{1,17},{9,25},{17,1},{25,9},{2,18},{10... | collective-permute-start | bytes 1179656 | tf_op jit(solution)/shard_map/ppermute | solution.py:659
  140.8 10.0 %collective-permute-start.7 = (bf16[8,96,256]{2,1,0:T(8,128)(2,1)S(1)}, bf16[8,96,256]{2,1,0:T(8,128)(2,1)S(1)}, u32[]{:S(2)}, u32[]{:S(2)}) collective-permute-start(bf16[8,96,256]{2,1,0:T(8,128)(2,1)S(1)} %all-to-all-done.3.own_ref), channel_id=1, source_target_pairs={{0,8},{8,0},{16,24},{24,16},{1,9},{9,1},{17,25},{25,17},{2,10},{10... | collective-permute-start | bytes 1179656 | tf_op jit(solution)/shard_map/ppermute | solution.py:662
  150.8 1.7 %collective-permute-start.11 = (bf16[8,96,256]{2,1,0:T(8,128)(2,1)S(1)}, bf16[8,96,256]{2,1,0:T(8,128)(2,1)S(1)}, u32[]{:S(2)}, u32[]{:S(2)}) collective-permute-start(bf16[8,96,256]{2,1,0:T(8,128)(2,1)S(1)} %collective-permute-done.8.far_ref), channel_id=1, source_target_pairs={{0,8},{8,0},{16,24},{24,16},{1,9},{9,1},{17,25},{25,17},{2,10},{10... | collective-permute-start | bytes 1179656 | tf_op jit(solution)/shard_map/ppermute | solution.py:663
  (9 other events, 8.7 us)

commit v9 on v8

--- a/solution.py
+++ b/solution.py
@@ -613,7 +613,7 @@
 
     def launch(chunk, token):
         first = sum(counts[:chunk])
-        grant = 44 if chunk == 2 else 56
+        grant = 56
         keep, send = synth(
             first, counts[chunk], grant, orders, token, coeffs, synth_weight, legendre
         )
@@ -634,7 +634,7 @@
     pass_on(0, after(kept[1]))
     pass_on(1, after(outgoing[0]))
     if len(counts) == 3:
-        launch(2, after(outgoing[1]))
+        launch(2, after(outgoing[1], incoming[0]))
         pass_on(2, after(deliver(slice(0, 2), after(kept[2]))))
         tables = slot_tables(lax.optimization_barrier((orders, outgoing[2]))[0], device_count)
         places, sort, unsort, token = lax.optimization_barrier((*tables, where))
@@ -643,7 +643,7 @@
         deliver(slice(0, 1), after(outgoing[1]))
         deliver(slice(1, 2), after(outgoing[1]))
         places, sort, unsort = slot_tables(orders, device_count)
-    early = 32 * ((5 * units) // 8)
+    early = 32 * (units // 2)
     sizes = (early, local_orders - early)
     analysed = cycle_work(
         arrived, sizes, places, sort, unsort, cycle_offset, where, cycle_weight

time: 160 us -> 160 us (level)
  starting transfers between devices: 18 us -> 21 us
    ppermute x1, waiting for transfers between devices: 4.51 us -> 0.01 us  [body(): far = lax.ppermute(own[0], 'row', far_pairs)]
    ppermute x1, waiting for transfers between devices: 1.37 us -> 5.56 us  [body(): far_part = lax.ppermute(own_part, 'row', far_pairs)]
    all_to_all x1, waiting for transfers between devices: 9.4 us -> 12.5 us  [body(): lax.all_to_all(piece, 'ma', split_axis=0, concat_axis=0, tiled=True)]
    ppermute x3, waiting for transfers between devices: 2.78 us -> 0.01 us  [launch(): others.append(lax.ppermute(send, 'row', core_pairs))]
    ppermute x3, starting transfers between devices: 4.35 us -> 7.04 us  [pass_on(): incoming.append(lax.ppermute(outgoing[chunk], 'row', far_pairs))]
    all_to_all x1, blocking collectives: 19.8 us -> 17.1 us  [body(): lax.all_to_all(piece, 'ma', split_axis=0, concat_axis=0, tiled=True)]
    unnamed x38 -> x36, local copies, waits for them, and re-layouts: 8.05 us -> 6.87 us
  transfers between devices with their start and end apart: 14 -> 14, of which waited for: 8 -> 6; matrix products, arithmetic and copies ran while one was open for 1% -> 1% of each run, Pallas kernels for 20% -> 20%
where the time goes in v9:
time: 160 us; the launch traced here: 158 us
  Pallas kernels  61.7 us (39%)
  blocking collectives  34.1 us (21%)
  waiting for transfers between devices  31.8 us (20%)
  starting transfers between devices  21 us (13%)
  local copies, waits for them, and re-layouts  7.9 us (5%)
  other arithmetic  1.82 us (1%)
    pallas_call x3, Pallas kernels, synth(): pl.pallas_call(functools.partial(synth_kernel, first), grid_spec=pltpu.Pr...  26.8 us
    all_to_all x1, blocking collectives, body(): lax.all_to_all(piece, 'ma', split_axis=0, concat_axis=0, tiled=True)  17.1 us
    all_to_all x1, blocking collectives, deliver(): lax.all_to_all(summed, 'ma', split_axis=0, concat_axis=0, tiled=True)  16.9 us
    pallas_call x2, Pallas kernels, adjoint(): pl.pallas_call(functools.partial(adjoint_kernel, first), grid_spec=pltpu....  13.7 us
    pallas_call x1, Pallas kernels, cycle_work(): pl.pallas_call(functools.partial(cycle_kernel, groups, sizes), grid_spec=...  13.4 us
    all_to_all x1, waiting for transfers between devices, body(): lax.all_to_all(piece, 'ma', split_axis=0, concat_axis=0, tiled=True)  12.5 us
    ppermute x3, waiting for transfers between devices, pass_on(): incoming.append(lax.ppermute(outgoing[chunk], 'row', far_pairs))  11.5 us
    ppermute x3, starting transfers between devices, pass_on(): incoming.append(lax.ppermute(outgoing[chunk], 'row', far_pairs))  7.04 us
  transfers between devices with their start and end apart: 14, of which 6 were waited for; matrix products, arithmetic and copies ran while one was open for 1% of the time, Pallas kernels for 20%

profile of v9, /device:TPU:0, one launch (start us, length us, event | category | flops | bytes accessed | tf_op | source)
XLA Modules:
  0.0 158.4 jit_solution(3453662876729639414)
XLA Ops:
  0.7 3.1 %filter_weights.1 = (bf16[512,256]{1,0:T(8,128)(2,1)}, bf16[256,512]{1,0:T(8,128)(2,1)}) custom-call(s32[64]{0:T(128)} %node_ref.1, f32[64]{0:T(128)} %radial_ref.1, f32[64,512]{1,0:T(8,128)} %alpha_ref.1, f32[64,512]{1,0:T(8,128)} %beta_ref.1), custom_call_target="tpu_custom_call" | custom-call | tf_op jit(solution)/shard_map/filter_weights/pallas_call | solution.py:117
  3.7 7.3 %synth.4 = (f32[2,8,64,256]{3,2,1,0:T(8,128)}, f32[2,8,64,256]{3,2,1,0:T(8,128)}) custom-call(s32[2048]{0:T(1024)} %order_ref.9, s32[2]{0:T(128)} %pad_add_fusion.where_ref.token_ref, f32[2,256,512]{2,1,0:T(8,128)} %coeffs_ref.5, bf16[512,256]{1,0:T(8,128)(2,1)} %get-tuple-element.29.weight_ref, bf16[256,32,512]{2,1,0:T(8,128)(2,1)} %legendre_ref.9), custom_call_target="tpu_custom_call" | custom-call | flops 2147483648 | bytes 4194304 | tf_op jit(solution)/shard_map/synth/pallas_call | solution.py:188
  11.6 9.7 %synth.3 = (f32[2,8,96,256]{3,2,1,0:T(8,128)}, f32[2,8,96,256]{3,2,1,0:T(8,128)}) custom-call(s32[2048]{0:T(1024)} %order_ref.9, s32[2]{0:T(128)} %pad_add_fusion.where_ref.token_ref, f32[2,256,512]{2,1,0:T(8,128)} %coeffs_ref.5, bf16[512,256]{1,0:T(8,128)(2,1)} %get-tuple-element.29.weight_ref, bf16[256,32,512]{2,1,0:T(8,128)(2,1)} %legendre_ref.9), custom_call_target="tpu_custom_call" | custom-call | flops 3221225472 | bytes 6291456 | tf_op jit(solution)/shard_map/synth/pallas_call | solution.py:188
  22.1 2.9 %collective-permute-start.2 = (bf16[8,64,256]{2,1,0:T(8,128)(2,1)S(1)}, bf16[8,64,256]{2,1,0:T(8,128)(2,1)S(1)}, u32[]{:S(2)}, u32[]{:S(2)}) collective-permute-start(bf16[8,64,256]{2,1,0:T(8,128)(2,1)S(1)} %core_sum.3), channel_id=1, source_target_pairs={{0,16},{8,24},{16,0},{24,8},{1,17},{9,25},{17,1},{25,9},{2,18},{10... | collective-permute-start | bytes 786440 | tf_op jit(solution)/shard_map/ppermute | solution.py:625
  25.7 2.7 %collective-permute-start.3 = (bf16[8,96,256]{2,1,0:T(8,128)(2,1)S(1)}, bf16[8,96,256]{2,1,0:T(8,128)(2,1)S(1)}, u32[]{:S(2)}, u32[]{:S(2)}) collective-permute-start(bf16[8,96,256]{2,1,0:T(8,128)(2,1)S(1)} %core_sum.4), channel_id=1, source_target_pairs={{0,16},{8,24},{16,0},{24,8},{1,17},{9,25},{17,1},{25,9},{2,18},{10... | collective-permute-start | bytes 1179656 | tf_op jit(solution)/shard_map/ppermute | solution.py:625
  28.3 3.8 %collective-permute-done.2.refs_2_ = bf16[8,64,256]{2,1,0:T(8,128)(2,1)S(1)} collective-permute-done((bf16[8,64,256]{2,1,0:T(8,128)(2,1)S(1)}, bf16[8,64,256]{2,1,0:T(8,128)(2,1)S(1)}, u32[]{:S(2)}, u32[]{:S(2)}) %collective-permute-start.2) | collective-permute-done | bytes 262176 | tf_op jit(solution)/shard_map/ppermute | solution.py:625
  32.1 9.7 %synth.5 = (f32[2,8,96,256]{3,2,1,0:T(8,128)}, f32[2,8,96,256]{3,2,1,0:T(8,128)}) custom-call(s32[2048]{0:T(1024)} %order_ref.9, s32[2]{0:T(128)} %pad_add_fusion.where_ref.token_ref, f32[2,256,512]{2,1,0:T(8,128)} %coeffs_ref.5, bf16[512,256]{1,0:T(8,128)(2,1)} %get-tuple-element.29.weight_ref, bf16[256,32,512]{2,1,0:T(8,128)(2,1)} %legendre_ref.9), custom_call_target="tpu_custom_call" | custom-call | flops 3221225472 | bytes 6291456 | tf_op jit(solution)/shard_map/synth/pallas_call | solution.py:188
  41.9 1.5 full_sum.2
  43.4 6.4 %all-to-all-start = ((bf16[8,160,256]{2,1,0:T(8,128)(2,1)}), bf16[8,160,256]{2,1,0:T(8,128)(2,1)}, u32[]{:S(2)}, u32[]{:S(2)}) async-start(bf16[8,160,256]{2,1,0:T(8,128)(2,1)} %full_sum.2), calls=%async_computation | async-start | bytes 1310720 | tf_op jit(solution)/shard_map/all_to_all | solution.py:629
  49.8 1.4 copy-done.14
  52.6 1.5 collective-permute-start.5
  56.3 7.7 %collective-permute-done.5.refs_2_ = bf16[8,96,256]{2,1,0:T(8,128)(2,1)S(1)} collective-permute-done((bf16[8,96,256]{2,1,0:T(8,128)(2,1)}, bf16[8,96,256]{2,1,0:T(8,128)(2,1)S(1)}, u32[]{:S(2)}, u32[]{:S(2)}) %collective-permute-start.5) | collective-permute-done | bytes 393248 | tf_op jit(solution)/shard_map/ppermute | solution.py:625
  65.8 1.4 copy-done.15
  67.9 16.9 %all_to_all.20.refs_1_ = bf16[8,96,256]{2,1,0:T(8,128)(2,1)S(1)} all-to-all(bf16[8,96,256]{2,1,0:T(8,128)(2,1)S(1)} %full_sum.3), channel_id=1, replica_groups=mesh['row'=4,'ma'=8] {'ma'}, dimensions={0} | all-to-all | bytes 786432 | tf_op jit(solution)/shard_map/all_to_all | solution.py:629
  87.1 13.4 %cycle_work.1 = (bf16[8,128,256]{2,1,0:T(8,128)(2,1)S(1)}, bf16[8,128,256]{2,1,0:T(8,128)(2,1)S(1)}) custom-call(s32[4]{0:T(128)S(1)} %copy-done.10, s32[2]{0:T(128)S(1)} %copy-done.4, f32[4]{0:T(128)S(1)} %copy-done.11, bf16[8,160,256]{2,1,0:T(8,128)(2,1)} %all-to-all-done.refs_0_, bf16[8,96,256]{2,1,0:T(8,128)(2,1)S(1)} %all_to_all.20.refs_1_, ...), custom_call_target="tpu_custom_call" | custom-call | flops 4294967296 | bytes 8388608 | tf_op jit(solution)/shard_map/cycle_work/pallas_call | solution.py:436
  100.5 17.1 %all_to_all.21.own_ref = bf16[8,128,256]{2,1,0:T(8,128)(2,1)S(1)} all-to-all(bf16[8,128,256]{2,1,0:T(8,128)(2,1)S(1)} %get-tuple-element.46), channel_id=1, replica_groups=mesh['row'=4,'ma'=8] {'ma'}, dimensions={0} | all-to-all | bytes 1048576 | tf_op jit(solution)/shard_map/all_to_all | solution.py:652
  117.6 3.6 %all-to-all-start.3 = ((bf16[8,128,256]{2,1,0:T(8,128)(2,1)}), bf16[8,128,256]{2,1,0:T(8,128)(2,1)S(1)}, u32[]{:S(2)}, u32[]{:S(2)}) async-start(bf16[8,128,256]{2,1,0:T(8,128)(2,1)} %copy-done.1), calls=%async_computation.3 | async-start | bytes 1048576 | tf_op jit(solution)/shard_map/all_to_all | solution.py:652
  121.3 1.5 collective-permute-start.6
  122.8 12.5 %all-to-all-done.3.own_ref = bf16[8,128,256]{2,1,0:T(8,128)(2,1)S(1)} async-done(((bf16[8,128,256]{2,1,0:T(8,128)(2,1)}), bf16[8,128,256]{2,1,0:T(8,128)(2,1)S(1)}, u32[]{:S(2)}, u32[]{:S(2)}) %all-to-all-start.3) | async-done | bytes 524320 | tf_op jit(solution)/shard_map/all_to_all | solution.py:652
  135.3 1.5 collective-permute-start.8
  137.2 6.9 %adjoint.2.refs_0_ = f32[2,256,512]{2,1,0:T(8,128)} custom-call(s32[2048]{0:T(1024)S(1)} %copy-done.2, s32[2]{0:T(128)S(1)} %copy-done.4, bf16[8,128,256]{2,1,0:T(8,128)(2,1)S(1)} %all_to_all.21.own_ref, bf16[8,128,256]{2,1,0:T(8,128)(2,1)S(1)} %collective-permute-done.9.core_ref, bf16[8,128,256]{2,1,0:T(8,128)(2,1)S(1)} %collective-permute-done.6.far_ref, ...), custom_call_target="tpu_custom_call" | custom-call | flops 2147483648 | bytes 6291456 | tf_op jit(solution)/shard_map/adjoint/pallas_call | solution.py:538
  144.1 5.6 %collective-permute-done.8.far_ref = bf16[8,128,256]{2,1,0:T(8,128)(2,1)S(1)} collective-permute-done((bf16[8,128,256]{2,1,0:T(8,128)(2,1)S(1)}, bf16[8,128,256]{2,1,0:T(8,128)(2,1)S(1)}, u32[]{:S(2)}, u32[]{:S(2)}) %collective-permute-start.8) | collective-permute-done | bytes 524320 | tf_op jit(solution)/shard_map/ppermute | solution.py:659
  149.7 1.9 %collective-permute-done.11.corner_ref = bf16[8,128,256]{2,1,0:T(8,128)(2,1)S(1)} collective-permute-done((bf16[8,128,256]{2,1,0:T(8,128)(2,1)S(1)}, bf16[8,128,256]{2,1,0:T(8,128)(2,1)S(1)}, u32[]{:S(2)}, u32[]{:S(2)}) %collective-permute-start.11) | collective-permute-done | bytes 524320 | tf_op jit(solution)/shard_map/ppermute | solution.py:663
  151.6 6.8 %adjoint.3 = f32[2,256,512]{2,1,0:T(8,128)} custom-call(s32[2048]{0:T(1024)S(1)} %copy-done.2, s32[2]{0:T(128)S(1)} %copy-done.4, bf16[8,128,256]{2,1,0:T(8,128)(2,1)S(1)} %all-to-all-done.3.own_ref, bf16[8,128,256]{2,1,0:T(8,128)(2,1)S(1)} %collective-permute-done.7.core_ref, ...), custom_call_target="tpu_custom_call", output_to_operand_aliasing={{}: (8, {})} | custom-call | flops 2147483648 | bytes 6291456 | tf_op jit(solution)/shard_map/adjoint/pallas_call | solution.py:538
  (62 shorter events, 11.3 us)
Async XLA Ops:
  11.1 10.5 %copy-start.3 = (s32[2]{0:T(128)S(1)}, s32[2]{0:T(128)}, u32[]{:S(2)}) copy-start(s32[2]{0:T(128)} %pad_add_fusion.where_ref.token_ref) | copy-start | bytes 28
  11.1 10.5 %copy-start.7 = (f32[2,8,64,256]{3,2,1,0:T(8,128)S(1)}, f32[2,8,64,256]{3,2,1,0:T(8,128)}, u32[]{:S(2)}) copy-start(f32[2,8,64,256]{3,2,1,0:T(8,128)} %get-tuple-element.32.keep_ref.refs_0_) | copy-start | bytes 3145732
  11.1 10.4 %collective-permute-start.1 = (f32[2,8,64,256]{3,2,1,0:T(8,128)}, f32[2,8,64,256]{3,2,1,0:T(8,128)S(1)}, u32[]{:S(2)}, u32[]{:S(2)}) collective-permute-start(f32[2,8,64,256]{3,2,1,0:T(8,128)} %get-tuple-element.33), channel_id=1, source_target_pairs={{0,8},{8,0},{16,24},{24,16},{1,9},{9,1},{17,25},{25,17},{2,10},{10... | collective-permute-start | bytes 3145736 | tf_op jit(solution)/shard_map/ppermute | solution.py:621
  21.3 3.7 %collective-permute-start = (f32[2,8,96,256]{3,2,1,0:T(8,128)}, f32[2,8,96,256]{3,2,1,0:T(8,128)S(1)}, u32[]{:S(2)}, u32[]{:S(2)}) collective-permute-start(f32[2,8,96,256]{3,2,1,0:T(8,128)} %get-tuple-element.31), channel_id=1, source_target_pairs={{0,8},{8,0},{16,24},{24,16},{1,9},{9,1},{17,25},{25,17},{2,10},{10... | collective-permute-start | bytes 4718600 | tf_op jit(solution)/shard_map/ppermute | solution.py:621
  21.5 3.5 %copy-start.16 = (f32[2,8,96,256]{3,2,1,0:T(8,128)S(1)}, f32[2,8,96,256]{3,2,1,0:T(8,128)}, u32[]{:S(2)}) copy-start(f32[2,8,96,256]{3,2,1,0:T(8,128)} %get-tuple-element.30.keep_ref.refs_3_) | copy-start | bytes 4718596
  22.1 10.0 %collective-permute-start.2 = (bf16[8,64,256]{2,1,0:T(8,128)(2,1)S(1)}, bf16[8,64,256]{2,1,0:T(8,128)(2,1)S(1)}, u32[]{:S(2)}, u32[]{:S(2)}) collective-permute-start(bf16[8,64,256]{2,1,0:T(8,128)(2,1)S(1)} %core_sum.3), channel_id=1, source_target_pairs={{0,16},{8,24},{16,0},{24,8},{1,17},{9,25},{17,1},{25,9},{2,18},{10... | collective-permute-start | bytes 786440 | tf_op jit(solution)/shard_map/ppermute | solution.py:625
  25.6 16.2 %copy-start.4 = (s32[2]{0:T(128)S(1)}, s32[2]{0:T(128)}, u32[]{:S(2)}) copy-start(s32[2]{0:T(128)} %pad_add_fusion.where_ref.token_ref) | copy-start | bytes 28
  25.7 16.2 %collective-permute-start.3 = (bf16[8,96,256]{2,1,0:T(8,128)(2,1)S(1)}, bf16[8,96,256]{2,1,0:T(8,128)(2,1)S(1)}, u32[]{:S(2)}, u32[]{:S(2)}) collective-permute-start(bf16[8,96,256]{2,1,0:T(8,128)(2,1)S(1)} %core_sum.4), channel_id=1, source_target_pairs={{0,16},{8,24},{16,0},{24,8},{1,17},{9,25},{17,1},{25,9},{2,18},{10... | collective-permute-start | bytes 1179656 | tf_op jit(solution)/shard_map/ppermute | solution.py:625
  41.8 7.9 %collective-permute-start.4 = (f32[2,8,96,256]{3,2,1,0:T(8,128)}, f32[2,8,96,256]{3,2,1,0:T(8,128)S(1)}, u32[]{:S(2)}, u32[]{:S(2)}) collective-permute-start(f32[2,8,96,256]{3,2,1,0:T(8,128)} %get-tuple-element.39), channel_id=1, source_target_pairs={{0,8},{8,0},{16,24},{24,16},{1,9},{9,1},{17,25},{25,17},{2,10},{10... | collective-permute-start | bytes 4718600 | tf_op jit(solution)/shard_map/ppermute | solution.py:621
  43.4 24.5 %all-to-all-start = ((bf16[8,160,256]{2,1,0:T(8,128)(2,1)}), bf16[8,160,256]{2,1,0:T(8,128)(2,1)}, u32[]{:S(2)}, u32[]{:S(2)}) async-start(bf16[8,160,256]{2,1,0:T(8,128)(2,1)} %full_sum.2), calls=%async_computation | async-start | bytes 1310720 | tf_op jit(solution)/shard_map/all_to_all | solution.py:629
  49.8 4.3 %copy-start.2 = (s32[2048]{0:T(1024)S(1)}, s32[2048]{0:T(1024)}, u32[]{:S(2)}) copy-start(s32[2048]{0:T(1024)} %order_ref.9) | copy-start | bytes 24580
  49.8 1.4 copy-start.14
  52.6 11.4 %collective-permute-start.5 = (bf16[8,96,256]{2,1,0:T(8,128)(2,1)}, bf16[8,96,256]{2,1,0:T(8,128)(2,1)S(1)}, u32[]{:S(2)}, u32[]{:S(2)}) collective-permute-start(bf16[8,96,256]{2,1,0:T(8,128)(2,1)} %core_sum.5), channel_id=1, source_target_pairs={{0,16},{8,24},{16,0},{24,8},{1,17},{9,25},{17,1},{25,9},{2,18},{10... | collective-permute-start | bytes 1179656 | tf_op jit(solution)/shard_map/ppermute | solution.py:625
  55.2 9.5 %copy-start.6 = (f32[2,8,96,256]{3,2,1,0:T(8,128)S(1)}, f32[2,8,96,256]{3,2,1,0:T(8,128)}, u32[]{:S(2)}) copy-start(f32[2,8,96,256]{3,2,1,0:T(8,128)} %copy-done.5) | copy-start | bytes 4718596
  67.2 17.6 %copy-start.10 = (s32[4]{0:T(128)S(1)}, s32[4]{0:T(128)}, u32[]{:S(2)}) copy-start(s32[4]{0:T(128)} %offset_ref.1) | copy-start | bytes 52
  100.5 17.2 %copy-start.1 = (bf16[8,128,256]{2,1,0:T(8,128)(2,1)}, bf16[8,128,256]{2,1,0:T(8,128)(2,1)S(1)}, u32[]{:S(2)}) copy-start(bf16[8,128,256]{2,1,0:T(8,128)(2,1)S(1)} %get-tuple-element.47) | copy-start | bytes 1572868
  100.5 36.8 %copy-start = (bf16[256,512]{1,0:T(8,128)(2,1)S(1)}, bf16[256,512]{1,0:T(8,128)(2,1)}, u32[]{:S(2)}) copy-start(bf16[256,512]{1,0:T(8,128)(2,1)} %get-tuple-element.50.weight_ref) | copy-start | bytes 786436
  117.6 17.7 %all-to-all-start.3 = ((bf16[8,128,256]{2,1,0:T(8,128)(2,1)}), bf16[8,128,256]{2,1,0:T(8,128)(2,1)S(1)}, u32[]{:S(2)}, u32[]{:S(2)}) async-start(bf16[8,128,256]{2,1,0:T(8,128)(2,1)} %copy-done.1), calls=%async_computation.3 | async-start | bytes 1048576 | tf_op jit(solution)/shard_map/all_to_all | solution.py:652
  121.3 14.0 %collective-permute-start.6 = (bf16[8,128,256]{2,1,0:T(8,128)(2,1)S(1)}, bf16[8,128,256]{2,1,0:T(8,128)(2,1)S(1)}, u32[]{:S(2)}, u32[]{:S(2)}) collective-permute-start(bf16[8,128,256]{2,1,0:T(8,128)(2,1)S(1)} %all_to_all.21.own_ref), channel_id=1, source_target_pairs={{0,16},{8,24},{16,0},{24,8},{1,17},{9,25},{17,1},{25,9},{2,18},{10... | collective-permute-start | bytes 1572872 | tf_op jit(solution)/shard_map/ppermute | solution.py:654
  122.8 14.3 %collective-permute-start.9 = (bf16[8,128,256]{2,1,0:T(8,128)(2,1)S(1)}, bf16[8,128,256]{2,1,0:T(8,128)(2,1)S(1)}, u32[]{:S(2)}, u32[]{:S(2)}) collective-permute-start(bf16[8,128,256]{2,1,0:T(8,128)(2,1)S(1)} %all_to_all.21.own_ref), channel_id=1, source_target_pairs={{0,8},{8,0},{16,24},{24,16},{1,9},{9,1},{17,25},{25,17},{2,10},{10... | collective-permute-start | bytes 1572872 | tf_op jit(solution)/shard_map/ppermute | solution.py:662
  135.3 1.9 %collective-permute-start.10 = (bf16[8,128,256]{2,1,0:T(8,128)(2,1)S(1)}, bf16[8,128,256]{2,1,0:T(8,128)(2,1)S(1)}, u32[]{:S(2)}, u32[]{:S(2)}) collective-permute-start(bf16[8,128,256]{2,1,0:T(8,128)(2,1)S(1)} %collective-permute-done.6.far_ref), channel_id=1, source_target_pairs={{0,8},{8,0},{16,24},{24,16},{1,9},{9,1},{17,25},{25,17},{2,10},{10... | collective-permute-start | bytes 1572872 | tf_op jit(solution)/shard_map/ppermute | solution.py:663
  135.3 14.3 %collective-permute-start.8 = (bf16[8,128,256]{2,1,0:T(8,128)(2,1)S(1)}, bf16[8,128,256]{2,1,0:T(8,128)(2,1)S(1)}, u32[]{:S(2)}, u32[]{:S(2)}) collective-permute-start(bf16[8,128,256]{2,1,0:T(8,128)(2,1)S(1)} %all-to-all-done.3.own_ref), channel_id=1, source_target_pairs={{0,16},{8,24},{16,0},{24,8},{1,17},{9,25},{17,1},{25,9},{2,18},{10... | collective-permute-start | bytes 1572872 | tf_op jit(solution)/shard_map/ppermute | solution.py:659
  136.8 12.8 %collective-permute-start.7 = (bf16[8,128,256]{2,1,0:T(8,128)(2,1)S(1)}, bf16[8,128,256]{2,1,0:T(8,128)(2,1)S(1)}, u32[]{:S(2)}, u32[]{:S(2)}) collective-permute-start(bf16[8,128,256]{2,1,0:T(8,128)(2,1)S(1)} %all-to-all-done.3.own_ref), channel_id=1, source_target_pairs={{0,8},{8,0},{16,24},{24,16},{1,9},{9,1},{17,25},{25,17},{2,10},{10... | collective-permute-start | bytes 1572872 | tf_op jit(solution)/shard_map/ppermute | solution.py:662
  149.7 1.9 %collective-permute-start.11 = (bf16[8,128,256]{2,1,0:T(8,128)(2,1)S(1)}, bf16[8,128,256]{2,1,0:T(8,128)(2,1)S(1)}, u32[]{:S(2)}, u32[]{:S(2)}) collective-permute-start(bf16[8,128,256]{2,1,0:T(8,128)(2,1)S(1)} %collective-permute-done.8.far_ref), channel_id=1, source_target_pairs={{0,8},{8,0},{16,24},{24,16},{1,9},{9,1},{17,25},{25,17},{2,10},{10... | collective-permute-start | bytes 1572872 | tf_op jit(solution)/shard_map/ppermute | solution.py:663
  (8 other events, 7.5 us)

commit v10 on v7

--- a/solution.py
+++ b/solution.py
@@ -139,8 +139,8 @@
 ):
     keep_ref, send_ref, terms_even, terms_odd, sums_even, sums_odd = refs[-6:]
     step = pl.program_id(0)
-    row = where_ref[0]
-    base = where_ref[1] + first + step * SYNTH_BLOCK
+    row = where_ref[0] >> 12
+    base = (where_ref[0] & 4095) + first + step * SYNTH_BLOCK
     degrees = coeffs_ref.shape[2]
     cycles = legendre_ref.shape[1]
     owners = cycles // 4
@@ -232,6 +232,42 @@
     )(keep, other, order)
 
 
+def own_sum_kernel(keep_ref, other_ref, token_ref, out_ref):
+    out_ref[...] = keep_ref[0] + other_ref[0]
+
+
+def own_sum(keep, other, token):
+    shape = keep.shape[1:]
+    half = pl.BlockSpec((1,) + shape, lambda t: (0, 0, 0, 0))
+    return pl.pallas_call(
+        own_sum_kernel,
+        grid=(1,),
+        in_specs=[half, half, pl.BlockSpec(memory_space=pltpu.SMEM)],
+        out_specs=pl.BlockSpec(shape, lambda t: (0, 0, 0)),
+        out_shape=jax.ShapeDtypeStruct(shape, F32),
+        compiler_params=pltpu.CompilerParams(vmem_limit_bytes=16 * MIB),
+        cost_estimate=pl.CostEstimate(flops=10**7, bytes_accessed=MIB, transcendentals=0),
+        name="own_sum",
+    )(keep, other, token)
+
+
+def last_sum_kernel(own_ref, incoming_ref, token_ref, out_ref):
+    out_ref[...] = (own_ref[...] + incoming_ref[...].astype(F32)).astype(BF16)
+
+
+def last_sum(own, incoming, token):
+    return pl.pallas_call(
+        last_sum_kernel,
+        grid=(1,),
+        in_specs=[whole(own.shape), whole(own.shape), pl.BlockSpec(memory_space=pltpu.SMEM)],
+        out_specs=whole(own.shape),
+        out_shape=jax.ShapeDtypeStruct(own.shape, BF16),
+        compiler_params=pltpu.CompilerParams(vmem_limit_bytes=16 * MIB),
+        cost_estimate=pl.CostEstimate(flops=4 * 10**10, bytes_accessed=MIB, transcendentals=0),
+        name="last_sum",
+    )(own, incoming, token)
+
+
 def full_sum_kernel(token_ref, *refs):
     out_ref = refs[-1]
     start = 0
@@ -273,8 +309,8 @@
     spread_scr, gather_scr, sorted_scr, middle_scr, product_scr, back_scr, sems = refs[-7:]
     device_count, blocks = place_ref.shape[:2]
     lanes = pieces[0].shape[2] // 2
-    turned = offset_ref[where_ref[0]]
-    scale = weight_ref[where_ref[0]]
+    turned = offset_ref[where_ref[0] >> 12]
+    scale = weight_ref[where_ref[0] >> 12]
     lane = lax.broadcasted_iota(jnp.int32, (SIDE, lanes), 1)
 
     def spread_copy(block):
@@ -465,8 +501,8 @@
 ):
     out_ref, values_even, values_odd, terms_even, terms_odd = refs[-5:]
     step = pl.program_id(0)
-    row = where_ref[0]
-    base = where_ref[1] + first + step * BLOCK
+    row = where_ref[0] >> 12
+    base = (where_ref[0] & 4095) + first + step * BLOCK
     degrees = weight_ref.shape[1]
     cycles = legendre_ref.shape[1]
     owners = cycles // 4
@@ -595,7 +631,7 @@
     device_count = lax.axis_size("ma")
     row_count = lax.axis_size("row")
     local_orders = coeffs.shape[1]
-    where = jnp.stack([row_id, ma_id * local_orders]).astype(jnp.int32)
+    where = (row_id * 4096 + ma_id * local_orders).astype(jnp.int32).reshape(1)
     synth_weight, adjoint_weight = filter_weights(
         radius_index, radial_weight, alpha_table, beta_table
     )
@@ -634,8 +670,10 @@
         launch(2, after(outgoing[1]))
         pass_on(2, after(deliver(slice(0, 2), after(kept[2]))))
         tables = slot_tables(lax.optimization_barrier((orders, outgoing[2]))[0], device_count)
-        places, sort, unsort, token = lax.optimization_barrier((*tables, where))
-        deliver(slice(2, 3), token)
+        half = own_sum(kept[2], others[2], after(outgoing[2]))
+        places, sort, unsort, half, token = lax.optimization_barrier((*tables, half, where))
+        summed = last_sum(half, incoming[2], token)
+        arrived.append(lax.all_to_all(summed, "ma", split_axis=0, concat_axis=0, tiled=True))
     else:
         deliver(slice(0, 1), after(outgoing[1]))
         deliver(slice(1, 2), after(outgoing[1]))

time: 158 us -> 154 us (0.975)
  local copies, waits for them, and re-layouts: 4.45 us -> 1.28 us
    unnamed x32 -> x22, local copies, waits for them, and re-layouts: 4.03 us -> 0.85 us
    pallas_call x0 -> x2, Pallas kernels: none -> 2.5 us  [the longest x1 1.37 us: own_sum(): pl.pallas_call(own_sum_kernel, grid=(1,), in_specs=[half, half, pl.BlockS...]
    pallas_call x2 -> x1, Pallas kernels: 2.69 us -> 0.95 us  [full_sum(): pl.pallas_call(full_sum_kernel, grid=(1,), in_specs=specs, out_specs=pl.B...]
  transfers between devices with their start and end apart: 14 -> 14, of which waited for: 5 -> 5; matrix products, arithmetic and copies ran while one was open for 1% -> 1% of each run, Pallas kernels for 20% -> 21%
where the time goes in v10:
time: 154 us; the launch traced here: 152 us
  Pallas kernels  62.5 us (41%)
  blocking collectives  36.9 us (24%)
  waiting for transfers between devices  33 us (21%)
  starting transfers between devices  17.3 us (11%)
    pallas_call x3, Pallas kernels, synth(): pl.pallas_call(functools.partial(synth_kernel, first), grid_spec=pltpu.Pr...  26.6 us
    all_to_all x1, blocking collectives, body(): lax.all_to_all(summed, 'ma', split_axis=0, concat_axis=0, tiled=True)  19.4 us
    all_to_all x1, blocking collectives, body(): lax.all_to_all(piece, 'ma', split_axis=0, concat_axis=0, tiled=True)  17.6 us
    pallas_call x2, Pallas kernels, adjoint(): pl.pallas_call(functools.partial(adjoint_kernel, first), grid_spec=pltpu....  13.7 us
    all_to_all x1, waiting for transfers between devices, body(): lax.all_to_all(piece, 'ma', split_axis=0, concat_axis=0, tiled=True)  13.5 us
    pallas_call x1, Pallas kernels, cycle_work(): pl.pallas_call(functools.partial(cycle_kernel, groups, sizes), grid_spec=...  13.4 us
    ppermute x3, waiting for transfers between devices, pass_on(): incoming.append(lax.ppermute(outgoing[chunk], 'row', far_pairs))  10.8 us
    ppermute x3, starting transfers between devices, pass_on(): incoming.append(lax.ppermute(outgoing[chunk], 'row', far_pairs))  5.83 us
  transfers between devices with their start and end apart: 14, of which 5 were waited for; matrix products, arithmetic and copies ran while one was open for 1% of the time, Pallas kernels for 21%

profile of v10, /device:TPU:0, one launch (start us, length us, event | category | flops | bytes accessed | tf_op | source)
XLA Modules:
  0.0 152.3 jit_solution(8087904990405602903)
XLA Ops:
  0.0 3.1 %filter_weights.1 = (bf16[512,256]{1,0:T(8,128)(2,1)}, bf16[256,512]{1,0:T(8,128)(2,1)}) custom-call(s32[64]{0:T(128)} %node_ref.1, f32[64]{0:T(128)} %radial_ref.1, f32[64,512]{1,0:T(8,128)} %alpha_ref.1, f32[64,512]{1,0:T(8,128)} %beta_ref.1), custom_call_target="tpu_custom_call" | custom-call | tf_op jit(solution)/shard_map/filter_weights/pallas_call | solution.py:117
  3.1 7.3 %synth.4 = (f32[2,8,64,256]{3,2,1,0:T(8,128)}, f32[2,8,64,256]{3,2,1,0:T(8,128)}) custom-call(s32[2048]{0:T(1024)} %order_ref.9, s32[1]{0:T(128)} %bitcast.where_ref.token_ref, f32[2,256,512]{2,1,0:T(8,128)} %coeffs_ref.5, bf16[512,256]{1,0:T(8,128)(2,1)} %get-tuple-element.31.weight_ref, bf16[256,32,512]{2,1,0:T(8,128)(2,1)} %legendre_ref.9), custom_call_target="tpu_custom_call" | custom-call | flops 2147483648 | bytes 4194304 | tf_op jit(solution)/shard_map/synth/pallas_call | solution.py:187
  10.8 7.3 %synth.3 = (f32[2,8,64,256]{3,2,1,0:T(8,128)}, f32[2,8,64,256]{3,2,1,0:T(8,128)}) custom-call(s32[2048]{0:T(1024)} %order_ref.9, s32[1]{0:T(128)} %bitcast.where_ref.token_ref, f32[2,256,512]{2,1,0:T(8,128)} %coeffs_ref.5, bf16[512,256]{1,0:T(8,128)(2,1)} %get-tuple-element.31.weight_ref, bf16[256,32,512]{2,1,0:T(8,128)(2,1)} %legendre_ref.9), custom_call_target="tpu_custom_call" | custom-call | flops 2147483648 | bytes 4194304 | tf_op jit(solution)/shard_map/synth/pallas_call | solution.py:187
  18.4 2.9 %collective-permute-start.2 = (bf16[8,64,256]{2,1,0:T(8,128)(2,1)S(1)}, bf16[8,64,256]{2,1,0:T(8,128)(2,1)S(1)}, u32[]{:S(2)}, u32[]{:S(2)}) collective-permute-start(bf16[8,64,256]{2,1,0:T(8,128)(2,1)S(1)} %core_sum.3), channel_id=1, source_target_pairs={{0,16},{8,24},{16,0},{24,8},{1,17},{9,25},{17,1},{25,9},{2,18},{10... | collective-permute-start | bytes 786440 | tf_op jit(solution)/shard_map/ppermute | solution.py:658
  21.3 2.5 %collective-permute-start.3 = (bf16[8,64,256]{2,1,0:T(8,128)(2,1)S(1)}, bf16[8,64,256]{2,1,0:T(8,128)(2,1)S(1)}, u32[]{:S(2)}, u32[]{:S(2)}) collective-permute-start(bf16[8,64,256]{2,1,0:T(8,128)(2,1)S(1)} %core_sum.4), channel_id=1, source_target_pairs={{0,16},{8,24},{16,0},{24,8},{1,17},{9,25},{17,1},{25,9},{2,18},{10... | collective-permute-start | bytes 786440 | tf_op jit(solution)/shard_map/ppermute | solution.py:658
  23.8 12.0 %synth.5 = (f32[2,8,128,256]{3,2,1,0:T(8,128)}, f32[2,8,128,256]{3,2,1,0:T(8,128)}) custom-call(s32[2048]{0:T(1024)} %order_ref.9, s32[1]{0:T(128)} %bitcast.where_ref.token_ref, f32[2,256,512]{2,1,0:T(8,128)} %coeffs_ref.5, bf16[512,256]{1,0:T(8,128)(2,1)} %get-tuple-element.31.weight_ref, bf16[256,32,512]{2,1,0:T(8,128)(2,1)} %legendre_ref.9), custom_call_target="tpu_custom_call" | custom-call | flops 4294967296 | bytes 8388608 | tf_op jit(solution)/shard_map/synth/pallas_call | solution.py:187
  35.8 0.9 full_sum.1
  36.8 5.8 %all-to-all-start = ((bf16[8,128,256]{2,1,0:T(8,128)(2,1)}), bf16[8,128,256]{2,1,0:T(8,128)(2,1)}, u32[]{:S(2)}, u32[]{:S(2)}) async-start(bf16[8,128,256]{2,1,0:T(8,128)(2,1)} %full_sum.1), calls=%async_computation | async-start | bytes 1048576 | tf_op jit(solution)/shard_map/all_to_all | solution.py:662
  42.6 2.2 %core_sum.5 = bf16[8,128,256]{2,1,0:T(8,128)(2,1)} custom-call(f32[2,8,128,256]{3,2,1,0:T(8,128)S(1)} %copy-done, f32[2,8,128,256]{3,2,1,0:T(8,128)} %collective-permute-done.4.other_ref, s32[1]{0:T(128)} %bitcast.where_ref.token_ref), custom_call_target="tpu_custom_call" | custom-call | flops 40000000000 | bytes 1048576 | tf_op jit(solution)/shard_map/core_sum/pallas_call | solution.py:223
  45.9 1.4 own_sum.1.own_ref
  47.3 0.7 fusion.1
  48.4 10.8 %collective-permute-done.5.incoming_ref = bf16[8,128,256]{2,1,0:T(8,128)(2,1)} collective-permute-done((bf16[8,128,256]{2,1,0:T(8,128)(2,1)}, bf16[8,128,256]{2,1,0:T(8,128)(2,1)}, u32[]{:S(2)}, u32[]{:S(2)}) %collective-permute-start.5) | collective-permute-done | bytes 524320 | tf_op jit(solution)/shard_map/ppermute | solution.py:658
  59.1 1.1 last_sum.1
  60.3 0.8 copy-done.3
  61.1 19.4 %all_to_all.20.refs_1_ = bf16[8,128,256]{2,1,0:T(8,128)(2,1)S(1)} all-to-all(bf16[8,128,256]{2,1,0:T(8,128)(2,1)} %copy-done.3), channel_id=1, replica_groups=mesh['row'=4,'ma'=8] {'ma'}, dimensions={0} | all-to-all | bytes 1048576 | tf_op jit(solution)/shard_map/all_to_all | solution.py:676
  80.5 13.4 %cycle_work.1 = (bf16[8,128,256]{2,1,0:T(8,128)(2,1)S(1)}, bf16[8,128,256]{2,1,0:T(8,128)(2,1)S(1)}) custom-call(s32[4]{0:T(128)S(1)} %copy-done.7, s32[1]{0:T(128)} %bitcast.where_ref.token_ref, f32[4]{0:T(128)S(1)} %copy-done.8, bf16[8,128,256]{2,1,0:T(8,128)(2,1)} %all-to-all-done.refs_0_, bf16[8,128,256]{2,1,0:T(8,128)(2,1)S(1)} %all_to_all.20.refs_1_, ...), custom_call_target="tpu_custom_call" | custom-call | flops 4294967296 | bytes 8388608 | tf_op jit(solution)/shard_map/cycle_work/pallas_call | solution.py:470
  93.9 17.6 %all_to_all.21.own_ref = bf16[8,128,256]{2,1,0:T(8,128)(2,1)S(1)} all-to-all(bf16[8,128,256]{2,1,0:T(8,128)(2,1)S(1)} %get-tuple-element.50), channel_id=1, replica_groups=mesh['row'=4,'ma'=8] {'ma'}, dimensions={0} | all-to-all | bytes 1048576 | tf_op jit(solution)/shard_map/all_to_all | solution.py:687
  111.5 3.6 %all-to-all-start.3 = ((bf16[8,128,256]{2,1,0:T(8,128)(2,1)}), bf16[8,128,256]{2,1,0:T(8,128)(2,1)S(1)}, u32[]{:S(2)}, u32[]{:S(2)}) async-start(bf16[8,128,256]{2,1,0:T(8,128)(2,1)} %copy-done.2), calls=%async_computation.3 | async-start | bytes 1048576 | tf_op jit(solution)/shard_map/all_to_all | solution.py:687
  115.6 13.5 %all-to-all-done.3.own_ref = bf16[8,128,256]{2,1,0:T(8,128)(2,1)S(1)} async-done(((bf16[8,128,256]{2,1,0:T(8,128)(2,1)}), bf16[8,128,256]{2,1,0:T(8,128)(2,1)S(1)}, u32[]{:S(2)}, u32[]{:S(2)}) %all-to-all-start.3) | async-done | bytes 524320 | tf_op jit(solution)/shard_map/all_to_all | solution.py:687
  129.9 1.2 collective-permute-done.10.corner_ref
  131.1 6.8 %adjoint.2.refs_0_ = f32[2,256,512]{2,1,0:T(8,128)} custom-call(s32[2048]{0:T(1024)S(1)} %copy-done.4, s32[1]{0:T(128)} %bitcast.where_ref.token_ref, bf16[8,128,256]{2,1,0:T(8,128)(2,1)S(1)} %all_to_all.21.own_ref, bf16[8,128,256]{2,1,0:T(8,128)(2,1)S(1)} %collective-permute-done.9.core_ref, bf16[8,128,256]{2,1,0:T(8,128)(2,1)S(1)} %collective-permute-done.6.far_ref, ...), custom_call_target="tpu_custom_call" | custom-call | flops 2147483648 | bytes 6291456 | tf_op jit(solution)/shard_map/adjoint/pallas_call | solution.py:572
  137.9 5.6 %collective-permute-done.8.far_ref = bf16[8,128,256]{2,1,0:T(8,128)(2,1)S(1)} collective-permute-done((bf16[8,128,256]{2,1,0:T(8,128)(2,1)S(1)}, bf16[8,128,256]{2,1,0:T(8,128)(2,1)S(1)}, u32[]{:S(2)}, u32[]{:S(2)}) %collective-permute-start.8) | collective-permute-done | bytes 524320 | tf_op jit(solution)/shard_map/ppermute | solution.py:694
  143.5 1.9 %collective-permute-done.11.corner_ref = bf16[8,128,256]{2,1,0:T(8,128)(2,1)S(1)} collective-permute-done((bf16[8,128,256]{2,1,0:T(8,128)(2,1)S(1)}, bf16[8,128,256]{2,1,0:T(8,128)(2,1)S(1)}, u32[]{:S(2)}, u32[]{:S(2)}) %collective-permute-start.11) | collective-permute-done | bytes 524320 | tf_op jit(solution)/shard_map/ppermute | solution.py:698
  145.4 6.9 %adjoint.3 = f32[2,256,512]{2,1,0:T(8,128)} custom-call(s32[2048]{0:T(1024)S(1)} %copy-done.4, s32[1]{0:T(128)} %bitcast.where_ref.token_ref, bf16[8,128,256]{2,1,0:T(8,128)(2,1)S(1)} %all-to-all-done.3.own_ref, bf16[8,128,256]{2,1,0:T(8,128)(2,1)S(1)} %collective-permute-done.7.core_ref, ...), custom_call_target="tpu_custom_call", output_to_operand_aliasing={{}: (8, {})} | custom-call | flops 2147483648 | bytes 6291456 | tf_op jit(solution)/shard_map/adjoint/pallas_call | solution.py:572
  (48 shorter events, 3.5 us)
Async XLA Ops:
  10.4 7.9 %copy-start.5 = (f32[2,8,64,256]{3,2,1,0:T(8,128)S(1)}, f32[2,8,64,256]{3,2,1,0:T(8,128)}, u32[]{:S(2)}) copy-start(f32[2,8,64,256]{3,2,1,0:T(8,128)} %get-tuple-element.34.keep_ref.refs_0_) | copy-start | bytes 3145732
  10.4 7.9 %collective-permute-start.1 = (f32[2,8,64,256]{3,2,1,0:T(8,128)}, f32[2,8,64,256]{3,2,1,0:T(8,128)S(1)}, u32[]{:S(2)}, u32[]{:S(2)}) collective-permute-start(f32[2,8,64,256]{3,2,1,0:T(8,128)} %get-tuple-element.35), channel_id=1, source_target_pairs={{0,8},{8,0},{16,24},{24,16},{1,9},{9,1},{17,25},{25,17},{2,10},{10... | collective-permute-start | bytes 3145736 | tf_op jit(solution)/shard_map/ppermute | solution.py:654
  18.1 3.2 %collective-permute-start = (f32[2,8,64,256]{3,2,1,0:T(8,128)}, f32[2,8,64,256]{3,2,1,0:T(8,128)S(1)}, u32[]{:S(2)}, u32[]{:S(2)}) collective-permute-start(f32[2,8,64,256]{3,2,1,0:T(8,128)} %get-tuple-element.33), channel_id=1, source_target_pairs={{0,8},{8,0},{16,24},{24,16},{1,9},{9,1},{17,25},{25,17},{2,10},{10... | collective-permute-start | bytes 3145736 | tf_op jit(solution)/shard_map/ppermute | solution.py:654
  18.3 3.0 %copy-start.6 = (f32[2,8,64,256]{3,2,1,0:T(8,128)S(1)}, f32[2,8,64,256]{3,2,1,0:T(8,128)}, u32[]{:S(2)}) copy-start(f32[2,8,64,256]{3,2,1,0:T(8,128)} %get-tuple-element.32.keep_ref.refs_3_) | copy-start | bytes 3145732
  18.4 17.5 %collective-permute-start.2 = (bf16[8,64,256]{2,1,0:T(8,128)(2,1)S(1)}, bf16[8,64,256]{2,1,0:T(8,128)(2,1)S(1)}, u32[]{:S(2)}, u32[]{:S(2)}) collective-permute-start(bf16[8,64,256]{2,1,0:T(8,128)(2,1)S(1)} %core_sum.3), channel_id=1, source_target_pairs={{0,16},{8,24},{16,0},{24,8},{1,17},{9,25},{17,1},{25,9},{2,18},{10... | collective-permute-start | bytes 786440 | tf_op jit(solution)/shard_map/ppermute | solution.py:658
  21.3 14.5 %collective-permute-start.3 = (bf16[8,64,256]{2,1,0:T(8,128)(2,1)S(1)}, bf16[8,64,256]{2,1,0:T(8,128)(2,1)S(1)}, u32[]{:S(2)}, u32[]{:S(2)}) collective-permute-start(bf16[8,64,256]{2,1,0:T(8,128)(2,1)S(1)} %core_sum.4), channel_id=1, source_target_pairs={{0,16},{8,24},{16,0},{24,8},{1,17},{9,25},{17,1},{25,9},{2,18},{10... | collective-permute-start | bytes 786440 | tf_op jit(solution)/shard_map/ppermute | solution.py:658
  35.7 6.9 %copy-start = (f32[2,8,128,256]{3,2,1,0:T(8,128)S(1)}, f32[2,8,128,256]{3,2,1,0:T(8,128)}, u32[]{:S(2)}) copy-start(f32[2,8,128,256]{3,2,1,0:T(8,128)} %get-tuple-element.39.keep_ref) | copy-start | bytes 6291460
  35.8 6.9 %collective-permute-start.4 = (f32[2,8,128,256]{3,2,1,0:T(8,128)}, f32[2,8,128,256]{3,2,1,0:T(8,128)}, u32[]{:S(2)}, u32[]{:S(2)}) collective-permute-start(f32[2,8,128,256]{3,2,1,0:T(8,128)} %get-tuple-element.41), channel_id=1, source_target_pairs={{0,8},{8,0},{16,24},{24,16},{1,9},{9,1},{17,25},{25,17},{2,10},{10... | collective-permute-start | bytes 6291464 | tf_op jit(solution)/shard_map/ppermute | solution.py:654
  36.8 24.3 %all-to-all-start = ((bf16[8,128,256]{2,1,0:T(8,128)(2,1)}), bf16[8,128,256]{2,1,0:T(8,128)(2,1)}, u32[]{:S(2)}, u32[]{:S(2)}) async-start(bf16[8,128,256]{2,1,0:T(8,128)(2,1)} %full_sum.1), calls=%async_computation | async-start | bytes 1048576 | tf_op jit(solution)/shard_map/all_to_all | solution.py:662
  42.6 2.7 %copy-start.4 = (s32[2048]{0:T(1024)S(1)}, s32[2048]{0:T(1024)}, u32[]{:S(2)}) copy-start(s32[2048]{0:T(1024)} %order_ref.9) | copy-start | bytes 24580
  44.8 14.3 %collective-permute-start.5 = (bf16[8,128,256]{2,1,0:T(8,128)(2,1)}, bf16[8,128,256]{2,1,0:T(8,128)(2,1)}, u32[]{:S(2)}, u32[]{:S(2)}) collective-permute-start(bf16[8,128,256]{2,1,0:T(8,128)(2,1)} %core_sum.5), channel_id=1, source_target_pairs={{0,16},{8,24},{16,0},{24,8},{1,17},{9,25},{17,1},{25,9},{2,18},{10... | collective-permute-start | bytes 1572872 | tf_op jit(solution)/shard_map/ppermute | solution.py:658
  48.3 32.1 %copy-start.7 = (s32[4]{0:T(128)S(1)}, s32[4]{0:T(128)}, u32[]{:S(2)}) copy-start(s32[4]{0:T(128)} %offset_ref.1) | copy-start | bytes 52
  48.3 32.1 %copy-start.8 = (f32[4]{0:T(128)S(1)}, f32[4]{0:T(128)}, u32[]{:S(2)}) copy-start(f32[4]{0:T(128)} %weight_ref.1) | copy-start | bytes 52
  48.4 32.1 %copy-start.9 = (bf16[256,128]{1,0:T(8,128)(2,1)S(1)}, bf16[256,128]{1,0:T(8,128)(2,1)}, u32[]{:S(2)}) copy-start(bf16[256,128]{1,0:T(8,128)(2,1)} %constant.67.clone.refs_7_) | copy-start | bytes 196612
  48.4 32.1 %copy-start.10 = (bf16[128,128]{1,0:T(8,128)(2,1)S(1)}, bf16[128,128]{1,0:T(8,128)(2,1)}, u32[]{:S(2)}) copy-start(bf16[128,128]{1,0:T(8,128)(2,1)} %constant.66.clone.refs_6_) | copy-start | bytes 98308
  93.9 17.6 %copy-start.2 = (bf16[8,128,256]{2,1,0:T(8,128)(2,1)}, bf16[8,128,256]{2,1,0:T(8,128)(2,1)S(1)}, u32[]{:S(2)}) copy-start(bf16[8,128,256]{2,1,0:T(8,128)(2,1)S(1)} %get-tuple-element.51) | copy-start | bytes 1572868
  93.9 37.2 %copy-start.1 = (bf16[256,512]{1,0:T(8,128)(2,1)S(1)}, bf16[256,512]{1,0:T(8,128)(2,1)}, u32[]{:S(2)}) copy-start(bf16[256,512]{1,0:T(8,128)(2,1)} %get-tuple-element.54.weight_ref) | copy-start | bytes 786436
  111.5 17.7 %all-to-all-start.3 = ((bf16[8,128,256]{2,1,0:T(8,128)(2,1)}), bf16[8,128,256]{2,1,0:T(8,128)(2,1)S(1)}, u32[]{:S(2)}, u32[]{:S(2)}) async-start(bf16[8,128,256]{2,1,0:T(8,128)(2,1)} %copy-done.2), calls=%async_computation.3 | async-start | bytes 1048576 | tf_op jit(solution)/shard_map/all_to_all | solution.py:687
  115.1 14.0 %collective-permute-start.6 = (bf16[8,128,256]{2,1,0:T(8,128)(2,1)S(1)}, bf16[8,128,256]{2,1,0:T(8,128)(2,1)S(1)}, u32[]{:S(2)}, u32[]{:S(2)}) collective-permute-start(bf16[8,128,256]{2,1,0:T(8,128)(2,1)S(1)} %all_to_all.21.own_ref), channel_id=1, source_target_pairs={{0,16},{8,24},{16,0},{24,8},{1,17},{9,25},{17,1},{25,9},{2,18},{10... | collective-permute-start | bytes 1572872 | tf_op jit(solution)/shard_map/ppermute | solution.py:689
  115.6 14.3 %collective-permute-start.9 = (bf16[8,128,256]{2,1,0:T(8,128)(2,1)S(1)}, bf16[8,128,256]{2,1,0:T(8,128)(2,1)S(1)}, u32[]{:S(2)}, u32[]{:S(2)}) collective-permute-start(bf16[8,128,256]{2,1,0:T(8,128)(2,1)S(1)} %all_to_all.21.own_ref), channel_id=1, source_target_pairs={{0,8},{8,0},{16,24},{24,16},{1,9},{9,1},{17,25},{25,17},{2,10},{10... | collective-permute-start | bytes 1572872 | tf_op jit(solution)/shard_map/ppermute | solution.py:697
  129.2 1.9 %collective-permute-start.10 = (bf16[8,128,256]{2,1,0:T(8,128)(2,1)S(1)}, bf16[8,128,256]{2,1,0:T(8,128)(2,1)S(1)}, u32[]{:S(2)}, u32[]{:S(2)}) collective-permute-start(bf16[8,128,256]{2,1,0:T(8,128)(2,1)S(1)} %collective-permute-done.6.far_ref), channel_id=1, source_target_pairs={{0,8},{8,0},{16,24},{24,16},{1,9},{9,1},{17,25},{25,17},{2,10},{10... | collective-permute-start | bytes 1572872 | tf_op jit(solution)/shard_map/ppermute | solution.py:698
  129.2 14.3 %collective-permute-start.8 = (bf16[8,128,256]{2,1,0:T(8,128)(2,1)S(1)}, bf16[8,128,256]{2,1,0:T(8,128)(2,1)S(1)}, u32[]{:S(2)}, u32[]{:S(2)}) collective-permute-start(bf16[8,128,256]{2,1,0:T(8,128)(2,1)S(1)} %all-to-all-done.3.own_ref), channel_id=1, source_target_pairs={{0,16},{8,24},{16,0},{24,8},{1,17},{9,25},{17,1},{25,9},{2,18},{10... | collective-permute-start | bytes 1572872 | tf_op jit(solution)/shard_map/ppermute | solution.py:694
  129.7 13.8 %collective-permute-start.7 = (bf16[8,128,256]{2,1,0:T(8,128)(2,1)S(1)}, bf16[8,128,256]{2,1,0:T(8,128)(2,1)S(1)}, u32[]{:S(2)}, u32[]{:S(2)}) collective-permute-start(bf16[8,128,256]{2,1,0:T(8,128)(2,1)S(1)} %all-to-all-done.3.own_ref), channel_id=1, source_target_pairs={{0,8},{8,0},{16,24},{24,16},{1,9},{9,1},{17,25},{25,17},{2,10},{10... | collective-permute-start | bytes 1572872 | tf_op jit(solution)/shard_map/ppermute | solution.py:697
  143.5 1.9 %collective-permute-start.11 = (bf16[8,128,256]{2,1,0:T(8,128)(2,1)S(1)}, bf16[8,128,256]{2,1,0:T(8,128)(2,1)S(1)}, u32[]{:S(2)}, u32[]{:S(2)}) collective-permute-start(bf16[8,128,256]{2,1,0:T(8,128)(2,1)S(1)} %collective-permute-done.8.far_ref), channel_id=1, source_target_pairs={{0,8},{8,0},{16,24},{24,16},{1,9},{9,1},{17,25},{25,17},{2,10},{10... | collective-permute-start | bytes 1572872 | tf_op jit(solution)/shard_map/ppermute | solution.py:698
  (1 other events, 0.8 us)

commit v11 on v10

--- a/solution.py
+++ b/solution.py
@@ -463,7 +463,8 @@
 
 def cycle_work(pieces, sizes, places, sort, unsort, offset, where, cycle_weight):
     groups = len(pieces)
-    device_count, count, lanes = pieces[0].shape
+    device_count, _, lanes = pieces[0].shape
+    count = sum(piece.shape[1] for piece in pieces)
     out_shapes = [(device_count, size, lanes) for size in sizes]
     spread, pixel, back, gather = [jnp.asarray(table) for table in fourier_tables()]
     tables = [places, sort, unsort]
@@ -480,7 +481,7 @@
             scratch_shapes=[
                 pltpu.VMEM(spread.shape[1:], BF16),
                 pltpu.VMEM(gather.shape[1:], BF16),
-                pltpu.VMEM((device_count, groups * count, lanes), BF16),
+                pltpu.VMEM((device_count, count, lanes), BF16),
                 pltpu.VMEM((SIDE * PADDED, lanes // 2), F32),
                 pltpu.VMEM((SIDE, SIDE, lanes // 2), F32),
                 pltpu.VMEM((SIDE * PADDED, lanes // 2), F32),
@@ -638,8 +639,10 @@
     core_pairs = [(i, i ^ 1) for i in range(row_count)]
     far_pairs = [(i, i ^ 2) for i in range(row_count)]
     units = local_orders // 32
-    counts = (units // 4, units // 4, units // 2) if units >= 4 else (units // 2, units // 2)
-    counts = [32 * count for count in counts]
+    if local_orders >= 256:
+        counts = [5 * local_orders // 16, 5 * local_orders // 16, 6 * local_orders // 16]
+    else:
+        counts = [local_orders // 2, local_orders // 2]
     kept, others, outgoing, incoming, arrived = [], [], [], [], []
 
     def after(*values):

time: 154 us -> 156 us (1.013)
  local copies, waits for them, and re-layouts: 1.28 us -> 9.13 us
  Pallas kernels: 62.5 us -> 58 us
  blocking collectives: 36.9 us -> 33.1 us
  starting transfers between devices: 17.3 us -> 20.8 us
  waiting for transfers between devices: 33 us -> 30.7 us
    unnamed x22 -> x32, local copies, waits for them, and re-layouts: 0.85 us -> 6.83 us
    ppermute x3, waiting for transfers between devices: 10.8 us -> 6.3 us  [pass_on(): incoming.append(lax.ppermute(outgoing[chunk], 'row', far_pairs))]
    all_to_all x1, waiting for transfers between devices: 0.01 us -> 4.01 us  [deliver(): lax.all_to_all(summed, 'ma', split_axis=0, concat_axis=0, tiled=True)]
    all_to_all x1, blocking collectives: 19.4 us -> 15.6 us  [body(): lax.all_to_all(summed, 'ma', split_axis=0, concat_axis=0, tiled=True)]
  transfers between devices with their start and end apart: 14 -> 14, of which waited for: 5 -> 8; matrix products, arithmetic and copies ran while one was open for 1% -> 3% of each run, Pallas kernels for 21% -> 17%
where the time goes in v11:
time: 156 us; the launch traced here: 154 us
  Pallas kernels  58 us (37%)
  blocking collectives  33.1 us (21%)
  waiting for transfers between devices  30.7 us (20%)
  starting transfers between devices  20.8 us (13%)
  local copies, waits for them, and re-layouts  9.13 us (6%)
  other arithmetic  2.47 us (2%)
    pallas_call x3, Pallas kernels, synth(): pl.pallas_call(functools.partial(synth_kernel, first), grid_spec=pltpu.Pr...  26.6 us
    all_to_all x1, blocking collectives, body(): lax.all_to_all(piece, 'ma', split_axis=0, concat_axis=0, tiled=True)  17.6 us
    all_to_all x1, blocking collectives, body(): lax.all_to_all(summed, 'ma', split_axis=0, concat_axis=0, tiled=True)  15.6 us
    pallas_call x2, Pallas kernels, adjoint(): pl.pallas_call(functools.partial(adjoint_kernel, first), grid_spec=pltpu....  13.7 us
    pallas_call x1, Pallas kernels, cycle_work(): pl.pallas_call(functools.partial(cycle_kernel, groups, sizes), grid_spec=...  13.4 us
    all_to_all x1, waiting for transfers between devices, body(): lax.all_to_all(piece, 'ma', split_axis=0, concat_axis=0, tiled=True)  12.6 us
    ppermute x3, starting transfers between devices, pass_on(): incoming.append(lax.ppermute(outgoing[chunk], 'row', far_pairs))  7.17 us
    unnamed x32, local copies, waits for them, and re-layouts  6.83 us
  transfers between devices with their start and end apart: 14, of which 8 were waited for; matrix products, arithmetic and copies ran while one was open for 3% of the time, Pallas kernels for 17%

profile of v11, /device:TPU:0, one launch (start us, length us, event | category | flops | bytes accessed | tf_op | source)
XLA Modules:
  0.0 154.3 jit_solution(4626495417843941834)
XLA Ops:
  0.0 3.0 %filter_weights.1 = (bf16[512,256]{1,0:T(8,128)(2,1)}, bf16[256,512]{1,0:T(8,128)(2,1)}) custom-call(s32[64]{0:T(128)} %node_ref.1, f32[64]{0:T(128)} %radial_ref.1, f32[64,512]{1,0:T(8,128)} %alpha_ref.1, f32[64,512]{1,0:T(8,128)} %beta_ref.1), custom_call_target="tpu_custom_call" | custom-call | tf_op jit(solution)/shard_map/filter_weights/pallas_call | solution.py:117
  3.1 8.5 %synth.4 = (f32[2,8,80,256]{3,2,1,0:T(8,128)}, f32[2,8,80,256]{3,2,1,0:T(8,128)}) custom-call(s32[2048]{0:T(1024)} %order_ref.9, s32[1]{0:T(128)} %bitcast.where_ref.token_ref, f32[2,256,512]{2,1,0:T(8,128)} %coeffs_ref.5, bf16[512,256]{1,0:T(8,128)(2,1)} %get-tuple-element.31.weight_ref, bf16[256,32,512]{2,1,0:T(8,128)(2,1)} %legendre_ref.9), custom_call_target="tpu_custom_call" | custom-call | flops 2684354560 | bytes 5242880 | tf_op jit(solution)/shard_map/synth/pallas_call | solution.py:187
  12.0 8.5 %synth.3 = (f32[2,8,80,256]{3,2,1,0:T(8,128)}, f32[2,8,80,256]{3,2,1,0:T(8,128)}) custom-call(s32[2048]{0:T(1024)} %order_ref.9, s32[1]{0:T(128)} %bitcast.where_ref.token_ref, f32[2,256,512]{2,1,0:T(8,128)} %coeffs_ref.5, bf16[512,256]{1,0:T(8,128)(2,1)} %get-tuple-element.31.weight_ref, bf16[256,32,512]{2,1,0:T(8,128)(2,1)} %legendre_ref.9), custom_call_target="tpu_custom_call" | custom-call | flops 2684354560 | bytes 5242880 | tf_op jit(solution)/shard_map/synth/pallas_call | solution.py:187
  20.8 2.9 %collective-permute-start.2 = (bf16[8,80,256]{2,1,0:T(8,128)(2,1)S(1)}, bf16[8,80,256]{2,1,0:T(8,128)(2,1)S(1)}, u32[]{:S(2)}, u32[]{:S(2)}) collective-permute-start(bf16[8,80,256]{2,1,0:T(8,128)(2,1)S(1)} %core_sum.3), channel_id=1, source_target_pairs={{0,16},{8,24},{16,0},{24,8},{1,17},{9,25},{17,1},{25,9},{2,18},{10... | collective-permute-start | bytes 983048 | tf_op jit(solution)/shard_map/ppermute | solution.py:661
  23.8 2.7 %collective-permute-start.3 = (bf16[8,80,256]{2,1,0:T(8,128)(2,1)S(1)}, bf16[8,80,256]{2,1,0:T(8,128)(2,1)S(1)}, u32[]{:S(2)}, u32[]{:S(2)}) collective-permute-start(bf16[8,80,256]{2,1,0:T(8,128)(2,1)S(1)} %core_sum.4), channel_id=1, source_target_pairs={{0,16},{8,24},{16,0},{24,8},{1,17},{9,25},{17,1},{25,9},{2,18},{10... | collective-permute-start | bytes 983048 | tf_op jit(solution)/shard_map/ppermute | solution.py:661
  26.6 9.6 %synth.5 = (f32[2,8,96,256]{3,2,1,0:T(8,128)}, f32[2,8,96,256]{3,2,1,0:T(8,128)}) custom-call(s32[2048]{0:T(1024)} %order_ref.9, s32[1]{0:T(128)} %bitcast.where_ref.token_ref, f32[2,256,512]{2,1,0:T(8,128)} %coeffs_ref.5, bf16[512,256]{1,0:T(8,128)(2,1)} %get-tuple-element.31.weight_ref, bf16[256,32,512]{2,1,0:T(8,128)(2,1)} %legendre_ref.9), custom_call_target="tpu_custom_call" | custom-call | flops 3221225472 | bytes 6291456 | tf_op jit(solution)/shard_map/synth/pallas_call | solution.py:187
  36.3 2.5 %collective-permute-done.3.refs_5_ = bf16[8,80,256]{2,1,0:T(8,128)(2,1)S(1)} collective-permute-done((bf16[8,80,256]{2,1,0:T(8,128)(2,1)S(1)}, bf16[8,80,256]{2,1,0:T(8,128)(2,1)S(1)}, u32[]{:S(2)}, u32[]{:S(2)}) %collective-permute-start.3) | collective-permute-done | bytes 327712 | tf_op jit(solution)/shard_map/ppermute | solution.py:661
  38.7 1.3 copy-done.12
  42.4 6.0 %all-to-all-start = ((bf16[8,160,256]{2,1,0:T(8,128)(2,1)}), bf16[8,160,256]{2,1,0:T(8,128)(2,1)}, u32[]{:S(2)}, u32[]{:S(2)}) async-start(bf16[8,160,256]{2,1,0:T(8,128)(2,1)} %copy-done.2), calls=%async_computation | async-start | bytes 1310720 | tf_op jit(solution)/shard_map/all_to_all | solution.py:665
  49.2 1.5 collective-permute-start.5
  53.1 1.4 convert_element_type.14
  55.6 3.8 %collective-permute-done.5.incoming_ref = bf16[8,96,256]{2,1,0:T(8,128)(2,1)S(1)} collective-permute-done((bf16[8,96,256]{2,1,0:T(8,128)(2,1)}, bf16[8,96,256]{2,1,0:T(8,128)(2,1)S(1)}, u32[]{:S(2)}, u32[]{:S(2)}) %collective-permute-start.5) | collective-permute-done | bytes 393248 | tf_op jit(solution)/shard_map/ppermute | solution.py:661
  61.3 4.0 %all-to-all-done.refs_0_ = bf16[8,160,256]{2,1,0:T(8,128)(2,1)} async-done(((bf16[8,160,256]{2,1,0:T(8,128)(2,1)}), bf16[8,160,256]{2,1,0:T(8,128)(2,1)}, u32[]{:S(2)}, u32[]{:S(2)}) %all-to-all-start) | async-done | bytes 655392 | tf_op jit(solution)/shard_map/all_to_all | solution.py:665
  65.3 15.6 %all_to_all.20.refs_1_ = bf16[8,96,256]{2,1,0:T(8,128)(2,1)S(1)} all-to-all(bf16[8,96,256]{2,1,0:T(8,128)(2,1)S(1)} %last_sum.1), channel_id=1, replica_groups=mesh['row'=4,'ma'=8] {'ma'}, dimensions={0} | all-to-all | bytes 786432 | tf_op jit(solution)/shard_map/all_to_all | solution.py:679
  82.5 13.4 %cycle_work.1 = (bf16[8,128,256]{2,1,0:T(8,128)(2,1)S(1)}, bf16[8,128,256]{2,1,0:T(8,128)(2,1)S(1)}) custom-call(s32[4]{0:T(128)S(1)} %copy-done.7, s32[1]{0:T(128)} %bitcast.where_ref.token_ref, f32[4]{0:T(128)S(1)} %copy-done.8, bf16[8,160,256]{2,1,0:T(8,128)(2,1)} %all-to-all-done.refs_0_, bf16[8,96,256]{2,1,0:T(8,128)(2,1)S(1)} %all_to_all.20.refs_1_, ...), custom_call_target="tpu_custom_call" | custom-call | flops 4294967296 | bytes 8388608 | tf_op jit(solution)/shard_map/cycle_work/pallas_call | solution.py:471
  95.9 17.6 %all_to_all.21.own_ref = bf16[8,128,256]{2,1,0:T(8,128)(2,1)S(1)} all-to-all(bf16[8,128,256]{2,1,0:T(8,128)(2,1)S(1)} %get-tuple-element.50), channel_id=1, replica_groups=mesh['row'=4,'ma'=8] {'ma'}, dimensions={0} | all-to-all | bytes 1048576 | tf_op jit(solution)/shard_map/all_to_all | solution.py:690
  113.5 3.6 %all-to-all-start.3 = ((bf16[8,128,256]{2,1,0:T(8,128)(2,1)}), bf16[8,128,256]{2,1,0:T(8,128)(2,1)S(1)}, u32[]{:S(2)}, u32[]{:S(2)}) async-start(bf16[8,128,256]{2,1,0:T(8,128)(2,1)} %copy-done.3), calls=%async_computation.3 | async-start | bytes 1048576 | tf_op jit(solution)/shard_map/all_to_all | solution.py:690
  117.0 1.6 %collective-permute-start.6 = (bf16[8,128,256]{2,1,0:T(8,128)(2,1)S(1)}, bf16[8,128,256]{2,1,0:T(8,128)(2,1)S(1)}, u32[]{:S(2)}, u32[]{:S(2)}) collective-permute-start(bf16[8,128,256]{2,1,0:T(8,128)(2,1)S(1)} %all_to_all.21.own_ref), channel_id=1, source_target_pairs={{0,16},{8,24},{16,0},{24,8},{1,17},{9,25},{17,1},{25,9},{2,18},{10... | collective-permute-start | bytes 1572872 | tf_op jit(solution)/shard_map/ppermute | solution.py:692
  118.6 12.6 %all-to-all-done.3.own_ref = bf16[8,128,256]{2,1,0:T(8,128)(2,1)S(1)} async-done(((bf16[8,128,256]{2,1,0:T(8,128)(2,1)}), bf16[8,128,256]{2,1,0:T(8,128)(2,1)S(1)}, u32[]{:S(2)}, u32[]{:S(2)}) %all-to-all-start.3) | async-done | bytes 524320 | tf_op jit(solution)/shard_map/all_to_all | solution.py:690
  131.2 1.5 collective-permute-start.8
  133.1 6.8 %adjoint.2.refs_0_ = f32[2,256,512]{2,1,0:T(8,128)} custom-call(s32[2048]{0:T(1024)S(1)} %copy-done.4, s32[1]{0:T(128)} %bitcast.where_ref.token_ref, bf16[8,128,256]{2,1,0:T(8,128)(2,1)S(1)} %all_to_all.21.own_ref, bf16[8,128,256]{2,1,0:T(8,128)(2,1)S(1)} %collective-permute-done.9.core_ref, bf16[8,128,256]{2,1,0:T(8,128)(2,1)S(1)} %collective-permute-done.6.far_ref, ...), custom_call_target="tpu_custom_call" | custom-call | flops 2147483648 | bytes 6291456 | tf_op jit(solution)/shard_map/adjoint/pallas_call | solution.py:573
  140.0 5.6 %collective-permute-done.8.far_ref = bf16[8,128,256]{2,1,0:T(8,128)(2,1)S(1)} collective-permute-done((bf16[8,128,256]{2,1,0:T(8,128)(2,1)S(1)}, bf16[8,128,256]{2,1,0:T(8,128)(2,1)S(1)}, u32[]{:S(2)}, u32[]{:S(2)}) %collective-permute-start.8) | collective-permute-done | bytes 524320 | tf_op jit(solution)/shard_map/ppermute | solution.py:697
  145.6 1.9 %collective-permute-done.11.corner_ref = bf16[8,128,256]{2,1,0:T(8,128)(2,1)S(1)} collective-permute-done((bf16[8,128,256]{2,1,0:T(8,128)(2,1)S(1)}, bf16[8,128,256]{2,1,0:T(8,128)(2,1)S(1)}, u32[]{:S(2)}, u32[]{:S(2)}) %collective-permute-start.11) | collective-permute-done | bytes 524320 | tf_op jit(solution)/shard_map/ppermute | solution.py:701
  147.5 6.9 %adjoint.3 = f32[2,256,512]{2,1,0:T(8,128)} custom-call(s32[2048]{0:T(1024)S(1)} %copy-done.4, s32[1]{0:T(128)} %bitcast.where_ref.token_ref, bf16[8,128,256]{2,1,0:T(8,128)(2,1)S(1)} %all-to-all-done.3.own_ref, bf16[8,128,256]{2,1,0:T(8,128)(2,1)S(1)} %collective-permute-done.7.core_ref, ...), custom_call_target="tpu_custom_call", output_to_operand_aliasing={{}: (8, {})} | custom-call | flops 2147483648 | bytes 6291456 | tf_op jit(solution)/shard_map/adjoint/pallas_call | solution.py:573
  (58 shorter events, 11.3 us)
Async XLA Ops:
  11.6 9.1 %copy-start.11 = (f32[2,8,80,256]{3,2,1,0:T(8,128)S(1)}, f32[2,8,80,256]{3,2,1,0:T(8,128)}, u32[]{:S(2)}) copy-start(f32[2,8,80,256]{3,2,1,0:T(8,128)} %get-tuple-element.34.keep_ref.refs_0_) | copy-start | bytes 3932164
  11.6 9.1 %collective-permute-start.1 = (f32[2,8,80,256]{3,2,1,0:T(8,128)}, f32[2,8,80,256]{3,2,1,0:T(8,128)S(1)}, u32[]{:S(2)}, u32[]{:S(2)}) collective-permute-start(f32[2,8,80,256]{3,2,1,0:T(8,128)} %get-tuple-element.35), channel_id=1, source_target_pairs={{0,8},{8,0},{16,24},{24,16},{1,9},{9,1},{17,25},{25,17},{2,10},{10... | collective-permute-start | bytes 3932168 | tf_op jit(solution)/shard_map/ppermute | solution.py:657
  20.5 3.2 %collective-permute-start = (f32[2,8,80,256]{3,2,1,0:T(8,128)}, f32[2,8,80,256]{3,2,1,0:T(8,128)S(1)}, u32[]{:S(2)}, u32[]{:S(2)}) collective-permute-start(f32[2,8,80,256]{3,2,1,0:T(8,128)} %get-tuple-element.33), channel_id=1, source_target_pairs={{0,8},{8,0},{16,24},{24,16},{1,9},{9,1},{17,25},{25,17},{2,10},{10... | collective-permute-start | bytes 3932168 | tf_op jit(solution)/shard_map/ppermute | solution.py:657
  20.7 3.1 %copy-start.13 = (f32[2,8,80,256]{3,2,1,0:T(8,128)S(1)}, f32[2,8,80,256]{3,2,1,0:T(8,128)}, u32[]{:S(2)}) copy-start(f32[2,8,80,256]{3,2,1,0:T(8,128)} %get-tuple-element.32.keep_ref.refs_3_) | copy-start | bytes 3932164
  20.8 15.5 %collective-permute-start.2 = (bf16[8,80,256]{2,1,0:T(8,128)(2,1)S(1)}, bf16[8,80,256]{2,1,0:T(8,128)(2,1)S(1)}, u32[]{:S(2)}, u32[]{:S(2)}) collective-permute-start(bf16[8,80,256]{2,1,0:T(8,128)(2,1)S(1)} %core_sum.3), channel_id=1, source_target_pairs={{0,16},{8,24},{16,0},{24,8},{1,17},{9,25},{17,1},{25,9},{2,18},{10... | collective-permute-start | bytes 983048 | tf_op jit(solution)/shard_map/ppermute | solution.py:661
  23.8 14.9 %collective-permute-start.3 = (bf16[8,80,256]{2,1,0:T(8,128)(2,1)S(1)}, bf16[8,80,256]{2,1,0:T(8,128)(2,1)S(1)}, u32[]{:S(2)}, u32[]{:S(2)}) collective-permute-start(bf16[8,80,256]{2,1,0:T(8,128)(2,1)S(1)} %core_sum.4), channel_id=1, source_target_pairs={{0,16},{8,24},{16,0},{24,8},{1,17},{9,25},{17,1},{25,9},{2,18},{10... | collective-permute-start | bytes 983048 | tf_op jit(solution)/shard_map/ppermute | solution.py:661
  36.2 12.2 %copy-start = (f32[2,8,96,256]{3,2,1,0:T(8,128)S(1)}, f32[2,8,96,256]{3,2,1,0:T(8,128)}, u32[]{:S(2)}) copy-start(f32[2,8,96,256]{3,2,1,0:T(8,128)} %get-tuple-element.39.keep_ref) | copy-start | bytes 4718596
  36.2 12.2 %collective-permute-start.4 = (f32[2,8,96,256]{3,2,1,0:T(8,128)}, f32[2,8,96,256]{3,2,1,0:T(8,128)S(1)}, u32[]{:S(2)}, u32[]{:S(2)}) collective-permute-start(f32[2,8,96,256]{3,2,1,0:T(8,128)} %get-tuple-element.41), channel_id=1, source_target_pairs={{0,8},{8,0},{16,24},{24,16},{1,9},{9,1},{17,25},{25,17},{2,10},{10... | collective-permute-start | bytes 4718600 | tf_op jit(solution)/shard_map/ppermute | solution.py:657
  38.7 1.3 copy-start.12
  40.0 1.3 copy-start.14
  42.4 22.9 %all-to-all-start = ((bf16[8,160,256]{2,1,0:T(8,128)(2,1)}), bf16[8,160,256]{2,1,0:T(8,128)(2,1)}, u32[]{:S(2)}, u32[]{:S(2)}) async-start(bf16[8,160,256]{2,1,0:T(8,128)(2,1)} %copy-done.2), calls=%async_computation | async-start | bytes 1310720 | tf_op jit(solution)/shard_map/all_to_all | solution.py:665
  48.4 2.4 %copy-start.4 = (s32[2048]{0:T(1024)S(1)}, s32[2048]{0:T(1024)}, u32[]{:S(2)}) copy-start(s32[2048]{0:T(1024)} %order_ref.9) | copy-start | bytes 24580
  49.2 10.3 %collective-permute-start.5 = (bf16[8,96,256]{2,1,0:T(8,128)(2,1)}, bf16[8,96,256]{2,1,0:T(8,128)(2,1)S(1)}, u32[]{:S(2)}, u32[]{:S(2)}) collective-permute-start(bf16[8,96,256]{2,1,0:T(8,128)(2,1)} %core_sum.5), channel_id=1, source_target_pairs={{0,16},{8,24},{16,0},{24,8},{1,17},{9,25},{17,1},{25,9},{2,18},{10... | collective-permute-start | bytes 1179656 | tf_op jit(solution)/shard_map/ppermute | solution.py:661
  61.2 19.7 %copy-start.7 = (s32[4]{0:T(128)S(1)}, s32[4]{0:T(128)}, u32[]{:S(2)}) copy-start(s32[4]{0:T(128)} %offset_ref.1) | copy-start | bytes 52
  61.2 19.7 %copy-start.8 = (f32[4]{0:T(128)S(1)}, f32[4]{0:T(128)}, u32[]{:S(2)}) copy-start(f32[4]{0:T(128)} %weight_ref.1) | copy-start | bytes 52
  95.9 17.6 %copy-start.3 = (bf16[8,128,256]{2,1,0:T(8,128)(2,1)}, bf16[8,128,256]{2,1,0:T(8,128)(2,1)S(1)}, u32[]{:S(2)}) copy-start(bf16[8,128,256]{2,1,0:T(8,128)(2,1)S(1)} %get-tuple-element.51) | copy-start | bytes 1572868
  95.9 37.3 %copy-start.1 = (bf16[256,512]{1,0:T(8,128)(2,1)S(1)}, bf16[256,512]{1,0:T(8,128)(2,1)}, u32[]{:S(2)}) copy-start(bf16[256,512]{1,0:T(8,128)(2,1)} %get-tuple-element.54.weight_ref) | copy-start | bytes 786436
  113.5 17.8 %all-to-all-start.3 = ((bf16[8,128,256]{2,1,0:T(8,128)(2,1)}), bf16[8,128,256]{2,1,0:T(8,128)(2,1)S(1)}, u32[]{:S(2)}, u32[]{:S(2)}) async-start(bf16[8,128,256]{2,1,0:T(8,128)(2,1)} %copy-done.3), calls=%async_computation.3 | async-start | bytes 1048576 | tf_op jit(solution)/shard_map/all_to_all | solution.py:690
  117.0 14.2 %collective-permute-start.6 = (bf16[8,128,256]{2,1,0:T(8,128)(2,1)S(1)}, bf16[8,128,256]{2,1,0:T(8,128)(2,1)S(1)}, u32[]{:S(2)}, u32[]{:S(2)}) collective-permute-start(bf16[8,128,256]{2,1,0:T(8,128)(2,1)S(1)} %all_to_all.21.own_ref), channel_id=1, source_target_pairs={{0,16},{8,24},{16,0},{24,8},{1,17},{9,25},{17,1},{25,9},{2,18},{10... | collective-permute-start | bytes 1572872 | tf_op jit(solution)/shard_map/ppermute | solution.py:692
  118.6 14.4 %collective-permute-start.9 = (bf16[8,128,256]{2,1,0:T(8,128)(2,1)S(1)}, bf16[8,128,256]{2,1,0:T(8,128)(2,1)S(1)}, u32[]{:S(2)}, u32[]{:S(2)}) collective-permute-start(bf16[8,128,256]{2,1,0:T(8,128)(2,1)S(1)} %all_to_all.21.own_ref), channel_id=1, source_target_pairs={{0,8},{8,0},{16,24},{24,16},{1,9},{9,1},{17,25},{25,17},{2,10},{10... | collective-permute-start | bytes 1572872 | tf_op jit(solution)/shard_map/ppermute | solution.py:700
  131.2 1.9 %collective-permute-start.10 = (bf16[8,128,256]{2,1,0:T(8,128)(2,1)S(1)}, bf16[8,128,256]{2,1,0:T(8,128)(2,1)S(1)}, u32[]{:S(2)}, u32[]{:S(2)}) collective-permute-start(bf16[8,128,256]{2,1,0:T(8,128)(2,1)S(1)} %collective-permute-done.6.far_ref), channel_id=1, source_target_pairs={{0,8},{8,0},{16,24},{24,16},{1,9},{9,1},{17,25},{25,17},{2,10},{10... | collective-permute-start | bytes 1572872 | tf_op jit(solution)/shard_map/ppermute | solution.py:701
  131.2 14.3 %collective-permute-start.8 = (bf16[8,128,256]{2,1,0:T(8,128)(2,1)S(1)}, bf16[8,128,256]{2,1,0:T(8,128)(2,1)S(1)}, u32[]{:S(2)}, u32[]{:S(2)}) collective-permute-start(bf16[8,128,256]{2,1,0:T(8,128)(2,1)S(1)} %all-to-all-done.3.own_ref), channel_id=1, source_target_pairs={{0,16},{8,24},{16,0},{24,8},{1,17},{9,25},{17,1},{25,9},{2,18},{10... | collective-permute-start | bytes 1572872 | tf_op jit(solution)/shard_map/ppermute | solution.py:697
  132.8 12.8 %collective-permute-start.7 = (bf16[8,128,256]{2,1,0:T(8,128)(2,1)S(1)}, bf16[8,128,256]{2,1,0:T(8,128)(2,1)S(1)}, u32[]{:S(2)}, u32[]{:S(2)}) collective-permute-start(bf16[8,128,256]{2,1,0:T(8,128)(2,1)S(1)} %all-to-all-done.3.own_ref), channel_id=1, source_target_pairs={{0,8},{8,0},{16,24},{24,16},{1,9},{9,1},{17,25},{25,17},{2,10},{10... | collective-permute-start | bytes 1572872 | tf_op jit(solution)/shard_map/ppermute | solution.py:700
  145.6 1.9 %collective-permute-start.11 = (bf16[8,128,256]{2,1,0:T(8,128)(2,1)S(1)}, bf16[8,128,256]{2,1,0:T(8,128)(2,1)S(1)}, u32[]{:S(2)}, u32[]{:S(2)}) collective-permute-start(bf16[8,128,256]{2,1,0:T(8,128)(2,1)S(1)} %collective-permute-done.8.far_ref), channel_id=1, source_target_pairs={{0,8},{8,0},{16,24},{24,16},{1,9},{9,1},{17,25},{25,17},{2,10},{10... | collective-permute-start | bytes 1572872 | tf_op jit(solution)/shard_map/ppermute | solution.py:701
  (6 other events, 5.0 us)
